TPU v7x, 32 devices: a whole 2x2x4 slice. The times are simulated.
32 devices in a mesh: gx: 4 (over y, x), gy: 4 (over z), gz: 2 (over core).
Axes of the slice: x: 2, y: 2, z: 4, core: 2. Of those that a mesh axis runs over, the one named last changes fastest.
Arguments:
- velocity: float32 [3, 32, 64, 8192], P(None, 'gz', 'gx', 'gy'), may hold values from -6 to 6
- blade_pos: float32 [64, 3, 128], P(('gx', 'gy', 'gz')), as said below
- block_turbine: int32 [64], P(('gx', 'gy', 'gz')), may hold values from 0 to 3, as said below
- blade_vel: float32 [64, 3, 128], P(('gx', 'gy', 'gz')), may hold values from -6 to 6
- lift_coeff: float32 [64, 128], P(('gx', 'gy', 'gz')), may hold values from 0.2 to 2
Outputs:
- new_velocity: float32 [3, 32, 64, 8192], P(None, 'gz', 'gx', 'gy')
- point_force: float32 [64, 3, 128], P(('gx', 'gy', 'gz'))
Inputs may be any that keep to these rules, and one draw needn't show every extreme that they name: `block_turbine`: in each turbine row (blocks r * 4 * 2 * 2 onward, one row for each index of gx) every turbine number is named by exactly 4 blocks. `blade_pos`: the points of a block lie in its column: streamwise within its row's cells, spanwise within its turbine's cells, vertically between level 0 and the top level.
All inputs are finite; a program needn't handle non-finite values.
Results may differ from a plain program's by a relative error of at most 0.0003.
Values sent between devices are 32-bit elements; how exact they have to be, the bound alone decides.
No kernel may reach another device: no remote copies, remote signals or barrier semaphores. Data moves between devices by JAX's collectives and lax.ppermute only.
A program may use at most 192 MiB of HBM per device.

v0:
```python
import math

import jax
import jax.numpy as jnp
from jax import lax
from jax.sharding import PartitionSpec as P

mean_wind = 1.0
viscosity = 0.2
smag_coeff = 0.17
time_step = 0.2
smear = 2.0
smear_norm = 1.0 / (smear**3 * math.pi**1.5)


def extended(cells, sides, width):
    for axis, dim in sides:
        count = lax.axis_size(axis)
        ends = count - 1
        head = lax.slice_in_dim(cells, 0, width, axis=dim)
        tail = lax.slice_in_dim(cells, cells.shape[dim] - width, cells.shape[dim], axis=dim)
        cells = jnp.concatenate(
            [
                lax.ppermute(tail, axis, [(i, (i + 1) % count) for i in range(ends)]),
                cells,
                lax.ppermute(head, axis, [((i + 1) % count, i) for i in range(ends)]),
            ],
            axis=dim,
        )
    return cells


def shifted(padded, axis_dim, offset):
    slicer = [slice(None), slice(2, -2), slice(2, -2), slice(2, -2)]
    extent = padded.shape[axis_dim] - 4
    slicer[axis_dim] = slice(2 + offset, 2 + offset + extent)
    return padded[tuple(slicer)]


def derivative(padded, axis_dim):
    near = shifted(padded, axis_dim, 1) - shifted(padded, axis_dim, -1)
    far = shifted(padded, axis_dim, 2) - shifted(padded, axis_dim, -2)
    return (8.0 * near - far) / 12.0


def second(padded, axis_dim):
    return (
        -shifted(padded, axis_dim, 2)
        + 16.0 * shifted(padded, axis_dim, 1)
        - 30.0 * shifted(padded, axis_dim, 0)
        + 16.0 * shifted(padded, axis_dim, -1)
        - shifted(padded, axis_dim, -2)
    ) / 12.0


def tendency(padded, body_force):
    along_x = derivative(padded, 2)
    along_y = derivative(padded, 3)
    along_z = derivative(padded, 1)
    gradients = (along_x, along_y, along_z)
    strain_sq = jnp.zeros(along_x.shape[1:], jnp.float32)
    for row_comp in range(3):
        for col_comp in range(3):
            strain = 0.5 * (gradients[col_comp][row_comp] + gradients[row_comp][col_comp])
            strain_sq = strain_sq + strain * strain
    eddy_visc = smag_coeff * smag_coeff * jnp.sqrt(2.0 * strain_sq)
    laplacian = second(padded, 1) + second(padded, 2) + second(padded, 3)
    return -mean_wind * along_x + (viscosity + eddy_visc[None]) * laplacian + body_force


def blade_force(sampled, blade_vel, lift_coeff):
    relative = sampled - blade_vel
    rel_speed = jnp.sqrt(jnp.sum(relative * relative, axis=1, keepdims=True))
    return -lift_coeff[:, None, :] * rel_speed * relative


def profile(anchor, count, centers):
    cells = (anchor + jnp.arange(count, dtype=jnp.int32)).astype(jnp.float32)
    gap = cells[:, None] - centers[None, :]
    return jnp.exp(-gap * gap / (smear * smear))


def local(velocity, blade_pos, block_turbine, blade_vel, lift_coeff):
    high = lax.Precision.HIGHEST
    components, depth_cells, row_cells, col_cells = velocity.shape
    owned_count = blade_pos.shape[0]
    point_count = blade_pos.shape[2]
    group_size = lax.axis_size(("gy", "gz"))
    row_blocks = owned_count * group_size
    per_turbine = row_blocks // lax.axis_size("gy")
    count = per_turbine * point_count
    turbine = lax.axis_index("gy")
    level_start = lax.axis_index("gz") * depth_cells
    row_start = lax.axis_index("gx") * row_cells
    col_start = turbine * col_cells
    padded = extended(velocity, (("gz", 1), ("gx", 2), ("gy", 3)), 2)
    row_pos, row_turb = (
        lax.all_gather(blade_pos, ("gy", "gz"), axis=0, tiled=True),
        lax.all_gather(block_turbine, ("gy", "gz"), axis=0, tiled=True),
    )
    matched = (row_turb == turbine).astype(jnp.int32)
    ranks = jnp.cumsum(matched) - 1
    slot_range = jnp.arange(per_turbine, dtype=jnp.int32)
    picker = ((ranks[None, :] == slot_range[:, None]) & (matched[None, :] == 1)).astype(jnp.float32)
    mine = jnp.einsum("ks,scp->kcp", picker, row_pos, precision=high)
    centers = mine.transpose(1, 0, 2).reshape(3, count)
    weight_x = profile(row_start, row_cells, centers[0])
    weight_y = profile(col_start, col_cells, centers[1])
    weight_z = profile(level_start, depth_cells, centers[2])
    plane = (weight_z[:, None, :] * weight_x[None, :, :]).reshape(depth_cells * row_cells, count)
    flat_vel = velocity.reshape(components * depth_cells * row_cells, col_cells)
    along = jnp.dot(flat_vel, weight_y, precision=high, preferred_element_type=jnp.float32)
    along = along.reshape(components, depth_cells * row_cells, count)
    partial_value = smear_norm * jnp.sum(along * plane[None], axis=1)
    partial_value = partial_value.reshape(components, per_turbine, point_count).transpose(1, 0, 2)
    table = jnp.einsum("ks,kcp->scp", picker, partial_value, precision=high)
    sampled = lax.psum_scatter(table, ("gy", "gz"), scatter_dimension=0, tiled=True)
    forces = blade_force(sampled, blade_vel, lift_coeff)
    row_force = lax.all_gather(forces, ("gy", "gz"), axis=0, tiled=True)
    slot_force = jnp.einsum("ks,scp->kcp", picker, row_force, precision=high)
    flat_force = slot_force.transpose(1, 0, 2).reshape(components, count)
    weighted = (smear_norm * flat_force[:, None, :] * plane[None]).reshape(
        components * depth_cells * row_cells, count
    )
    body_force = lax.dot_general(
        weighted,
        weight_y,
        (((1,), (1,)), ((), ())),
        precision=high,
        preferred_element_type=jnp.float32,
    )
    body_force = body_force.reshape(components, depth_cells, row_cells, col_cells)
    new_velocity = velocity + time_step * tendency(padded, body_force)
    return (new_velocity, forces)


def solution(mesh):
    in_specs = (
        P(None, "gz", "gx", "gy"),
        P(("gx", "gy", "gz"), None, None),
        P(("gx", "gy", "gz")),
        P(("gx", "gy", "gz"), None, None),
        P(("gx", "gy", "gz"), None),
    )
    out_specs = (P(None, "gz", "gx", "gy"), P(("gx", "gy", "gz"), None, None))
    return jax.shard_map(local, mesh=mesh, in_specs=in_specs, out_specs=out_specs, check_vma=False)
```

profile of v0, /device:TPU:6, one launch (start us, length us, event | category | flops | bytes accessed | tf_op | source)
XLA Modules:
  0.0 288.9 jit_solution(8681396335287077347)
XLA Ops:
  0.6 2.7 fusion.72
  3.3 2.6 collective-permute-start
  6.0 1.3 collective-permute-start.1
  7.3 1.4 fusion.73
  9.2 0.9 dynamic-update-slice
  10.1 10.7 %all-reduce = s32[16]{0:T(128)S(1)} all-reduce(s32[16]{0:T(128)S(1)} %dynamic-update-slice), channel_id=1, replica_groups=mesh['gx'=4,'gy'=4,'gz'=2] {'gy','gz'}, use_global_device_ids=true, to_apply=%add | all-reduce | flops 16 | bytes 128
  21.0 0.7 copy.16
  21.7 14.0 %all_gather.10 = f32[16,3,128]{2,1,0:T(4,128)S(1)} all-gather(f32[2,3,128]{2,1,0:T(4,128)S(1)} %copy.16), channel_id=1, replica_groups=mesh['gx'=4,'gy'=4,'gz'=2] {'gy','gz'}, dimensions={0}, use_global_device_ids=true | all-gather | bytes 27648 | tf_op jit(solution)/shard_map/all_gather | solution.py:98
  35.9 24.0 %fusion.48 = f32[768,512]{0,1:T(8,128)S(1)} fusion(f32[768,2048]{1,0:T(8,128)} %bitcast.45, f32[512]{0:T(512)S(1)} %get-tuple-element.19, f32[2048]{0:T(1024)S(1)} %add_convert_fusion), kind=kOutput, calls=%fused_computation.67 | convolution fusion | flops 9667870720 | bytes 7874560 | tf_op jit(solution)/shard_map/dot_general | solution.py:112
  60.8 0.5 copy-done.1
  62.2 26.1 %all-reduce.1 = f32[16,3,128]{2,0,1:T(8,128)S(1)} all-reduce(f32[16,3,128]{2,0,1:T(8,128)S(1)} %fusion.60), channel_id=2, replica_groups=mesh['gx'=4,'gy'=4,'gz'=2] {'gy','gz'}, use_global_device_ids=true, to_apply=%region_2.3.clone | all-reduce | flops 6144 | bytes 49152
  88.4 14.2 %all_gather.11 = f32[16,3,128]{2,1,0:T(4,128)S(1)} all-gather(f32[2,3,128]{2,1,0:T(4,128)S(1)} %copy.19), channel_id=1, replica_groups=mesh['gx'=4,'gy'=4,'gz'=2] {'gy','gz'}, dimensions={0}, use_global_device_ids=true | all-gather | bytes 27648 | tf_op jit(solution)/shard_map/all_gather | solution.py:119
  102.6 2.5 constant_dynamic-update-slice_fusion.6
  105.1 11.8 %constant_dynamic-update-slice_fusion.4 = (f32[3,18,16,2048]{3,2,1,0:T(8,128)}, f32[3,18,16,2048]{3,2,1,0:T(8,128)}, f32[3,20,16,2048]{3,2,1,0:T(8,128)}) fusion(f32[3,16,16,2048]{3,2,1,0:T(8,128)} %param.5, f32[3,18,16,2048]{3,2,1,0:T(8,128)} %get-tuple-element.15, f32[3,20,16,2048]{3,2,1,0:T(8,128)} %get-tuple-element.16), kind=kLoop, calls=%fused_computation.89 | loop fusion | bytes 25165824
  116.9 2.5 constant_dynamic-update-slice_fusion.3
  119.4 4.5 %fusion.71 = (f32[3,20,2,2048]{3,2,1,0:T(2,128)S(1)}, f32[3,20,2,2048]{3,2,1,0:T(2,128)S(1)}) fusion(f32[3,20,16,2048]{3,2,1,0:T(8,128)} %get-tuple-element.14), kind=kLoop, calls=%fused_computation.115 | loop fusion | bytes 3932160 | tf_op jit(solution)/shard_map/slice | solution.py:21
  123.9 2.5 collective-permute-start.2
  126.4 1.3 collective-permute-start.3
  127.8 12.9 %subtract_multiply_fusion = f32[3,16,16,2048]{3,2,1,0:T(8,128)} fusion(f32[3,18,16,2048]{3,2,1,0:T(8,128)} %get-tuple-element.9, f32[3,18,16,2048]{3,2,1,0:T(8,128)} %get-tuple-element.13), kind=kLoop, calls=%fused_computation.18 | loop fusion | flops 7864320 | bytes 31457280 | tf_op jit(solution)/shard_map/div | solution.py:43
  140.7 7.1 %collective-permute-done.2 = f32[3,20,2,2048]{3,2,1,0:T(2,128)S(1)} collective-permute-done((f32[3,20,2,2048]{3,2,1,0:T(2,128)S(1)}, f32[3,20,2,2048]{3,2,1,0:T(2,128)S(1)}, u32[]{:S(2)}, u32[]{:S(2)}) %collective-permute-start.2) | collective-permute-done | bytes 983072 | tf_op jit(solution)/shard_map/ppermute | solution.py:26
  147.8 23.0 %collective-permute-done.3 = f32[3,20,2,2048]{3,2,1,0:T(2,128)S(1)} collective-permute-done((f32[3,20,2,2048]{3,2,1,0:T(2,128)S(1)}, f32[3,20,2,2048]{3,2,1,0:T(2,128)S(1)}, u32[]{:S(2)}, u32[]{:S(2)}) %collective-permute-start.3) | collective-permute-done | bytes 983072 | tf_op jit(solution)/shard_map/ppermute | solution.py:24
  170.7 1.3 pad_maximum_fusion.5
  172.1 1.6 copy.11
  173.7 1.3 collective-permute-start.4
  175.4 4.8 %collective-permute-start.5 = (f32[3,20,20,2]{2,3,1,0:T(2,128)S(1)}, f32[3,20,20,2]{2,3,1,0:T(2,128)S(1)}, u32[]{:S(2)}, u32[]{:S(2)}) collective-permute-start(f32[3,20,20,2]{2,3,1,0:T(2,128)S(1)} %copy.13), channel_id=1, source_target_pairs={{0,2},{2,4},{4,6},{1,3},{3,5},{5,7},{8,10},{10,12},{12,14},{9,11},... | collective-permute-start | bytes 28808 | tf_op jit(solution)/shard_map/ppermute | solution.py:24
  180.2 15.6 %fusion.7 = f32[3,16,16,2048]{3,2,1,0:T(8,128)} fusion(f32[3,20,2,2048]{3,2,1,0:T(2,128)S(1)} %collective-permute-done.2, f32[3,20,16,2048]{3,2,1,0:T(8,128)} %get-tuple-element.14, f32[3,20,2,2048]{3,2,1,0:T(2,128)S(1)} %collective-permute-done.3), kind=kLoop, calls=%fused_computation.21 | loop fusion | flops 14155776 | bytes 16121856 | tf_op jit(solution)/shard_map/div | solution.py:43
  195.9 1.4 copy.12
  197.2 1.4 copy.14
  198.6 21.2 %pad_maximum_fusion = (f32[3,20,20,2050]{3,2,1,0:T(8,128)}, f32[3,20,20,2050]{3,2,1,0:T(8,128)}) fusion(f32[3,20,20,2]{3,2,1,0:T(8,128)} %copy.12, f32[3,20,2,2048]{3,2,1,0:T(2,128)S(1)} %collective-permute-done.2, f32[3,20,16,2048]{3,2,1,0:T(8,128)} %get-tuple-element.14, f32[3,20,2,2048]{3,2,1,0:T(2,128)} %copy-done, f32[3,20,20,2]{3,2,1,0:T(8,128)} %copy.14), kind=kLoop, calls=%fused_computation | loop fusion | flops 14760000 | bytes 29529600 | tf_op jit(solution)/shard_map/concatenate | solution.py:22
  219.8 18.2 %subtract_multiply_fusion.1 = f32[3,16,16,2048]{3,2,1,0:T(8,128)} fusion(f32[3,20,20,2050]{3,2,1,0:T(8,128)} %get-tuple-element.3, f32[3,20,20,2050]{3,2,1,0:T(8,128)} %get-tuple-element.2), kind=kLoop, calls=%fused_computation.19 | loop fusion | flops 7864320 | bytes 31457280 | tf_op jit(solution)/shard_map/div | solution.py:43
  238.0 6.9 %fusion.23 = f32[16,16,2048]{2,1,0:T(8,128)} fusion(f32[3,16,16,2048]{3,2,1,0:T(8,128)} %subtract_multiply_fusion, f32[3,16,16,2048]{3,2,1,0:T(8,128)} %subtract_multiply_fusion.1, f32[3,16,16,2048]{3,2,1,0:T(8,128)S(1)} %bitcast.44), kind=kLoop, calls=%fused_computation.36 | loop fusion | flops 15728640 | bytes 20971520 | tf_op jit(solution)/shard_map/mul | solution.py:68
  244.9 43.8 %fusion.4 = f32[3,16,16,2048]{3,2,1,0:T(8,128)} fusion(f32[3,16,16,2048]{3,2,1,0:T(8,128)} %param.5, f32[3,20,20,2050]{3,2,1,0:T(8,128)} %get-tuple-element.3, f32[3,20,20,2050]{3,2,1,0:T(8,128)} %get-tuple-element.2, f32[3,18,16,2048]{3,2,1,0:T(8,128)} %get-tuple-element.9, f32[3,18,16,2048]{3,2,1,0:T(8,128)} %get-tuple-element.13, ...), kind=kOutput, calls=%fused_computation.13 | convolution fusion | flops 9728032768 | bytes 75382784 | tf_op jit(solution)/shard_map/dot_general | solution.py:125
  (47 shorter events, 2.2 us)
Async XLA Ops:
  3.3 99.3 %collective-permute-start = (f32[3,2,16,2048]{3,2,1,0:T(8,128)}, f32[3,2,16,2048]{3,2,1,0:T(8,128)}, u32[]{:S(2)}, u32[]{:S(2)}) collective-permute-start(f32[3,2,16,2048]{3,2,1,0:T(8,128)} %get-tuple-element.12), channel_id=1, source_target_pairs={{0,1},{2,3},{4,5},{6,7},{8,9},{10,11},{12,13},{14,15},{16,17},{18,... | collective-permute-start | bytes 2359304 | tf_op jit(solution)/shard_map/ppermute | solution.py:24
  6.0 110.9 %collective-permute-start.1 = (f32[3,2,16,2048]{3,2,1,0:T(8,128)}, f32[3,2,16,2048]{3,2,1,0:T(8,128)}, u32[]{:S(2)}, u32[]{:S(2)}) collective-permute-start(f32[3,2,16,2048]{3,2,1,0:T(8,128)} %get-tuple-element.11), channel_id=1, source_target_pairs={{1,0},{3,2},{5,4},{7,6},{9,8},{11,10},{13,12},{15,14},{17,16},{19,... | collective-permute-start | bytes 2359304 | tf_op jit(solution)/shard_map/ppermute | solution.py:26
  35.9 52.4 %copy-start.3 = (f32[2,3,128]{2,0,1:T(2,128)S(1)}, f32[2,3,128]{2,0,1:T(2,128)}, u32[]{:S(2)}) copy-start(f32[2,3,128]{2,0,1:T(2,128)} %param.8) | copy-start | bytes 9220
  35.9 52.4 %copy-start.4 = (f32[2,128]{1,0:T(2,128)S(1)}, f32[2,128]{1,0:T(2,128)}, u32[]{:S(2)}) copy-start(f32[2,128]{1,0:T(2,128)} %param.9) | copy-start | bytes 3076
  60.5 0.8 copy-start.1
  88.4 28.5 %copy-start.2 = (f32[2,3,128]{2,0,1:T(2,128)}, f32[2,3,128]{2,0,1:T(2,128)S(1)}, u32[]{:S(2)}) copy-start(f32[2,3,128]{2,0,1:T(2,128)S(1)} %broadcast_multiply_fusion.2) | copy-start | bytes 9220
  119.4 51.3 %slice-start = ((s8[7864320]{0:T(1024)(128)(4,1)}), s8[4194304]{0:T(1024)(128)(4,1)S(1)}, s32[]{:S(2)}) async-start(s8[7864320]{0:T(1024)(128)(4,1)} %bitcast.41), calls=%async_computation | async-start | bytes 8388608
  123.9 23.9 %collective-permute-start.2 = (f32[3,20,2,2048]{3,2,1,0:T(2,128)S(1)}, f32[3,20,2,2048]{3,2,1,0:T(2,128)S(1)}, u32[]{:S(2)}, u32[]{:S(2)}) collective-permute-start(f32[3,20,2,2048]{3,2,1,0:T(2,128)S(1)} %get-tuple-element.7), channel_id=1, source_target_pairs={{8,0},{16,8},{24,16},{9,1},{17,9},{25,17},{10,2},{18,10},{26,18},{... | collective-permute-start | bytes 2949128 | tf_op jit(solution)/shard_map/ppermute | solution.py:26
  126.4 44.4 %collective-permute-start.3 = (f32[3,20,2,2048]{3,2,1,0:T(2,128)S(1)}, f32[3,20,2,2048]{3,2,1,0:T(2,128)S(1)}, u32[]{:S(2)}, u32[]{:S(2)}) collective-permute-start(f32[3,20,2,2048]{3,2,1,0:T(2,128)S(1)} %get-tuple-element.6), channel_id=1, source_target_pairs={{0,8},{8,16},{16,24},{1,9},{9,17},{17,25},{2,10},{10,18},{18,26},{... | collective-permute-start | bytes 2949128 | tf_op jit(solution)/shard_map/ppermute | solution.py:24
  127.8 42.9 %slice-start.1 = ((s8[7864320]{0:T(1024)(128)(4,1)}), s8[3670016]{0:T(1024)(128)(4,1)S(1)}, s32[]{:S(2)}) async-start(s8[7864320]{0:T(1024)(128)(4,1)} %bitcast.41), calls=%async_computation.1 | async-start | bytes 7340032
  170.7 9.5 %copy-start = (f32[3,20,2,2048]{3,2,1,0:T(2,128)}, f32[3,20,2,2048]{3,2,1,0:T(2,128)S(1)}, u32[]{:S(2)}) copy-start(f32[3,20,2,2048]{3,2,1,0:T(2,128)S(1)} %collective-permute-done.3) | copy-start | bytes 2949124
  173.7 22.2 %collective-permute-start.4 = (f32[3,20,20,2]{2,3,1,0:T(2,128)S(1)}, f32[3,20,20,2]{2,3,1,0:T(2,128)S(1)}, u32[]{:S(2)}, u32[]{:S(2)}) collective-permute-start(f32[3,20,20,2]{2,3,1,0:T(2,128)S(1)} %copy.11), channel_id=1, source_target_pairs={{2,0},{4,2},{6,4},{3,1},{5,3},{7,5},{10,8},{12,10},{14,12},{11,9},... | collective-permute-start | bytes 28808 | tf_op jit(solution)/shard_map/ppermute | solution.py:26
  175.4 21.8 %collective-permute-start.5 = (f32[3,20,20,2]{2,3,1,0:T(2,128)S(1)}, f32[3,20,20,2]{2,3,1,0:T(2,128)S(1)}, u32[]{:S(2)}, u32[]{:S(2)}) collective-permute-start(f32[3,20,20,2]{2,3,1,0:T(2,128)S(1)} %copy.13), channel_id=1, source_target_pairs={{0,2},{2,4},{4,6},{1,3},{3,5},{5,7},{8,10},{10,12},{12,14},{9,11},... | collective-permute-start | bytes 28808 | tf_op jit(solution)/shard_map/ppermute | solution.py:24
  197.2 40.7 %slice-start.2 = ((s8[6291456]{0:T(1024)(128)(4,1)}), s8[2097152]{0:T(1024)(128)(4,1)S(1)}, s32[]{:S(2)}) async-start(s8[6291456]{0:T(1024)(128)(4,1)} %bitcast.43), calls=%async_computation.2 | async-start | bytes 4194304
  198.6 39.4 %slice-start.3 = ((s8[6291456]{0:T(1024)(128)(4,1)}), s8[4194304]{0:T(1024)(128)(4,1)S(1)}, s32[]{:S(2)}) async-start(s8[6291456]{0:T(1024)(128)(4,1)} %bitcast.43), calls=%async_computation.3 | async-start | bytes 8388608
where the time goes:
time: 289 us
  other arithmetic  76.7 us (27%)
  matrix products  68.2 us (24%)
  blocking collectives  65 us (22%)
  local copies, waits for them, and re-layouts  32.8 us (11%)
  waiting for transfers between devices  30 us (10%)
  starting transfers between devices  13.7 us (5%)
    div x3, other arithmetic, derivative(): return (8.0 * near - far) / 12.0  46.7 us
    dot_general x1, matrix products, local(): lax.dot_general(weighted, weight_y, (((1,), (1,)), ((), ())), precision=h...  43.8 us
    unnamed x2, blocking collectives  36.8 us
    dot_general x1, matrix products, local(): jnp.dot(flat_vel, weight_y, precision=high, preferred_element_type=jnp.fl...  24 us
    ppermute x3, waiting for transfers between devices, extended(): lax.ppermute(tail, axis, [(i, (i + 1) % count) for i in range(ends)])  23 us
    concatenate x1, other arithmetic, extended(): jnp.concatenate([lax.ppermute(tail, axis, [(i, (i + 1) % count) for i in...  21.2 us
    unnamed x25, local copies, waits for them, and re-layouts  17.8 us
    all_gather x1, blocking collectives, local(): row_force = lax.all_gather(forces, ('gy', 'gz'), axis=0, tiled=True)  14.2 us
  transfers between devices with their start and end apart: 6, of which 2 were waited for; matrix products, arithmetic and copies ran while one was open for 25% of the time, Pallas kernels for 0%

commit v1 on v0

v1 whole, which is shorter than its diff:
```python
import functools
import math

import jax
import jax.numpy as jnp
import ml_dtypes
import numpy as np
from jax import lax
from jax.experimental import pallas as pl
from jax.experimental.pallas import tpu as pltpu
from jax.sharding import PartitionSpec as P

mean_wind = 1.0
viscosity = 0.2
smag_coeff = 0.17
time_step = 0.2
smear = 2.0
smear_norm = 1.0 / (smear**3 * math.pi**1.5)

F32 = jnp.float32
BF16 = jnp.bfloat16
VMEM_LIMIT = 60 * 1024 * 1024
LEVELS = 8
STEP = 256
SAMPLE_STEP = 512


def split(value):
    high = value.astype(BF16)
    return high, (value - high.astype(F32)).astype(BF16)


def dot(left, right, contract=0):
    return lax.dot_general(
        left, right, (((1,), (contract,)), ((), ())), preferred_element_type=F32
    )


def gaussian(first, count, centers):
    shape = (count, centers.shape[1])
    cells = (first + lax.broadcasted_iota(jnp.int32, shape, 0)).astype(F32)
    gap = cells - centers
    return jnp.exp(-gap * gap / (smear * smear))


def stencil_operator(row_cells):
    inner = (LEVELS + 4) * row_cells
    width = inner + 4 * LEVELS
    op = np.zeros((2, LEVELS, row_cells, width), np.float32)

    def column(level, row):
        if 0 <= row < row_cells:
            return (level + 2) * row_cells + row
        if row < 0:
            return inner + level * 2 + row + 2
        return inner + 2 * LEVELS + level * 2 + row - row_cells

    for level in range(LEVELS):
        for row in range(row_cells):
            for offset, first, second in ((-2, 1, -1), (-1, -8, 16), (1, 8, 16), (2, -1, -1)):
                op[0, level, row, column(level, row + offset)] += first
                op[1, level, row, column(level, row + offset)] += second
                op[1, level, row, column(level + offset, row)] += second
            op[1, level, row, column(level, row)] -= 90
    return op.reshape(2 * LEVELS * row_cells, width).astype(ml_dtypes.bfloat16)


def edges_kernel(vel_ref, head_ref, tail_ref):
    levels, rows = vel_ref.shape[1:3]
    for level in range(levels):
        head_ref[0, 2 * level : 2 * level + 2, :] = vel_ref[0, level, 0:2, :]
        tail_ref[0, 2 * level : 2 * level + 2, :] = vel_ref[0, level, rows - 2 : rows, :]


def edges(velocity, chunk):
    components, _, rows, cols = velocity.shape
    shape = jax.ShapeDtypeStruct((components, 2 * LEVELS, cols), F32)
    return pl.pallas_call(
        edges_kernel,
        grid=(components,),
        in_specs=[pl.BlockSpec((1, LEVELS, rows, cols), lambda i: (i, chunk, 0, 0))],
        out_specs=[pl.BlockSpec((1, 2 * LEVELS, cols), lambda i: (i, 0, 0))] * 2,
        out_shape=[shape, shape],
        compiler_params=pltpu.CompilerParams(vmem_limit_bytes=VMEM_LIMIT),
        name="edges",
    )(velocity)


def find_slots(turb_ref, turbine, per_turbine, slots_ref):
    found = jnp.int32(0)
    for row in range(turb_ref.shape[0]):
        slots_ref[found] = row
        hit = turb_ref[row] == turbine.astype(F32)
        found = found + hit.astype(jnp.int32)
        found = jnp.minimum(found, per_turbine)


def sample_kernel(
    per_turbine, place_ref, turb_ref, table_ref, vel_ref,
    part_ref, own_ref, high_ref, low_ref, slots_ref, acc_ref,
):
    step = pl.program_id(0)
    components, depth, rows, width = vel_ref.shape
    points = table_ref.shape[2]
    count = per_turbine * points

    @pl.when(step == 0)
    def _():
        find_slots(turb_ref, place_ref[1], per_turbine, slots_ref)
        for k in range(per_turbine):
            own_ref[:, k * points : (k + 1) * points] = table_ref[slots_ref[k]]

    first = (place_ref[1] * pl.num_programs(0) + step) * width
    along_y = gaussian(first, width, own_ref[1:2, :])
    high, low = split(along_y)
    high_ref[...] = high
    low_ref[...] = low
    vel_high, vel_low = split(vel_ref[...].reshape(components * depth * rows, width))
    update = dot(vel_high, high) + dot(vel_high, low) + dot(vel_low, high)

    @pl.when(step == 0)
    def _():
        acc_ref[...] = update

    @pl.when(step > 0)
    def _():
        acc_ref[...] += update

    @pl.when(step == pl.num_programs(0) - 1)
    def _():
        along_x = gaussian(place_ref[0] * rows, rows, own_ref[0:1, :])
        along_z = gaussian(place_ref[2] * depth, depth, own_ref[2:3, :])
        for i in range(components):
            total = jnp.zeros((rows, count), F32)
            for level in range(depth):
                at = (i * depth + level) * rows
                total += acc_ref[at : at + rows, :] * along_z[level : level + 1, :]
            part_ref[i : i + 1, :] = smear_norm * jnp.sum(total * along_x, axis=0, keepdims=True)
        part_ref[components:, :] = jnp.zeros((8 - components, count), F32)


def sample(place, turbines, table, velocity, per_turbine):
    components, depth, rows, cols = velocity.shape
    points = table.shape[2]
    count = per_turbine * points
    smem = pl.BlockSpec(memory_space=pltpu.SMEM)
    whole = pl.BlockSpec((8, count), lambda j: (0, 0))
    weight = pl.BlockSpec((SAMPLE_STEP, count), lambda j: (j, 0))
    return pl.pallas_call(
        functools.partial(sample_kernel, per_turbine),
        grid=(cols // SAMPLE_STEP,),
        in_specs=[
            smem,
            smem,
            pl.BlockSpec(table.shape, lambda j: (0, 0, 0)),
            pl.BlockSpec((components, depth, rows, SAMPLE_STEP), lambda j: (0, 0, 0, j)),
        ],
        out_specs=[whole, whole, weight, weight],
        out_shape=[
            jax.ShapeDtypeStruct((8, count), F32),
            jax.ShapeDtypeStruct((8, count), F32),
            jax.ShapeDtypeStruct((cols, count), BF16),
            jax.ShapeDtypeStruct((cols, count), BF16),
        ],
        scratch_shapes=[
            pltpu.SMEM((per_turbine + 1,), jnp.int32),
            pltpu.VMEM((components * depth * rows, count), F32),
        ],
        compiler_params=pltpu.CompilerParams(vmem_limit_bytes=VMEM_LIMIT),
        name="sample",
    )(place, turbines, table, velocity)


def force_kernel(
    per_turbine, owned, place_ref, turb_ref, mine_ref, other_ref, own_ref,
    force_ref, home_ref, slots_ref,
):
    find_slots(turb_ref, place_ref[1], per_turbine, slots_ref)
    points = own_ref.shape[1] // per_turbine
    relative = mine_ref[0:3, :] + other_ref[0:3, :] - own_ref[3:6, :]
    speed = jnp.sqrt(jnp.sum(relative * relative, axis=0, keepdims=True))
    force = -own_ref[6:7, :] * speed * relative
    force_ref[...] = jnp.zeros(force_ref.shape, F32)
    force_ref[0:3, :] = force
    home_ref[...] = jnp.zeros(home_ref.shape, F32)
    group = 2 * owned
    for k in range(per_turbine):
        slot = slots_ref[k]
        shift = slot // group
        at = slot - shift * group - place_ref[2] * owned

        @pl.when((at >= 0) & (at < owned))
        def _():
            home_ref[shift, at, 0:3, :] = force[:, k * points : (k + 1) * points]


def point_forces(place, turbines, mine, other, own, per_turbine, owned):
    count = own.shape[1]
    points = count // per_turbine
    shifts = turbines.shape[0] // (2 * owned)
    smem = pl.BlockSpec(memory_space=pltpu.SMEM)
    return pl.pallas_call(
        functools.partial(force_kernel, per_turbine, owned),
        in_specs=[smem, smem] + [pl.BlockSpec(memory_space=pltpu.VMEM)] * 3,
        out_specs=[pl.BlockSpec(memory_space=pltpu.VMEM)] * 2,
        out_shape=[
            jax.ShapeDtypeStruct((8, count), F32),
            jax.ShapeDtypeStruct((shifts, owned, 8, points), F32),
        ],
        scratch_shapes=[pltpu.SMEM((per_turbine + 1,), jnp.int32)],
        name="force",
    )(place, turbines, mine, other, own)


def update_kernel(
    chunk, chunks, place_ref, own_ref, force_ref, op_ref, prev_ref, next_ref, high_ref, low_ref,
    vel_ref, lev_ref, left_ref, right_ref, *rest,
):
    out_ref, pad_ref, wide_high, wide_low, grad_ref, lap_ref, body_ref, sems, edge_sems = rest[-9:]
    step = pl.program_id(0)
    steps = pl.num_programs(0)
    components, _, rows, cols = vel_ref.shape
    cells = LEVELS * rows
    low_level = 2 if chunk == 0 else 0
    high_level = LEVELS + 2 if chunk == chunks - 1 else LEVELS + 4
    source = chunk * LEVELS - 2 + low_level
    levels = high_level - low_level

    def column_copy(at):
        return pltpu.make_async_copy(
            vel_ref.at[:, pl.ds(source, levels), :, pl.ds(pl.multiple_of(at * STEP, STEP), STEP)],
            pad_ref.at[:, pl.ds(low_level, levels), :, pl.ds(pl.multiple_of(at * STEP + 128, 128), STEP)],
            sems.at[at],
        )

    left_copy = pltpu.make_async_copy(
        left_ref.at[:, pl.ds(chunk * LEVELS, LEVELS)],
        pad_ref.at[:, pl.ds(2, LEVELS), :, pl.ds(0, 128)],
        edge_sems.at[0],
    )
    right_copy = pltpu.make_async_copy(
        right_ref.at[:, pl.ds(chunk * LEVELS, LEVELS)],
        pad_ref.at[:, pl.ds(2, LEVELS), :, pl.ds(cols + 128, 128)],
        edge_sems.at[1],
    )

    def level_edge(at, core, sem):
        copy = pltpu.make_async_copy(
            lev_ref, pad_ref.at[:, pl.ds(at, 2), :, pl.ds(128, cols)], edge_sems.at[sem]
        )

        @pl.when(place_ref[2] == core)
        def _():
            copy.start()
            copy.wait()

        @pl.when(place_ref[2] != core)
        def _():
            pad_ref[:, at : at + 2, :, 128 : cols + 128] = jnp.zeros((components, 2, rows, cols), F32)

    @pl.when(step == 0)
    def _():
        column_copy(0).start()
        left_copy.start()
        column_copy(1).start()
        for at in range(2, cols // STEP):
            column_copy(at).start()
        right_copy.start()
        if chunk == 0:
            level_edge(0, 1, 2)
        if chunk == chunks - 1:
            level_edge(LEVELS + 2, 0, 3)
        along_x = gaussian(place_ref[0] * rows, rows, own_ref[0:1, :])
        first = (place_ref[2] * chunks + chunk) * LEVELS
        along_z = gaussian(first, LEVELS, own_ref[2:3, :])
        for i in range(components):
            scaled = (time_step * smear_norm) * force_ref[i : i + 1, :] * along_x
            for level in range(LEVELS):
                at = i * cells + level * rows
                high, low = split(scaled * along_z[level : level + 1, :])
                wide_high[at : at + rows, :] = high
                wide_low[at : at + rows, :] = low
        left_copy.wait()
        column_copy(0).wait()

    @pl.when(step < steps - 1)
    def _():
        column_copy(step + 1).wait()

    @pl.when(step == steps - 1)
    def _():
        right_copy.wait()

    base = pl.multiple_of(step * STEP, STEP)
    center = pl.ds(pl.multiple_of(step * STEP + 128, 128), STEP)
    op = op_ref[...]
    for i in range(components):
        inner = pad_ref[i, :, :, center].reshape((LEVELS + 4) * rows, STEP)
        inner_high, inner_low = split(inner)
        prev_high, prev_low = split(prev_ref[i])
        next_high, next_low = split(next_ref[i])
        result = dot(op, jnp.concatenate([inner_high, prev_high, next_high], axis=0))
        result += dot(op, jnp.concatenate([inner_low, prev_low, next_low], axis=0))
        grad_ref[i] = result[:cells].reshape(LEVELS, rows, STEP)
        lap_ref[i] = result[cells:].reshape(LEVELS, rows, STEP)
    high = high_ref[...]
    body = dot(wide_high[...], high, 1) + dot(wide_low[...], high, 1) + dot(wide_high[...], low_ref[...], 1)
    body_ref[...] = body.reshape(components, LEVELS, rows, STEP)

    for level in range(LEVELS):
        along_y, lap, along_z = [], [], []
        for i in range(components):
            window = pad_ref[i, level + 2, :, pl.ds(base, STEP + 256)]
            width = STEP + 256
            middle = window[:, 128 : STEP + 128]
            ahead = pltpu.roll(window, width - 1, 1)[:, 128 : STEP + 128]
            behind = pltpu.roll(window, 1, 1)[:, 128 : STEP + 128]
            ahead2 = pltpu.roll(window, width - 2, 1)[:, 128 : STEP + 128]
            behind2 = pltpu.roll(window, 2, 1)[:, 128 : STEP + 128]
            along_y.append(8.0 * (ahead - behind) - (ahead2 - behind2))
            lap.append(lap_ref[i, level] + (16.0 * (ahead + behind) - (ahead2 + behind2)))
            near = pad_ref[i, level + 3, :, center] - pad_ref[i, level + 1, :, center]
            far = pad_ref[i, level + 4, :, center] - pad_ref[i, level, :, center]
            along_z.append(8.0 * near - far)
        along_x = [grad_ref[i, level] for i in range(components)]
        same = along_x[0] * along_x[0] + along_y[1] * along_y[1] + along_z[2] * along_z[2]
        xy = along_x[1] + along_y[0]
        xz = along_x[2] + along_z[0]
        yz = along_y[2] + along_z[1]
        strain = 2.0 * same + (xy * xy + xz * xz + yz * yz)
        mixing = viscosity + (smag_coeff * smag_coeff / 12.0) * jnp.sqrt(strain)
        for i in range(components):
            change = mixing * lap[i] - mean_wind * along_x[i]
            out_ref[i, level] = (
                pad_ref[i, level + 2, :, center] + (time_step / 12.0) * change + body_ref[i, level]
            )


def update(chunk, chunks, place, own, force, operator, prev, after, high, low, velocity, lev, left, right, partial):
    components, depth, rows, cols = velocity.shape
    count = own.shape[1]
    cells = LEVELS * rows
    smem = pl.BlockSpec(memory_space=pltpu.SMEM)
    hbm = pl.BlockSpec(memory_space=pl.ANY)
    whole = pl.BlockSpec((8, count), lambda j: (0, 0))
    side = pl.BlockSpec((components, 2 * LEVELS, STEP), lambda j: (0, 0, j))
    weight = pl.BlockSpec((STEP, count), lambda j: (j, 0))
    operands = [place, own, force, operator, prev, after, high, low, velocity, lev, left, right]
    in_specs = [smem, whole, whole, pl.BlockSpec(operator.shape, lambda j: (0, 0)), side, side, weight, weight]
    in_specs += [hbm] * 4
    aliases = {}
    if partial is not None:
        aliases = {len(operands): 0}
        operands.append(partial)
        in_specs.append(hbm)
    field = pltpu.VMEM((components, LEVELS, rows, STEP), F32)
    return pl.pallas_call(
        functools.partial(update_kernel, chunk, chunks),
        grid=(cols // STEP,),
        in_specs=in_specs,
        out_specs=pl.BlockSpec((components, LEVELS, rows, STEP), lambda j: (0, chunk, 0, j)),
        out_shape=jax.ShapeDtypeStruct(velocity.shape, F32),
        scratch_shapes=[
            pltpu.VMEM((components, LEVELS + 4, rows, cols + 256), F32),
            pltpu.VMEM((components * cells, count), BF16),
            pltpu.VMEM((components * cells, count), BF16),
            field,
            field,
            field,
            pltpu.SemaphoreType.DMA((cols // STEP,)),
            pltpu.SemaphoreType.DMA((4,)),
        ],
        input_output_aliases=aliases,
        compiler_params=pltpu.CompilerParams(vmem_limit_bytes=VMEM_LIMIT),
        name="update",
    )(*operands)


def local(velocity, blade_pos, block_turbine, blade_vel, lift_coeff):
    components, depth, rows, cols = velocity.shape
    owned, _, points = blade_pos.shape
    gx, gy, gz = (lax.axis_size(axis) for axis in ("gx", "gy", "gz"))
    assert gz == 2 and depth % LEVELS == 0
    core = lax.axis_index("gz")
    place = jnp.stack([lax.axis_index(axis) for axis in ("gx", "gy", "gz")]).astype(jnp.int32)
    per_turbine = owned * gz
    chunks = depth // LEVELS
    swap = [(0, 1), (1, 0)]
    up_x = [(i, i + 1) for i in range(gx - 1)]
    down_x = [(i + 1, i) for i in range(gx - 1)]
    up_y = [(i, i + 1) for i in range(gy - 1)]
    down_y = [(i + 1, i) for i in range(gy - 1)]

    packed = jnp.concatenate(
        [
            blade_pos,
            blade_vel,
            lift_coeff[:, None, :],
            jnp.broadcast_to(block_turbine.astype(F32)[:, None, None], (owned, 1, points)),
        ],
        axis=1,
    )
    twin = lax.ppermute(packed, "gz", swap)
    pair = jnp.where(
        core == 0, jnp.concatenate([packed, twin], axis=0), jnp.concatenate([twin, packed], axis=0)
    )

    before, after = [], []
    for chunk in range(chunks):
        head, tail = edges(velocity, chunk)
        before.append(lax.ppermute(tail, "gx", up_x))
        after.append(lax.ppermute(head, "gx", down_x))

    parts = [pair]
    for shift in range(1, gy):
        parts.append(lax.ppermute(pair, "gy", [(i, (i + shift) % gy) for i in range(gy)]))
    table = jnp.concatenate(parts, axis=0)
    turbines = table[:, 7, 0]

    facing = lax.dynamic_slice_in_dim(velocity, jnp.where(core == 0, depth - 2, 0), 2, axis=1)
    lev = lax.ppermute(facing, "gz", swap)
    left = lax.ppermute(velocity[..., cols - 128 :], "gy", up_y)
    right = lax.ppermute(velocity[..., :128], "gy", down_y)

    mine, own, high, low = sample(place, turbines, table, velocity, per_turbine)
    other = lax.ppermute(mine, "gz", swap)
    force, home = point_forces(place, turbines, mine, other, own, per_turbine, owned)
    result = home[0]
    for shift in range(1, gy):
        result += lax.ppermute(home[shift], "gy", [((i + shift) % gy, i) for i in range(gy)])

    operator = jnp.asarray(stencil_operator(rows))
    new_velocity = None
    for chunk in range(chunks):
        new_velocity = update(
            chunk, chunks, place, own, force, operator, before[chunk], after[chunk],
            high, low, velocity, lev, left, right, new_velocity,
        )
    return (new_velocity, result[:, :3, :])


def solution(mesh):
    in_specs = (
        P(None, "gz", "gx", "gy"),
        P(("gx", "gy", "gz"), None, None),
        P(("gx", "gy", "gz")),
        P(("gx", "gy", "gz"), None, None),
        P(("gx", "gy", "gz"), None),
    )
    out_specs = (P(None, "gz", "gx", "gy"), P(("gx", "gy", "gz"), None, None))
    return jax.shard_map(local, mesh=mesh, in_specs=in_specs, out_specs=out_specs, check_vma=False)
```

time: 289 us -> 101 us (0.35)
  the two profiles are of different devices: /device:TPU:6 before, /device:TPU:0 now
where the time goes in v1:
time: 101 us; the launch traced here: 100 us
  Pallas kernels  43.2 us (43%)
  starting transfers between devices  28.9 us (29%)
  waiting for transfers between devices  16.3 us (16%)
  local copies, waits for them, and re-layouts  8.23 us (8%)
  other arithmetic  2.75 us (3%)
    pallas_call x2, Pallas kernels, update(): pl.pallas_call(functools.partial(update_kernel, chunk, chunks), grid=(col...  25 us
    ppermute x2, waiting for transfers between devices, local(): after.append(lax.ppermute(head, 'gx', down_x))  10.4 us
    pallas_call x1, Pallas kernels, sample(): pl.pallas_call(functools.partial(sample_kernel, per_turbine), grid=(cols...  9.51 us
    ppermute x2, starting transfers between devices, local(): before.append(lax.ppermute(tail, 'gx', up_x))  7.97 us
    pallas_call x2, Pallas kernels, edges(): pl.pallas_call(edges_kernel, grid=(components,), in_specs=[pl.BlockSpec((...  7.24 us
    ppermute x3, starting transfers between devices, local(): lax.ppermute(home[shift], 'gy', [((i + shift) % gy, i) for i in range(gy)])  6.23 us
    ppermute x1, starting transfers between devices, local(): left = lax.ppermute(velocity[..., cols - 128:], 'gy', up_y)  5.14 us
    ppermute x3, starting transfers between devices, local(): lax.ppermute(pair, 'gy', [(i, (i + shift) % gy) for i in range(gy)])  5.1 us
  transfers between devices with their start and end apart: 15, of which 7 were waited for; matrix products, arithmetic and copies ran while one was open for 6% of the time, Pallas kernels for 30%

profile of v1, /device:TPU:0, one launch (start us, length us, event | category | flops | bytes accessed | tf_op | source)
XLA Modules:
  0.0 100.1 jit_solution(12541939032907406987)
XLA Ops:
  2.7 0.7 pad_maximum_fusion.1
  3.9 1.2 %fusion = (f32[3,16,16,128]{3,2,1,0:T(8,128)S(1)}, f32[3,16,16,128]{3,2,1,0:T(8,128)S(1)}) fusion(f32[3,16,16,2048]{3,2,1,0:T(8,128)} %vel_ref.9), kind=kLoop, calls=%fused_computation.13 | loop fusion | bytes 1572864 | tf_op jit(solution)/shard_map/slice | solution.py:423
  5.1 1.3 %collective-permute-start.9 = (f32[3,16,16,128]{3,2,1,0:T(8,128)S(1)}, f32[3,16,16,128]{3,2,1,0:T(8,128)S(1)}, u32[]{:S(2)}, u32[]{:S(2)}) collective-permute-start(f32[3,16,16,128]{3,2,1,0:T(8,128)S(1)} %get-tuple-element.26), channel_id=1, source_target_pairs={{2,0},{4,2},{6,4},{3,1},{5,3},{7,5},{10,8},{12,10},{14,12},{11,9},... | collective-permute-start | bytes 1179656 | tf_op jit(solution)/shard_map/ppermute | solution.py:423
  6.4 5.1 %collective-permute-start.8 = (f32[3,16,16,128]{3,2,1,0:T(8,128)S(1)}, f32[3,16,16,128]{3,2,1,0:T(8,128)S(1)}, u32[]{:S(2)}, u32[]{:S(2)}) collective-permute-start(f32[3,16,16,128]{3,2,1,0:T(8,128)S(1)} %get-tuple-element.27), channel_id=1, source_target_pairs={{0,2},{2,4},{4,6},{1,3},{3,5},{5,7},{8,10},{10,12},{12,14},{9,11},... | collective-permute-start | bytes 1179656 | tf_op jit(solution)/shard_map/ppermute | solution.py:422
  11.6 1.2 %constant_dynamic-slice_fusion = f32[3,2,16,2048]{3,2,1,0:T(8,128)S(1)} fusion(f32[3,16,16,2048]{3,2,1,0:T(8,128)} %vel_ref.9, s32[]{:T(128)S(6)} %select_n.15), kind=kLoop, calls=%fused_computation.12 | loop fusion | bytes 1572868 | tf_op jit(solution)/shard_map/dynamic_slice | solution.py:420
  12.8 0.8 maximum_select_fusion
  13.6 1.9 %collective-permute-start.3 = (f32[4,8,128]{2,1,0:T(8,128)S(1)}, f32[4,8,128]{2,1,0:T(8,128)S(1)}, u32[]{:S(2)}, u32[]{:S(2)}) collective-permute-start(f32[4,8,128]{2,1,0:T(8,128)S(1)} %maximum_select_fusion), channel_id=1, source_target_pairs={{0,6},{2,0},{4,2},{6,4},{1,7},{3,1},{5,3},{7,5},{8,14},{10,8},{12,... | collective-permute-start | bytes 49160 | tf_op jit(solution)/shard_map/ppermute | solution.py:416
  15.5 1.6 %collective-permute-start.2 = (f32[4,8,128]{2,1,0:T(8,128)S(1)}, f32[4,8,128]{2,1,0:T(8,128)S(1)}, u32[]{:S(2)}, u32[]{:S(2)}) collective-permute-start(f32[4,8,128]{2,1,0:T(8,128)S(1)} %maximum_select_fusion), channel_id=1, source_target_pairs={{0,4},{2,6},{4,0},{6,2},{1,5},{3,7},{5,1},{7,3},{8,12},{10,14},{12... | collective-permute-start | bytes 49160 | tf_op jit(solution)/shard_map/ppermute | solution.py:416
  17.1 1.6 %collective-permute-start.1 = (f32[4,8,128]{2,1,0:T(8,128)S(1)}, f32[4,8,128]{2,1,0:T(8,128)S(1)}, u32[]{:S(2)}, u32[]{:S(2)}) collective-permute-start(f32[4,8,128]{2,1,0:T(8,128)S(1)} %maximum_select_fusion), channel_id=1, source_target_pairs={{0,2},{2,4},{4,6},{6,0},{1,3},{3,5},{5,7},{7,1},{8,10},{10,12},{12... | collective-permute-start | bytes 49160 | tf_op jit(solution)/shard_map/ppermute | solution.py:416
  19.3 2.0 %collective-permute-done.3 = f32[4,8,128]{2,1,0:T(8,128)S(1)} collective-permute-done((f32[4,8,128]{2,1,0:T(8,128)S(1)}, f32[4,8,128]{2,1,0:T(8,128)S(1)}, u32[]{:S(2)}, u32[]{:S(2)}) %collective-permute-start.3) | collective-permute-done | bytes 16416 | tf_op jit(solution)/shard_map/ppermute | solution.py:416
  21.5 1.2 %collective-permute-done.1 = f32[4,8,128]{2,1,0:T(8,128)S(1)} collective-permute-done((f32[4,8,128]{2,1,0:T(8,128)S(1)}, f32[4,8,128]{2,1,0:T(8,128)S(1)}, u32[]{:S(2)}, u32[]{:S(2)}) %collective-permute-start.1) | collective-permute-done | bytes 16416 | tf_op jit(solution)/shard_map/ppermute | solution.py:416
  22.6 0.7 slice_reduce_fusion.turb_ref
  23.4 9.5 %sample.1 = (f32[8,512]{1,0:T(8,128)}, f32[8,512]{1,0:T(8,128)}, bf16[2048,512]{1,0:T(8,128)(2,1)}, bf16[2048,512]{1,0:T(8,128)(2,1)}) custom-call(s32[3]{0:T(128)} %pad_add_fusion.place_ref, f32[16]{0:T(128)} %slice_reduce_fusion.turb_ref, f32[16,8,128]{2,1,0:T(8,128)} %copy-done.7, f32[3,16,16,2048]{3,2,1,0:T(8,128)} %vel_ref.9), custom_call_target="tpu_custom_call" | custom-call | tf_op jit(solution)/shard_map/sample/pallas_call | solution.py:149
  32.9 1.4 %collective-permute-done.4.other_ref = f32[8,512]{1,0:T(8,128)S(1)} collective-permute-done((f32[8,512]{1,0:T(8,128)}, f32[8,512]{1,0:T(8,128)S(1)}, u32[]{:S(2)}, u32[]{:S(2)}) %collective-permute-start.4) | collective-permute-done | bytes 16416 | tf_op jit(solution)/shard_map/ppermute | solution.py:426
  34.9 1.5 %force.1 = (f32[8,512]{1,0:T(8,128)}, f32[4,2,8,128]{3,2,1,0:T(8,128)}) custom-call(s32[3]{0:T(128)} %pad_add_fusion.place_ref, f32[16]{0:T(128)} %slice_reduce_fusion.turb_ref, f32[8,512]{1,0:T(8,128)} %get-tuple-element.13.mine_ref, f32[8,512]{1,0:T(8,128)} %copy-done.8, f32[8,512]{1,0:T(8,128)} %get-tuple-element.12.own_ref), custom_call_target="tpu_custom_call" | custom-call | tf_op jit(solution)/shard_map/force/pallas_call | solution.py:202
  36.4 0.7 slice_bitcast_fusion.3
  37.2 1.5 %collective-permute-start.14 = (f32[2,8,128]{2,1,0:T(8,128)S(1)}, f32[2,8,128]{2,1,0:T(8,128)S(1)}, u32[]{:S(2)}, u32[]{:S(2)}) collective-permute-start(f32[2,8,128]{2,1,0:T(8,128)S(1)} %get-tuple-element.29), channel_id=1, source_target_pairs={{6,0},{0,2},{2,4},{4,6},{7,1},{1,3},{3,5},{5,7},{14,8},{8,10},{10,... | collective-permute-start | bytes 24584 | tf_op jit(solution)/shard_map/ppermute | solution.py:430
  38.6 2.8 %collective-permute-start.13 = (f32[2,8,128]{2,1,0:T(8,128)S(1)}, f32[2,8,128]{2,1,0:T(8,128)S(1)}, u32[]{:S(2)}, u32[]{:S(2)}) collective-permute-start(f32[2,8,128]{2,1,0:T(8,128)S(1)} %get-tuple-element.30), channel_id=1, source_target_pairs={{4,0},{6,2},{0,4},{2,6},{5,1},{7,3},{1,5},{3,7},{12,8},{14,10},{8,... | collective-permute-start | bytes 24584 | tf_op jit(solution)/shard_map/ppermute | solution.py:430
  41.5 1.2 %collective-permute-done.14 = f32[2,8,128]{2,1,0:T(8,128)S(1)} collective-permute-done((f32[2,8,128]{2,1,0:T(8,128)S(1)}, f32[2,8,128]{2,1,0:T(8,128)S(1)}, u32[]{:S(2)}, u32[]{:S(2)}) %collective-permute-start.14) | collective-permute-done | bytes 8224 | tf_op jit(solution)/shard_map/ppermute | solution.py:430
  42.6 1.9 %collective-permute-start.12 = (f32[2,8,128]{2,1,0:T(8,128)S(1)}, f32[2,8,128]{2,1,0:T(8,128)S(1)}, u32[]{:S(2)}, u32[]{:S(2)}) collective-permute-start(f32[2,8,128]{2,1,0:T(8,128)S(1)} %get-tuple-element.31), channel_id=1, source_target_pairs={{2,0},{4,2},{6,4},{0,6},{3,1},{5,3},{7,5},{1,7},{10,8},{12,10},{14... | collective-permute-start | bytes 24584 | tf_op jit(solution)/shard_map/ppermute | solution.py:430
  44.5 3.6 %edges.3 = (f32[3,16,2048]{2,1,0:T(8,128)}, f32[3,16,2048]{2,1,0:T(8,128)}) custom-call(f32[3,16,16,2048]{3,2,1,0:T(8,128)} %vel_ref.9), custom_call_target="tpu_custom_call" | custom-call | tf_op jit(solution)/shard_map/edges/pallas_call | solution.py:78
  48.2 3.4 %collective-permute-start.10 = (f32[3,16,2048]{2,1,0:T(8,128)}, f32[3,16,2048]{2,1,0:T(8,128)S(1)}, u32[]{:S(2)}, u32[]{:S(2)}) collective-permute-start(f32[3,16,2048]{2,1,0:T(8,128)} %get-tuple-element.19), channel_id=1, source_target_pairs={{0,8},{8,16},{16,24},{1,9},{9,17},{17,25},{2,10},{10,18},{18,26},{... | collective-permute-start | bytes 1179656 | tf_op jit(solution)/shard_map/ppermute | solution.py:411
  51.6 1.3 %collective-permute-start.11 = (f32[3,16,2048]{2,1,0:T(8,128)}, f32[3,16,2048]{2,1,0:T(8,128)S(1)}, u32[]{:S(2)}, u32[]{:S(2)}) collective-permute-start(f32[3,16,2048]{2,1,0:T(8,128)} %get-tuple-element.20), channel_id=1, source_target_pairs={{8,0},{16,8},{24,16},{9,1},{17,9},{25,17},{10,2},{18,10},{26,18},{... | collective-permute-start | bytes 1179656 | tf_op jit(solution)/shard_map/ppermute | solution.py:412
  52.9 3.6 %edges.2 = (f32[3,16,2048]{2,1,0:T(8,128)}, f32[3,16,2048]{2,1,0:T(8,128)}) custom-call(f32[3,16,16,2048]{3,2,1,0:T(8,128)} %vel_ref.9), custom_call_target="tpu_custom_call" | custom-call | tf_op jit(solution)/shard_map/edges/pallas_call | solution.py:78
  56.5 4.6 %collective-permute-start.5 = (f32[3,16,2048]{2,1,0:T(8,128)}, f32[3,16,2048]{2,1,0:T(8,128)S(1)}, u32[]{:S(2)}, u32[]{:S(2)}) collective-permute-start(f32[3,16,2048]{2,1,0:T(8,128)} %get-tuple-element.15), channel_id=1, source_target_pairs={{0,8},{8,16},{16,24},{1,9},{9,17},{17,25},{2,10},{10,18},{18,26},{... | collective-permute-start | bytes 1179656 | tf_op jit(solution)/shard_map/ppermute | solution.py:411
  61.1 1.3 %collective-permute-start.6 = (f32[3,16,2048]{2,1,0:T(8,128)}, f32[3,16,2048]{2,1,0:T(8,128)S(1)}, u32[]{:S(2)}, u32[]{:S(2)}) collective-permute-start(f32[3,16,2048]{2,1,0:T(8,128)} %get-tuple-element.16), channel_id=1, source_target_pairs={{8,0},{16,8},{24,16},{9,1},{17,9},{25,17},{10,2},{18,10},{26,18},{... | collective-permute-start | bytes 1179656 | tf_op jit(solution)/shard_map/ppermute | solution.py:412
  63.0 8.7 %collective-permute-done.11.next_ref = f32[3,16,2048]{2,1,0:T(8,128)S(1)} collective-permute-done((f32[3,16,2048]{2,1,0:T(8,128)}, f32[3,16,2048]{2,1,0:T(8,128)S(1)}, u32[]{:S(2)}, u32[]{:S(2)}) %collective-permute-start.11) | collective-permute-done | bytes 393248 | tf_op jit(solution)/shard_map/ppermute | solution.py:412
  71.7 0.7 copy-done.5
  72.7 11.8 %update.2.rest_0_ = f32[3,16,16,2048]{3,2,1,0:T(8,128)} custom-call(s32[3]{0:T(128)} %pad_add_fusion.place_ref, f32[8,512]{1,0:T(8,128)} %get-tuple-element.12.own_ref, f32[8,512]{1,0:T(8,128)} %get-tuple-element.14.force_ref, bf16[256,224]{1,0:T(8,128)(2,1)} %constant.19.clone.op_ref, f32[3,16,2048]{2,1,0:T(8,128)} %copy-done.3, f32[3,16,2048]{2,1,0:T(8,128)} %copy-done.5, ...), custom_call_target="tpu_custom_call" | custom-call | tf_op jit(solution)/shard_map/update/pallas_call | solution.py:357
  84.5 1.7 %collective-permute-done.6.next_ref = f32[3,16,2048]{2,1,0:T(8,128)S(1)} collective-permute-done((f32[3,16,2048]{2,1,0:T(8,128)}, f32[3,16,2048]{2,1,0:T(8,128)S(1)}, u32[]{:S(2)}, u32[]{:S(2)}) %collective-permute-start.6) | collective-permute-done | bytes 393248 | tf_op jit(solution)/shard_map/ppermute | solution.py:412
  86.2 0.8 copy-done.6
  87.0 13.1 %update.3 = f32[3,16,16,2048]{3,2,1,0:T(8,128)} custom-call(s32[3]{0:T(128)} %pad_add_fusion.place_ref, f32[8,512]{1,0:T(8,128)} %get-tuple-element.12.own_ref, f32[8,512]{1,0:T(8,128)} %get-tuple-element.14.force_ref, bf16[256,224]{1,0:T(8,128)(2,1)} %constant.19.clone.op_ref, f32[3,16,2048]{2,1,0:T(8,128)} %copy-done.4, ...), custom_call_target="tpu_custom_call", output_to_operand_aliasing={{}: (12, {})} | custom-call | tf_op jit(solution)/shard_map/update/pallas_call | solution.py:357
  (36 shorter events, 4.9 us)
Async XLA Ops:
  3.4 9.4 %collective-permute-start = (f32[2,8,128]{2,1,0:T(8,128)S(1)}, f32[2,8,128]{2,1,0:T(8,128)S(1)}, u32[]{:S(2)}, u32[]{:S(2)}) collective-permute-start(f32[2,8,128]{2,1,0:T(8,128)S(1)} %pad_maximum_fusion.1), channel_id=1, source_target_pairs={{0,1},{1,0},{2,3},{3,2},{4,5},{5,4},{6,7},{7,6},{8,9},{9,8},{10,11... | collective-permute-start | bytes 24584 | tf_op jit(solution)/shard_map/ppermute | solution.py:403
  5.1 51.4 %collective-permute-start.9 = (f32[3,16,16,128]{3,2,1,0:T(8,128)S(1)}, f32[3,16,16,128]{3,2,1,0:T(8,128)S(1)}, u32[]{:S(2)}, u32[]{:S(2)}) collective-permute-start(f32[3,16,16,128]{3,2,1,0:T(8,128)S(1)} %get-tuple-element.26), channel_id=1, source_target_pairs={{2,0},{4,2},{6,4},{3,1},{5,3},{7,5},{10,8},{12,10},{14,12},{11,9},... | collective-permute-start | bytes 1179656 | tf_op jit(solution)/shard_map/ppermute | solution.py:423
  6.4 54.6 %collective-permute-start.8 = (f32[3,16,16,128]{3,2,1,0:T(8,128)S(1)}, f32[3,16,16,128]{3,2,1,0:T(8,128)S(1)}, u32[]{:S(2)}, u32[]{:S(2)}) collective-permute-start(f32[3,16,16,128]{3,2,1,0:T(8,128)S(1)} %get-tuple-element.27), channel_id=1, source_target_pairs={{0,2},{2,4},{4,6},{1,3},{3,5},{5,7},{8,10},{10,12},{12,14},{9,11},... | collective-permute-start | bytes 1179656 | tf_op jit(solution)/shard_map/ppermute | solution.py:422
  13.6 7.7 %collective-permute-start.3 = (f32[4,8,128]{2,1,0:T(8,128)S(1)}, f32[4,8,128]{2,1,0:T(8,128)S(1)}, u32[]{:S(2)}, u32[]{:S(2)}) collective-permute-start(f32[4,8,128]{2,1,0:T(8,128)S(1)} %maximum_select_fusion), channel_id=1, source_target_pairs={{0,6},{2,0},{4,2},{6,4},{1,7},{3,1},{5,3},{7,5},{8,14},{10,8},{12,... | collective-permute-start | bytes 49160 | tf_op jit(solution)/shard_map/ppermute | solution.py:416
  15.5 6.0 %collective-permute-start.2 = (f32[4,8,128]{2,1,0:T(8,128)S(1)}, f32[4,8,128]{2,1,0:T(8,128)S(1)}, u32[]{:S(2)}, u32[]{:S(2)}) collective-permute-start(f32[4,8,128]{2,1,0:T(8,128)S(1)} %maximum_select_fusion), channel_id=1, source_target_pairs={{0,4},{2,6},{4,0},{6,2},{1,5},{3,7},{5,1},{7,3},{8,12},{10,14},{12... | collective-permute-start | bytes 49160 | tf_op jit(solution)/shard_map/ppermute | solution.py:416
  17.1 5.5 %collective-permute-start.1 = (f32[4,8,128]{2,1,0:T(8,128)S(1)}, f32[4,8,128]{2,1,0:T(8,128)S(1)}, u32[]{:S(2)}, u32[]{:S(2)}) collective-permute-start(f32[4,8,128]{2,1,0:T(8,128)S(1)} %maximum_select_fusion), channel_id=1, source_target_pairs={{0,2},{2,4},{4,6},{6,0},{1,3},{3,5},{5,7},{7,1},{8,10},{10,12},{12... | collective-permute-start | bytes 49160 | tf_op jit(solution)/shard_map/ppermute | solution.py:416
  21.3 50.4 %collective-permute-start.7 = (f32[3,2,16,2048]{3,2,1,0:T(8,128)S(1)}, f32[3,2,16,2048]{3,2,1,0:T(8,128)S(1)}, u32[]{:S(2)}, u32[]{:S(2)}) collective-permute-start(f32[3,2,16,2048]{3,2,1,0:T(8,128)S(1)} %constant_dynamic-slice_fusion), channel_id=1, source_target_pairs={{0,1},{1,0},{2,3},{3,2},{4,5},{5,4},{6,7},{7,6},{8,9},{9,8},{10,11... | collective-permute-start | bytes 2359304 | tf_op jit(solution)/shard_map/ppermute | solution.py:421
  22.6 0.7 copy-start.7
  32.9 1.4 %collective-permute-start.4 = (f32[8,512]{1,0:T(8,128)}, f32[8,512]{1,0:T(8,128)S(1)}, u32[]{:S(2)}, u32[]{:S(2)}) collective-permute-start(f32[8,512]{1,0:T(8,128)} %get-tuple-element.13.mine_ref), channel_id=1, source_target_pairs={{0,1},{1,0},{2,3},{3,2},{4,5},{5,4},{6,7},{7,6},{8,9},{9,8},{10,11... | collective-permute-start | bytes 49160 | tf_op jit(solution)/shard_map/ppermute | solution.py:426
  34.3 0.6 copy-start.8
  37.2 5.4 %collective-permute-start.14 = (f32[2,8,128]{2,1,0:T(8,128)S(1)}, f32[2,8,128]{2,1,0:T(8,128)S(1)}, u32[]{:S(2)}, u32[]{:S(2)}) collective-permute-start(f32[2,8,128]{2,1,0:T(8,128)S(1)} %get-tuple-element.29), channel_id=1, source_target_pairs={{6,0},{0,2},{2,4},{4,6},{7,1},{1,3},{3,5},{5,7},{14,8},{8,10},{10,... | collective-permute-start | bytes 24584 | tf_op jit(solution)/shard_map/ppermute | solution.py:430
  38.6 9.5 %collective-permute-start.13 = (f32[2,8,128]{2,1,0:T(8,128)S(1)}, f32[2,8,128]{2,1,0:T(8,128)S(1)}, u32[]{:S(2)}, u32[]{:S(2)}) collective-permute-start(f32[2,8,128]{2,1,0:T(8,128)S(1)} %get-tuple-element.30), channel_id=1, source_target_pairs={{4,0},{6,2},{0,4},{2,6},{5,1},{7,3},{1,5},{3,7},{12,8},{14,10},{8,... | collective-permute-start | bytes 24584 | tf_op jit(solution)/shard_map/ppermute | solution.py:430
  42.6 9.0 %collective-permute-start.12 = (f32[2,8,128]{2,1,0:T(8,128)S(1)}, f32[2,8,128]{2,1,0:T(8,128)S(1)}, u32[]{:S(2)}, u32[]{:S(2)}) collective-permute-start(f32[2,8,128]{2,1,0:T(8,128)S(1)} %get-tuple-element.31), channel_id=1, source_target_pairs={{2,0},{4,2},{6,4},{0,6},{3,1},{5,3},{7,5},{1,7},{10,8},{12,10},{14... | collective-permute-start | bytes 24584 | tf_op jit(solution)/shard_map/ppermute | solution.py:430
  48.2 14.9 %collective-permute-start.10 = (f32[3,16,2048]{2,1,0:T(8,128)}, f32[3,16,2048]{2,1,0:T(8,128)S(1)}, u32[]{:S(2)}, u32[]{:S(2)}) collective-permute-start(f32[3,16,2048]{2,1,0:T(8,128)} %get-tuple-element.19), channel_id=1, source_target_pairs={{0,8},{8,16},{16,24},{1,9},{9,17},{17,25},{2,10},{10,18},{18,26},{... | collective-permute-start | bytes 1179656 | tf_op jit(solution)/shard_map/ppermute | solution.py:411
  51.6 20.1 %collective-permute-start.11 = (f32[3,16,2048]{2,1,0:T(8,128)}, f32[3,16,2048]{2,1,0:T(8,128)S(1)}, u32[]{:S(2)}, u32[]{:S(2)}) collective-permute-start(f32[3,16,2048]{2,1,0:T(8,128)} %get-tuple-element.20), channel_id=1, source_target_pairs={{8,0},{16,8},{24,16},{9,1},{17,9},{25,17},{10,2},{18,10},{26,18},{... | collective-permute-start | bytes 1179656 | tf_op jit(solution)/shard_map/ppermute | solution.py:412
  56.5 15.2 %copy-start.1 = (f32[3,16,16,128]{3,2,1,0:T(8,128)}, f32[3,16,16,128]{3,2,1,0:T(8,128)S(1)}, u32[]{:S(2)}) copy-start(f32[3,16,16,128]{3,2,1,0:T(8,128)S(1)} %collective-permute-done.9.right_ref) | copy-start | bytes 1179652
  56.5 28.0 %collective-permute-start.5 = (f32[3,16,2048]{2,1,0:T(8,128)}, f32[3,16,2048]{2,1,0:T(8,128)S(1)}, u32[]{:S(2)}, u32[]{:S(2)}) collective-permute-start(f32[3,16,2048]{2,1,0:T(8,128)} %get-tuple-element.15), channel_id=1, source_target_pairs={{0,8},{8,16},{16,24},{1,9},{9,17},{17,25},{2,10},{10,18},{18,26},{... | collective-permute-start | bytes 1179656 | tf_op jit(solution)/shard_map/ppermute | solution.py:411
  61.1 10.6 %copy-start.2 = (f32[3,16,16,128]{3,2,1,0:T(8,128)}, f32[3,16,16,128]{3,2,1,0:T(8,128)S(1)}, u32[]{:S(2)}) copy-start(f32[3,16,16,128]{3,2,1,0:T(8,128)S(1)} %collective-permute-done.8.left_ref) | copy-start | bytes 1179652
  61.1 25.1 %collective-permute-start.6 = (f32[3,16,2048]{2,1,0:T(8,128)}, f32[3,16,2048]{2,1,0:T(8,128)S(1)}, u32[]{:S(2)}, u32[]{:S(2)}) collective-permute-start(f32[3,16,2048]{2,1,0:T(8,128)} %get-tuple-element.16), channel_id=1, source_target_pairs={{8,0},{16,8},{24,16},{9,1},{17,9},{25,17},{10,2},{18,10},{26,18},{... | collective-permute-start | bytes 1179656 | tf_op jit(solution)/shard_map/ppermute | solution.py:412
  63.0 8.7 %copy-start.3 = (f32[3,16,2048]{2,1,0:T(8,128)}, f32[3,16,2048]{2,1,0:T(8,128)S(1)}, u32[]{:S(2)}) copy-start(f32[3,16,2048]{2,1,0:T(8,128)S(1)} %collective-permute-done.10.prev_ref) | copy-start | bytes 1179652
  71.7 0.7 copy-start.5
  71.7 1.0 %copy-start = (f32[3,2,16,2048]{3,2,1,0:T(8,128)}, f32[3,2,16,2048]{3,2,1,0:T(8,128)S(1)}, u32[]{:S(2)}) copy-start(f32[3,2,16,2048]{3,2,1,0:T(8,128)S(1)} %collective-permute-done.7.lev_ref) | copy-start | bytes 2359300
  84.5 1.7 %copy-start.4 = (f32[3,16,2048]{2,1,0:T(8,128)}, f32[3,16,2048]{2,1,0:T(8,128)S(1)}, u32[]{:S(2)}) copy-start(f32[3,16,2048]{2,1,0:T(8,128)S(1)} %collective-permute-done.5.prev_ref) | copy-start | bytes 1179652
  86.2 0.8 copy-start.6

commit v2 on v1

v2 whole, which is shorter than its diff:
```python
import functools
import math

import jax
import jax.numpy as jnp
import ml_dtypes
import numpy as np
from jax import lax
from jax.experimental import pallas as pl
from jax.experimental.pallas import tpu as pltpu
from jax.sharding import PartitionSpec as P

mean_wind = 1.0
viscosity = 0.2
smag_coeff = 0.17
time_step = 0.2
smear = 2.0
smear_norm = 1.0 / (smear**3 * math.pi**1.5)

F32 = jnp.float32
BF16 = jnp.bfloat16
MIB = 1024 * 1024
LEVELS = 8
STEP = 256
LIGHT = pl.CostEstimate(flops=0, bytes_accessed=0, transcendentals=0)


def split(value):
    high = value.astype(BF16)
    return high, (value - high.astype(F32)).astype(BF16)


def dot(left, right, contract=0):
    return lax.dot_general(
        left, right, (((1,), (contract,)), ((), ())), preferred_element_type=F32
    )


def gaussian(first, count, centers):
    shape = (count, centers.shape[1])
    cells = (first + lax.broadcasted_iota(jnp.int32, shape, 0)).astype(F32)
    gap = cells - centers
    return jnp.exp(-gap * gap / (smear * smear))


def stencil_operator(row_cells):
    inner = (LEVELS + 4) * row_cells
    width = inner + 4 * LEVELS
    op = np.zeros((2, LEVELS, row_cells, width), np.float32)

    def column(level, row):
        if 0 <= row < row_cells:
            return (level + 2) * row_cells + row
        if row < 0:
            return inner + level * 2 + row + 2
        return inner + 2 * LEVELS + level * 2 + row - row_cells

    for level in range(LEVELS):
        for row in range(row_cells):
            for offset, first, second in ((-2, 1, -1), (-1, -8, 16), (1, 8, 16), (2, -1, -1)):
                op[0, level, row, column(level, row + offset)] += first
                op[1, level, row, column(level, row + offset)] += second
                op[1, level, row, column(level + offset, row)] += second
            op[1, level, row, column(level, row)] -= 90
    op = op.reshape(2 * LEVELS * row_cells, width)
    op = np.pad(op, ((0, 0), (0, -width % 128)))
    return np.concatenate([op, op], axis=1).astype(ml_dtypes.bfloat16)


def prep_kernel(
    turb_ref, pos_ref, speed_ref, lift_ref, vel_ref, up_ref, down_ref, lev_ref, *sides
):
    component = pl.program_id(0)
    levels, rows, cols = vel_ref.shape[1:]
    owned, coords, points = pos_ref.shape
    heads, tails = sides[: len(sides) // 2], sides[len(sides) // 2 :]

    @pl.when(component == 0)
    def _():
        for ref in (up_ref, down_ref):
            for k in range(owned):
                ref[k, 0:coords, :] = pos_ref[k]
                ref[k, coords : 2 * coords, :] = speed_ref[k]
                ref[k, 2 * coords : 2 * coords + 1, :] = lift_ref[k : k + 1, :]
                ref[k, 7:8, :] = jnp.full((1, points), turb_ref[k].astype(F32))

    lev_ref[0] = vel_ref[0, pl.ds(jnp.where(lax.axis_index("gz") == 0, levels - 2, 0), 2)]
    parts = levels * rows // 128
    last = vel_ref[0, :, :, cols - 128 :].reshape(levels * rows, 128)
    first = vel_ref[0, :, :, :128].reshape(levels * rows, 128)
    for part in range(parts):
        cells = slice(part * 128, part * 128 + 128)
        up_ref[owned + component * parts + part] = last[cells].T[120:]
        down_ref[owned + component * parts + part] = first[cells].T[:8]

    row = lax.broadcasted_iota(jnp.int32, (8, cols), 0) // 2
    for group in range(levels // 4):
        at = (group * 4) // LEVELS
        to = (group * 8) % (2 * LEVELS)
        head = tail = None
        for k in range(4):
            top = vel_ref[0, group * 4 + k, 0:8, :]
            end = vel_ref[0, group * 4 + k, rows - 8 : rows, :]
            if k:
                top = pltpu.roll(top, 2 * k, 0)
            if k < 3:
                end = pltpu.roll(end, 2 * k + 2, 0)
            head = top if head is None else jnp.where(row == k, top, head)
            tail = end if tail is None else jnp.where(row == k, end, tail)
        heads[at][0, to : to + 8, :] = head
        tails[at][0, to : to + 8, :] = tail


def prep(velocity, blade_pos, block_turbine, blade_vel, lift_coeff):
    components, levels, rows, cols = velocity.shape
    owned, coords, points = blade_pos.shape
    chunks = levels // LEVELS
    tiles = owned + components * levels * rows // 128
    whole = pl.BlockSpec((owned, coords, points), lambda i: (0, 0, 0))
    message = pl.BlockSpec((tiles, 8, 128), lambda i: (0, 0, 0))
    side = pl.BlockSpec((1, 2 * LEVELS, cols), lambda i: (i, 0, 0))
    side_shape = jax.ShapeDtypeStruct((components, 2 * LEVELS, cols), F32)
    return pl.pallas_call(
        prep_kernel,
        grid=(components,),
        in_specs=[
            pl.BlockSpec(memory_space=pltpu.SMEM),
            whole,
            whole,
            pl.BlockSpec((owned, points), lambda i: (0, 0)),
            pl.BlockSpec((1, levels, rows, cols), lambda i: (i, 0, 0, 0)),
        ],
        out_specs=[
            message,
            message,
            pl.BlockSpec((1, 2, rows, cols), lambda i: (i, 0, 0, 0)),
        ] + [side] * (2 * chunks),
        out_shape=[
            jax.ShapeDtypeStruct((tiles, 8, 128), F32),
            jax.ShapeDtypeStruct((tiles, 8, 128), F32),
            jax.ShapeDtypeStruct((components, 2, rows, cols), F32),
        ] + [side_shape] * (2 * chunks),
        compiler_params=pltpu.CompilerParams(vmem_limit_bytes=24 * MIB),
        cost_estimate=LIGHT,
        name="prep",
    )(block_turbine, blade_pos, blade_vel, lift_coeff, velocity)


def match(mine_ref, twin_ref, per_turbine):
    core = lax.axis_index("gz")
    turbine = lax.axis_index("gy").astype(F32)
    half = mine_ref.shape[0]
    first = [(mine_ref[k, 7:8, :] == turbine).astype(F32) for k in range(half)]
    second = [(twin_ref[k, 7:8, :] == turbine).astype(F32) for k in range(half)]
    masks = []
    for hits, others, leads in ((first, second, core == 0), (second, first, core == 1)):
        rank = jnp.where(leads, jnp.zeros_like(hits[0]), sum(others))
        for hit in hits:
            masks.append([(hit > 0.5) & (rank == k) for k in range(per_turbine)])
            rank = rank + hit
    return masks


def sample_kernel(
    per_turbine, mine_ref, twin_ref, vel_ref, part_ref, own_ref, weight_ref, even_ref, odd_ref, acc_ref
):
    step = pl.program_id(0)
    steps = pl.num_programs(0)
    components, depth, rows, width = vel_ref.shape
    points = mine_ref.shape[2]
    count = per_turbine * points
    half = width // 2
    start = lax.axis_index("gy") * steps * width

    def weights(at, ref):
        high, low = split(gaussian(start + at * half, half, own_ref[1:2, :]))
        ref[:, :count] = high
        ref[:, count:] = low

    def multiply(side, ref):
        cells = vel_ref[:, :, :, side * half : side * half + half]
        high, low = split(cells.reshape(components * depth * rows, half))
        acc_ref[...] += dot(
            jnp.concatenate([high, high, low], axis=1),
            jnp.concatenate([ref[:, :count], ref[:, count:], ref[:, :count]], axis=0),
        )
        weight_ref[side * half : side * half + half, :] = ref[...]

    @pl.when(step == 0)
    def _():
        masks = match(mine_ref, twin_ref, per_turbine)
        blocks = mine_ref.shape[0]
        for k in range(per_turbine):
            total = jnp.zeros((8, points), F32)
            for row, mask in enumerate(masks):
                tile = mine_ref[row] if row < blocks else twin_ref[row - blocks]
                total = jnp.where(mask[k], tile, total)
            own_ref[:, k * points : (k + 1) * points] = total
        weights(0, even_ref)
        acc_ref[...] = jnp.zeros(acc_ref.shape, F32)

    weights(2 * step + 1, odd_ref)
    multiply(0, even_ref)
    weights(2 * step + 2, even_ref)
    multiply(1, odd_ref)

    @pl.when(step == steps - 1)
    def _():
        along_x = gaussian(lax.axis_index("gx") * rows, rows, own_ref[0:1, :])
        along_z = gaussian(lax.axis_index("gz") * depth, depth, own_ref[2:3, :])
        for i in range(components):
            total = jnp.zeros((rows, count), F32)
            for level in range(depth):
                at = (i * depth + level) * rows
                total += acc_ref[at : at + rows, :] * along_z[level : level + 1, :]
            part_ref[i : i + 1, :] = smear_norm * jnp.sum(total * along_x, axis=0, keepdims=True)
        part_ref[components:, :] = jnp.zeros((8 - components, count), F32)


def sample(mine, twin, velocity, per_turbine):
    components, depth, rows, cols = velocity.shape
    points = mine.shape[2]
    count = per_turbine * points
    whole = pl.BlockSpec((8, count), lambda j: (0, 0))
    table = pl.BlockSpec(mine.shape, lambda j: (0, 0, 0))
    return pl.pallas_call(
        functools.partial(sample_kernel, per_turbine),
        grid=(cols // (2 * STEP),),
        in_specs=[
            table,
            table,
            pl.BlockSpec((components, depth, rows, 2 * STEP), lambda j: (0, 0, 0, j)),
        ],
        out_specs=[whole, whole, pl.BlockSpec((2 * STEP, 2 * count), lambda j: (j, 0))],
        out_shape=[
            jax.ShapeDtypeStruct((8, count), F32),
            jax.ShapeDtypeStruct((8, count), F32),
            jax.ShapeDtypeStruct((cols, 2 * count), BF16),
        ],
        scratch_shapes=[
            pltpu.VMEM((STEP, 2 * count), BF16),
            pltpu.VMEM((STEP, 2 * count), BF16),
            pltpu.VMEM((components * depth * rows, count), F32),
        ],
        compiler_params=pltpu.CompilerParams(vmem_limit_bytes=40 * MIB),
        cost_estimate=LIGHT,
        name="sample",
    )(mine, twin, velocity)


def force_kernel(
    per_turbine, owned, mine_ref, twin_ref, part_ref, other_ref, own_ref, force_ref, home_ref
):
    points = own_ref.shape[1] // per_turbine
    relative = part_ref[0:3, :] + other_ref[0:3, :] - own_ref[3:6, :]
    speed = jnp.sqrt(jnp.sum(relative * relative, axis=0, keepdims=True))
    force = -own_ref[6:7, :] * speed * relative
    force_ref[...] = jnp.zeros(force_ref.shape, F32)
    force_ref[0:3, :] = force
    masks = match(mine_ref, twin_ref, per_turbine)
    for row in range(mine_ref.shape[0]):
        total = jnp.zeros((3, points), F32)
        for k in range(per_turbine):
            total = jnp.where(masks[row][k], force[:, k * points : (k + 1) * points], total)
        home_ref[row // owned, row % owned, 0:3, :] = total
        home_ref[row // owned, row % owned, 3:8, :] = jnp.zeros((5, points), F32)


def point_forces(mine, twin, part, other, own, per_turbine, owned):
    count = own.shape[1]
    points = count // per_turbine
    shifts = mine.shape[0] // owned
    return pl.pallas_call(
        functools.partial(force_kernel, per_turbine, owned),
        in_specs=[pl.BlockSpec(memory_space=pltpu.VMEM)] * 5,
        out_specs=[pl.BlockSpec(memory_space=pltpu.VMEM)] * 2,
        out_shape=[
            jax.ShapeDtypeStruct((8, count), F32),
            jax.ShapeDtypeStruct((shifts, owned, 8, points), F32),
        ],
        cost_estimate=LIGHT,
        name="force",
    )(mine, twin, part, other, own)


def update_kernel(chunk, chunks, *refs):
    own_ref, force_ref, op_ref = refs[:3]
    prev_refs, next_refs, weight_refs = refs[3:6], refs[6:9], refs[9:12]
    vel_ref, lev_ref, left_ref, right_ref = refs[12:16]
    out_ref, pad_ref, wide_ref, even, odd, sems, edge_sems = refs[-7:]
    step = pl.program_id(0)
    steps = pl.num_programs(0)
    components, _, rows, cols = vel_ref.shape
    count = own_ref.shape[1]
    cells = LEVELS * rows
    inner = (LEVELS + 4) * rows
    fill = op_ref.shape[1] // 2 - inner - 4 * LEVELS
    blocks = cols // STEP
    low_level = 2 if chunk == 0 else 0
    high_level = LEVELS + 2 if chunk == chunks - 1 else LEVELS + 4
    source = chunk * LEVELS - 2 + low_level
    levels = high_level - low_level

    def column_copy(at):
        return pltpu.make_async_copy(
            vel_ref.at[:, pl.ds(source, levels), :, pl.ds(pl.multiple_of(at * STEP, STEP), STEP)],
            pad_ref.at[:, pl.ds(low_level, levels), :, pl.ds(pl.multiple_of(at * STEP + 128, 128), STEP)],
            sems.at[at],
        )

    def level_edge(at, core, sem):
        copy = pltpu.make_async_copy(
            lev_ref, pad_ref.at[:, pl.ds(at, 2), :, pl.ds(128, cols)], edge_sems.at[sem]
        )

        @pl.when(lax.axis_index("gz") == core)
        def _():
            copy.start()
            copy.wait()

        @pl.when(lax.axis_index("gz") != core)
        def _():
            pad_ref[:, at : at + 2, :, 128 : cols + 128] = jnp.zeros((components, 2, rows, cols), F32)

    def side_columns(ref, present, lane):
        per_part = 128 // rows
        parts = ref.shape[0] // components
        for i in range(components):
            for level in range(LEVELS):
                at = chunk * LEVELS + level
                tile = jnp.where(present, ref[i * parts + at // per_part], 0.0)
                if level % per_part == 0 or level == 0:
                    turned = tile.T
                row = (at % per_part) * rows
                pad_ref[i, level + 2, :, lane : lane + 8] = turned[row : row + rows, :]

    def matrix_part(at, which, bufs):
        grad_ref, lap_ref, body_ref = bufs
        center = pl.ds(pl.multiple_of(at * STEP + 128, 128), STEP)
        op = op_ref[...]
        empty = [jnp.zeros((fill, STEP), BF16)] if fill else []
        for i in range(components):
            inner_high, inner_low = split(pad_ref[i, :, :, center].reshape(inner, STEP))
            prev_high, prev_low = split(prev_refs[which][i])
            next_high, next_low = split(next_refs[which][i])
            high = [inner_high, prev_high, next_high] + empty
            low = [inner_low, prev_low, next_low] + empty
            result = dot(op, jnp.concatenate(high + low, axis=0))
            grad_ref[i] = result[:cells].reshape(LEVELS, rows, STEP)
            lap_ref[i] = result[cells:].reshape(LEVELS, rows, STEP)
        high = weight_refs[which][:, :count]
        low = weight_refs[which][:, count:]
        body = dot(wide_ref[...], jnp.concatenate([high, high, low], axis=1), 1)
        body_ref[...] = body.reshape(components, LEVELS, rows, STEP)

    def vector_part(at, bufs, lane):
        grad_ref, lap_ref, body_ref = bufs
        base = pl.multiple_of(at * STEP, STEP)
        center = pl.ds(pl.multiple_of(at * STEP + 128, 128), STEP)
        width = STEP + 256
        for level in range(LEVELS):
            for row in range(0, rows, 8):
                band = slice(row, row + 8)
                along_y, lap, along_z = [], [], []
                for i in range(components):
                    window = pad_ref[i, level + 2, band, pl.ds(base, width)]
                    ahead = pltpu.roll(window, width - 1, 1)[:, 128 : STEP + 128]
                    behind = pltpu.roll(window, 1, 1)[:, 128 : STEP + 128]
                    ahead2 = pltpu.roll(window, width - 2, 1)[:, 128 : STEP + 128]
                    behind2 = pltpu.roll(window, 2, 1)[:, 128 : STEP + 128]
                    along_y.append(8.0 * (ahead - behind) - (ahead2 - behind2))
                    lap.append(lap_ref[i, level, band] + (16.0 * (ahead + behind) - (ahead2 + behind2)))
                    near = pad_ref[i, level + 3, band, center] - pad_ref[i, level + 1, band, center]
                    far = pad_ref[i, level + 4, band, center] - pad_ref[i, level, band, center]
                    along_z.append(8.0 * near - far)
                along_x = [grad_ref[i, level, band] for i in range(components)]
                same = along_x[0] * along_x[0] + along_y[1] * along_y[1] + along_z[2] * along_z[2]
                xy = along_x[1] + along_y[0]
                xz = along_x[2] + along_z[0]
                yz = along_y[2] + along_z[1]
                strain = 2.0 * same + (xy * xy + xz * xz + yz * yz)
                mixing = viscosity + (smag_coeff * smag_coeff / 12.0) * jnp.sqrt(strain)
                for i in range(components):
                    change = mixing * lap[i] - mean_wind * along_x[i]
                    out_ref[i, level, band, lane : lane + STEP] = (
                        pad_ref[i, level + 2, band, center]
                        + (time_step / 12.0) * change
                        + body_ref[i, level, band]
                    )

    @pl.when(step == 0)
    def _():
        for at in range(blocks):
            column_copy(at).start()
        if chunk == 0:
            level_edge(0, 1, 0)
        if chunk == chunks - 1:
            level_edge(LEVELS + 2, 0, 1)
        turbine = lax.axis_index("gy")
        side_columns(left_ref, turbine > 0, 120)
        side_columns(right_ref, turbine < lax.axis_size("gy") - 1, cols + 128)
        along_x = gaussian(lax.axis_index("gx") * rows, rows, own_ref[0:1, :])
        first = (lax.axis_index("gz") * chunks + chunk) * LEVELS
        along_z = gaussian(first, LEVELS, own_ref[2:3, :])
        for i in range(components):
            scaled = (time_step * smear_norm) * force_ref[i : i + 1, :] * along_x
            for level in range(LEVELS):
                band = pl.ds(i * cells + level * rows, rows)
                high, low = split(scaled * along_z[level : level + 1, :])
                wide_ref[band, :count] = high
                wide_ref[band, count : 2 * count] = low
                wide_ref[band, 2 * count :] = high
        column_copy(0).wait()
        matrix_part(0, 0, even)

    column_copy(2 * step + 1).wait()

    @pl.when(step < steps - 1)
    def _():
        column_copy(2 * step + 2).wait()

    matrix_part(2 * step + 1, 1, odd)
    vector_part(2 * step, even, 0)
    matrix_part(jnp.minimum(2 * step + 2, blocks - 1), 2, even)
    vector_part(2 * step + 1, odd, STEP)


def update(chunk, chunks, own, force, operator, prev, after, weight, velocity, lev, left, right, partial):
    components, depth, rows, cols = velocity.shape
    count = own.shape[1]
    cells = LEVELS * rows
    blocks = cols // STEP
    hbm = pl.BlockSpec(memory_space=pl.ANY)
    places = [lambda j: 0, lambda j: 2 * j + 1, lambda j: jnp.minimum(2 * j + 2, blocks - 1)]
    whole = pl.BlockSpec((8, count), lambda j: (0, 0))
    sides = [
        pl.BlockSpec((components, 2 * LEVELS, STEP), lambda j, at=at: (0, 0, at(j))) for at in places
    ]
    weights = [pl.BlockSpec((STEP, 2 * count), lambda j, at=at: (at(j), 0)) for at in places]
    column = pl.BlockSpec(left.shape, lambda j: (0, 0, 0))
    operands = [own, force, operator] + [prev] * 3 + [after] * 3 + [weight] * 3
    operands += [velocity, lev, left, right]
    in_specs = [whole, whole, pl.BlockSpec(operator.shape, lambda j: (0, 0))]
    in_specs += sides + sides + weights + [hbm, hbm, column, column]
    aliases = {}
    if partial is not None:
        aliases = {len(operands): 0}
        operands.append(partial)
        in_specs.append(hbm)
    fields = [pltpu.VMEM((components, LEVELS, rows, STEP), F32)] * 3
    return pl.pallas_call(
        functools.partial(update_kernel, chunk, chunks),
        grid=(blocks // 2,),
        in_specs=in_specs,
        out_specs=pl.BlockSpec((components, LEVELS, rows, 2 * STEP), lambda j: (0, chunk, 0, j)),
        out_shape=jax.ShapeDtypeStruct(velocity.shape, F32),
        scratch_shapes=[
            pltpu.VMEM((components, LEVELS + 4, rows, cols + 256), F32),
            pltpu.VMEM((components * cells, 3 * count), BF16),
            fields,
            fields,
            pltpu.SemaphoreType.DMA((blocks,)),
            pltpu.SemaphoreType.DMA((2,)),
        ],
        input_output_aliases=aliases,
        compiler_params=pltpu.CompilerParams(vmem_limit_bytes=40 * MIB),
        cost_estimate=LIGHT,
        name="update",
    )(*operands)


def local(velocity, blade_pos, block_turbine, blade_vel, lift_coeff):
    components, depth, rows, cols = velocity.shape
    owned, _, points = blade_pos.shape
    gx, gy, gz = (lax.axis_size(axis) for axis in ("gx", "gy", "gz"))
    assert gz == 2 and depth % LEVELS == 0
    per_turbine = owned * gz
    chunks = depth // LEVELS
    swap = [(0, 1), (1, 0)]
    up_x = [(i, i + 1) for i in range(gx - 1)]
    down_x = [(i + 1, i) for i in range(gx - 1)]

    def around(shift):
        return [(i, (i + shift) % gy) for i in range(gy)]

    up, down, facing, *sides = prep(velocity, blade_pos, block_turbine, blade_vel, lift_coeff)
    before = [lax.ppermute(tail, "gx", up_x) for tail in sides[chunks:]]
    after = [lax.ppermute(head, "gx", down_x) for head in sides[:chunks]]
    left = lax.ppermute(up, "gy", around(1))
    right = lax.ppermute(down, "gy", around(gy - 1))
    blocks = up[:owned]
    parts = [blocks, left[:owned]]
    parts += [lax.ppermute(blocks, "gy", around(shift)) for shift in range(2, gy - 1)]
    parts.append(right[:owned])
    mine = jnp.concatenate(parts, axis=0)
    twin = lax.ppermute(mine, "gz", swap)
    lev = lax.ppermute(facing, "gz", swap)

    part, own, weight = sample(mine, twin, velocity, per_turbine)
    other = lax.ppermute(part, "gz", swap)
    force, home = point_forces(mine, twin, part, other, own, per_turbine, owned)
    result = home[0]
    for shift in range(1, gy):
        result += lax.ppermute(home[shift], "gy", around(gy - shift))

    operator = jnp.asarray(stencil_operator(rows))
    new_velocity = None
    for chunk in range(chunks):
        new_velocity = update(
            chunk, chunks, own, force, operator, before[chunk], after[chunk],
            weight, velocity, lev, left[owned:], right[owned:], new_velocity,
        )
    return (new_velocity, result[:, :3, :])


def solution(mesh):
    in_specs = (
        P(None, "gz", "gx", "gy"),
        P(("gx", "gy", "gz"), None, None),
        P(("gx", "gy", "gz")),
        P(("gx", "gy", "gz"), None, None),
        P(("gx", "gy", "gz"), None),
    )
    out_specs = (P(None, "gz", "gx", "gy"), P(("gx", "gy", "gz"), None, None))
    return jax.shard_map(local, mesh=mesh, in_specs=in_specs, out_specs=out_specs, check_vma=False)
```

time: 101 us -> 86.9 us (0.86)
  Pallas kernels: 43.2 us -> 29.2 us
  local copies, waits for them, and re-layouts: 8.23 us -> 16.5 us
  starting transfers between devices: 28.9 us -> 20.7 us
  other arithmetic: 2.75 us -> 0.01 us
  waiting for transfers between devices: 16.3 us -> 19 us
    pallas_call x4 -> x3, Pallas kernels: 32.2 us -> 20.7 us  [the longest x2 19.5 us: update(): pl.pallas_call(functools.partial(update_kernel, chunk, chunks), grid=(blo...]
    unnamed x21 -> x33, local copies, waits for them, and re-layouts: 4.31 us -> 15.7 us
    ppermute x14 -> x12, starting transfers between devices: 28.8 us -> 20.7 us  [the longest x2 7.98 us: local(): before = [lax.ppermute(tail, 'gx', up_x) for tail in sides[chunks:]]]
    ppermute x14 -> x12, waiting for transfers between devices: 16.3 us -> 19 us  [the longest x2 10.4 us: local(): after = [lax.ppermute(head, 'gx', down_x) for head in sides[:chunks]]]
    pallas_call x1, Pallas kernels: 9.51 us -> 7.1 us  [sample(): pl.pallas_call(functools.partial(sample_kernel, per_turbine), grid=(cols...]
    slice x2 -> x5, local copies, waits for them, and re-layouts: 1.91 us -> 0.01 us  [the longest x1 0.01 us: local(): right[owned:]]
    dynamic_slice x1 -> x0, local copies, waits for them, and re-layouts: 1.19 us -> none  [local(): lax.dynamic_slice_in_dim(velocity, jnp.where(core == 0, depth - 2, 0), 2,...]
  transfers between devices with their start and end apart: 15 -> 13, of which waited for: 7 -> 6; matrix products, arithmetic and copies ran while one was open for 6% -> 2% of each run, Pallas kernels for 30% -> 21%
where the time goes in v2:
time: 86.9 us; the launch traced here: 86.2 us
  Pallas kernels  29.2 us (34%)
  starting transfers between devices  20.7 us (24%)
  waiting for transfers between devices  19 us (22%)
  local copies, waits for them, and re-layouts  16.5 us (19%)
    pallas_call x2, Pallas kernels, update(): pl.pallas_call(functools.partial(update_kernel, chunk, chunks), grid=(blo...  19.5 us
    unnamed x33, local copies, waits for them, and re-layouts  15.7 us
    ppermute x2, waiting for transfers between devices, local(): after = [lax.ppermute(head, 'gx', down_x) for head in sides[:chunks]]  10.4 us
    ppermute x2, starting transfers between devices, local(): before = [lax.ppermute(tail, 'gx', up_x) for tail in sides[chunks:]]  7.98 us
    pallas_call x1, Pallas kernels, sample(): pl.pallas_call(functools.partial(sample_kernel, per_turbine), grid=(cols...  7.1 us
    ppermute x1, starting transfers between devices, local(): right = lax.ppermute(down, 'gy', around(gy - 1))  5.1 us
    ppermute x1, waiting for transfers between devices, local(): left = lax.ppermute(up, 'gy', around(1))  4.11 us
    ppermute x3, starting transfers between devices, local(): result += lax.ppermute(home[shift], 'gy', around(gy - shift))  3.83 us
  transfers between devices with their start and end apart: 13, of which 6 were waited for; matrix products, arithmetic and copies ran while one was open for 2% of the time, Pallas kernels for 21%

profile of v2, /device:TPU:0, one launch (start us, length us, event | category | flops | bytes accessed | tf_op | source)
XLA Modules:
  0.0 86.2 jit_solution(2212969592797663692)
XLA Ops:
  0.6 0.7 copy.9.pos_ref
  1.3 0.7 copy.10.speed_ref
  2.0 2.8 %copy-done.2 = f32[3,16,16,2048]{3,2,1,0:T(8,128)S(1)} copy-done((f32[3,16,16,2048]{3,2,1,0:T(8,128)S(1)}, f32[3,16,16,2048]{3,2,1,0:T(8,128)}, u32[]{:S(2)}) %copy-start.2) | copy-done | bytes 6291480
  4.8 0.7 copy-done.12
  5.5 0.7 copy-done.13
  6.1 1.2 %prep.1 = (f32[8,8,128]{2,1,0:T(8,128)S(1)}, f32[8,8,128]{2,1,0:T(8,128)S(1)}, f32[3,2,16,2048]{3,2,1,0:T(8,128)S(1)}, f32[3,16,2048]{2,1,0:T(8,128)S(1)}, f32[3...) custom-call(s32[2]{0:T(128)S(1)} %copy-done.13, f32[2,3,128]{2,1,0:T(4,128)S(1)} %copy.9.pos_ref, ...), custom_call_target="tpu_custom_call" | custom-call | tf_op jit(solution)/shard_map/prep/pallas_call | solution.py:123
  7.3 5.1 %collective-permute-start.2 = (f32[8,8,128]{2,1,0:T(8,128)S(1)}, f32[8,8,128]{2,1,0:T(8,128)S(1)}, u32[]{:S(2)}, u32[]{:S(2)}) collective-permute-start(f32[8,8,128]{2,1,0:T(8,128)S(1)} %get-tuple-element.15), channel_id=1, source_target_pairs={{0,6},{2,0},{4,2},{6,4},{1,7},{3,1},{5,3},{7,5},{8,14},{10,8},{12,... | collective-permute-start | bytes 98312 | tf_op jit(solution)/shard_map/ppermute | solution.py:490
  12.4 1.0 %collective-permute-start.1 = (f32[2,8,128]{2,1,0:T(8,128)S(1)}, f32[2,8,128]{2,1,0:T(8,128)S(1)}, u32[]{:S(2)}, u32[]{:S(2)}) collective-permute-start(f32[2,8,128]{2,1,0:T(8,128)S(1)} %slice.32), channel_id=1, source_target_pairs={{0,4},{2,6},{4,0},{6,2},{1,5},{3,7},{5,1},{7,3},{8,12},{10,14},{12... | collective-permute-start | bytes 24584 | tf_op jit(solution)/shard_map/ppermute | solution.py:493
  14.0 4.1 %collective-permute-done = f32[8,8,128]{2,1,0:T(8,128)S(1)} collective-permute-done((f32[8,8,128]{2,1,0:T(8,128)S(1)}, f32[8,8,128]{2,1,0:T(8,128)S(1)}, u32[]{:S(2)}, u32[]{:S(2)}) %collective-permute-start) | collective-permute-done | bytes 32800 | tf_op jit(solution)/shard_map/ppermute | solution.py:489
  18.3 1.2 %collective-permute-done.3.twin_ref = f32[8,8,128]{2,1,0:T(8,128)S(1)} collective-permute-done((f32[8,8,128]{2,1,0:T(8,128)S(1)}, f32[8,8,128]{2,1,0:T(8,128)S(1)}, u32[]{:S(2)}, u32[]{:S(2)}) %collective-permute-start.3) | collective-permute-done | bytes 32800 | tf_op jit(solution)/shard_map/ppermute | solution.py:496
  19.5 7.1 %sample.1 = (f32[8,512]{1,0:T(8,128)S(1)}, f32[8,512]{1,0:T(8,128)S(1)}, bf16[2048,1024]{1,0:T(8,128)(2,1)S(1)}) custom-call(f32[8,8,128]{2,1,0:T(8,128)S(1)} %pad_maximum_fusion.mine_ref, f32[8,8,128]{2,1,0:T(8,128)S(1)} %collective-permute-done.3.twin_ref, f32[3,16,16,2048]{3,2,1,0:T(8,128)S(1)} %copy-done.3), custom_call_target="tpu_custom_call" | custom-call | tf_op jit(solution)/shard_map/sample/pallas_call | solution.py:226
  26.6 2.0 %copy-done = bf16[2048,1024]{1,0:T(8,128)(2,1)} copy-done((bf16[2048,1024]{1,0:T(8,128)(2,1)}, bf16[2048,1024]{1,0:T(8,128)(2,1)S(1)}, u32[]{:S(2)}) %copy-start) | copy-done | bytes 4194328
  28.6 0.6 copy-done.7
  29.3 1.0 %collective-permute-done.4.other_ref = f32[8,512]{1,0:T(8,128)S(1)} collective-permute-done((f32[8,512]{1,0:T(8,128)S(1)}, f32[8,512]{1,0:T(8,128)S(1)}, u32[]{:S(2)}, u32[]{:S(2)}) %collective-permute-start.4) | collective-permute-done | bytes 16416 | tf_op jit(solution)/shard_map/ppermute | solution.py:500
  30.4 0.6 copy-done.14
  31.0 1.5 %force.1 = (f32[8,512]{1,0:T(8,128)}, f32[4,2,8,128]{3,2,1,0:T(8,128)}) custom-call(f32[8,8,128]{2,1,0:T(8,128)} %copy-done.6, f32[8,8,128]{2,1,0:T(8,128)} %copy-done.9, f32[8,512]{1,0:T(8,128)} %copy-done.11, f32[8,512]{1,0:T(8,128)} %copy-done.14, f32[8,512]{1,0:T(8,128)} %copy-done.7), custom_call_target="tpu_custom_call" | custom-call | tf_op jit(solution)/shard_map/force/pallas_call | solution.py:273
  32.4 0.7 slice_bitcast_fusion.3
  33.7 2.6 %collective-permute-start.11 = (f32[2,8,128]{2,1,0:T(8,128)S(1)}, f32[2,8,128]{2,1,0:T(8,128)S(1)}, u32[]{:S(2)}, u32[]{:S(2)}) collective-permute-start(f32[2,8,128]{2,1,0:T(8,128)S(1)} %get-tuple-element.30), channel_id=1, source_target_pairs={{0,4},{2,6},{4,0},{6,2},{1,5},{3,7},{5,1},{7,3},{8,12},{10,14},{12... | collective-permute-start | bytes 24584 | tf_op jit(solution)/shard_map/ppermute | solution.py:504
  36.3 0.7 collective-permute-start.10
  37.0 3.4 %collective-permute-start.8 = (f32[3,16,2048]{2,1,0:T(8,128)S(1)}, f32[3,16,2048]{2,1,0:T(8,128)S(1)}, u32[]{:S(2)}, u32[]{:S(2)}) collective-permute-start(f32[3,16,2048]{2,1,0:T(8,128)S(1)} %get-tuple-element.23), channel_id=1, source_target_pairs={{0,8},{8,16},{16,24},{1,9},{9,17},{17,25},{2,10},{10,18},{18,26},{... | collective-permute-start | bytes 1179656 | tf_op jit(solution)/shard_map/ppermute | solution.py:487
  40.4 1.3 %collective-permute-start.9 = (f32[3,16,2048]{2,1,0:T(8,128)S(1)}, f32[3,16,2048]{2,1,0:T(8,128)S(1)}, u32[]{:S(2)}, u32[]{:S(2)}) collective-permute-start(f32[3,16,2048]{2,1,0:T(8,128)S(1)} %get-tuple-element.24), channel_id=1, source_target_pairs={{8,0},{16,8},{24,16},{9,1},{17,9},{25,17},{10,2},{18,10},{26,18},{... | collective-permute-start | bytes 1179656 | tf_op jit(solution)/shard_map/ppermute | solution.py:488
  41.7 4.6 %collective-permute-start.5 = (f32[3,16,2048]{2,1,0:T(8,128)S(1)}, f32[3,16,2048]{2,1,0:T(8,128)S(1)}, u32[]{:S(2)}, u32[]{:S(2)}) collective-permute-start(f32[3,16,2048]{2,1,0:T(8,128)S(1)} %get-tuple-element.19), channel_id=1, source_target_pairs={{0,8},{8,16},{16,24},{1,9},{9,17},{17,25},{2,10},{10,18},{18,26},{... | collective-permute-start | bytes 1179656 | tf_op jit(solution)/shard_map/ppermute | solution.py:487
  46.3 1.3 %collective-permute-start.6 = (f32[3,16,2048]{2,1,0:T(8,128)S(1)}, f32[3,16,2048]{2,1,0:T(8,128)S(1)}, u32[]{:S(2)}, u32[]{:S(2)}) collective-permute-start(f32[3,16,2048]{2,1,0:T(8,128)S(1)} %get-tuple-element.20), channel_id=1, source_target_pairs={{8,0},{16,8},{24,16},{9,1},{17,9},{25,17},{10,2},{18,10},{26,18},{... | collective-permute-start | bytes 1179656 | tf_op jit(solution)/shard_map/ppermute | solution.py:488
  47.7 0.6 copy.11
  48.2 1.7 %collective-permute-done.8.refs_3_.refs_4_.refs_5_ = f32[3,16,2048]{2,1,0:T(8,128)S(1)} collective-permute-done((f32[3,16,2048]{2,1,0:T(8,128)S(1)}, f32[3,16,2048]{2,1,0:T(8,128)S(1)}, u32[]{:S(2)}, u32[]{:S(2)}) %collective-permute-start.8) | collective-permute-done | bytes 393248 | tf_op jit(solution)/shard_map/ppermute | solution.py:487
  49.9 10.4 %collective-permute-done.9.refs_6_.refs_7_.refs_8_ = f32[3,16,2048]{2,1,0:T(8,128)S(1)} collective-permute-done((f32[3,16,2048]{2,1,0:T(8,128)S(1)}, f32[3,16,2048]{2,1,0:T(8,128)S(1)}, u32[]{:S(2)}, u32[]{:S(2)}) %collective-permute-start.9) | collective-permute-done | bytes 393248 | tf_op jit(solution)/shard_map/ppermute | solution.py:488
  60.3 2.2 %copy-done.1 = bf16[2048,1024]{1,0:T(8,128)(2,1)S(1)} copy-done((bf16[2048,1024]{1,0:T(8,128)(2,1)S(1)}, bf16[2048,1024]{1,0:T(8,128)(2,1)}, u32[]{:S(2)}) %copy-start.1) | copy-done | bytes 4194328
  62.5 2.8 %copy-done.4 = f32[3,16,16,2048]{3,2,1,0:T(8,128)S(1)} copy-done((f32[3,16,16,2048]{3,2,1,0:T(8,128)S(1)}, f32[3,16,16,2048]{3,2,1,0:T(8,128)}, u32[]{:S(2)}) %copy-start.4) | copy-done | bytes 6291480
  65.3 0.7 copy-done.8
  66.0 0.7 copy-done.10
  66.7 9.7 %update.2.refs_16_ = f32[3,16,16,2048]{3,2,1,0:T(8,128)} custom-call(f32[8,512]{1,0:T(8,128)S(1)} %copy-done.8, f32[8,512]{1,0:T(8,128)S(1)} %copy-done.10, bf16[256,512]{1,0:T(8,128)(2,1)S(1)} %copy-done.5, f32[3,16,2048]{2,1,0:T(8,128)S(1)} %collective-permute-done.8.refs_3_.refs_4_.refs_5_, ...), custom_call_target="tpu_custom_call" | custom-call | tf_op jit(solution)/shard_map/update/pallas_call | solution.py:451
  76.4 9.8 %update.3 = f32[3,16,16,2048]{3,2,1,0:T(8,128)} custom-call(f32[8,512]{1,0:T(8,128)S(1)} %copy-done.8, f32[8,512]{1,0:T(8,128)S(1)} %copy-done.10, bf16[256,512]{1,0:T(8,128)(2,1)S(1)} %copy-done.5, f32[3,16,2048]{2,1,0:T(8,128)S(1)} %collective-permute-done.5.refs_3_.refs_4_.refs_5_, ...), custom_call_target="tpu_custom_call", output_to_operand_aliasing={{}: (16, {})} | custom-call | tf_op jit(solution)/shard_map/update/pallas_call | solution.py:451
  (40 shorter events, 1.5 us)
Async XLA Ops:
  2.0 2.8 %copy-start.2 = (f32[3,16,16,2048]{3,2,1,0:T(8,128)S(1)}, f32[3,16,16,2048]{3,2,1,0:T(8,128)}, u32[]{:S(2)}) copy-start(f32[3,16,16,2048]{3,2,1,0:T(8,128)} %refs_12_.3) | copy-start | bytes 18874372
  4.8 0.7 copy-start.12
  5.5 0.7 copy-start.13
  6.1 13.3 %copy-start.3 = (f32[3,16,16,2048]{3,2,1,0:T(8,128)S(1)}, f32[3,16,16,2048]{3,2,1,0:T(8,128)}, u32[]{:S(2)}) copy-start(f32[3,16,16,2048]{3,2,1,0:T(8,128)} %refs_12_.3) | copy-start | bytes 18874372
  6.1 54.2 %copy-start.5 = (bf16[256,512]{1,0:T(8,128)(2,1)S(1)}, bf16[256,512]{1,0:T(8,128)(2,1)}, u32[]{:S(2)}) copy-start(bf16[256,512]{1,0:T(8,128)(2,1)} %constant.2.clone.refs_2_) | copy-start | bytes 786436
  7.3 6.7 %collective-permute-start.2 = (f32[8,8,128]{2,1,0:T(8,128)S(1)}, f32[8,8,128]{2,1,0:T(8,128)S(1)}, u32[]{:S(2)}, u32[]{:S(2)}) collective-permute-start(f32[8,8,128]{2,1,0:T(8,128)S(1)} %get-tuple-element.15), channel_id=1, source_target_pairs={{0,6},{2,0},{4,2},{6,4},{1,7},{3,1},{5,3},{7,5},{8,14},{10,8},{12,... | collective-permute-start | bytes 98312 | tf_op jit(solution)/shard_map/ppermute | solution.py:490
  12.4 5.7 %collective-permute-start = (f32[8,8,128]{2,1,0:T(8,128)S(1)}, f32[8,8,128]{2,1,0:T(8,128)S(1)}, u32[]{:S(2)}, u32[]{:S(2)}) collective-permute-start(f32[8,8,128]{2,1,0:T(8,128)S(1)} %get-tuple-element.14), channel_id=1, source_target_pairs={{0,2},{2,4},{4,6},{6,0},{1,3},{3,5},{5,7},{7,1},{8,10},{10,12},{12... | collective-permute-start | bytes 98312 | tf_op jit(solution)/shard_map/ppermute | solution.py:489
  12.4 5.7 %collective-permute-start.1 = (f32[2,8,128]{2,1,0:T(8,128)S(1)}, f32[2,8,128]{2,1,0:T(8,128)S(1)}, u32[]{:S(2)}, u32[]{:S(2)}) collective-permute-start(f32[2,8,128]{2,1,0:T(8,128)S(1)} %slice.32), channel_id=1, source_target_pairs={{0,4},{2,6},{4,0},{6,2},{1,5},{3,7},{5,1},{7,3},{8,12},{10,14},{12... | collective-permute-start | bytes 24584 | tf_op jit(solution)/shard_map/ppermute | solution.py:493
  13.5 46.8 %collective-permute-start.7 = (f32[3,2,16,2048]{3,2,1,0:T(8,128)S(1)}, f32[3,2,16,2048]{3,2,1,0:T(8,128)S(1)}, u32[]{:S(2)}, u32[]{:S(2)}) collective-permute-start(f32[3,2,16,2048]{3,2,1,0:T(8,128)S(1)} %get-tuple-element.22), channel_id=1, source_target_pairs={{0,1},{1,0},{2,3},{3,2},{4,5},{5,4},{6,7},{7,6},{8,9},{9,8},{10,11... | collective-permute-start | bytes 2359304 | tf_op jit(solution)/shard_map/ppermute | solution.py:497
  18.2 12.8 %copy-start.6 = (f32[8,8,128]{2,1,0:T(8,128)}, f32[8,8,128]{2,1,0:T(8,128)S(1)}, u32[]{:S(2)}) copy-start(f32[8,8,128]{2,1,0:T(8,128)S(1)} %pad_maximum_fusion.mine_ref) | copy-start | bytes 98308
  18.2 1.3 %collective-permute-start.3 = (f32[8,8,128]{2,1,0:T(8,128)S(1)}, f32[8,8,128]{2,1,0:T(8,128)S(1)}, u32[]{:S(2)}, u32[]{:S(2)}) collective-permute-start(f32[8,8,128]{2,1,0:T(8,128)S(1)} %pad_maximum_fusion.mine_ref), channel_id=1, source_target_pairs={{0,1},{1,0},{2,3},{3,2},{4,5},{5,4},{6,7},{7,6},{8,9},{9,8},{10,11... | collective-permute-start | bytes 98312 | tf_op jit(solution)/shard_map/ppermute | solution.py:496
  19.5 11.5 %copy-start.9 = (f32[8,8,128]{2,1,0:T(8,128)}, f32[8,8,128]{2,1,0:T(8,128)S(1)}, u32[]{:S(2)}) copy-start(f32[8,8,128]{2,1,0:T(8,128)S(1)} %collective-permute-done.3.twin_ref) | copy-start | bytes 98308
  26.6 2.0 %copy-start = (bf16[2048,1024]{1,0:T(8,128)(2,1)}, bf16[2048,1024]{1,0:T(8,128)(2,1)S(1)}, u32[]{:S(2)}) copy-start(bf16[2048,1024]{1,0:T(8,128)(2,1)S(1)} %get-tuple-element.21.refs_9_.refs_10_.refs_11_) | copy-start | bytes 12582916
  28.6 0.6 copy-start.7
  29.2 1.8 %copy-start.11 = (f32[8,512]{1,0:T(8,128)}, f32[8,512]{1,0:T(8,128)S(1)}, u32[]{:S(2)}) copy-start(f32[8,512]{1,0:T(8,128)S(1)} %get-tuple-element.17.part_ref) | copy-start | bytes 49156
  29.2 1.2 %collective-permute-start.4 = (f32[8,512]{1,0:T(8,128)S(1)}, f32[8,512]{1,0:T(8,128)S(1)}, u32[]{:S(2)}, u32[]{:S(2)}) collective-permute-start(f32[8,512]{1,0:T(8,128)S(1)} %get-tuple-element.17.part_ref), channel_id=1, source_target_pairs={{0,1},{1,0},{2,3},{3,2},{4,5},{5,4},{6,7},{7,6},{8,9},{9,8},{10,11... | collective-permute-start | bytes 49160 | tf_op jit(solution)/shard_map/ppermute | solution.py:500
  30.4 0.6 copy-start.14
  33.2 7.2 %collective-permute-start.12 = (f32[2,8,128]{2,1,0:T(8,128)S(1)}, f32[2,8,128]{2,1,0:T(8,128)S(1)}, u32[]{:S(2)}, u32[]{:S(2)}) collective-permute-start(f32[2,8,128]{2,1,0:T(8,128)S(1)} %get-tuple-element.29), channel_id=1, source_target_pairs={{0,2},{2,4},{4,6},{6,0},{1,3},{3,5},{5,7},{7,1},{8,10},{10,12},{12... | collective-permute-start | bytes 24584 | tf_op jit(solution)/shard_map/ppermute | solution.py:504
  33.7 8.0 %collective-permute-start.11 = (f32[2,8,128]{2,1,0:T(8,128)S(1)}, f32[2,8,128]{2,1,0:T(8,128)S(1)}, u32[]{:S(2)}, u32[]{:S(2)}) collective-permute-start(f32[2,8,128]{2,1,0:T(8,128)S(1)} %get-tuple-element.30), channel_id=1, source_target_pairs={{0,4},{2,6},{4,0},{6,2},{1,5},{3,7},{5,1},{7,3},{8,12},{10,14},{12... | collective-permute-start | bytes 24584 | tf_op jit(solution)/shard_map/ppermute | solution.py:504
  36.3 10.0 %collective-permute-start.10 = (f32[2,8,128]{2,1,0:T(8,128)S(1)}, f32[2,8,128]{2,1,0:T(8,128)S(1)}, u32[]{:S(2)}, u32[]{:S(2)}) collective-permute-start(f32[2,8,128]{2,1,0:T(8,128)S(1)} %get-tuple-element.31), channel_id=1, source_target_pairs={{0,6},{2,0},{4,2},{6,4},{1,7},{3,1},{5,3},{7,5},{8,14},{10,8},{12,... | collective-permute-start | bytes 24584 | tf_op jit(solution)/shard_map/ppermute | solution.py:504
  37.0 12.9 %collective-permute-start.8 = (f32[3,16,2048]{2,1,0:T(8,128)S(1)}, f32[3,16,2048]{2,1,0:T(8,128)S(1)}, u32[]{:S(2)}, u32[]{:S(2)}) collective-permute-start(f32[3,16,2048]{2,1,0:T(8,128)S(1)} %get-tuple-element.23), channel_id=1, source_target_pairs={{0,8},{8,16},{16,24},{1,9},{9,17},{17,25},{2,10},{10,18},{18,26},{... | collective-permute-start | bytes 1179656 | tf_op jit(solution)/shard_map/ppermute | solution.py:487
  40.4 19.9 %collective-permute-start.9 = (f32[3,16,2048]{2,1,0:T(8,128)S(1)}, f32[3,16,2048]{2,1,0:T(8,128)S(1)}, u32[]{:S(2)}, u32[]{:S(2)}) collective-permute-start(f32[3,16,2048]{2,1,0:T(8,128)S(1)} %get-tuple-element.24), channel_id=1, source_target_pairs={{8,0},{16,8},{24,16},{9,1},{17,9},{25,17},{10,2},{18,10},{26,18},{... | collective-permute-start | bytes 1179656 | tf_op jit(solution)/shard_map/ppermute | solution.py:488
  41.7 34.7 %collective-permute-start.5 = (f32[3,16,2048]{2,1,0:T(8,128)S(1)}, f32[3,16,2048]{2,1,0:T(8,128)S(1)}, u32[]{:S(2)}, u32[]{:S(2)}) collective-permute-start(f32[3,16,2048]{2,1,0:T(8,128)S(1)} %get-tuple-element.19), channel_id=1, source_target_pairs={{0,8},{8,16},{16,24},{1,9},{9,17},{17,25},{2,10},{10,18},{18,26},{... | collective-permute-start | bytes 1179656 | tf_op jit(solution)/shard_map/ppermute | solution.py:487
  46.3 30.1 %collective-permute-start.6 = (f32[3,16,2048]{2,1,0:T(8,128)S(1)}, f32[3,16,2048]{2,1,0:T(8,128)S(1)}, u32[]{:S(2)}, u32[]{:S(2)}) collective-permute-start(f32[3,16,2048]{2,1,0:T(8,128)S(1)} %get-tuple-element.20), channel_id=1, source_target_pairs={{8,0},{16,8},{24,16},{9,1},{17,9},{25,17},{10,2},{18,10},{26,18},{... | collective-permute-start | bytes 1179656 | tf_op jit(solution)/shard_map/ppermute | solution.py:488
  60.3 2.2 %copy-start.1 = (bf16[2048,1024]{1,0:T(8,128)(2,1)S(1)}, bf16[2048,1024]{1,0:T(8,128)(2,1)}, u32[]{:S(2)}) copy-start(bf16[2048,1024]{1,0:T(8,128)(2,1)} %copy-done) | copy-start | bytes 12582916
  62.5 2.8 %copy-start.4 = (f32[3,16,16,2048]{3,2,1,0:T(8,128)S(1)}, f32[3,16,16,2048]{3,2,1,0:T(8,128)}, u32[]{:S(2)}) copy-start(f32[3,16,16,2048]{3,2,1,0:T(8,128)} %refs_12_.3) | copy-start | bytes 18874372
  65.3 0.7 copy-start.8
  66.0 0.7 copy-start.10

commit v3 on v2

v3 whole, which is shorter than its diff:
```python
import functools
import math

import jax
import jax.numpy as jnp
import ml_dtypes
import numpy as np
from jax import lax
from jax.experimental import pallas as pl
from jax.experimental.pallas import tpu as pltpu
from jax.sharding import PartitionSpec as P

mean_wind = 1.0
viscosity = 0.2
smag_coeff = 0.17
time_step = 0.2
smear = 2.0
smear_norm = 1.0 / (smear**3 * math.pi**1.5)

F32 = jnp.float32
BF16 = jnp.bfloat16
MIB = 1024 * 1024
LEVELS = 8
STEP = 256
WIDE = 512
LIGHT = pl.CostEstimate(flops=0, bytes_accessed=0, transcendentals=0)


def split(value):
    high = value.astype(BF16)
    return high, (value - high.astype(F32)).astype(BF16)


def dot(left, right, contract=0):
    return lax.dot_general(
        left, right, (((1,), (contract,)), ((), ())), preferred_element_type=F32
    )


def gaussian(first, count, centers):
    shape = (count, centers.shape[1])
    cells = (first + lax.broadcasted_iota(jnp.int32, shape, 0)).astype(F32)
    gap = cells - centers
    return jnp.exp(-gap * gap / (smear * smear))


def stencil_operator(row_cells):
    inner = (LEVELS + 4) * row_cells
    width = inner + 4 * LEVELS
    op = np.zeros((2, LEVELS, row_cells, width), np.float32)

    def column(level, row):
        if 0 <= row < row_cells:
            return (level + 2) * row_cells + row
        if row < 0:
            return inner + level * 2 + row + 2
        return inner + 2 * LEVELS + level * 2 + row - row_cells

    for level in range(LEVELS):
        for row in range(row_cells):
            for offset, first, second in ((-2, 1, -1), (-1, -8, 16), (1, 8, 16), (2, -1, -1)):
                op[0, level, row, column(level, row + offset)] += first
                op[1, level, row, column(level, row + offset)] += second
                op[1, level, row, column(level + offset, row)] += second
            op[1, level, row, column(level, row)] -= 90
    op = op.reshape(2 * LEVELS * row_cells, width)
    op = np.pad(op, ((0, 0), (0, -width % 128)))
    return np.concatenate([op, op], axis=1).astype(ml_dtypes.bfloat16)


def prep_kernel(
    turb_ref, pos_ref, speed_ref, lift_ref, vel_ref, up_ref, down_ref, lev_ref, head_ref, tail_ref
):
    component = pl.program_id(0)
    levels, rows, cols = vel_ref.shape[1:]
    coords, owned, points = pos_ref.shape

    @pl.when(component == 0)
    def _():
        for ref in (up_ref, down_ref):
            for k in range(owned):
                for i in range(coords):
                    ref[k, i : i + 1, :] = pos_ref[i, k : k + 1, :]
                    ref[k, coords + i : coords + i + 1, :] = speed_ref[i, k : k + 1, :]
                ref[k, 2 * coords : 2 * coords + 1, :] = lift_ref[k : k + 1, :]
                ref[k, 7:8, :] = jnp.full((1, points), turb_ref[k].astype(F32))

    lev_ref[0] = vel_ref[0, pl.ds(jnp.where(lax.axis_index("gz") == 0, levels - 2, 0), 2)]
    parts = levels * rows // 128
    last = vel_ref[0, :, :, cols - 128 :].reshape(levels * rows, 128)
    first = vel_ref[0, :, :, :128].reshape(levels * rows, 128)
    for part in range(parts):
        cells = slice(part * 128, part * 128 + 128)
        up_ref[owned + component * parts + part] = last[cells].T[120:]
        down_ref[owned + component * parts + part] = first[cells].T[:8]

    row = lax.broadcasted_iota(jnp.int32, (8, cols), 0) // 2
    for group in range(levels // 4):
        head = tail = None
        for k in range(4):
            top = vel_ref[0, group * 4 + k, 0:8, :]
            end = vel_ref[0, group * 4 + k, rows - 8 : rows, :]
            if k:
                top = pltpu.roll(top, 2 * k, 0)
            if k < 3:
                end = pltpu.roll(end, 2 * k + 2, 0)
            head = top if head is None else jnp.where(row == k, top, head)
            tail = end if tail is None else jnp.where(row == k, end, tail)
        head_ref[0, group * 8 : group * 8 + 8, :] = head
        tail_ref[0, group * 8 : group * 8 + 8, :] = tail


def prep(velocity, blade_pos, block_turbine, blade_vel, lift_coeff):
    components, levels, rows, cols = velocity.shape
    owned, coords, points = blade_pos.shape
    tiles = owned + components * levels * rows // 128
    whole = pl.BlockSpec((coords, owned, points), lambda i: (0, 0, 0))
    message = pl.BlockSpec((tiles, 8, 128), lambda i: (0, 0, 0))
    side = pl.BlockSpec((1, 2 * levels, cols), lambda i: (i, 0, 0))
    return pl.pallas_call(
        prep_kernel,
        grid=(components,),
        in_specs=[
            pl.BlockSpec(memory_space=pltpu.SMEM),
            whole,
            whole,
            pl.BlockSpec((owned, points), lambda i: (0, 0)),
            pl.BlockSpec((1, levels, rows, cols), lambda i: (i, 0, 0, 0)),
        ],
        out_specs=[
            message,
            message,
            pl.BlockSpec((1, 2, rows, cols), lambda i: (i, 0, 0, 0)),
            side,
            side,
        ],
        out_shape=[
            jax.ShapeDtypeStruct((tiles, 8, 128), F32),
            jax.ShapeDtypeStruct((tiles, 8, 128), F32),
            jax.ShapeDtypeStruct((components, 2, rows, cols), F32),
            jax.ShapeDtypeStruct((components, 2 * levels, cols), F32),
            jax.ShapeDtypeStruct((components, 2 * levels, cols), F32),
        ],
        compiler_params=pltpu.CompilerParams(vmem_limit_bytes=60 * MIB),
        cost_estimate=LIGHT,
        name="prep",
    )(
        block_turbine,
        blade_pos.transpose(1, 0, 2),
        blade_vel.transpose(1, 0, 2),
        lift_coeff,
        velocity,
    )


def match(mine_ref, twin_ref, per_turbine):
    core = lax.axis_index("gz")
    turbine = lax.axis_index("gy").astype(F32)
    half = mine_ref.shape[0]
    first = [(mine_ref[k, 7:8, :] == turbine).astype(F32) for k in range(half)]
    second = [(twin_ref[k, 7:8, :] == turbine).astype(F32) for k in range(half)]
    masks = []
    for hits, others, leads in ((first, second, core == 0), (second, first, core == 1)):
        rank = jnp.where(leads, jnp.zeros_like(hits[0]), sum(others))
        for hit in hits:
            masks.append([(hit > 0.5) & (rank == k) for k in range(per_turbine)])
            rank = rank + hit
    return masks


def sample_kernel(
    per_turbine, mine_ref, twin_ref, vel_ref, part_ref, own_ref, weight_ref,
    even_ref, odd_ref, center_ref, plane_ref, acc_ref,
):
    step = pl.program_id(0)
    steps = pl.num_programs(0)
    components, depth, rows, width = vel_ref.shape
    points = mine_ref.shape[2]
    count = per_turbine * points
    cells = depth * rows
    half = width // 2
    start = lax.axis_index("gy") * steps * width

    def bell(cell, center):
        gap = cell.astype(F32) - center
        return jnp.exp(-gap * gap / (smear * smear))

    def weights(at, ref):
        lane = lax.broadcasted_iota(jnp.int32, (1, 128), 1)
        for part in range(half // 128):
            cell = start + at * half + part * 128 + lane
            ref[:, part * 128 : part * 128 + 128] = bell(cell, center_ref[...])

    def multiply(side, ref):
        for i in range(components):
            column = vel_ref[i, :, :, side * half : side * half + half].reshape(cells, half)
            high, low = split(column)
            field = dot(plane_ref[...], jnp.concatenate([high, high, low], axis=0))
            product = field * ref[...]
            total = acc_ref[i]
            for part in range(half // 128):
                total += product[:, part * 128 : part * 128 + 128]
            acc_ref[i] = total
        high, low = split(ref[...])
        weight_ref[:count, side * half : side * half + half] = high
        weight_ref[count:, side * half : side * half + half] = low

    @pl.when(step == 0)
    def _():
        masks = match(mine_ref, twin_ref, per_turbine)
        blocks = mine_ref.shape[0]
        lane = lax.broadcasted_iota(jnp.int32, (1, cells), 1)
        level = lax.axis_index("gz") * depth + lane // rows
        row = lax.axis_index("gx") * rows + lane % rows
        for k in range(per_turbine):
            total = jnp.zeros((8, points), F32)
            for at, mask in enumerate(masks):
                tile = mine_ref[at] if at < blocks else twin_ref[at - blocks]
                total = jnp.where(mask[k], tile, total)
            band = slice(k * points, (k + 1) * points)
            own_ref[:, band] = total
            turned = total.T
            center_ref[band, :] = jnp.broadcast_to(turned[:, 1:2], (points, 128))
            plane = bell(row, turned[:, 0:1]) * bell(level, turned[:, 2:3])
            high, low = split(plane)
            plane_ref[band, :cells] = high
            plane_ref[band, cells : 2 * cells] = low
            plane_ref[band, 2 * cells :] = high
        acc_ref[...] = jnp.zeros(acc_ref.shape, F32)
        weights(0, even_ref)

    weights(2 * step + 1, odd_ref)
    multiply(0, even_ref)
    weights(2 * step + 2, even_ref)
    multiply(1, odd_ref)

    @pl.when(step == steps - 1)
    def _():
        for i in range(components):
            for k in range(per_turbine):
                band = slice(k * points, (k + 1) * points)
                total = jnp.sum(acc_ref[i, band, :].T, axis=0, keepdims=True)
                part_ref[i : i + 1, band] = smear_norm * total
        part_ref[components:, :] = jnp.zeros((8 - components, count), F32)


def sample(mine, twin, velocity, per_turbine):
    components, depth, rows, cols = velocity.shape
    points = mine.shape[2]
    count = per_turbine * points
    whole = pl.BlockSpec((8, count), lambda j: (0, 0))
    table = pl.BlockSpec(mine.shape, lambda j: (0, 0, 0))
    return pl.pallas_call(
        functools.partial(sample_kernel, per_turbine),
        grid=(cols // (2 * STEP),),
        in_specs=[
            table,
            table,
            pl.BlockSpec((components, depth, rows, 2 * STEP), lambda j: (0, 0, 0, j)),
        ],
        out_specs=[whole, whole, pl.BlockSpec((2 * count, 2 * STEP), lambda j: (0, j))],
        out_shape=[
            jax.ShapeDtypeStruct((8, count), F32),
            jax.ShapeDtypeStruct((8, count), F32),
            jax.ShapeDtypeStruct((2 * count, cols), BF16),
        ],
        scratch_shapes=[
            pltpu.VMEM((count, STEP), F32),
            pltpu.VMEM((count, STEP), F32),
            pltpu.VMEM((count, 128), F32),
            pltpu.VMEM((count, 3 * depth * rows), BF16),
            pltpu.VMEM((components, count, 128), F32),
        ],
        compiler_params=pltpu.CompilerParams(vmem_limit_bytes=20 * MIB),
        cost_estimate=LIGHT,
        name="sample",
    )(mine, twin, velocity)


def force_kernel(
    per_turbine, owned, mine_ref, twin_ref, part_ref, other_ref, own_ref, force_ref, home_ref
):
    points = own_ref.shape[1] // per_turbine
    relative = part_ref[0:3, :] + other_ref[0:3, :] - own_ref[3:6, :]
    speed = jnp.sqrt(jnp.sum(relative * relative, axis=0, keepdims=True))
    force = -own_ref[6:7, :] * speed * relative
    force_ref[...] = jnp.zeros(force_ref.shape, F32)
    force_ref[0:3, :] = force
    masks = match(mine_ref, twin_ref, per_turbine)
    for row in range(mine_ref.shape[0]):
        total = jnp.zeros((3, points), F32)
        for k in range(per_turbine):
            total = jnp.where(masks[row][k], force[:, k * points : (k + 1) * points], total)
        home_ref[row // owned, row % owned, 0:3, :] = total
        home_ref[row // owned, row % owned, 3:8, :] = jnp.zeros((5, points), F32)


def point_forces(mine, twin, part, other, own, per_turbine, owned):
    count = own.shape[1]
    points = count // per_turbine
    shifts = mine.shape[0] // owned
    return pl.pallas_call(
        functools.partial(force_kernel, per_turbine, owned),
        in_specs=[pl.BlockSpec(memory_space=pltpu.VMEM)] * 5,
        out_specs=[pl.BlockSpec(memory_space=pltpu.VMEM)] * 2,
        out_shape=[
            jax.ShapeDtypeStruct((8, count), F32),
            jax.ShapeDtypeStruct((shifts, owned, 8, points), F32),
        ],
        compiler_params=pltpu.CompilerParams(vmem_limit_bytes=8 * MIB),
        cost_estimate=LIGHT,
        name="force",
    )(mine, twin, part, other, own)


def update_kernel(
    own_ref, force_ref, op_ref, prev0_ref, prev1_ref, prev2_ref, next0_ref, next1_ref, next2_ref,
    weight0_ref, weight1_ref, weight2_ref, vel_ref, lev_ref, left_ref, right_ref,
    out_ref, pad_ref, wide_ref, even, odd, sems, edge_sem,
):
    step = pl.program_id(0)
    steps = pl.num_programs(0)
    components, depth, rows, cols = vel_ref.shape
    width = cols // steps
    cells = LEVELS * rows
    inner = (LEVELS + 4) * rows
    fill = op_ref.shape[1] // 2 - inner - 4 * LEVELS
    core = lax.axis_index("gz")
    turbine = lax.axis_index("gy")

    def column_copy(at):
        here = pl.multiple_of(at * width, 128)
        there = pl.multiple_of(at * width + 128, 128)
        return pltpu.make_async_copy(
            vel_ref.at[:, :, :, pl.ds(here, width)],
            pad_ref.at[:, pl.ds(2, depth), :, pl.ds(there, width)],
            sems.at[at],
        )

    def level_edge(at, owner):
        copy = pltpu.make_async_copy(
            lev_ref, pad_ref.at[:, pl.ds(at, 2), :, pl.ds(128, cols)], edge_sem
        )

        @pl.when(core == owner)
        def _():
            copy.start()
            copy.wait()

        @pl.when(core != owner)
        def _():
            pad_ref[:, at : at + 2, :, 128 : cols + 128] = jnp.zeros((components, 2, rows, cols), F32)

    def side_columns(ref, present, lane):
        per_part = 128 // rows
        parts = ref.shape[0] // components
        for tile in range(ref.shape[0]):
            turned = jnp.where(present, ref[tile], 0.0).T
            for k in range(per_part):
                level = (tile % parts) * per_part + k
                pad_ref[tile // parts, level + 2, :, lane : lane + 8] = turned[k * rows : (k + 1) * rows, :]

    def matrix_part(half, at, prev_ref, next_ref, weight_ref, bufs):
        grad_ref, lap_ref, body_ref = bufs
        center = pl.ds(pl.multiple_of(at * width + 128, 128), width)
        op = op_ref[...]
        empty = [jnp.zeros((fill, width), BF16)] if fill else []
        for i in range(components):
            column = pad_ref[i, half * LEVELS : (half + 1) * LEVELS + 4, :, center]
            inner_high, inner_low = split(column.reshape(inner, width))
            prev_high, prev_low = split(prev_ref[i])
            next_high, next_low = split(next_ref[i])
            high = [inner_high, prev_high, next_high] + empty
            low = [inner_low, prev_low, next_low] + empty
            result = dot(op, jnp.concatenate(high + low, axis=0))
            grad_ref[i] = result[:cells].reshape(LEVELS, rows, width)
            lap_ref[i] = result[cells:].reshape(LEVELS, rows, width)
        count = weight_ref.shape[0] // 2
        high = weight_ref[:count, :]
        body = dot(wide_ref[half], jnp.concatenate([high, high, weight_ref[count:, :]], axis=0))
        body_ref[...] = body.reshape(components, LEVELS, rows, width)

    def vector_part(half, at, bufs):
        grad_ref, lap_ref, body_ref = bufs
        base = at * width
        lane = lax.broadcasted_iota(jnp.int32, (8, 128), 1)
        shifts = ((1, lane < 1), (2, lane < 2), (127, lane >= 127), (126, lane >= 126))

        def cell(i, level, band, block):
            return pad_ref[i, level, band, pl.ds(pl.multiple_of(base + block * 128, 128), 128)]

        for level in range(LEVELS):
            here = half * LEVELS + level + 2
            for row in range(0, rows, 8):
                band = slice(row, row + 8)
                turned = {}

                def turn(i, block, shift, here=here, band=band, turned=turned):
                    if (i, block, shift) not in turned:
                        turned[i, block, shift] = pltpu.roll(cell(i, here, band, block), shift, 1)
                    return turned[i, block, shift]

                for block in range(1, width // 128 + 1):
                    lanes = slice(block * 128 - 128, block * 128)
                    along_y, lap, along_z = [], [], []
                    for i in range(components):
                        behind, behind2, ahead, ahead2 = [
                            jnp.where(
                                wrapped,
                                turn(i, block - 1 if shift < 64 else block + 1, shift),
                                turn(i, block, shift),
                            )
                            for shift, wrapped in shifts
                        ]
                        along_y.append(8.0 * (ahead - behind) - (ahead2 - behind2))
                        lap.append(
                            lap_ref[i, level, band, lanes]
                            + (16.0 * (ahead + behind) - (ahead2 + behind2))
                        )
                        near = cell(i, here + 1, band, block) - cell(i, here - 1, band, block)
                        far = cell(i, here + 2, band, block) - cell(i, here - 2, band, block)
                        along_z.append(8.0 * near - far)
                    along_x = [grad_ref[i, level, band, lanes] for i in range(components)]
                    same = along_x[0] * along_x[0] + along_y[1] * along_y[1] + along_z[2] * along_z[2]
                    xy = along_x[1] + along_y[0]
                    xz = along_x[2] + along_z[0]
                    yz = along_y[2] + along_z[1]
                    strain = 2.0 * same + (xy * xy + xz * xz + yz * yz)
                    mixing = (time_step / 12.0) * viscosity + (
                        time_step * smag_coeff * smag_coeff / 144.0
                    ) * jnp.sqrt(strain)
                    for i in range(components):
                        change = mixing * lap[i] - (time_step * mean_wind / 12.0) * along_x[i]
                        out_ref[i, half * LEVELS + level, band, lanes] = (
                            cell(i, here, band, block) + body_ref[i, level, band, lanes] + change
                        )

    @pl.when(step == 0)
    def _():
        for at in range(cols // width):
            column_copy(at).start()
        level_edge(0, 1)
        level_edge(depth + 2, 0)
        side_columns(left_ref, turbine > 0, 120)
        side_columns(right_ref, turbine < lax.axis_size("gy") - 1, cols + 128)
        along_x = gaussian(lax.axis_index("gx") * rows, rows, own_ref[0:1, :])
        along_z = gaussian(core * depth, depth, own_ref[2:3, :])
        count = own_ref.shape[1]
        for i in range(components):
            scaled = (time_step * smear_norm) * force_ref[i : i + 1, :] * along_x
            for level in range(depth):
                band = slice(i * cells + level % LEVELS * rows, i * cells + (level % LEVELS + 1) * rows)
                high, low = split(scaled * along_z[level : level + 1, :])
                wide_ref[level // LEVELS, band, :count] = high
                wide_ref[level // LEVELS, band, count : 2 * count] = low
                wide_ref[level // LEVELS, band, 2 * count :] = high
        column_copy(0).wait()
        matrix_part(0, 0, prev0_ref, next0_ref, weight0_ref, even)

    @pl.when(step < steps - 1)
    def _():
        column_copy(step + 1).wait()

    matrix_part(1, step, prev1_ref, next1_ref, weight1_ref, odd)
    vector_part(0, step, even)
    matrix_part(0, jnp.minimum(step + 1, steps - 1), prev2_ref, next2_ref, weight2_ref, even)
    vector_part(1, step, odd)


def update(own, force, operator, prev, after, weight, velocity, lev, left, right):
    components, depth, rows, cols = velocity.shape
    count = own.shape[1]
    steps = cols // WIDE
    hbm = pl.BlockSpec(memory_space=pl.ANY)
    places = [(0, lambda j: 0), (1, lambda j: j), (0, lambda j: jnp.minimum(j + 1, steps - 1))]
    whole = pl.BlockSpec((8, count), lambda j: (0, 0))
    sides = [
        pl.BlockSpec((components, 2 * LEVELS, WIDE), lambda j, half=half, at=at: (0, half, at(j)))
        for half, at in places
    ]
    weights = [pl.BlockSpec((2 * count, WIDE), lambda j, at=at: (0, at(j))) for _, at in places]
    column = pl.BlockSpec(left.shape, lambda j: (0, 0, 0))
    fields = [pltpu.VMEM((components, LEVELS, rows, WIDE), F32)] * 3
    return pl.pallas_call(
        update_kernel,
        grid=(steps,),
        in_specs=[whole, whole, pl.BlockSpec(operator.shape, lambda j: (0, 0))]
        + sides + sides + weights + [hbm, hbm, column, column],
        out_specs=pl.BlockSpec((components, depth, rows, WIDE), lambda j: (0, 0, 0, j)),
        out_shape=jax.ShapeDtypeStruct(velocity.shape, F32),
        scratch_shapes=[
            pltpu.VMEM((components, depth + 4, rows, cols + 256), F32),
            pltpu.VMEM((2, components * LEVELS * rows, 3 * count), BF16),
            fields,
            fields,
            pltpu.SemaphoreType.DMA((steps,)),
            pltpu.SemaphoreType.DMA,
        ],
        compiler_params=pltpu.CompilerParams(vmem_limit_bytes=44 * MIB),
        cost_estimate=LIGHT,
        name="update",
    )(
        own, force, operator, *([prev] * 3), *([after] * 3), *([weight] * 3),
        velocity, lev, left, right,
    )


def local(velocity, blade_pos, block_turbine, blade_vel, lift_coeff):
    components, depth, rows, cols = velocity.shape
    owned, _, points = blade_pos.shape
    gx, gy, gz = (lax.axis_size(axis) for axis in ("gx", "gy", "gz"))
    assert gz == 2 and depth == 2 * LEVELS
    per_turbine = owned * gz
    swap = [(0, 1), (1, 0)]

    def around(shift):
        return [(i, (i + shift) % gy) for i in range(gy)]

    up, down, facing, head, tail = prep(velocity, blade_pos, block_turbine, blade_vel, lift_coeff)
    before = lax.ppermute(tail, "gx", [(i, i + 1) for i in range(gx - 1)])
    after = lax.ppermute(head, "gx", [(i + 1, i) for i in range(gx - 1)])
    left = lax.ppermute(up, "gy", around(1))
    right = lax.ppermute(down, "gy", around(gy - 1))
    blocks = up[:owned]
    parts = [blocks, left[:owned]]
    parts += [lax.ppermute(blocks, "gy", around(shift)) for shift in range(2, gy - 1)]
    parts.append(right[:owned])
    mine = jnp.concatenate(parts, axis=0)
    twin = lax.ppermute(mine, "gz", swap)
    lev = lax.ppermute(facing, "gz", swap)

    part, own, weight = sample(mine, twin, velocity, per_turbine)
    other = lax.ppermute(part, "gz", swap)
    force, home = point_forces(mine, twin, part, other, own, per_turbine, owned)
    result = home[0]
    for shift in range(1, gy):
        result += lax.ppermute(home[shift], "gy", around(gy - shift))

    operator = jnp.asarray(stencil_operator(rows))
    new_velocity = update(
        own, force, operator, before, after, weight, velocity, lev, left[owned:], right[owned:]
    )
    return (new_velocity, result[:, :3, :])


def solution(mesh):
    in_specs = (
        P(None, "gz", "gx", "gy"),
        P(("gx", "gy", "gz"), None, None),
        P(("gx", "gy", "gz")),
        P(("gx", "gy", "gz"), None, None),
        P(("gx", "gy", "gz"), None),
    )
    out_specs = (P(None, "gz", "gx", "gy"), P(("gx", "gy", "gz"), None, None))
    return jax.shard_map(local, mesh=mesh, in_specs=in_specs, out_specs=out_specs, check_vma=False)
```

time: 86.9 us -> 65.2 us (0.75)
  local copies, waits for them, and re-layouts: 16.5 us -> 4.09 us
  starting transfers between devices: 20.7 us -> 14.9 us
  waiting for transfers between devices: 19 us -> 13.8 us
  Pallas kernels: 29.2 us -> 30.9 us
    unnamed x33 -> x5, local copies, waits for them, and re-layouts: 15.7 us -> 3.37 us
    ppermute x4 -> x2, waiting for transfers between devices: 12.1 us -> 0.01 us  [the longest x1 0.01 us: local(): before = lax.ppermute(tail, 'gx', [(i, i + 1) for i in range(gx - 1)])]
    ppermute x3, waiting for transfers between devices: 0.01 us -> 6.15 us  [local(): result += lax.ppermute(home[shift], 'gy', around(gy - shift))]
    ppermute x4 -> x2, starting transfers between devices: 10.6 us -> 6.17 us  [the longest x1 4.88 us: local(): before = lax.ppermute(tail, 'gx', [(i, i + 1) for i in range(gx - 1)])]
    ppermute x1, waiting for transfers between devices: 0.01 us -> 3.89 us  [local(): lax.ppermute(blocks, 'gy', around(shift))]
    pallas_call x1, Pallas kernels: 1.21 us -> 5.09 us  [prep(): pl.pallas_call(prep_kernel, grid=(components,), in_specs=[pl.BlockSpec(me...]
    ppermute x1, starting transfers between devices: 5.1 us -> 2.25 us  [local(): right = lax.ppermute(down, 'gy', around(gy - 1))]
    ppermute x1, waiting for transfers between devices: 4.11 us -> 1.54 us  [local(): left = lax.ppermute(up, 'gy', around(1))]
  transfers between devices with their start and end apart: 13 -> 11, of which waited for: 6 -> 6; matrix products, arithmetic and copies ran while one was open for 2% -> 2% of each run, Pallas kernels for 21% -> 12%
where the time goes in v3:
time: 65.2 us; the launch traced here: 64.4 us
  Pallas kernels  30.9 us (47%)
  starting transfers between devices  14.9 us (23%)
  waiting for transfers between devices  13.8 us (21%)
  local copies, waits for them, and re-layouts  4.09 us (6%)
  between operations  0.73 us (1%)
    pallas_call x1, Pallas kernels, update(): pl.pallas_call(update_kernel, grid=(steps,), in_specs=[whole, whole, pl.B...  17.8 us
    pallas_call x1, Pallas kernels, sample(): pl.pallas_call(functools.partial(sample_kernel, per_turbine), grid=(cols...  7.94 us
    ppermute x3, waiting for transfers between devices, local(): result += lax.ppermute(home[shift], 'gy', around(gy - shift))  6.15 us
    pallas_call x1, Pallas kernels, prep(): pl.pallas_call(prep_kernel, grid=(components,), in_specs=[pl.BlockSpec(me...  5.09 us
    ppermute x1, starting transfers between devices, local(): before = lax.ppermute(tail, 'gx', [(i, i + 1) for i in range(gx - 1)])  4.88 us
    ppermute x1, waiting for transfers between devices, local(): lax.ppermute(blocks, 'gy', around(shift))  3.89 us
    ppermute x3, starting transfers between devices, local(): result += lax.ppermute(home[shift], 'gy', around(gy - shift))  3.87 us
    unnamed x5, local copies, waits for them, and re-layouts  3.37 us
  transfers between devices with their start and end apart: 11, of which 6 were waited for; matrix products, arithmetic and copies ran while one was open for 2% of the time, Pallas kernels for 12%

profile of v3, /device:TPU:0, one launch (start us, length us, event | category | flops | bytes accessed | tf_op | source)
XLA Modules:
  0.0 64.4 jit_solution(15344327461822324007)
XLA Ops:
  0.6 0.0 copy-start.1
  0.6 5.1 %prep.1 = (f32[8,8,128]{2,1,0:T(8,128)}, f32[8,8,128]{2,1,0:T(8,128)}, f32[3,2,16,2048]{3,2,1,0:T(8,128)}, f32[3,32,2048]{2,1,0:T(8,128)}, f32[3,32,2048]{2,1,0:T(8,128)}) custom-call(s32[2]{0:T(128)} %turb_ref.1, f32[3,2,128]{2,1,0:T(2,128)} %bitcast.10, f32[3,2,128]{2,1,0:T(2,128)} %bitcast.11, f32[2,128]{1,0:T(2,128)} %lift_ref.1, f32[3,16,16,2048]{3,2,1,0:T(8,128)} %vel_ref.5), custom_call_target="tpu_custom_call" | custom-call | tf_op jit(solution)/shard_map/prep/pallas_call | solution.py:120
  5.7 4.9 %collective-permute-start.5 = (f32[3,32,2048]{2,1,0:T(8,128)}, f32[3,32,2048]{2,1,0:T(8,128)S(1)}, u32[]{:S(2)}, u32[]{:S(2)}) collective-permute-start(f32[3,32,2048]{2,1,0:T(8,128)} %get-tuple-element.17), channel_id=1, source_target_pairs={{0,8},{8,16},{16,24},{1,9},{9,17},{17,25},{2,10},{10,18},{18,26},{... | collective-permute-start | bytes 2359304 | tf_op jit(solution)/shard_map/ppermute | solution.py:520
  10.6 1.3 %collective-permute-start.6 = (f32[3,32,2048]{2,1,0:T(8,128)}, f32[3,32,2048]{2,1,0:T(8,128)S(1)}, u32[]{:S(2)}, u32[]{:S(2)}) collective-permute-start(f32[3,32,2048]{2,1,0:T(8,128)} %get-tuple-element.18), channel_id=1, source_target_pairs={{8,0},{16,8},{24,16},{9,1},{17,9},{25,17},{10,2},{18,10},{26,18},{... | collective-permute-start | bytes 2359304 | tf_op jit(solution)/shard_map/ppermute | solution.py:521
  11.9 0.1 collective-permute-start.7
  12.0 1.6 %collective-permute-start = (f32[8,8,128]{2,1,0:T(8,128)}, f32[8,8,128]{2,1,0:T(8,128)S(1)}, u32[]{:S(2)}, u32[]{:S(2)}) collective-permute-start(f32[8,8,128]{2,1,0:T(8,128)} %get-tuple-element.12), channel_id=1, source_target_pairs={{0,2},{2,4},{4,6},{6,0},{1,3},{3,5},{5,7},{7,1},{8,10},{10,12},{12... | collective-permute-start | bytes 98312 | tf_op jit(solution)/shard_map/ppermute | solution.py:522
  13.6 2.2 %collective-permute-start.2 = (f32[8,8,128]{2,1,0:T(8,128)}, f32[8,8,128]{2,1,0:T(8,128)S(1)}, u32[]{:S(2)}, u32[]{:S(2)}) collective-permute-start(f32[8,8,128]{2,1,0:T(8,128)} %get-tuple-element.13), channel_id=1, source_target_pairs={{0,6},{2,0},{4,2},{6,4},{1,7},{3,1},{5,3},{7,5},{8,14},{10,8},{12,... | collective-permute-start | bytes 98312 | tf_op jit(solution)/shard_map/ppermute | solution.py:523
  15.9 0.7 %slice.30 = f32[2,8,128]{2,1,0:T(8,128)S(1)} slice(f32[8,8,128]{2,1,0:T(8,128)} %get-tuple-element.12), slice={[0:2], [0:8], [0:128]} | slice | bytes 16384 | tf_op jit(solution)/shard_map/slice | solution.py:524
  16.6 1.5 %collective-permute-done = f32[8,8,128]{2,1,0:T(8,128)S(1)} collective-permute-done((f32[8,8,128]{2,1,0:T(8,128)}, f32[8,8,128]{2,1,0:T(8,128)S(1)}, u32[]{:S(2)}, u32[]{:S(2)}) %collective-permute-start) | collective-permute-done | bytes 32800 | tf_op jit(solution)/shard_map/ppermute | solution.py:522
  18.1 0.7 %collective-permute-start.1 = (f32[2,8,128]{2,1,0:T(8,128)S(1)}, f32[2,8,128]{2,1,0:T(8,128)S(1)}, u32[]{:S(2)}, u32[]{:S(2)}) collective-permute-start(f32[2,8,128]{2,1,0:T(8,128)S(1)} %slice.30), channel_id=1, source_target_pairs={{0,4},{2,6},{4,0},{6,2},{1,5},{3,7},{5,1},{7,3},{8,12},{10,14},{12... | collective-permute-start | bytes 24584 | tf_op jit(solution)/shard_map/ppermute | solution.py:526
  18.8 0.0 collective-permute-done.2
  18.8 3.9 %collective-permute-done.1 = f32[2,8,128]{2,1,0:T(8,128)S(1)} collective-permute-done((f32[2,8,128]{2,1,0:T(8,128)S(1)}, f32[2,8,128]{2,1,0:T(8,128)S(1)}, u32[]{:S(2)}, u32[]{:S(2)}) %collective-permute-start.1) | collective-permute-done | bytes 8224 | tf_op jit(solution)/shard_map/ppermute | solution.py:526
  22.7 0.0 collective-permute-start.3
  22.7 1.2 %collective-permute-done.3.twin_ref = f32[8,8,128]{2,1,0:T(8,128)S(1)} collective-permute-done((f32[8,8,128]{2,1,0:T(8,128)S(1)}, f32[8,8,128]{2,1,0:T(8,128)S(1)}, u32[]{:S(2)}, u32[]{:S(2)}) %collective-permute-start.3) | collective-permute-done | bytes 32800 | tf_op jit(solution)/shard_map/ppermute | solution.py:529
  23.9 0.0 copy-start
  23.9 2.8 %copy-done = f32[3,16,16,2048]{3,2,1,0:T(8,128)S(1)} copy-done((f32[3,16,16,2048]{3,2,1,0:T(8,128)S(1)}, f32[3,16,16,2048]{3,2,1,0:T(8,128)}, u32[]{:S(2)}) %copy-start) | copy-done | bytes 6291480
  26.7 7.9 %sample.1 = (f32[8,512]{1,0:T(8,128)S(1)}, f32[8,512]{1,0:T(8,128)S(1)}, bf16[1024,2048]{1,0:T(8,128)(2,1)S(1)}) custom-call(f32[8,8,128]{2,1,0:T(8,128)S(1)} %pad_maximum_fusion.mine_ref, f32[8,8,128]{2,1,0:T(8,128)S(1)} %collective-permute-done.3.twin_ref, f32[3,16,16,2048]{3,2,1,0:T(8,128)S(1)} %copy-done), custom_call_target="tpu_custom_call" | custom-call | tf_op jit(solution)/shard_map/sample/pallas_call | solution.py:253
  34.6 0.2 collective-permute-start.4
  34.8 1.0 %collective-permute-done.4.other_ref = f32[8,512]{1,0:T(8,128)S(1)} collective-permute-done((f32[8,512]{1,0:T(8,128)S(1)}, f32[8,512]{1,0:T(8,128)S(1)}, u32[]{:S(2)}, u32[]{:S(2)}) %collective-permute-start.4) | collective-permute-done | bytes 16416 | tf_op jit(solution)/shard_map/ppermute | solution.py:533
  35.9 0.1 force.1
  35.9 0.1 collective-permute-start.10
  36.0 3.8 %collective-permute-start.8 = (f32[2,8,128]{2,1,0:T(8,128)S(1)}, f32[2,8,128]{2,1,0:T(8,128)S(1)}, u32[]{:S(2)}, u32[]{:S(2)}) collective-permute-start(f32[2,8,128]{2,1,0:T(8,128)S(1)} %get-tuple-element.27), channel_id=1, source_target_pairs={{0,6},{2,0},{4,2},{6,4},{1,7},{3,1},{5,3},{7,5},{8,14},{10,8},{12,... | collective-permute-start | bytes 24584 | tf_op jit(solution)/shard_map/ppermute | solution.py:537
  39.8 1.6 %collective-permute-done.10 = f32[2,8,128]{2,1,0:T(8,128)S(1)} collective-permute-done((f32[2,8,128]{2,1,0:T(8,128)S(1)}, f32[2,8,128]{2,1,0:T(8,128)S(1)}, u32[]{:S(2)}, u32[]{:S(2)}) %collective-permute-start.10) | collective-permute-done | bytes 8224 | tf_op jit(solution)/shard_map/ppermute | solution.py:537
  41.4 0.0 collective-permute-start.9
  41.4 0.0 collective-permute-done.8
  41.5 4.5 %collective-permute-done.9 = f32[2,8,128]{2,1,0:T(8,128)S(1)} collective-permute-done((f32[2,8,128]{2,1,0:T(8,128)S(1)}, f32[2,8,128]{2,1,0:T(8,128)S(1)}, u32[]{:S(2)}, u32[]{:S(2)}) %collective-permute-start.9) | collective-permute-done | bytes 8224 | tf_op jit(solution)/shard_map/ppermute | solution.py:537
  46.0 0.6 copy.8
  46.6 0.0 collective-permute-done.5.prev0_ref.prev1_ref.prev2_ref
  46.6 0.0 collective-permute-done.6.next0_ref.next1_ref.next2_ref
  46.6 0.0 collective-permute-done.7.lev_ref
  46.6 0.0 copy-done.1
  46.6 17.8 %update.1 = f32[3,16,16,2048]{3,2,1,0:T(8,128)} custom-call(f32[8,512]{1,0:T(8,128)S(1)} %get-tuple-element.14.own_ref, f32[8,512]{1,0:T(8,128)S(1)} %get-tuple-element.16.force_ref, bf16[256,512]{1,0:T(8,128)(2,1)S(1)} %copy-done.1, f32[3,32,2048]{2,1,0:T(8,128)S(1)} %collective-permute-done.5.prev0_ref.prev1_ref.prev2_ref, ...), custom_call_target="tpu_custom_call" | custom-call | tf_op jit(solution)/shard_map/update/pallas_call | solution.py:484
  (7 shorter events, 0.0 us)
Async XLA Ops:
  0.6 46.0 %copy-start.1 = (bf16[256,512]{1,0:T(8,128)(2,1)S(1)}, bf16[256,512]{1,0:T(8,128)(2,1)}, u32[]{:S(2)}) copy-start(bf16[256,512]{1,0:T(8,128)(2,1)} %constant.2.clone.op_ref) | copy-start | bytes 786436
  5.7 40.8 %collective-permute-start.5 = (f32[3,32,2048]{2,1,0:T(8,128)}, f32[3,32,2048]{2,1,0:T(8,128)S(1)}, u32[]{:S(2)}, u32[]{:S(2)}) collective-permute-start(f32[3,32,2048]{2,1,0:T(8,128)} %get-tuple-element.17), channel_id=1, source_target_pairs={{0,8},{8,16},{16,24},{1,9},{9,17},{17,25},{2,10},{10,18},{18,26},{... | collective-permute-start | bytes 2359304 | tf_op jit(solution)/shard_map/ppermute | solution.py:520
  10.6 36.0 %collective-permute-start.6 = (f32[3,32,2048]{2,1,0:T(8,128)}, f32[3,32,2048]{2,1,0:T(8,128)S(1)}, u32[]{:S(2)}, u32[]{:S(2)}) collective-permute-start(f32[3,32,2048]{2,1,0:T(8,128)} %get-tuple-element.18), channel_id=1, source_target_pairs={{8,0},{16,8},{24,16},{9,1},{17,9},{25,17},{10,2},{18,10},{26,18},{... | collective-permute-start | bytes 2359304 | tf_op jit(solution)/shard_map/ppermute | solution.py:521
  11.9 34.7 %collective-permute-start.7 = (f32[3,2,16,2048]{3,2,1,0:T(8,128)}, f32[3,2,16,2048]{3,2,1,0:T(8,128)S(1)}, u32[]{:S(2)}, u32[]{:S(2)}) collective-permute-start(f32[3,2,16,2048]{3,2,1,0:T(8,128)} %get-tuple-element.20), channel_id=1, source_target_pairs={{0,1},{1,0},{2,3},{3,2},{4,5},{5,4},{6,7},{7,6},{8,9},{9,8},{10,11... | collective-permute-start | bytes 2359304 | tf_op jit(solution)/shard_map/ppermute | solution.py:530
  12.0 6.1 %collective-permute-start = (f32[8,8,128]{2,1,0:T(8,128)}, f32[8,8,128]{2,1,0:T(8,128)S(1)}, u32[]{:S(2)}, u32[]{:S(2)}) collective-permute-start(f32[8,8,128]{2,1,0:T(8,128)} %get-tuple-element.12), channel_id=1, source_target_pairs={{0,2},{2,4},{4,6},{6,0},{1,3},{3,5},{5,7},{7,1},{8,10},{10,12},{12... | collective-permute-start | bytes 98312 | tf_op jit(solution)/shard_map/ppermute | solution.py:522
  13.6 5.1 %collective-permute-start.2 = (f32[8,8,128]{2,1,0:T(8,128)}, f32[8,8,128]{2,1,0:T(8,128)S(1)}, u32[]{:S(2)}, u32[]{:S(2)}) collective-permute-start(f32[8,8,128]{2,1,0:T(8,128)} %get-tuple-element.13), channel_id=1, source_target_pairs={{0,6},{2,0},{4,2},{6,4},{1,7},{3,1},{5,3},{7,5},{8,14},{10,8},{12,... | collective-permute-start | bytes 98312 | tf_op jit(solution)/shard_map/ppermute | solution.py:523
  18.1 4.5 %collective-permute-start.1 = (f32[2,8,128]{2,1,0:T(8,128)S(1)}, f32[2,8,128]{2,1,0:T(8,128)S(1)}, u32[]{:S(2)}, u32[]{:S(2)}) collective-permute-start(f32[2,8,128]{2,1,0:T(8,128)S(1)} %slice.30), channel_id=1, source_target_pairs={{0,4},{2,6},{4,0},{6,2},{1,5},{3,7},{5,1},{7,3},{8,12},{10,14},{12... | collective-permute-start | bytes 24584 | tf_op jit(solution)/shard_map/ppermute | solution.py:526
  22.7 1.2 %collective-permute-start.3 = (f32[8,8,128]{2,1,0:T(8,128)S(1)}, f32[8,8,128]{2,1,0:T(8,128)S(1)}, u32[]{:S(2)}, u32[]{:S(2)}) collective-permute-start(f32[8,8,128]{2,1,0:T(8,128)S(1)} %pad_maximum_fusion.mine_ref), channel_id=1, source_target_pairs={{0,1},{1,0},{2,3},{3,2},{4,5},{5,4},{6,7},{7,6},{8,9},{9,8},{10,11... | collective-permute-start | bytes 98312 | tf_op jit(solution)/shard_map/ppermute | solution.py:529
  23.9 2.8 %copy-start = (f32[3,16,16,2048]{3,2,1,0:T(8,128)S(1)}, f32[3,16,16,2048]{3,2,1,0:T(8,128)}, u32[]{:S(2)}) copy-start(f32[3,16,16,2048]{3,2,1,0:T(8,128)} %vel_ref.5) | copy-start | bytes 18874372
  34.6 1.2 %collective-permute-start.4 = (f32[8,512]{1,0:T(8,128)S(1)}, f32[8,512]{1,0:T(8,128)S(1)}, u32[]{:S(2)}, u32[]{:S(2)}) collective-permute-start(f32[8,512]{1,0:T(8,128)S(1)} %get-tuple-element.15.part_ref), channel_id=1, source_target_pairs={{0,1},{1,0},{2,3},{3,2},{4,5},{5,4},{6,7},{7,6},{8,9},{9,8},{10,11... | collective-permute-start | bytes 49160 | tf_op jit(solution)/shard_map/ppermute | solution.py:533
  35.9 5.5 %collective-permute-start.10 = (f32[2,8,128]{2,1,0:T(8,128)S(1)}, f32[2,8,128]{2,1,0:T(8,128)S(1)}, u32[]{:S(2)}, u32[]{:S(2)}) collective-permute-start(f32[2,8,128]{2,1,0:T(8,128)S(1)} %get-tuple-element.25), channel_id=1, source_target_pairs={{0,2},{2,4},{4,6},{6,0},{1,3},{3,5},{5,7},{7,1},{8,10},{10,12},{12... | collective-permute-start | bytes 24584 | tf_op jit(solution)/shard_map/ppermute | solution.py:537
  36.0 5.5 %collective-permute-start.8 = (f32[2,8,128]{2,1,0:T(8,128)S(1)}, f32[2,8,128]{2,1,0:T(8,128)S(1)}, u32[]{:S(2)}, u32[]{:S(2)}) collective-permute-start(f32[2,8,128]{2,1,0:T(8,128)S(1)} %get-tuple-element.27), channel_id=1, source_target_pairs={{0,6},{2,0},{4,2},{6,4},{1,7},{3,1},{5,3},{7,5},{8,14},{10,8},{12,... | collective-permute-start | bytes 24584 | tf_op jit(solution)/shard_map/ppermute | solution.py:537
  41.4 4.5 %collective-permute-start.9 = (f32[2,8,128]{2,1,0:T(8,128)S(1)}, f32[2,8,128]{2,1,0:T(8,128)S(1)}, u32[]{:S(2)}, u32[]{:S(2)}) collective-permute-start(f32[2,8,128]{2,1,0:T(8,128)S(1)} %get-tuple-element.26), channel_id=1, source_target_pairs={{0,4},{2,6},{4,0},{6,2},{1,5},{3,7},{5,1},{7,3},{8,12},{10,14},{12... | collective-permute-start | bytes 24584 | tf_op jit(solution)/shard_map/ppermute | solution.py:537

commit v4 on v3

v4 whole, which is shorter than its diff:
```python
import functools
import math

import jax
import jax.numpy as jnp
import ml_dtypes
import numpy as np
from jax import lax
from jax.experimental import pallas as pl
from jax.experimental.pallas import tpu as pltpu
from jax.sharding import PartitionSpec as P

mean_wind = 1.0
viscosity = 0.2
smag_coeff = 0.17
time_step = 0.2
smear = 2.0
smear_norm = 1.0 / (smear**3 * math.pi**1.5)

F32 = jnp.float32
BF16 = jnp.bfloat16
MIB = 1024 * 1024
LEVELS = 8
STEP = 256
WIDE = 256
LIGHT = pl.CostEstimate(flops=0, bytes_accessed=0, transcendentals=0)


def split(value):
    high = value.astype(BF16)
    return high, (value - high.astype(F32)).astype(BF16)


def dot(left, right, contract=0):
    return lax.dot_general(
        left, right, (((1,), (contract,)), ((), ())), preferred_element_type=F32
    )


def gaussian(first, count, centers):
    shape = (count, centers.shape[1])
    cells = (first + lax.broadcasted_iota(jnp.int32, shape, 0)).astype(F32)
    gap = cells - centers
    return jnp.exp(-gap * gap / (smear * smear))


def stencil_operator(row_cells):
    inner = (LEVELS + 4) * row_cells
    width = inner + 4 * LEVELS
    op = np.zeros((2, LEVELS, row_cells, width), np.float32)

    def column(level, row):
        if 0 <= row < row_cells:
            return (level + 2) * row_cells + row
        if row < 0:
            return inner + level * 2 + row + 2
        return inner + 2 * LEVELS + level * 2 + row - row_cells

    for level in range(LEVELS):
        for row in range(row_cells):
            for offset, first, second in ((-2, 1, -1), (-1, -8, 16), (1, 8, 16), (2, -1, -1)):
                op[0, level, row, column(level, row + offset)] += first
                op[1, level, row, column(level, row + offset)] += second
                op[1, level, row, column(level + offset, row)] += second
            op[1, level, row, column(level, row)] -= 90
    op = op.reshape(2 * LEVELS * row_cells, width)
    op = np.pad(op, ((0, 0), (0, -width % 128)))
    return np.concatenate([op, op], axis=1).astype(ml_dtypes.bfloat16)


def prep_kernel(
    turb_in, pos_in, speed_in, lift_in, vel_in, blocks_ref, up_ref, down_ref, head_ref, tail_ref,
    turb_ref, pos_ref, speed_ref, lift_ref, vel_ref, sems,
):
    components, levels, rows, cols = vel_ref.shape
    coords, owned, points = pos_ref.shape
    small = [
        pltpu.make_async_copy(source, target, sems.at[components + k])
        for k, (source, target) in enumerate(
            ((turb_in, turb_ref), (pos_in, pos_ref), (speed_in, speed_ref), (lift_in, lift_ref))
        )
    ]
    large = [
        pltpu.make_async_copy(vel_in.at[i], vel_ref.at[i], sems.at[i]) for i in range(components)
    ]
    for copy in small + large:
        copy.start()
    for copy in small:
        copy.wait()
    for ref in (blocks_ref, up_ref, down_ref):
        for k in range(owned):
            for i in range(coords):
                ref[k, i : i + 1, :] = pos_ref[i, k : k + 1, :]
                ref[k, coords + i : coords + i + 1, :] = speed_ref[i, k : k + 1, :]
            ref[k, 2 * coords : 2 * coords + 1, :] = lift_ref[k : k + 1, :]
            ref[k, 7:8, :] = jnp.full((1, points), turb_ref[k].astype(F32))
    parts = levels * rows // 128
    row = lax.broadcasted_iota(jnp.int32, (8, cols), 0) // 2
    for component in range(components):
        large[component].wait()
        last = vel_ref[component, :, :, cols - 128 :].reshape(levels * rows, 128)
        first = vel_ref[component, :, :, :128].reshape(levels * rows, 128)
        for part in range(parts):
            cells = slice(part * 128, part * 128 + 128)
            up_ref[owned + component * parts + part] = last[cells].T[120:]
            down_ref[owned + component * parts + part] = first[cells].T[:8]
        for group in range(levels // 4):
            head = tail = None
            for k in range(4):
                top = vel_ref[component, group * 4 + k, 0:8, :]
                end = vel_ref[component, group * 4 + k, rows - 8 : rows, :]
                if k:
                    top = pltpu.roll(top, 2 * k, 0)
                if k < 3:
                    end = pltpu.roll(end, 2 * k + 2, 0)
                head = top if head is None else jnp.where(row == k, top, head)
                tail = end if tail is None else jnp.where(row == k, end, tail)
            head_ref[component, group * 8 : group * 8 + 8, :] = head
            tail_ref[component, group * 8 : group * 8 + 8, :] = tail


def prep(velocity, blade_pos, block_turbine, blade_vel, lift_coeff):
    components, levels, rows, cols = velocity.shape
    owned, coords, points = blade_pos.shape
    tiles = owned + components * levels * rows // 128
    return pl.pallas_call(
        prep_kernel,
        in_specs=[pl.BlockSpec(memory_space=pltpu.HBM)] * 5,
        out_specs=[pl.BlockSpec(memory_space=pltpu.VMEM)] * 5,
        out_shape=[
            jax.ShapeDtypeStruct((owned, 8, points), F32),
            jax.ShapeDtypeStruct((tiles, 8, 128), F32),
            jax.ShapeDtypeStruct((tiles, 8, 128), F32),
            jax.ShapeDtypeStruct((components, 2 * levels, cols), F32),
            jax.ShapeDtypeStruct((components, 2 * levels, cols), F32),
        ],
        scratch_shapes=[
            pltpu.SMEM((owned,), jnp.int32),
            pltpu.VMEM((coords, owned, points), F32),
            pltpu.VMEM((coords, owned, points), F32),
            pltpu.VMEM((owned, points), F32),
            pltpu.VMEM(velocity.shape, F32),
            pltpu.SemaphoreType.DMA((components + 4,)),
        ],
        compiler_params=pltpu.CompilerParams(vmem_limit_bytes=60 * MIB),
        cost_estimate=LIGHT,
        name="prep",
    )(
        block_turbine,
        blade_pos.transpose(1, 0, 2),
        blade_vel.transpose(1, 0, 2),
        lift_coeff,
        velocity,
    )


def match(mine_ref, twin_ref, per_turbine):
    core = lax.axis_index("gz")
    turbine = lax.axis_index("gy").astype(F32)
    half = mine_ref.shape[0]
    first = [(mine_ref[k, 7:8, :] == turbine).astype(F32) for k in range(half)]
    second = [(twin_ref[k, 7:8, :] == turbine).astype(F32) for k in range(half)]
    masks = []
    for hits, others, leads in ((first, second, core == 0), (second, first, core == 1)):
        rank = jnp.where(leads, jnp.zeros_like(hits[0]), sum(others))
        for hit in hits:
            masks.append([(hit > 0.5) & (rank == k) for k in range(per_turbine)])
            rank = rank + hit
    return masks


def sample_kernel(
    per_turbine, mine_ref, twin_ref, vel_in, part_ref, own_ref, weight_ref, lev_ref,
    even_ref, odd_ref, center_ref, plane_ref, acc_ref, vel_ref, sems, lev_sem,
):
    step = pl.program_id(0)
    steps = pl.num_programs(0)
    components, depth, rows, cols = vel_ref.shape
    points = mine_ref.shape[2]
    count = per_turbine * points
    cells = depth * rows
    half = cols // (2 * steps)
    core = lax.axis_index("gz")
    start = lax.axis_index("gy") * cols

    def column_copy(at):
        column = pl.ds(pl.multiple_of(at * 2 * half, 128), 2 * half)
        return pltpu.make_async_copy(
            vel_in.at[:, :, :, column], vel_ref.at[:, :, :, column], sems.at[at]
        )

    lev_copy = pltpu.make_async_copy(
        vel_in.at[:, pl.ds(jnp.where(core == 0, depth - 2, 0), 2)], lev_ref, lev_sem
    )

    def bell(cell, center):
        gap = cell.astype(F32) - center
        return jnp.exp(gap * gap * (-1.0 / (smear * smear)))

    def weights(at, ref, slot):
        band = slice(slot * points, (slot + 1) * points)
        lane = lax.broadcasted_iota(jnp.int32, (1, 128), 1)
        for part in range(half // 128):
            cell = start + at * half + part * 128 + lane
            ref[band, part * 128 : part * 128 + 128] = bell(cell, center_ref[band, :])

    def multiply(side, ref, i):
        column = pl.ds(pl.multiple_of((2 * step + side) * half, 128), half)
        high, low = split(vel_ref[i, :, :, column].reshape(cells, half))
        field = dot(plane_ref[...], jnp.concatenate([high, high, low], axis=0))
        product = field * ref[...]
        total = acc_ref[i]
        for part in range(half // 128):
            total += product[:, part * 128 : part * 128 + 128]
        acc_ref[i] = total

    def hand_out(side, ref, slot):
        band = slice(slot * points, (slot + 1) * points)
        high, low = split(ref[band, :])
        column = slice(side * half, side * half + half)
        weight_ref[band, column] = high
        weight_ref[count + slot * points : count + (slot + 1) * points, column] = low

    @pl.when(step == 0)
    def _():
        for at in range(cols // (2 * half)):
            column_copy(at).start()
        lev_copy.start()
        masks = match(mine_ref, twin_ref, per_turbine)
        blocks = mine_ref.shape[0]
        lane = lax.broadcasted_iota(jnp.int32, (1, cells), 1)
        level = core * depth + lane // rows
        row = lax.axis_index("gx") * rows + lane % rows
        for k in range(per_turbine):
            total = jnp.zeros((8, points), F32)
            for at, mask in enumerate(masks):
                tile = mine_ref[at] if at < blocks else twin_ref[at - blocks]
                total = jnp.where(mask[k], tile, total)
            band = slice(k * points, (k + 1) * points)
            own_ref[:, band] = total
            turned = total.T
            center_ref[band, :] = jnp.broadcast_to(turned[:, 1:2], (points, 128))
            plane = bell(row, turned[:, 0:1]) * bell(level, turned[:, 2:3])
            high, low = split(plane)
            plane_ref[band, :cells] = high
            plane_ref[band, cells : 2 * cells] = low
            plane_ref[band, 2 * cells :] = high
            weights(0, even_ref, k)
        acc_ref[...] = jnp.zeros(acc_ref.shape, F32)

    column_copy(step).wait()
    for side, now, later in ((0, even_ref, odd_ref), (1, odd_ref, even_ref)):
        for k in range(max(per_turbine, components)):
            if k < per_turbine:
                weights(2 * step + side + 1, later, k)
                hand_out(side, now, k)
            if k < components:
                multiply(side, now, k)

    @pl.when(step == steps - 1)
    def _():
        for i in range(components):
            for k in range(per_turbine):
                band = slice(k * points, (k + 1) * points)
                total = jnp.sum(acc_ref[i, band, :].T, axis=0, keepdims=True)
                part_ref[i : i + 1, band] = smear_norm * total
        part_ref[components:, :] = jnp.zeros((8 - components, count), F32)
        lev_copy.wait()


def sample(mine, twin, velocity, per_turbine):
    components, depth, rows, cols = velocity.shape
    points = mine.shape[2]
    count = per_turbine * points
    steps = cols // (2 * STEP)
    whole = pl.BlockSpec((8, count), lambda j: (0, 0))
    table = pl.BlockSpec(mine.shape, lambda j: (0, 0, 0))
    return pl.pallas_call(
        functools.partial(sample_kernel, per_turbine),
        grid=(steps,),
        in_specs=[table, table, pl.BlockSpec(memory_space=pltpu.HBM)],
        out_specs=[
            whole,
            whole,
            pl.BlockSpec((2 * count, 2 * STEP), lambda j: (0, j)),
            pl.BlockSpec((components, 2, rows, cols), lambda j: (0, 0, 0, 0)),
        ],
        out_shape=[
            jax.ShapeDtypeStruct((8, count), F32),
            jax.ShapeDtypeStruct((8, count), F32),
            jax.ShapeDtypeStruct((2 * count, cols), BF16),
            jax.ShapeDtypeStruct((components, 2, rows, cols), F32),
        ],
        scratch_shapes=[
            pltpu.VMEM((count, STEP), F32),
            pltpu.VMEM((count, STEP), F32),
            pltpu.VMEM((count, 128), F32),
            pltpu.VMEM((count, 3 * depth * rows), BF16),
            pltpu.VMEM((components, count, 128), F32),
            pltpu.VMEM(velocity.shape, F32),
            pltpu.SemaphoreType.DMA((steps,)),
            pltpu.SemaphoreType.DMA,
        ],
        compiler_params=pltpu.CompilerParams(vmem_limit_bytes=60 * MIB),
        cost_estimate=LIGHT,
        name="sample",
    )(mine, twin, velocity)


def force_kernel(
    per_turbine, owned, mine_ref, twin_ref, part_ref, other_ref, own_ref, force_ref, home_ref
):
    points = own_ref.shape[1] // per_turbine
    relative = part_ref[0:3, :] + other_ref[0:3, :] - own_ref[3:6, :]
    speed = jnp.sqrt(jnp.sum(relative * relative, axis=0, keepdims=True))
    force = -own_ref[6:7, :] * speed * relative
    force_ref[...] = jnp.zeros(force_ref.shape, F32)
    force_ref[0:3, :] = force
    masks = match(mine_ref, twin_ref, per_turbine)
    for row in range(mine_ref.shape[0]):
        total = jnp.zeros((3, points), F32)
        for k in range(per_turbine):
            total = jnp.where(masks[row][k], force[:, k * points : (k + 1) * points], total)
        for i in range(3):
            home_ref[row // owned, i, row % owned : row % owned + 1, :] = total[i : i + 1]


def point_forces(mine, twin, part, other, own, per_turbine, owned):
    count = own.shape[1]
    points = count // per_turbine
    shifts = mine.shape[0] // owned
    return pl.pallas_call(
        functools.partial(force_kernel, per_turbine, owned),
        in_specs=[pl.BlockSpec(memory_space=pltpu.VMEM)] * 5,
        out_specs=[pl.BlockSpec(memory_space=pltpu.VMEM)] * 2,
        out_shape=[
            jax.ShapeDtypeStruct((8, count), F32),
            jax.ShapeDtypeStruct((shifts, 3, owned, points), F32),
        ],
        compiler_params=pltpu.CompilerParams(vmem_limit_bytes=8 * MIB),
        cost_estimate=LIGHT,
        name="force",
    )(mine, twin, part, other, own)


def update_kernel(
    own_ref, force_ref, op_ref, prev0_ref, prev1_ref, prev2_ref, next0_ref, next1_ref, next2_ref,
    weight0_ref, weight1_ref, weight2_ref, vel_ref, lev_ref, left_ref, right_ref,
    out_ref, pad_ref, high_ref, low_ref, even, odd, sems, edge_sem,
):
    step = pl.program_id(0)
    steps = pl.num_programs(0)
    components, depth, rows, cols = vel_ref.shape
    halves = depth // LEVELS
    width = cols // (2 * steps)
    cells = LEVELS * rows
    inner = (LEVELS + 4) * rows
    fill = op_ref.shape[1] // 2 - inner - 4 * LEVELS
    count = own_ref.shape[1]
    core = lax.axis_index("gz")
    turbine = lax.axis_index("gy")

    def column_copy(at):
        here = pl.multiple_of(at * width, 128)
        there = pl.multiple_of(at * width + 128, 128)
        return pltpu.make_async_copy(
            vel_ref.at[:, :, :, pl.ds(here, width)],
            pad_ref.at[:, pl.ds(2, depth), :, pl.ds(there, width)],
            sems.at[at],
        )

    def level_edge(at, owner):
        copy = pltpu.make_async_copy(
            lev_ref, pad_ref.at[:, pl.ds(at, 2), :, pl.ds(128, cols)], edge_sem
        )

        @pl.when(core == owner)
        def _():
            copy.start()
            copy.wait()

        @pl.when(core != owner)
        def _():
            pad_ref[:, at : at + 2, :, 128 : cols + 128] = jnp.zeros((components, 2, rows, cols), F32)

    def side_columns(ref, present, lane):
        per_part = 128 // rows
        parts = ref.shape[0] // components
        for tile in range(ref.shape[0]):
            turned = jnp.where(present, ref[tile], 0.0).T
            for k in range(per_part):
                level = (tile % parts) * per_part + k
                pad_ref[tile // parts, level + 2, :, lane : lane + 8] = turned[k * rows : (k + 1) * rows, :]

    def matrix_parts(at, prev_ref, next_ref, weight_ref, bufs):
        grad_ref, lap_ref, body_ref = bufs
        center = pl.ds(pl.multiple_of(at * width + 128, 128), width)

        def stencil(i, half):
            levels = slice(half * LEVELS, (half + 1) * LEVELS)
            column = pad_ref[i, half * LEVELS : (half + 1) * LEVELS + 4, :, center]
            inner_high, inner_low = split(column.reshape(inner, width))
            side = slice(half * 2 * LEVELS, (half + 1) * 2 * LEVELS)
            prev_high, prev_low = split(prev_ref[i, side])
            next_high, next_low = split(next_ref[i, side])
            empty = [jnp.zeros((fill, width), BF16)] if fill else []
            high = [inner_high, prev_high, next_high] + empty
            low = [inner_low, prev_low, next_low] + empty
            result = dot(op_ref[...], jnp.concatenate(high + low, axis=0))
            grad_ref[i, levels] = result[:cells].reshape(LEVELS, rows, width)
            lap_ref[i, levels] = result[cells:].reshape(LEVELS, rows, width)

        def body(wide_ref, band, first):
            result = dot(wide_ref[...], weight_ref[band, :])
            result = result.reshape(components, depth, rows, width)
            body_ref[...] = result if first else body_ref[...] + result

        upper, lower = slice(0, count), slice(count, 2 * count)
        yield lambda: body(high_ref, upper, True)
        yield lambda: stencil(0, 0)
        yield lambda: stencil(0, 1)
        yield lambda: body(low_ref, upper, False)
        yield lambda: stencil(1, 0)
        yield lambda: stencil(1, 1)
        yield lambda: body(high_ref, lower, False)
        yield lambda: stencil(2, 0)
        yield lambda: stencil(2, 1)

    def vector_parts(at, bufs, offset):
        grad_ref, lap_ref, body_ref = bufs
        base = at * width
        lane = lax.broadcasted_iota(jnp.int32, (8, 128), 1)
        shifts = ((1, lane < 1), (2, lane < 2), (127, lane >= 127), (126, lane >= 126))

        def cell(i, level, band, block):
            return pad_ref[i, level, band, pl.ds(pl.multiple_of(base + block * 128, 128), 128)]

        def work(level, band):
            here = level + 2
            turned = {}

            def turn(i, block, shift):
                if (i, block, shift) not in turned:
                    turned[i, block, shift] = pltpu.roll(cell(i, here, band, block), shift, 1)
                return turned[i, block, shift]

            for block in range(1, width // 128 + 1):
                lanes = slice(block * 128 - 128, block * 128)
                along_y, lap, along_z = [], [], []
                for i in range(components):
                    behind, behind2, ahead, ahead2 = [
                        jnp.where(
                            wrapped,
                            turn(i, block - 1 if shift < 64 else block + 1, shift),
                            turn(i, block, shift),
                        )
                        for shift, wrapped in shifts
                    ]
                    along_y.append(8.0 * (ahead - behind) - (ahead2 - behind2))
                    lap.append(
                        lap_ref[i, level, band, lanes]
                        + (16.0 * (ahead + behind) - (ahead2 + behind2))
                    )
                    near = cell(i, here + 1, band, block) - cell(i, here - 1, band, block)
                    far = cell(i, here + 2, band, block) - cell(i, here - 2, band, block)
                    along_z.append(8.0 * near - far)
                along_x = [grad_ref[i, level, band, lanes] for i in range(components)]
                same = along_x[0] * along_x[0] + along_y[1] * along_y[1] + along_z[2] * along_z[2]
                xy = along_x[1] + along_y[0]
                xz = along_x[2] + along_z[0]
                yz = along_y[2] + along_z[1]
                strain = 2.0 * same + (xy * xy + xz * xz + yz * yz)
                mixing = (time_step / 12.0) * viscosity + (
                    time_step * smag_coeff * smag_coeff / 144.0
                ) * jnp.sqrt(strain)
                out_lanes = slice(offset + block * 128 - 128, offset + block * 128)
                for i in range(components):
                    change = mixing * lap[i] - (time_step * mean_wind / 12.0) * along_x[i]
                    out_ref[i, level, band, out_lanes] = (
                        cell(i, here, band, block) + body_ref[i, level, band, lanes] + change
                    )

        for level in range(depth):
            for row in range(0, rows, 8):
                yield functools.partial(work, level, slice(row, row + 8))

    def together(matrix, vector):
        matrix, vector = list(matrix), list(vector)
        done = 0
        for k, piece in enumerate(matrix):
            piece()
            until = (k + 1) * len(vector) // len(matrix)
            for other in vector[done:until]:
                other()
            done = until

    @pl.when(step == 0)
    def _():
        for at in range(cols // width):
            column_copy(at).start()
        level_edge(0, 1)
        level_edge(depth + 2, 0)
        side_columns(left_ref, turbine > 0, 120)
        side_columns(right_ref, turbine < lax.axis_size("gy") - 1, cols + 128)
        along_x = gaussian(lax.axis_index("gx") * rows, rows, own_ref[0:1, :])
        along_z = gaussian(core * depth, depth, own_ref[2:3, :])
        for i in range(components):
            scaled = (time_step * smear_norm) * force_ref[i : i + 1, :] * along_x
            for level in range(depth):
                band = slice((i * depth + level) * rows, (i * depth + level + 1) * rows)
                high, low = split(scaled * along_z[level : level + 1, :])
                high_ref[band, :] = high
                low_ref[band, :] = low
        column_copy(0).wait()
        for piece in matrix_parts(0, prev0_ref, next0_ref, weight0_ref, even):
            piece()

    column_copy(2 * step + 1).wait()

    @pl.when(step < steps - 1)
    def _():
        column_copy(2 * step + 2).wait()

    last = 2 * steps - 1
    together(
        matrix_parts(2 * step + 1, prev1_ref, next1_ref, weight1_ref, odd),
        vector_parts(2 * step, even, 0),
    )
    together(
        matrix_parts(jnp.minimum(2 * step + 2, last), prev2_ref, next2_ref, weight2_ref, even),
        vector_parts(2 * step + 1, odd, width),
    )


def update(own, force, operator, prev, after, weight, velocity, lev, left, right):
    components, depth, rows, cols = velocity.shape
    count = own.shape[1]
    steps = cols // (2 * WIDE)
    hbm = pl.BlockSpec(memory_space=pltpu.HBM)
    places = [lambda j: 0, lambda j: 2 * j + 1, lambda j: jnp.minimum(2 * j + 2, 2 * steps - 1)]
    whole = pl.BlockSpec((8, count), lambda j: (0, 0))
    sides = [
        pl.BlockSpec((components, 2 * depth, WIDE), lambda j, at=at: (0, 0, at(j))) for at in places
    ]
    weights = [pl.BlockSpec((2 * count, WIDE), lambda j, at=at: (0, at(j))) for at in places]
    column = pl.BlockSpec(left.shape, lambda j: (0, 0, 0))
    fields = [pltpu.VMEM((components, depth, rows, WIDE), F32)] * 3
    macs = components * depth * rows * cols * (3 * count + 4 * 256)
    return pl.pallas_call(
        update_kernel,
        grid=(steps,),
        in_specs=[whole, whole, pl.BlockSpec(operator.shape, lambda j: (0, 0))]
        + sides + sides + weights
        + [hbm, pl.BlockSpec(memory_space=pl.ANY), column, column],
        out_specs=pl.BlockSpec((components, depth, rows, 2 * WIDE), lambda j: (0, 0, 0, j)),
        out_shape=jax.ShapeDtypeStruct(velocity.shape, F32),
        scratch_shapes=[
            pltpu.VMEM((components, depth + 4, rows, cols + 256), F32),
            pltpu.VMEM((components * depth * rows, count), BF16),
            pltpu.VMEM((components * depth * rows, count), BF16),
            fields,
            fields,
            pltpu.SemaphoreType.DMA((2 * steps,)),
            pltpu.SemaphoreType.DMA,
        ],
        compiler_params=pltpu.CompilerParams(vmem_limit_bytes=63 * MIB),
        cost_estimate=pl.CostEstimate(
            flops=2 * macs, bytes_accessed=8 * velocity.size, transcendentals=velocity.size // 3
        ),
        name="update",
    )(
        own, force, operator, *([prev] * 3), *([after] * 3), *([weight] * 3),
        velocity, lev, left, right,
    )


def local(velocity, blade_pos, block_turbine, blade_vel, lift_coeff):
    components, depth, rows, cols = velocity.shape
    owned, _, points = blade_pos.shape
    gx, gy, gz = (lax.axis_size(axis) for axis in ("gx", "gy", "gz"))
    assert gz == 2 and depth == 2 * LEVELS
    per_turbine = owned * gz
    swap = [(0, 1), (1, 0)]

    def around(shift):
        return [(i, (i + shift) % gy) for i in range(gy)]

    blocks, up, down, head, tail = prep(velocity, blade_pos, block_turbine, blade_vel, lift_coeff)
    before = lax.ppermute(tail, "gx", [(i, i + 1) for i in range(gx - 1)])
    after = lax.ppermute(head, "gx", [(i + 1, i) for i in range(gx - 1)])
    def blade(blocks, up, down, velocity):
        left = lax.ppermute(up, "gy", around(1))
        right = lax.ppermute(down, "gy", around(gy - 1))
        parts = [blocks, left[:owned]]
        parts += [lax.ppermute(blocks, "gy", around(shift)) for shift in range(2, gy - 1)]
        parts.append(right[:owned])
        mine = jnp.concatenate(parts, axis=0)
        twin = lax.ppermute(mine, "gz", swap)
        part, own, weight, facing = sample(mine, twin, velocity, per_turbine)
        other = lax.ppermute(part, "gz", swap)
        force, home = point_forces(mine, twin, part, other, own, per_turbine, owned)
        return own, force, home, weight, facing, left[owned:], right[owned:]

    operands = (blocks, up, down, velocity)
    empty = [jnp.zeros(out.shape, out.dtype) for out in jax.eval_shape(blade, *operands)]
    own, force, home, weight, facing, left, right = lax.cond(
        block_turbine[0] >= 0, blade, lambda *_: tuple(empty), *operands
    )
    lev = lax.ppermute(facing, "gz", swap)
    result = home[0]
    for shift in range(1, gy):
        result += lax.ppermute(home[shift], "gy", around(gy - shift))

    operator = jnp.asarray(stencil_operator(rows))
    new_velocity = update(
        own, force, operator, before, after, weight, velocity, lev, left, right
    )
    return (new_velocity, result.transpose(1, 0, 2))


def solution(mesh):
    in_specs = (
        P(None, "gz", "gx", "gy"),
        P(("gx", "gy", "gz"), None, None),
        P(("gx", "gy", "gz")),
        P(("gx", "gy", "gz"), None, None),
        P(("gx", "gy", "gz"), None),
    )
    out_specs = (P(None, "gz", "gx", "gy"), P(("gx", "gy", "gz"), None, None))
    return jax.shard_map(local, mesh=mesh, in_specs=in_specs, out_specs=out_specs, check_vma=False)
```

time: 65.2 us -> 68.9 us (1.057)
  Pallas kernels: 30.9 us -> 36.7 us
  waiting for transfers between devices: 13.8 us -> 12.4 us
  starting transfers between devices: 14.9 us -> 14.1 us
    pallas_call x1, Pallas kernels: 17.8 us -> 21.9 us  [update(): pl.pallas_call(update_kernel, grid=(steps,), in_specs=[whole, whole, pl.B...]
    cond x0 -> x10, local copies, waits for them, and re-layouts: none -> 2.85 us
    unnamed x5 -> x6, local copies, waits for them, and re-layouts: 3.37 us -> 0.9 us
    ppermute x5, waiting for transfers between devices: 7.66 us -> 6.17 us  [the longest x1 2.41 us: blade(): lax.ppermute(blocks, 'gy', around(shift))]
    ppermute x3, starting transfers between devices: 3.87 us -> 2.81 us  [local(): result += lax.ppermute(home[shift], 'gy', around(gy - shift))]
    pallas_call x2, Pallas kernels: 13 us -> 14.1 us  [the longest x1 9.83 us: sample(): pl.pallas_call(functools.partial(sample_kernel, per_turbine), grid=(steps...]
    ppermute x1, waiting for transfers between devices: 0.01 us -> 0.99 us  [local(): after = lax.ppermute(head, 'gx', [(i + 1, i) for i in range(gx - 1)])]
    ppermute x3, waiting for transfers between devices: 6.15 us -> 5.27 us  [local(): result += lax.ppermute(home[shift], 'gy', around(gy - shift))]
  transfers between devices with their start and end apart: 11 -> 11, of which waited for: 6 -> 8; matrix products, arithmetic and copies ran while one was open for 2% -> 1% of each run, Pallas kernels for 12% -> 15%
where the time goes in v4:
time: 68.9 us; the launch traced here: 68.4 us
  Pallas kernels  36.7 us (53%)
  starting transfers between devices  14.1 us (20%)
  waiting for transfers between devices  12.4 us (18%)
  local copies, waits for them, and re-layouts  3.76 us (5%)
  between operations  0.72 us (1%)
    pallas_call x1, Pallas kernels, update(): pl.pallas_call(update_kernel, grid=(steps,), in_specs=[whole, whole, pl.B...  21.9 us
    pallas_call x1, Pallas kernels, sample(): pl.pallas_call(functools.partial(sample_kernel, per_turbine), grid=(steps...  9.83 us
    ppermute x3, waiting for transfers between devices, local(): result += lax.ppermute(home[shift], 'gy', around(gy - shift))  5.27 us
    ppermute x1, starting transfers between devices, local(): before = lax.ppermute(tail, 'gx', [(i, i + 1) for i in range(gx - 1)])  4.89 us
    pallas_call x1, Pallas kernels, prep(): pl.pallas_call(prep_kernel, in_specs=[pl.BlockSpec(memory_space=pltpu.HBM...  4.26 us
    cond x10, local copies, waits for them, and re-layouts  2.85 us
    ppermute x3, starting transfers between devices, local(): result += lax.ppermute(home[shift], 'gy', around(gy - shift))  2.81 us
    ppermute x1, waiting for transfers between devices, blade(): lax.ppermute(blocks, 'gy', around(shift))  2.41 us
  transfers between devices with their start and end apart: 11, of which 8 were waited for; matrix products, arithmetic and copies ran while one was open for 1% of the time, Pallas kernels for 15%

profile of v4, /device:TPU:0, one launch (start us, length us, event | category | flops | bytes accessed | tf_op | source)
XLA Modules:
  0.0 68.4 jit_solution(13492741748160866514)
XLA Ops:
  0.6 4.3 %prep.1 = (f32[2,8,128]{2,1,0:T(8,128)S(1)}, f32[8,8,128]{2,1,0:T(8,128)S(1)}, f32[8,8,128]{2,1,0:T(8,128)S(1)}, f32[3,32,2048]{2,1,0:T(8,128)}, f32[3,32,2048]{2,1,0:T(8,128)}) custom-call(s32[2]{0:T(128)} %turb_in.1, f32[3,2,128]{2,1,0:T(2,128)} %bitcast.20, f32[3,2,128]{2,1,0:T(2,128)} %bitcast.21, f32[2,128]{1,0:T(2,128)} %lift_in.1, ...), custom_call_target="tpu_custom_call" | custom-call | tf_op jit(solution)/shard_map/prep/pallas_call | solution.py:126
  4.9 4.9 %collective-permute-start.5 = (f32[3,32,2048]{2,1,0:T(8,128)}, f32[3,32,2048]{2,1,0:T(8,128)S(1)}, u32[]{:S(2)}, u32[]{:S(2)}) collective-permute-start(f32[3,32,2048]{2,1,0:T(8,128)} %get-tuple-element.37), channel_id=1, source_target_pairs={{0,8},{8,16},{16,24},{1,9},{9,17},{17,25},{2,10},{10,18},{18,26},{... | collective-permute-start | bytes 2359304 | tf_op jit(solution)/shard_map/ppermute | solution.py:589
  9.8 1.3 %collective-permute-start.6 = (f32[3,32,2048]{2,1,0:T(8,128)}, f32[3,32,2048]{2,1,0:T(8,128)}, u32[]{:S(2)}, u32[]{:S(2)}) collective-permute-start(f32[3,32,2048]{2,1,0:T(8,128)} %get-tuple-element.38), channel_id=1, source_target_pairs={{8,0},{16,8},{24,16},{9,1},{17,9},{25,17},{10,2},{18,10},{26,18},{... | collective-permute-start | bytes 2359304 | tf_op jit(solution)/shard_map/ppermute | solution.py:590
  11.2 24.6 %conditional.1 = (f32[8,512]{1,0:T(8,128)}, f32[8,512]{1,0:T(8,128)S(1)}, f32[4,3,2,128]{3,2,1,0:T(2,128)S(1)}, bf16[1024,2048]{1,0:T(8,128)(2,1)}, f32[3,2,16,2...) conditional(s32[]{:T(128)} %bitcast, () %tuple.16, (f32[8,8,128]{2,1,0:T(8,128)S(1)}, ...), branch_computations={%region_0.0_spmd, %region_1.0_spmd} | conditional | flops 24576 | bytes 5075026 | solution.py:606
  11.2 1.6 %collective-permute-start = (f32[8,8,128]{2,1,0:T(8,128)S(1)}, f32[8,8,128]{2,1,0:T(8,128)S(1)}, u32[]{:S(2)}, u32[]{:S(2)}) collective-permute-start(f32[8,8,128]{2,1,0:T(8,128)S(1)} %get-tuple-element.9), channel_id=1, source_target_pairs={{0,2},{2,4},{4,6},{6,0},{1,3},{3,5},{5,7},{7,1},{8,10},{10,12},{12... | collective-permute-start | bytes 98312 | tf_op jit(solution)/shard_map/cond/branch_1_fun/ppermute | solution.py:592
  12.8 2.2 %collective-permute-start.2 = (f32[8,8,128]{2,1,0:T(8,128)S(1)}, f32[8,8,128]{2,1,0:T(8,128)S(1)}, u32[]{:S(2)}, u32[]{:S(2)}) collective-permute-start(f32[8,8,128]{2,1,0:T(8,128)S(1)} %get-tuple-element.10), channel_id=1, source_target_pairs={{0,6},{2,0},{4,2},{6,4},{1,7},{3,1},{5,3},{7,5},{8,14},{10,8},{12,... | collective-permute-start | bytes 98312 | tf_op jit(solution)/shard_map/cond/branch_1_fun/ppermute | solution.py:593
  15.0 0.8 %collective-permute-start.1 = (f32[2,8,128]{2,1,0:T(8,128)S(1)}, f32[2,8,128]{2,1,0:T(8,128)S(1)}, u32[]{:S(2)}, u32[]{:S(2)}) collective-permute-start(f32[2,8,128]{2,1,0:T(8,128)S(1)} %get-tuple-element.8), channel_id=1, source_target_pairs={{0,4},{2,6},{4,0},{6,2},{1,5},{3,7},{5,1},{7,3},{8,12},{10,14},{12... | collective-permute-start | bytes 24584 | tf_op jit(solution)/shard_map/cond/branch_1_fun/ppermute | solution.py:595
  15.8 1.3 %collective-permute-done = f32[8,8,128]{2,1,0:T(8,128)S(1)} collective-permute-done((f32[8,8,128]{2,1,0:T(8,128)S(1)}, f32[8,8,128]{2,1,0:T(8,128)S(1)}, u32[]{:S(2)}, u32[]{:S(2)}) %collective-permute-start) | collective-permute-done | bytes 32800 | tf_op jit(solution)/shard_map/cond/branch_1_fun/ppermute | solution.py:592
  17.2 0.0 collective-permute-done.2
  17.2 2.4 %collective-permute-done.1 = f32[2,8,128]{2,1,0:T(8,128)S(1)} collective-permute-done((f32[2,8,128]{2,1,0:T(8,128)S(1)}, f32[2,8,128]{2,1,0:T(8,128)S(1)}, u32[]{:S(2)}, u32[]{:S(2)}) %collective-permute-start.1) | collective-permute-done | bytes 8224 | tf_op jit(solution)/shard_map/cond/branch_1_fun/ppermute | solution.py:595
  19.6 0.0 collective-permute-start.3
  19.6 1.2 %collective-permute-done.3.twin_ref = f32[8,8,128]{2,1,0:T(8,128)S(1)} collective-permute-done((f32[8,8,128]{2,1,0:T(8,128)S(1)}, f32[8,8,128]{2,1,0:T(8,128)S(1)}, u32[]{:S(2)}, u32[]{:S(2)}) %collective-permute-start.3) | collective-permute-done | bytes 32800 | tf_op jit(solution)/shard_map/cond/branch_1_fun/ppermute | solution.py:598
  20.8 0.6 copy-done.2
  21.4 9.8 %sample.1 = (f32[8,512]{1,0:T(8,128)}, f32[8,512]{1,0:T(8,128)}, bf16[1024,2048]{1,0:T(8,128)(2,1)}, f32[3,2,16,2048]{3,2,1,0:T(8,128)S(1)}) custom-call(f32[8,8,128]{2,1,0:T(8,128)} %copy-done, f32[8,8,128]{2,1,0:T(8,128)} %copy-done.2, f32[3,16,16,2048]{3,2,1,0:T(8,128)} %get-tuple-element.11.vel_in), custom_call_target="tpu_custom_call" | custom-call | tf_op jit(solution)/shard_map/cond/branch_1_fun/sample/pallas_call | solution.py:278
  31.3 0.2 collective-permute-start.4
  31.5 1.2 %collective-permute-done.4.other_ref = f32[8,512]{1,0:T(8,128)S(1)} collective-permute-done((f32[8,512]{1,0:T(8,128)}, f32[8,512]{1,0:T(8,128)S(1)}, u32[]{:S(2)}, u32[]{:S(2)}) %collective-permute-start.4) | collective-permute-done | bytes 16416 | tf_op jit(solution)/shard_map/cond/branch_1_fun/ppermute | solution.py:600
  32.7 0.8 %copy-done.1 = f32[8,8,128]{2,1,0:T(8,128)S(1)} copy-done((f32[8,8,128]{2,1,0:T(8,128)S(1)}, f32[8,8,128]{2,1,0:T(8,128)}, u32[]{:S(2)}) %copy-start.1) | copy-done | bytes 32792 | tf_op jit(solution)/shard_map/cond
  33.5 0.8 %copy-done.3 = f32[8,8,128]{2,1,0:T(8,128)S(1)} copy-done((f32[8,8,128]{2,1,0:T(8,128)S(1)}, f32[8,8,128]{2,1,0:T(8,128)}, u32[]{:S(2)}) %copy-start.3) | copy-done | bytes 32792 | tf_op jit(solution)/shard_map/cond
  34.2 0.7 %copy-done.4 = f32[8,512]{1,0:T(8,128)S(1)} copy-done((f32[8,512]{1,0:T(8,128)S(1)}, f32[8,512]{1,0:T(8,128)}, u32[]{:S(2)}) %copy-start.4) | copy-done | bytes 16408 | tf_op jit(solution)/shard_map/cond
  35.0 0.8 %force.1 = (f32[8,512]{1,0:T(8,128)S(1)}, f32[4,3,2,128]{3,2,1,0:T(2,128)S(1)}) custom-call(f32[8,8,128]{2,1,0:T(8,128)S(1)} %copy-done.1, f32[8,8,128]{2,1,0:T(8,128)S(1)} %copy-done.3, f32[8,512]{1,0:T(8,128)S(1)} %copy-done.4, f32[8,512]{1,0:T(8,128)S(1)} %collective-permute-done.4.other_ref, f32[8,512]{1,0:T(8,128)} %get-tuple-element.54.own_ref), custom_call_target="tpu_custom_call" | custom-call | tf_op jit(solution)/shard_map/cond/branch_1_fun/force/pallas_call | solution.py:332
  35.7 0.2 collective-permute-start.7
  36.0 1.8 %collective-permute-start.8 = (f32[3,2,128]{2,1,0:T(2,128)S(1)}, f32[3,2,128]{2,1,0:T(2,128)S(1)}, u32[]{:S(2)}, u32[]{:S(2)}) collective-permute-start(f32[3,2,128]{2,1,0:T(2,128)S(1)} %get-tuple-element.44), channel_id=1, source_target_pairs={{0,6},{2,0},{4,2},{6,4},{1,7},{3,1},{5,3},{7,5},{8,14},{10,8},{12,... | collective-permute-start | bytes 9224 | tf_op jit(solution)/shard_map/ppermute | solution.py:612
  37.8 0.2 collective-permute-start.10
  38.0 1.6 %collective-permute-done.8 = f32[3,2,128]{2,1,0:T(2,128)S(1)} collective-permute-done((f32[3,2,128]{2,1,0:T(2,128)S(1)}, f32[3,2,128]{2,1,0:T(2,128)S(1)}, u32[]{:S(2)}, u32[]{:S(2)}) %collective-permute-start.8) | collective-permute-done | bytes 3104 | tf_op jit(solution)/shard_map/ppermute | solution.py:612
  39.6 0.8 %collective-permute-start.9 = (f32[3,2,128]{2,1,0:T(2,128)S(1)}, f32[3,2,128]{2,1,0:T(2,128)S(1)}, u32[]{:S(2)}, u32[]{:S(2)}) collective-permute-start(f32[3,2,128]{2,1,0:T(2,128)S(1)} %get-tuple-element.46), channel_id=1, source_target_pairs={{0,4},{2,6},{4,0},{6,2},{1,5},{3,7},{5,1},{7,3},{8,12},{10,14},{12... | collective-permute-start | bytes 9224 | tf_op jit(solution)/shard_map/ppermute | solution.py:612
  40.4 2.8 %collective-permute-done.10 = f32[3,2,128]{2,1,0:T(2,128)S(1)} collective-permute-done((f32[3,2,128]{2,1,0:T(2,128)S(1)}, f32[3,2,128]{2,1,0:T(2,128)S(1)}, u32[]{:S(2)}, u32[]{:S(2)}) %collective-permute-start.10) | collective-permute-done | bytes 3104 | tf_op jit(solution)/shard_map/ppermute | solution.py:612
  43.2 0.9 %collective-permute-done.9 = f32[3,2,128]{2,1,0:T(2,128)S(1)} collective-permute-done((f32[3,2,128]{2,1,0:T(2,128)S(1)}, f32[3,2,128]{2,1,0:T(2,128)S(1)}, u32[]{:S(2)}, u32[]{:S(2)}) %collective-permute-start.9) | collective-permute-done | bytes 3104 | tf_op jit(solution)/shard_map/ppermute | solution.py:612
  44.1 0.6 fusion.2
  44.7 0.0 collective-permute-done.5.prev0_ref.prev1_ref.prev2_ref
  44.7 1.0 %collective-permute-done.6.next0_ref.next1_ref.next2_ref = f32[3,32,2048]{2,1,0:T(8,128)} collective-permute-done((f32[3,32,2048]{2,1,0:T(8,128)}, f32[3,32,2048]{2,1,0:T(8,128)}, u32[]{:S(2)}, u32[]{:S(2)}) %collective-permute-start.6) | collective-permute-done | bytes 786464 | tf_op jit(solution)/shard_map/ppermute | solution.py:590
  45.7 0.9 %copy-done.6 = f32[3,2,16,2048]{3,2,1,0:T(8,128)} copy-done((f32[3,2,16,2048]{3,2,1,0:T(8,128)}, f32[3,2,16,2048]{3,2,1,0:T(8,128)S(1)}, u32[]{:S(2)}) %copy-start.6) | copy-done | bytes 786456
  46.6 21.9 %update.1 = f32[3,16,16,2048]{3,2,1,0:T(8,128)} custom-call(f32[8,512]{1,0:T(8,128)} %get-tuple-element.35.own_ref, f32[8,512]{1,0:T(8,128)S(1)} %get-tuple-element.36.force_ref, bf16[256,512]{1,0:T(8,128)(2,1)} %constant.2.clone.op_ref, f32[3,32,2048]{2,1,0:T(8,128)} %copy-done.5, f32[3,32,2048]{2,1,0:T(8,128)} %copy-done.5, f32[3,32,2048]{2,1,0:T(8,128)} %copy-done.5, ...), custom_call_target="tpu_custom_call" | custom-call | flops 8053063680 | bytes 12582912 | tf_op jit(solution)/shard_map/update/pallas_call | solution.py:549
  (18 shorter events, 0.0 us)
Async XLA Ops:
  0.6 10.5 %copy-start.7 = (s32[2]{0:T(128)S(1)}, s32[2]{0:T(128)}, u32[]{:S(2)}) copy-start(s32[2]{0:T(128)} %turb_in.1) | copy-start | bytes 28
  4.9 39.7 %collective-permute-start.5 = (f32[3,32,2048]{2,1,0:T(8,128)}, f32[3,32,2048]{2,1,0:T(8,128)S(1)}, u32[]{:S(2)}, u32[]{:S(2)}) collective-permute-start(f32[3,32,2048]{2,1,0:T(8,128)} %get-tuple-element.37), channel_id=1, source_target_pairs={{0,8},{8,16},{16,24},{1,9},{9,17},{17,25},{2,10},{10,18},{18,26},{... | collective-permute-start | bytes 2359304 | tf_op jit(solution)/shard_map/ppermute | solution.py:589
  9.8 35.8 %collective-permute-start.6 = (f32[3,32,2048]{2,1,0:T(8,128)}, f32[3,32,2048]{2,1,0:T(8,128)}, u32[]{:S(2)}, u32[]{:S(2)}) collective-permute-start(f32[3,32,2048]{2,1,0:T(8,128)} %get-tuple-element.38), channel_id=1, source_target_pairs={{8,0},{16,8},{24,16},{9,1},{17,9},{25,17},{10,2},{18,10},{26,18},{... | collective-permute-start | bytes 2359304 | tf_op jit(solution)/shard_map/ppermute | solution.py:590
  11.2 6.0 %collective-permute-start = (f32[8,8,128]{2,1,0:T(8,128)S(1)}, f32[8,8,128]{2,1,0:T(8,128)S(1)}, u32[]{:S(2)}, u32[]{:S(2)}) collective-permute-start(f32[8,8,128]{2,1,0:T(8,128)S(1)} %get-tuple-element.9), channel_id=1, source_target_pairs={{0,2},{2,4},{4,6},{6,0},{1,3},{3,5},{5,7},{7,1},{8,10},{10,12},{12... | collective-permute-start | bytes 98312 | tf_op jit(solution)/shard_map/cond/branch_1_fun/ppermute | solution.py:592
  12.8 4.4 %collective-permute-start.2 = (f32[8,8,128]{2,1,0:T(8,128)S(1)}, f32[8,8,128]{2,1,0:T(8,128)S(1)}, u32[]{:S(2)}, u32[]{:S(2)}) collective-permute-start(f32[8,8,128]{2,1,0:T(8,128)S(1)} %get-tuple-element.10), channel_id=1, source_target_pairs={{0,6},{2,0},{4,2},{6,4},{1,7},{3,1},{5,3},{7,5},{8,14},{10,8},{12,... | collective-permute-start | bytes 98312 | tf_op jit(solution)/shard_map/cond/branch_1_fun/ppermute | solution.py:593
  15.0 4.5 %collective-permute-start.1 = (f32[2,8,128]{2,1,0:T(8,128)S(1)}, f32[2,8,128]{2,1,0:T(8,128)S(1)}, u32[]{:S(2)}, u32[]{:S(2)}) collective-permute-start(f32[2,8,128]{2,1,0:T(8,128)S(1)} %get-tuple-element.8), channel_id=1, source_target_pairs={{0,4},{2,6},{4,0},{6,2},{1,5},{3,7},{5,1},{7,3},{8,12},{10,14},{12... | collective-permute-start | bytes 24584 | tf_op jit(solution)/shard_map/cond/branch_1_fun/ppermute | solution.py:595
  19.6 1.2 %copy-start = (f32[8,8,128]{2,1,0:T(8,128)}, f32[8,8,128]{2,1,0:T(8,128)S(1)}, u32[]{:S(2)}) copy-start(f32[8,8,128]{2,1,0:T(8,128)S(1)} %pad_maximum_fusion.mine_ref) | copy-start | bytes 98308 | tf_op jit(solution)/shard_map/cond
  19.6 1.2 %collective-permute-start.3 = (f32[8,8,128]{2,1,0:T(8,128)S(1)}, f32[8,8,128]{2,1,0:T(8,128)S(1)}, u32[]{:S(2)}, u32[]{:S(2)}) collective-permute-start(f32[8,8,128]{2,1,0:T(8,128)S(1)} %pad_maximum_fusion.mine_ref), channel_id=1, source_target_pairs={{0,1},{1,0},{2,3},{3,2},{4,5},{5,4},{6,7},{7,6},{8,9},{9,8},{10,11... | collective-permute-start | bytes 98312 | tf_op jit(solution)/shard_map/cond/branch_1_fun/ppermute | solution.py:598
  20.8 0.6 copy-start.2
  31.3 1.5 %collective-permute-start.4 = (f32[8,512]{1,0:T(8,128)}, f32[8,512]{1,0:T(8,128)S(1)}, u32[]{:S(2)}, u32[]{:S(2)}) collective-permute-start(f32[8,512]{1,0:T(8,128)} %get-tuple-element.13.part_ref), channel_id=1, source_target_pairs={{0,1},{1,0},{2,3},{3,2},{4,5},{5,4},{6,7},{7,6},{8,9},{9,8},{10,11... | collective-permute-start | bytes 49160 | tf_op jit(solution)/shard_map/cond/branch_1_fun/ppermute | solution.py:600
  32.7 0.8 %copy-start.1 = (f32[8,8,128]{2,1,0:T(8,128)S(1)}, f32[8,8,128]{2,1,0:T(8,128)}, u32[]{:S(2)}) copy-start(f32[8,8,128]{2,1,0:T(8,128)} %copy-done) | copy-start | bytes 98308 | tf_op jit(solution)/shard_map/cond
  33.5 0.8 %copy-start.3 = (f32[8,8,128]{2,1,0:T(8,128)S(1)}, f32[8,8,128]{2,1,0:T(8,128)}, u32[]{:S(2)}) copy-start(f32[8,8,128]{2,1,0:T(8,128)} %copy-done.2) | copy-start | bytes 98308 | tf_op jit(solution)/shard_map/cond
  34.2 0.7 %copy-start.4 = (f32[8,512]{1,0:T(8,128)S(1)}, f32[8,512]{1,0:T(8,128)}, u32[]{:S(2)}) copy-start(f32[8,512]{1,0:T(8,128)} %get-tuple-element.13.part_ref) | copy-start | bytes 49156 | tf_op jit(solution)/shard_map/cond
  35.7 9.9 %collective-permute-start.7 = (f32[3,2,16,2048]{3,2,1,0:T(8,128)S(1)}, f32[3,2,16,2048]{3,2,1,0:T(8,128)S(1)}, u32[]{:S(2)}, u32[]{:S(2)}) collective-permute-start(f32[3,2,16,2048]{3,2,1,0:T(8,128)S(1)} %get-tuple-element.40), channel_id=1, source_target_pairs={{0,1},{1,0},{2,3},{3,2},{4,5},{5,4},{6,7},{7,6},{8,9},{9,8},{10,11... | collective-permute-start | bytes 2359304 | tf_op jit(solution)/shard_map/ppermute | solution.py:609
  36.0 3.6 %collective-permute-start.8 = (f32[3,2,128]{2,1,0:T(2,128)S(1)}, f32[3,2,128]{2,1,0:T(2,128)S(1)}, u32[]{:S(2)}, u32[]{:S(2)}) collective-permute-start(f32[3,2,128]{2,1,0:T(2,128)S(1)} %get-tuple-element.44), channel_id=1, source_target_pairs={{0,6},{2,0},{4,2},{6,4},{1,7},{3,1},{5,3},{7,5},{8,14},{10,8},{12,... | collective-permute-start | bytes 9224 | tf_op jit(solution)/shard_map/ppermute | solution.py:612
  37.8 5.4 %collective-permute-start.10 = (f32[3,2,128]{2,1,0:T(2,128)S(1)}, f32[3,2,128]{2,1,0:T(2,128)S(1)}, u32[]{:S(2)}, u32[]{:S(2)}) collective-permute-start(f32[3,2,128]{2,1,0:T(2,128)S(1)} %get-tuple-element.45), channel_id=1, source_target_pairs={{0,2},{2,4},{4,6},{6,0},{1,3},{3,5},{5,7},{7,1},{8,10},{10,12},{12... | collective-permute-start | bytes 9224 | tf_op jit(solution)/shard_map/ppermute | solution.py:612
  39.6 4.5 %collective-permute-start.9 = (f32[3,2,128]{2,1,0:T(2,128)S(1)}, f32[3,2,128]{2,1,0:T(2,128)S(1)}, u32[]{:S(2)}, u32[]{:S(2)}) collective-permute-start(f32[3,2,128]{2,1,0:T(2,128)S(1)} %get-tuple-element.46), channel_id=1, source_target_pairs={{0,4},{2,6},{4,0},{6,2},{1,5},{3,7},{5,1},{7,3},{8,12},{10,14},{12... | collective-permute-start | bytes 9224 | tf_op jit(solution)/shard_map/ppermute | solution.py:612
  44.7 1.9 %copy-start.5 = (f32[3,32,2048]{2,1,0:T(8,128)}, f32[3,32,2048]{2,1,0:T(8,128)S(1)}, u32[]{:S(2)}) copy-start(f32[3,32,2048]{2,1,0:T(8,128)S(1)} %collective-permute-done.5.prev0_ref.prev1_ref.prev2_ref) | copy-start | bytes 2359300
  45.7 0.9 %copy-start.6 = (f32[3,2,16,2048]{3,2,1,0:T(8,128)}, f32[3,2,16,2048]{3,2,1,0:T(8,128)S(1)}, u32[]{:S(2)}) copy-start(f32[3,2,16,2048]{3,2,1,0:T(8,128)S(1)} %collective-permute-done.7.lev_ref) | copy-start | bytes 2359300

commit v5 on v4

v5 whole, which is shorter than its diff:
```python
import functools
import math

import jax
import jax.numpy as jnp
import ml_dtypes
import numpy as np
from jax import lax
from jax.experimental import pallas as pl
from jax.experimental.pallas import tpu as pltpu
from jax.sharding import PartitionSpec as P

mean_wind = 1.0
viscosity = 0.2
smag_coeff = 0.17
time_step = 0.2
smear = 2.0
smear_norm = 1.0 / (smear**3 * math.pi**1.5)

F32 = jnp.float32
BF16 = jnp.bfloat16
MIB = 1024 * 1024
LEVELS = 8
STEP = 256
LIGHT = pl.CostEstimate(flops=0, bytes_accessed=0, transcendentals=0)


def split(value):
    high = value.astype(BF16)
    return high, (value - high.astype(F32)).astype(BF16)


def dot(left, right, contract=0):
    return lax.dot_general(
        left, right, (((1,), (contract,)), ((), ())), preferred_element_type=F32
    )


def gaussian(first, count, centers):
    shape = (count, centers.shape[1])
    cells = (first + lax.broadcasted_iota(jnp.int32, shape, 0)).astype(F32)
    gap = cells - centers
    return jnp.exp(-gap * gap / (smear * smear))


def stencil_operator(row_cells):
    inner = (LEVELS + 4) * row_cells
    width = inner + 4 * LEVELS
    op = np.zeros((2, LEVELS, row_cells, width), np.float32)

    def column(level, row):
        if 0 <= row < row_cells:
            return (level + 2) * row_cells + row
        if row < 0:
            return inner + level * 2 + row + 2
        return inner + 2 * LEVELS + level * 2 + row - row_cells

    for level in range(LEVELS):
        for row in range(row_cells):
            for offset, first, second in ((-2, 1, -1), (-1, -8, 16), (1, 8, 16), (2, -1, -1)):
                op[0, level, row, column(level, row + offset)] += first
                op[1, level, row, column(level, row + offset)] += second
                op[1, level, row, column(level + offset, row)] += second
            op[1, level, row, column(level, row)] -= 90
    op = op.reshape(2 * LEVELS * row_cells, width)
    op = np.pad(op, ((0, 0), (0, -width % 128)))
    return np.concatenate([op, op], axis=1).astype(ml_dtypes.bfloat16)


def prep_kernel(
    turb_in, pos_in, speed_in, lift_in, vel_in, blocks_ref, up_ref, down_ref, head_ref, tail_ref,
    turb_ref, pos_ref, speed_ref, lift_ref, vel_ref, sems,
):
    components, levels, rows, cols = vel_ref.shape
    coords, owned, points = pos_ref.shape
    small = [
        pltpu.make_async_copy(source, target, sems.at[components + k])
        for k, (source, target) in enumerate(
            ((turb_in, turb_ref), (pos_in, pos_ref), (speed_in, speed_ref), (lift_in, lift_ref))
        )
    ]
    large = [
        pltpu.make_async_copy(vel_in.at[i], vel_ref.at[i], sems.at[i]) for i in range(components)
    ]
    for copy in small + large:
        copy.start()
    for copy in small:
        copy.wait()
    for ref in (blocks_ref, up_ref, down_ref):
        for k in range(owned):
            for i in range(coords):
                ref[k, i : i + 1, :] = pos_ref[i, k : k + 1, :]
                ref[k, coords + i : coords + i + 1, :] = speed_ref[i, k : k + 1, :]
            ref[k, 2 * coords : 2 * coords + 1, :] = lift_ref[k : k + 1, :]
            ref[k, 7:8, :] = jnp.full((1, points), turb_ref[k].astype(F32))
    parts = levels * rows // 128
    row = lax.broadcasted_iota(jnp.int32, (8, cols), 0) // 2
    for component in range(components):
        large[component].wait()
        last = vel_ref[component, :, :, cols - 128 :].reshape(levels * rows, 128)
        first = vel_ref[component, :, :, :128].reshape(levels * rows, 128)
        for part in range(parts):
            cells = slice(part * 128, part * 128 + 128)
            up_ref[owned + component * parts + part] = last[cells].T[120:]
            down_ref[owned + component * parts + part] = first[cells].T[:8]
        for group in range(levels // 4):
            head = tail = None
            for k in range(4):
                top = vel_ref[component, group * 4 + k, 0:8, :]
                end = vel_ref[component, group * 4 + k, rows - 8 : rows, :]
                if k:
                    top = pltpu.roll(top, 2 * k, 0)
                if k < 3:
                    end = pltpu.roll(end, 2 * k + 2, 0)
                head = top if head is None else jnp.where(row == k, top, head)
                tail = end if tail is None else jnp.where(row == k, end, tail)
            head_ref[component, group * 8 : group * 8 + 8, :] = head
            tail_ref[component, group * 8 : group * 8 + 8, :] = tail


def prep(velocity, blade_pos, block_turbine, blade_vel, lift_coeff):
    components, levels, rows, cols = velocity.shape
    owned, coords, points = blade_pos.shape
    tiles = owned + components * levels * rows // 128
    return pl.pallas_call(
        prep_kernel,
        in_specs=[pl.BlockSpec(memory_space=pltpu.HBM)] * 5,
        out_specs=[pl.BlockSpec(memory_space=pltpu.VMEM)] * 5,
        out_shape=[
            jax.ShapeDtypeStruct((owned, 8, points), F32),
            jax.ShapeDtypeStruct((tiles, 8, 128), F32),
            jax.ShapeDtypeStruct((tiles, 8, 128), F32),
            jax.ShapeDtypeStruct((components, 2 * levels, cols), F32),
            jax.ShapeDtypeStruct((components, 2 * levels, cols), F32),
        ],
        scratch_shapes=[
            pltpu.SMEM((owned,), jnp.int32),
            pltpu.VMEM((coords, owned, points), F32),
            pltpu.VMEM((coords, owned, points), F32),
            pltpu.VMEM((owned, points), F32),
            pltpu.VMEM(velocity.shape, F32),
            pltpu.SemaphoreType.DMA((components + 4,)),
        ],
        compiler_params=pltpu.CompilerParams(vmem_limit_bytes=60 * MIB),
        cost_estimate=LIGHT,
        name="prep",
    )(
        block_turbine,
        blade_pos.transpose(1, 0, 2),
        blade_vel.transpose(1, 0, 2),
        lift_coeff,
        velocity,
    )


def match(mine_ref, twin_ref, per_turbine):
    core = lax.axis_index("gz")
    turbine = lax.axis_index("gy").astype(F32)
    half = mine_ref.shape[0]
    first = [(mine_ref[k, 7:8, :] == turbine).astype(F32) for k in range(half)]
    second = [(twin_ref[k, 7:8, :] == turbine).astype(F32) for k in range(half)]
    masks = []
    for hits, others, leads in ((first, second, core == 0), (second, first, core == 1)):
        rank = jnp.where(leads, jnp.zeros_like(hits[0]), sum(others))
        for hit in hits:
            masks.append([(hit > 0.5) & (rank == k) for k in range(per_turbine)])
            rank = rank + hit
    return masks


def sample_kernel(
    per_turbine, mine_ref, twin_ref, vel_in, part_ref, own_ref, mask_ref, weight_out, lev_ref,
    even_ref, odd_ref, center_ref, plane_ref, acc_ref, vel_ref, weight_ref, sems, out_sems, lev_sem,
):
    components, depth, rows, cols = vel_ref.shape
    points = mine_ref.shape[2]
    count = per_turbine * points
    cells = depth * rows
    chunks = cols // STEP
    core = lax.axis_index("gz")
    start = lax.axis_index("gy") * cols

    def column(at):
        return pl.ds(pl.multiple_of(at * STEP, STEP), STEP)

    def column_copy(at):
        return pltpu.make_async_copy(
            vel_in.at[:, :, :, column(at)], vel_ref.at[:, :, :, column(at)], sems.at[at]
        )

    def weight_copy(at):
        return pltpu.make_async_copy(
            weight_ref.at[:, column(at)], weight_out.at[:, column(at)], out_sems.at[at]
        )

    lev_copy = pltpu.make_async_copy(
        vel_in.at[:, pl.ds(jnp.where(core == 0, depth - 2, 0), 2)], lev_ref, lev_sem
    )

    def bell(cell, center):
        gap = cell.astype(F32) - center
        return jnp.exp(gap * gap * (-1.0 / (smear * smear)))

    def weights(at, ref):
        lane = lax.broadcasted_iota(jnp.int32, (1, 128), 1)
        for part in range(STEP // 128):
            cell = start + at * STEP + part * 128 + lane
            ref[:, part * 128 : part * 128 + 128] = bell(cell, center_ref[...])

    def multiply(at, ref):
        for i in range(components):
            high, low = split(vel_ref[i, :, :, column(at)].reshape(cells, STEP))
            field = dot(plane_ref[...], jnp.concatenate([high, high, low], axis=0))
            product = field * ref[...]
            total = acc_ref[i]
            for part in range(STEP // 128):
                total += product[:, part * 128 : part * 128 + 128]
            acc_ref[i] = total
        high, low = split(ref[...])
        weight_ref[:count, column(at)] = high
        weight_ref[count:, column(at)] = low

    for at in range(chunks):
        column_copy(at).start()
    lev_copy.start()
    masks = match(mine_ref, twin_ref, per_turbine)
    blocks = mine_ref.shape[0]
    lane = lax.broadcasted_iota(jnp.int32, (1, cells), 1)
    level = core * depth + lane // rows
    row = lax.axis_index("gx") * rows + lane % rows
    for k in range(per_turbine):
        total = jnp.zeros((8, points), F32)
        for at, mask in enumerate(masks):
            tile = mine_ref[at] if at < blocks else twin_ref[at - blocks]
            total = jnp.where(mask[k], tile, total)
        band = slice(k * points, (k + 1) * points)
        own_ref[:, band] = total
        turned = total.T
        center_ref[band, :] = jnp.broadcast_to(turned[:, 1:2], (points, 128))
        plane = bell(row, turned[:, 0:1]) * bell(level, turned[:, 2:3])
        high, low = split(plane)
        plane_ref[band, :cells] = high
        plane_ref[band, cells : 2 * cells] = low
        plane_ref[band, 2 * cells :] = high
    for at in range(blocks):
        for k in range(per_turbine):
            mask_ref[at, k : k + 1, :] = masks[at][k].astype(F32)
    acc_ref[...] = jnp.zeros(acc_ref.shape, F32)
    weights(0, even_ref)

    def pair(step, carry):
        column_copy(2 * step).wait()
        column_copy(2 * step + 1).wait()
        weights(2 * step + 1, odd_ref)
        multiply(2 * step, even_ref)
        weights(2 * step + 2, even_ref)
        multiply(2 * step + 1, odd_ref)
        weight_copy(2 * step).start()
        weight_copy(2 * step + 1).start()
        return carry

    lax.fori_loop(0, chunks // 2, pair, 0)
    for i in range(components):
        for k in range(per_turbine):
            band = slice(k * points, (k + 1) * points)
            total = jnp.sum(acc_ref[i, band, :].T, axis=0, keepdims=True)
            part_ref[i : i + 1, band] = smear_norm * total
    part_ref[components:, :] = jnp.zeros((8 - components, count), F32)
    lev_copy.wait()
    for at in range(chunks):
        weight_copy(at).wait()


def sample(mine, twin, velocity, per_turbine):
    components, depth, rows, cols = velocity.shape
    points = mine.shape[2]
    count = per_turbine * points
    chunks = cols // STEP
    vmem = pl.BlockSpec(memory_space=pltpu.VMEM)
    hbm = pl.BlockSpec(memory_space=pltpu.HBM)
    return pl.pallas_call(
        functools.partial(sample_kernel, per_turbine),
        in_specs=[vmem, vmem, hbm],
        out_specs=[vmem, vmem, vmem, hbm, vmem],
        out_shape=[
            jax.ShapeDtypeStruct((8, count), F32),
            jax.ShapeDtypeStruct((8, count), F32),
            jax.ShapeDtypeStruct((mine.shape[0], per_turbine, points), F32),
            jax.ShapeDtypeStruct((2 * count, cols), BF16),
            jax.ShapeDtypeStruct((components, 2, rows, cols), F32),
        ],
        scratch_shapes=[
            pltpu.VMEM((count, STEP), F32),
            pltpu.VMEM((count, STEP), F32),
            pltpu.VMEM((count, 128), F32),
            pltpu.VMEM((count, 3 * depth * rows), BF16),
            pltpu.VMEM((components, count, 128), F32),
            pltpu.VMEM(velocity.shape, F32),
            pltpu.VMEM((2 * count, cols), BF16),
            pltpu.SemaphoreType.DMA((chunks,)),
            pltpu.SemaphoreType.DMA((chunks,)),
            pltpu.SemaphoreType.DMA,
        ],
        compiler_params=pltpu.CompilerParams(vmem_limit_bytes=58 * MIB),
        cost_estimate=LIGHT,
        name="sample",
    )(mine, twin, velocity)


def force_kernel(
    per_turbine, owned, mask_ref, part_ref, other_ref, own_ref, force_ref, home_ref
):
    points = own_ref.shape[1] // per_turbine
    relative = part_ref[0:3, :] + other_ref[0:3, :] - own_ref[3:6, :]
    speed = jnp.sqrt(jnp.sum(relative * relative, axis=0, keepdims=True))
    force = -own_ref[6:7, :] * speed * relative
    force_ref[...] = jnp.zeros(force_ref.shape, F32)
    force_ref[0:3, :] = force
    for row in range(mask_ref.shape[0]):
        total = jnp.zeros((3, points), F32)
        for k in range(per_turbine):
            total = jnp.where(mask_ref[row, k : k + 1, :] > 0.5, force[:, k * points : (k + 1) * points], total)
        for i in range(3):
            home_ref[row // owned, i, row % owned : row % owned + 1, :] = total[i : i + 1]


def point_forces(mask, part, other, own, per_turbine, owned):
    count = own.shape[1]
    points = count // per_turbine
    shifts = mask.shape[0] // owned
    return pl.pallas_call(
        functools.partial(force_kernel, per_turbine, owned),
        in_specs=[pl.BlockSpec(memory_space=pltpu.VMEM)] * 4,
        out_specs=[pl.BlockSpec(memory_space=pltpu.VMEM)] * 2,
        out_shape=[
            jax.ShapeDtypeStruct((8, count), F32),
            jax.ShapeDtypeStruct((shifts, 3, owned, points), F32),
        ],
        compiler_params=pltpu.CompilerParams(vmem_limit_bytes=58 * MIB),
        cost_estimate=LIGHT,
        name="force",
    )(mask, part, other, own)


def update_kernel(
    own_ref, force_ref, op_ref, left_ref, right_ref, prev_in, next_in, weight_in, vel_in, lev_in,
    new_out, pad_ref, new_ref, prev_ref, next_ref, weight_ref, high_ref, low_ref, even, odd,
    vel_sems, side_sems, weight_sems, new_sems, lev_sem,
):
    components, depth, rows, cols = new_ref.shape
    chunks = cols // STEP
    cells = LEVELS * rows
    inner = (LEVELS + 4) * rows
    fill = op_ref.shape[1] // 2 - inner - 4 * LEVELS
    count = own_ref.shape[1]
    core = lax.axis_index("gz")
    turbine = lax.axis_index("gy")
    lane = lax.broadcasted_iota(jnp.int32, (8, 128), 1)
    shifts = ((1, lane < 1), (2, lane < 2), (127, lane >= 127), (126, lane >= 126))

    def column(at, first=0):
        return pl.ds(pl.multiple_of(at * STEP + first, 128), STEP)

    def arrivals(at):
        return [
            pltpu.make_async_copy(
                vel_in.at[:, :, :, column(at)],
                pad_ref.at[:, pl.ds(2, depth), :, column(at, 128)],
                vel_sems.at[at],
            ),
            pltpu.make_async_copy(
                weight_in.at[:, column(at)], weight_ref.at[:, column(at)], weight_sems.at[at]
            ),
            pltpu.make_async_copy(
                prev_in.at[:, :, column(at)], prev_ref.at[:, :, column(at)], side_sems.at[0, at]
            ),
            pltpu.make_async_copy(
                next_in.at[:, :, column(at)], next_ref.at[:, :, column(at)], side_sems.at[1, at]
            ),
        ]

    def departure(at):
        return pltpu.make_async_copy(
            new_ref.at[:, :, :, column(at)], new_out.at[:, :, :, column(at)], new_sems.at[at]
        )

    def level_copy(at):
        return pltpu.make_async_copy(
            lev_in, pad_ref.at[:, pl.ds(at, 2), :, pl.ds(128, cols)], lev_sem
        )

    def side_columns(ref, present, lane):
        per_part = 128 // rows
        parts = ref.shape[0] // components
        for tile in range(ref.shape[0]):
            turned = jnp.where(present, ref[tile], 0.0).T
            for k in range(per_part):
                level = (tile % parts) * per_part + k
                pad_ref[tile // parts, level + 2, :, lane : lane + 8] = turned[k * rows : (k + 1) * rows, :]

    def matrix_part(at, bufs):
        grad_ref, lap_ref, body_ref = bufs
        for i in range(components):
            for half in range(depth // LEVELS):
                levels = slice(half * LEVELS, (half + 1) * LEVELS)
                field = pad_ref[i, half * LEVELS : (half + 1) * LEVELS + 4, :, column(at, 128)]
                inner_high, inner_low = split(field.reshape(inner, STEP))
                side = slice(half * 2 * LEVELS, (half + 1) * 2 * LEVELS)
                prev_high, prev_low = split(prev_ref[i, side, column(at)])
                next_high, next_low = split(next_ref[i, side, column(at)])
                empty = [jnp.zeros((fill, STEP), BF16)] if fill else []
                high = [inner_high, prev_high, next_high] + empty
                low = [inner_low, prev_low, next_low] + empty
                result = dot(op_ref[...], jnp.concatenate(high + low, axis=0))
                grad_ref[i, levels] = result[:cells].reshape(LEVELS, rows, STEP)
                lap_ref[i, levels] = result[cells:].reshape(LEVELS, rows, STEP)
        upper = weight_ref[:count, column(at)]
        lower = weight_ref[count:, column(at)]
        wide = jnp.concatenate([high_ref[...], low_ref[...], high_ref[...]], axis=1)
        result = dot(wide, jnp.concatenate([upper, upper, lower], axis=0))
        body_ref[...] = result.reshape(components, depth, rows, STEP)

    def vector_part(at, bufs):
        grad_ref, lap_ref, body_ref = bufs

        def cell(i, level, band, block):
            return pad_ref[i, level, band, pl.ds(pl.multiple_of(at * STEP + block * 128, 128), 128)]

        def work(level, band):
            here = level + 2
            turned = {}

            def turn(i, block, shift):
                if (i, block, shift) not in turned:
                    turned[i, block, shift] = pltpu.roll(cell(i, here, band, block), shift, 1)
                return turned[i, block, shift]

            for block in range(1, STEP // 128 + 1):
                lanes = slice(block * 128 - 128, block * 128)
                along_y, lap, along_z = [], [], []
                for i in range(components):
                    behind, behind2, ahead, ahead2 = [
                        jnp.where(
                            wrapped,
                            turn(i, block - 1 if shift < 64 else block + 1, shift),
                            turn(i, block, shift),
                        )
                        for shift, wrapped in shifts
                    ]
                    along_y.append(8.0 * (ahead - behind) - (ahead2 - behind2))
                    lap.append(
                        lap_ref[i, level, band, lanes]
                        + (16.0 * (ahead + behind) - (ahead2 + behind2))
                    )
                    near = cell(i, here + 1, band, block) - cell(i, here - 1, band, block)
                    far = cell(i, here + 2, band, block) - cell(i, here - 2, band, block)
                    along_z.append(8.0 * near - far)
                along_x = [grad_ref[i, level, band, lanes] for i in range(components)]
                same = along_x[0] * along_x[0] + along_y[1] * along_y[1] + along_z[2] * along_z[2]
                xy = along_x[1] + along_y[0]
                xz = along_x[2] + along_z[0]
                yz = along_y[2] + along_z[1]
                strain = 2.0 * same + (xy * xy + xz * xz + yz * yz)
                mixing = (time_step / 12.0) * viscosity + (
                    time_step * smag_coeff * smag_coeff / 144.0
                ) * jnp.sqrt(strain)
                out_lanes = pl.ds(pl.multiple_of(at * STEP + block * 128 - 128, 128), 128)
                for i in range(components):
                    change = mixing * lap[i] - (time_step * mean_wind / 12.0) * along_x[i]
                    new_ref[i, level, band, out_lanes] = (
                        cell(i, here, band, block) + body_ref[i, level, band, lanes] + change
                    )

        for level in range(depth):
            for row in range(0, rows, 8):
                work(level, slice(row, row + 8))
        departure(at).start()

    for at in range(chunks):
        for copy in arrivals(at):
            copy.start()

    @pl.when(core == 1)
    def _():
        level_copy(0).start()
        pad_ref[:, depth + 2 :, :, 128 : cols + 128] = jnp.zeros((components, 2, rows, cols), F32)

    @pl.when(core == 0)
    def _():
        level_copy(depth + 2).start()
        pad_ref[:, 0:2, :, 128 : cols + 128] = jnp.zeros((components, 2, rows, cols), F32)

    side_columns(left_ref, turbine > 0, 120)
    side_columns(right_ref, turbine < lax.axis_size("gy") - 1, cols + 128)
    along_x = gaussian(lax.axis_index("gx") * rows, rows, own_ref[0:1, :])
    along_z = gaussian(core * depth, depth, own_ref[2:3, :])
    for i in range(components):
        scaled = (time_step * smear_norm) * force_ref[i : i + 1, :] * along_x
        for level in range(depth):
            band = slice((i * depth + level) * rows, (i * depth + level + 1) * rows)
            high, low = split(scaled * along_z[level : level + 1, :])
            high_ref[band, :] = high
            low_ref[band, :] = low
    level_copy(0).wait()
    for copy in arrivals(0):
        copy.wait()
    matrix_part(0, even)

    def pair(step, carry):
        for copy in arrivals(2 * step + 1) + arrivals(2 * step + 2):
            copy.wait()
        matrix_part(2 * step + 1, odd)
        vector_part(2 * step, even)
        matrix_part(2 * step + 2, even)
        vector_part(2 * step + 1, odd)
        return carry

    lax.fori_loop(0, chunks // 2 - 1, pair, 0)
    for copy in arrivals(chunks - 1):
        copy.wait()
    matrix_part(chunks - 1, odd)
    vector_part(chunks - 2, even)
    vector_part(chunks - 1, odd)
    for at in range(chunks):
        departure(at).wait()


def update(own, force, operator, prev, after, weight, velocity, lev, left, right):
    components, depth, rows, cols = velocity.shape
    count = own.shape[1]
    chunks = cols // STEP
    vmem = pl.BlockSpec(memory_space=pltpu.VMEM)
    hbm = pl.BlockSpec(memory_space=pltpu.HBM)
    fields = [pltpu.VMEM((components, depth, rows, STEP), F32)] * 3
    macs = components * depth * rows * cols * (3 * count + 4 * 256)
    return pl.pallas_call(
        update_kernel,
        in_specs=[vmem] * 5 + [hbm] * 5,
        out_specs=hbm,
        out_shape=jax.ShapeDtypeStruct(velocity.shape, F32),
        scratch_shapes=[
            pltpu.VMEM((components, depth + 4, rows, cols + 256), F32),
            pltpu.VMEM(velocity.shape, F32),
            pltpu.VMEM(prev.shape, F32),
            pltpu.VMEM(prev.shape, F32),
            pltpu.VMEM((2 * count, cols), BF16),
            pltpu.VMEM((components * depth * rows, count), BF16),
            pltpu.VMEM((components * depth * rows, count), BF16),
            fields,
            fields,
            pltpu.SemaphoreType.DMA((chunks,)),
            pltpu.SemaphoreType.DMA((2, chunks)),
            pltpu.SemaphoreType.DMA((chunks,)),
            pltpu.SemaphoreType.DMA((chunks,)),
            pltpu.SemaphoreType.DMA,
        ],
        compiler_params=pltpu.CompilerParams(vmem_limit_bytes=44 * MIB),
        cost_estimate=pl.CostEstimate(
            flops=2 * macs, bytes_accessed=8 * velocity.size, transcendentals=velocity.size // 3
        ),
        name="update",
    )(own, force, operator, left, right, prev, after, weight, velocity, lev)


def local(velocity, blade_pos, block_turbine, blade_vel, lift_coeff):
    components, depth, rows, cols = velocity.shape
    owned, _, points = blade_pos.shape
    gx, gy, gz = (lax.axis_size(axis) for axis in ("gx", "gy", "gz"))
    assert gz == 2 and depth == 2 * LEVELS
    per_turbine = owned * gz
    swap = [(0, 1), (1, 0)]

    def around(shift):
        return [(i, (i + shift) % gy) for i in range(gy)]

    blocks, up, down, head, tail = prep(velocity, blade_pos, block_turbine, blade_vel, lift_coeff)
    before = lax.ppermute(tail, "gx", [(i, i + 1) for i in range(gx - 1)])
    after = lax.ppermute(head, "gx", [(i + 1, i) for i in range(gx - 1)])
    def blade(blocks, up, down, velocity):
        left = lax.ppermute(up, "gy", around(1))
        right = lax.ppermute(down, "gy", around(gy - 1))
        parts = [blocks, left[:owned]]
        parts += [lax.ppermute(blocks, "gy", around(shift)) for shift in range(2, gy - 1)]
        parts.append(right[:owned])
        mine = jnp.concatenate(parts, axis=0)
        twin = lax.ppermute(mine, "gz", swap)
        part, own, mask, weight, facing = sample(mine, twin, velocity, per_turbine)
        other = lax.ppermute(part, "gz", swap)
        force, home = point_forces(mask, part, other, own, per_turbine, owned)
        return own, force, home, weight, facing, left[owned:], right[owned:]

    operands = (blocks, up, down, velocity)
    empty = [jnp.zeros(out.shape, out.dtype) for out in jax.eval_shape(blade, *operands)]
    own, force, home, weight, facing, left, right = lax.cond(
        block_turbine[0] >= 0, blade, lambda *_: tuple(empty), *operands
    )
    lev = lax.ppermute(facing, "gz", swap)
    result = home[0]
    for shift in range(1, gy):
        result += lax.ppermute(home[shift], "gy", around(gy - shift))

    operator = jnp.asarray(stencil_operator(rows))
    new_velocity = update(
        own, force, operator, before, after, weight, velocity, lev, left, right
    )
    return (new_velocity, result.transpose(1, 0, 2))


def solution(mesh):
    in_specs = (
        P(None, "gz", "gx", "gy"),
        P(("gx", "gy", "gz"), None, None),
        P(("gx", "gy", "gz")),
        P(("gx", "gy", "gz"), None, None),
        P(("gx", "gy", "gz"), None),
    )
    out_specs = (P(None, "gz", "gx", "gy"), P(("gx", "gy", "gz"), None, None))
    return jax.shard_map(local, mesh=mesh, in_specs=in_specs, out_specs=out_specs, check_vma=False)
```

time: 68.9 us -> 63.5 us (0.922)
  Pallas kernels: 36.7 us -> 33.5 us
  local copies, waits for them, and re-layouts: 3.76 us -> 1.22 us
    pallas_call x2, Pallas kernels: 31.7 us -> 28.5 us  [the longest x1 17.4 us: update(): pl.pallas_call(update_kernel, in_specs=[vmem] * 5 + [hbm] * 5, out_specs=...]
    cond x10 -> x6, local copies, waits for them, and re-layouts: 2.85 us -> 1.2 us
    unnamed x6 -> x4, local copies, waits for them, and re-layouts: 0.9 us -> 0.01 us
  transfers between devices with their start and end apart: 11 -> 11, of which waited for: 8 -> 9; matrix products, arithmetic and copies ran while one was open for 1% -> 1% of each run, Pallas kernels for 15% -> 19%
where the time goes in v5:
time: 63.5 us; the launch traced here: 63.1 us
  Pallas kernels  33.5 us (53%)
  starting transfers between devices  14.1 us (22%)
  waiting for transfers between devices  12.7 us (20%)
  local copies, waits for them, and re-layouts  1.22 us (2%)
  between operations  0.89 us (1%)
    pallas_call x1, Pallas kernels, update(): pl.pallas_call(update_kernel, in_specs=[vmem] * 5 + [hbm] * 5, out_specs=...  17.4 us
    pallas_call x1, Pallas kernels, sample(): pl.pallas_call(functools.partial(sample_kernel, per_turbine), in_specs=[v...  11.1 us
    ppermute x3, waiting for transfers between devices, local(): result += lax.ppermute(home[shift], 'gy', around(gy - shift))  5.27 us
    ppermute x1, starting transfers between devices, local(): before = lax.ppermute(tail, 'gx', [(i, i + 1) for i in range(gx - 1)])  4.89 us
    pallas_call x1, Pallas kernels, prep(): pl.pallas_call(prep_kernel, in_specs=[pl.BlockSpec(memory_space=pltpu.HBM...  4.22 us
    ppermute x3, starting transfers between devices, local(): result += lax.ppermute(home[shift], 'gy', around(gy - shift))  2.82 us
    ppermute x1, waiting for transfers between devices, blade(): lax.ppermute(blocks, 'gy', around(shift))  2.32 us
    ppermute x1, starting transfers between devices, blade(): right = lax.ppermute(down, 'gy', around(gy - 1))  2.25 us
  transfers between devices with their start and end apart: 11, of which 9 were waited for; matrix products, arithmetic and copies ran while one was open for 1% of the time, Pallas kernels for 19%

profile of v5, /device:TPU:0, one launch (start us, length us, event | category | flops | bytes accessed | tf_op | source)
XLA Modules:
  0.0 63.1 jit_solution(10505255990865643993)
XLA Ops:
  0.6 4.2 %prep.1 = (f32[2,8,128]{2,1,0:T(8,128)S(1)}, f32[8,8,128]{2,1,0:T(8,128)S(1)}, f32[8,8,128]{2,1,0:T(8,128)}, f32[3,32,2048]{2,1,0:T(8,128)}, f32[3,32,2048]{2,1,0:T(8,128)}) custom-call(s32[2]{0:T(128)} %turb_in.1, f32[3,2,128]{2,1,0:T(2,128)} %bitcast.20, f32[3,2,128]{2,1,0:T(2,128)} %bitcast.21, f32[2,128]{1,0:T(2,128)} %lift_in.1, f32[3,16,16,2048]{3,2,1,0:T(8,128)} %vel_in.3), custom_call_target="tpu_custom_call" | custom-call | tf_op jit(solution)/shard_map/prep/pallas_call | solution.py:125
  4.9 4.9 %collective-permute-start.5 = (f32[3,32,2048]{2,1,0:T(8,128)}, f32[3,32,2048]{2,1,0:T(8,128)S(1)}, u32[]{:S(2)}, u32[]{:S(2)}) collective-permute-start(f32[3,32,2048]{2,1,0:T(8,128)} %get-tuple-element.40), channel_id=1, source_target_pairs={{0,8},{8,16},{16,24},{1,9},{9,17},{17,25},{2,10},{10,18},{18,26},{... | collective-permute-start | bytes 2359304 | tf_op jit(solution)/shard_map/ppermute | solution.py:577
  9.8 1.3 %collective-permute-start.6 = (f32[3,32,2048]{2,1,0:T(8,128)}, f32[3,32,2048]{2,1,0:T(8,128)S(1)}, u32[]{:S(2)}, u32[]{:S(2)}) collective-permute-start(f32[3,32,2048]{2,1,0:T(8,128)} %get-tuple-element.41), channel_id=1, source_target_pairs={{8,0},{16,8},{24,16},{9,1},{17,9},{25,17},{10,2},{18,10},{26,18},{... | collective-permute-start | bytes 2359304 | tf_op jit(solution)/shard_map/ppermute | solution.py:578
  11.1 0.0 copy-start
  11.1 24.2 %conditional.1 = (f32[8,512]{1,0:T(8,128)}, f32[8,512]{1,0:T(8,128)S(1)}, f32[4,3,2,128]{3,2,1,0:T(2,128)S(1)}, bf16[1024,2048]{1,0:T(8,128)(2,1)S(1)}, f32[3,2,...) conditional(s32[]{:T(128)} %bitcast, () %tuple.16, (f32[8,8,128]{2,1,0:T(8,128)S(1)}, ...), branch_computations={%region_0.0_spmd, %region_1.0_spmd} | conditional | flops 24576 | bytes 5075026 | solution.py:594
  11.1 1.6 %collective-permute-start = (f32[8,8,128]{2,1,0:T(8,128)S(1)}, f32[8,8,128]{2,1,0:T(8,128)S(1)}, u32[]{:S(2)}, u32[]{:S(2)}) collective-permute-start(f32[8,8,128]{2,1,0:T(8,128)S(1)} %get-tuple-element.9), channel_id=1, source_target_pairs={{0,2},{2,4},{4,6},{6,0},{1,3},{3,5},{5,7},{7,1},{8,10},{10,12},{12... | collective-permute-start | bytes 98312 | tf_op jit(solution)/shard_map/cond/branch_1_fun/ppermute | solution.py:580
  12.8 2.2 %collective-permute-start.2 = (f32[8,8,128]{2,1,0:T(8,128)}, f32[8,8,128]{2,1,0:T(8,128)S(1)}, u32[]{:S(2)}, u32[]{:S(2)}) collective-permute-start(f32[8,8,128]{2,1,0:T(8,128)} %get-tuple-element.10), channel_id=1, source_target_pairs={{0,6},{2,0},{4,2},{6,4},{1,7},{3,1},{5,3},{7,5},{8,14},{10,8},{12,... | collective-permute-start | bytes 98312 | tf_op jit(solution)/shard_map/cond/branch_1_fun/ppermute | solution.py:581
  15.0 0.8 %collective-permute-start.1 = (f32[2,8,128]{2,1,0:T(8,128)S(1)}, f32[2,8,128]{2,1,0:T(8,128)S(1)}, u32[]{:S(2)}, u32[]{:S(2)}) collective-permute-start(f32[2,8,128]{2,1,0:T(8,128)S(1)} %get-tuple-element.8), channel_id=1, source_target_pairs={{0,4},{2,6},{4,0},{6,2},{1,5},{3,7},{5,1},{7,3},{8,12},{10,14},{12... | collective-permute-start | bytes 24584 | tf_op jit(solution)/shard_map/cond/branch_1_fun/ppermute | solution.py:583
  15.8 1.2 %collective-permute-done = f32[8,8,128]{2,1,0:T(8,128)S(1)} collective-permute-done((f32[8,8,128]{2,1,0:T(8,128)S(1)}, f32[8,8,128]{2,1,0:T(8,128)S(1)}, u32[]{:S(2)}, u32[]{:S(2)}) %collective-permute-start) | collective-permute-done | bytes 32800 | tf_op jit(solution)/shard_map/cond/branch_1_fun/ppermute | solution.py:580
  17.0 0.2 collective-permute-done.2
  17.2 2.3 %collective-permute-done.1 = f32[2,8,128]{2,1,0:T(8,128)S(1)} collective-permute-done((f32[2,8,128]{2,1,0:T(8,128)S(1)}, f32[2,8,128]{2,1,0:T(8,128)S(1)}, u32[]{:S(2)}, u32[]{:S(2)}) %collective-permute-start.1) | collective-permute-done | bytes 8224 | tf_op jit(solution)/shard_map/cond/branch_1_fun/ppermute | solution.py:583
  19.6 0.0 collective-permute-start.3
  19.6 1.2 %collective-permute-done.3.twin_ref = f32[8,8,128]{2,1,0:T(8,128)S(1)} collective-permute-done((f32[8,8,128]{2,1,0:T(8,128)S(1)}, f32[8,8,128]{2,1,0:T(8,128)S(1)}, u32[]{:S(2)}, u32[]{:S(2)}) %collective-permute-start.3) | collective-permute-done | bytes 32800 | tf_op jit(solution)/shard_map/cond/branch_1_fun/ppermute | solution.py:586
  20.8 0.0 copy-done.1
  20.8 0.6 copy-done.2
  21.4 11.1 %sample.1 = (f32[8,512]{1,0:T(8,128)}, f32[8,512]{1,0:T(8,128)}, f32[8,4,128]{2,1,0:T(4,128)}, bf16[1024,2048]{1,0:T(8,128)(2,1)S(1)}, f32[3,2,16,2048]{3,2,1,0:T(8,128)}) custom-call(f32[8,8,128]{2,1,0:T(8,128)} %copy-done.1, f32[8,8,128]{2,1,0:T(8,128)} %copy-done.2, f32[3,16,16,2048]{3,2,1,0:T(8,128)} %get-tuple-element.11.vel_in), custom_call_target="tpu_custom_call" | custom-call | tf_op jit(solution)/shard_map/cond/branch_1_fun/sample/pallas_call | solution.py:281
  32.5 0.2 collective-permute-start.4
  32.7 1.2 %collective-permute-done.4.other_ref = f32[8,512]{1,0:T(8,128)S(1)} collective-permute-done((f32[8,512]{1,0:T(8,128)}, f32[8,512]{1,0:T(8,128)S(1)}, u32[]{:S(2)}, u32[]{:S(2)}) %collective-permute-start.4) | collective-permute-done | bytes 16416 | tf_op jit(solution)/shard_map/cond/branch_1_fun/ppermute | solution.py:588
  33.9 0.6 copy-done.3
  34.5 0.8 %force.1 = (f32[8,512]{1,0:T(8,128)S(1)}, f32[4,3,2,128]{3,2,1,0:T(2,128)S(1)}) custom-call(f32[8,4,128]{2,1,0:T(4,128)} %get-tuple-element.13.mask_ref, f32[8,512]{1,0:T(8,128)} %get-tuple-element.14.part_ref, f32[8,512]{1,0:T(8,128)} %copy-done.3, f32[8,512]{1,0:T(8,128)} %get-tuple-element.55.own_ref), custom_call_target="tpu_custom_call" | custom-call | tf_op jit(solution)/shard_map/cond/branch_1_fun/force/pallas_call | solution.py:331
  35.3 0.2 collective-permute-start.7
  35.6 1.8 %collective-permute-start.8 = (f32[3,2,128]{2,1,0:T(2,128)S(1)}, f32[3,2,128]{2,1,0:T(2,128)S(1)}, u32[]{:S(2)}, u32[]{:S(2)}) collective-permute-start(f32[3,2,128]{2,1,0:T(2,128)S(1)} %get-tuple-element.45), channel_id=1, source_target_pairs={{0,6},{2,0},{4,2},{6,4},{1,7},{3,1},{5,3},{7,5},{8,14},{10,8},{12,... | collective-permute-start | bytes 9224 | tf_op jit(solution)/shard_map/ppermute | solution.py:600
  37.4 0.2 collective-permute-start.10
  37.6 1.6 %collective-permute-done.8 = f32[3,2,128]{2,1,0:T(2,128)S(1)} collective-permute-done((f32[3,2,128]{2,1,0:T(2,128)S(1)}, f32[3,2,128]{2,1,0:T(2,128)S(1)}, u32[]{:S(2)}, u32[]{:S(2)}) %collective-permute-start.8) | collective-permute-done | bytes 3104 | tf_op jit(solution)/shard_map/ppermute | solution.py:600
  39.2 0.8 %collective-permute-start.9 = (f32[3,2,128]{2,1,0:T(2,128)S(1)}, f32[3,2,128]{2,1,0:T(2,128)S(1)}, u32[]{:S(2)}, u32[]{:S(2)}) collective-permute-start(f32[3,2,128]{2,1,0:T(2,128)S(1)} %get-tuple-element.47), channel_id=1, source_target_pairs={{0,4},{2,6},{4,0},{6,2},{1,5},{3,7},{5,1},{7,3},{8,12},{10,14},{12... | collective-permute-start | bytes 9224 | tf_op jit(solution)/shard_map/ppermute | solution.py:600
  40.0 2.8 %collective-permute-done.10 = f32[3,2,128]{2,1,0:T(2,128)S(1)} collective-permute-done((f32[3,2,128]{2,1,0:T(2,128)S(1)}, f32[3,2,128]{2,1,0:T(2,128)S(1)}, u32[]{:S(2)}, u32[]{:S(2)}) %collective-permute-start.10) | collective-permute-done | bytes 3104 | tf_op jit(solution)/shard_map/ppermute | solution.py:600
  42.8 0.9 %collective-permute-done.9 = f32[3,2,128]{2,1,0:T(2,128)S(1)} collective-permute-done((f32[3,2,128]{2,1,0:T(2,128)S(1)}, f32[3,2,128]{2,1,0:T(2,128)S(1)}, u32[]{:S(2)}, u32[]{:S(2)}) %collective-permute-start.9) | collective-permute-done | bytes 3104 | tf_op jit(solution)/shard_map/ppermute | solution.py:600
  43.7 0.6 fusion.2
  44.3 0.0 collective-permute-done.5.prev_in
  44.3 1.2 %collective-permute-done.6.next_in = f32[3,32,2048]{2,1,0:T(8,128)S(1)} collective-permute-done((f32[3,32,2048]{2,1,0:T(8,128)}, f32[3,32,2048]{2,1,0:T(8,128)S(1)}, u32[]{:S(2)}, u32[]{:S(2)}) %collective-permute-start.6) | collective-permute-done | bytes 786464 | tf_op jit(solution)/shard_map/ppermute | solution.py:578
  45.5 0.0 collective-permute-done.7.lev_in
  45.5 17.4 %update.1 = f32[3,16,16,2048]{3,2,1,0:T(8,128)} custom-call(f32[8,512]{1,0:T(8,128)} %get-tuple-element.36.own_ref, f32[8,512]{1,0:T(8,128)S(1)} %get-tuple-element.37.force_ref, bf16[256,512]{1,0:T(8,128)(2,1)S(1)} %copy-done, f32[6,8,128]{2,1,0:T(8,128)S(1)} %get-tuple-element.38.left_ref, f32[6,8,128]{2,1,0:T(8,128)S(1)} %get-tuple-element.39.right_ref, ...), custom_call_target="tpu_custom_call" | custom-call | flops 8053063680 | bytes 12582912 | tf_op jit(solution)/shard_map/update/pallas_call | solution.py:536
  (12 shorter events, 0.0 us)
Async XLA Ops:
  0.6 10.4 %copy-start.4 = (s32[2]{0:T(128)S(1)}, s32[2]{0:T(128)}, u32[]{:S(2)}) copy-start(s32[2]{0:T(128)} %turb_in.1) | copy-start | bytes 28
  4.9 39.4 %collective-permute-start.5 = (f32[3,32,2048]{2,1,0:T(8,128)}, f32[3,32,2048]{2,1,0:T(8,128)S(1)}, u32[]{:S(2)}, u32[]{:S(2)}) collective-permute-start(f32[3,32,2048]{2,1,0:T(8,128)} %get-tuple-element.40), channel_id=1, source_target_pairs={{0,8},{8,16},{16,24},{1,9},{9,17},{17,25},{2,10},{10,18},{18,26},{... | collective-permute-start | bytes 2359304 | tf_op jit(solution)/shard_map/ppermute | solution.py:577
  9.8 35.7 %collective-permute-start.6 = (f32[3,32,2048]{2,1,0:T(8,128)}, f32[3,32,2048]{2,1,0:T(8,128)S(1)}, u32[]{:S(2)}, u32[]{:S(2)}) collective-permute-start(f32[3,32,2048]{2,1,0:T(8,128)} %get-tuple-element.41), channel_id=1, source_target_pairs={{8,0},{16,8},{24,16},{9,1},{17,9},{25,17},{10,2},{18,10},{26,18},{... | collective-permute-start | bytes 2359304 | tf_op jit(solution)/shard_map/ppermute | solution.py:578
  11.1 34.4 %copy-start = (bf16[256,512]{1,0:T(8,128)(2,1)S(1)}, bf16[256,512]{1,0:T(8,128)(2,1)}, u32[]{:S(2)}) copy-start(bf16[256,512]{1,0:T(8,128)(2,1)} %constant.2.clone.op_ref) | copy-start | bytes 786436
  11.1 5.9 %collective-permute-start = (f32[8,8,128]{2,1,0:T(8,128)S(1)}, f32[8,8,128]{2,1,0:T(8,128)S(1)}, u32[]{:S(2)}, u32[]{:S(2)}) collective-permute-start(f32[8,8,128]{2,1,0:T(8,128)S(1)} %get-tuple-element.9), channel_id=1, source_target_pairs={{0,2},{2,4},{4,6},{6,0},{1,3},{3,5},{5,7},{7,1},{8,10},{10,12},{12... | collective-permute-start | bytes 98312 | tf_op jit(solution)/shard_map/cond/branch_1_fun/ppermute | solution.py:580
  12.8 4.5 %collective-permute-start.2 = (f32[8,8,128]{2,1,0:T(8,128)}, f32[8,8,128]{2,1,0:T(8,128)S(1)}, u32[]{:S(2)}, u32[]{:S(2)}) collective-permute-start(f32[8,8,128]{2,1,0:T(8,128)} %get-tuple-element.10), channel_id=1, source_target_pairs={{0,6},{2,0},{4,2},{6,4},{1,7},{3,1},{5,3},{7,5},{8,14},{10,8},{12,... | collective-permute-start | bytes 98312 | tf_op jit(solution)/shard_map/cond/branch_1_fun/ppermute | solution.py:581
  15.0 4.5 %collective-permute-start.1 = (f32[2,8,128]{2,1,0:T(8,128)S(1)}, f32[2,8,128]{2,1,0:T(8,128)S(1)}, u32[]{:S(2)}, u32[]{:S(2)}) collective-permute-start(f32[2,8,128]{2,1,0:T(8,128)S(1)} %get-tuple-element.8), channel_id=1, source_target_pairs={{0,4},{2,6},{4,0},{6,2},{1,5},{3,7},{5,1},{7,3},{8,12},{10,14},{12... | collective-permute-start | bytes 24584 | tf_op jit(solution)/shard_map/cond/branch_1_fun/ppermute | solution.py:583
  19.6 1.2 %copy-start.1 = (f32[8,8,128]{2,1,0:T(8,128)}, f32[8,8,128]{2,1,0:T(8,128)S(1)}, u32[]{:S(2)}) copy-start(f32[8,8,128]{2,1,0:T(8,128)S(1)} %pad_maximum_fusion.mine_ref) | copy-start | bytes 98308 | tf_op jit(solution)/shard_map/cond
  19.6 1.2 %collective-permute-start.3 = (f32[8,8,128]{2,1,0:T(8,128)S(1)}, f32[8,8,128]{2,1,0:T(8,128)S(1)}, u32[]{:S(2)}, u32[]{:S(2)}) collective-permute-start(f32[8,8,128]{2,1,0:T(8,128)S(1)} %pad_maximum_fusion.mine_ref), channel_id=1, source_target_pairs={{0,1},{1,0},{2,3},{3,2},{4,5},{5,4},{6,7},{7,6},{8,9},{9,8},{10,11... | collective-permute-start | bytes 98312 | tf_op jit(solution)/shard_map/cond/branch_1_fun/ppermute | solution.py:586
  20.8 0.6 copy-start.2
  32.5 1.5 %collective-permute-start.4 = (f32[8,512]{1,0:T(8,128)}, f32[8,512]{1,0:T(8,128)S(1)}, u32[]{:S(2)}, u32[]{:S(2)}) collective-permute-start(f32[8,512]{1,0:T(8,128)} %get-tuple-element.14.part_ref), channel_id=1, source_target_pairs={{0,1},{1,0},{2,3},{3,2},{4,5},{5,4},{6,7},{7,6},{8,9},{9,8},{10,11... | collective-permute-start | bytes 49160 | tf_op jit(solution)/shard_map/cond/branch_1_fun/ppermute | solution.py:588
  33.9 0.6 copy-start.3
  35.3 10.2 %collective-permute-start.7 = (f32[3,2,16,2048]{3,2,1,0:T(8,128)}, f32[3,2,16,2048]{3,2,1,0:T(8,128)S(1)}, u32[]{:S(2)}, u32[]{:S(2)}) collective-permute-start(f32[3,2,16,2048]{3,2,1,0:T(8,128)} %get-tuple-element.43), channel_id=1, source_target_pairs={{0,1},{1,0},{2,3},{3,2},{4,5},{5,4},{6,7},{7,6},{8,9},{9,8},{10,11... | collective-permute-start | bytes 2359304 | tf_op jit(solution)/shard_map/ppermute | solution.py:597
  35.6 3.6 %collective-permute-start.8 = (f32[3,2,128]{2,1,0:T(2,128)S(1)}, f32[3,2,128]{2,1,0:T(2,128)S(1)}, u32[]{:S(2)}, u32[]{:S(2)}) collective-permute-start(f32[3,2,128]{2,1,0:T(2,128)S(1)} %get-tuple-element.45), channel_id=1, source_target_pairs={{0,6},{2,0},{4,2},{6,4},{1,7},{3,1},{5,3},{7,5},{8,14},{10,8},{12,... | collective-permute-start | bytes 9224 | tf_op jit(solution)/shard_map/ppermute | solution.py:600
  37.4 5.4 %collective-permute-start.10 = (f32[3,2,128]{2,1,0:T(2,128)S(1)}, f32[3,2,128]{2,1,0:T(2,128)S(1)}, u32[]{:S(2)}, u32[]{:S(2)}) collective-permute-start(f32[3,2,128]{2,1,0:T(2,128)S(1)} %get-tuple-element.46), channel_id=1, source_target_pairs={{0,2},{2,4},{4,6},{6,0},{1,3},{3,5},{5,7},{7,1},{8,10},{10,12},{12... | collective-permute-start | bytes 9224 | tf_op jit(solution)/shard_map/ppermute | solution.py:600
  39.2 4.5 %collective-permute-start.9 = (f32[3,2,128]{2,1,0:T(2,128)S(1)}, f32[3,2,128]{2,1,0:T(2,128)S(1)}, u32[]{:S(2)}, u32[]{:S(2)}) collective-permute-start(f32[3,2,128]{2,1,0:T(2,128)S(1)} %get-tuple-element.47), channel_id=1, source_target_pairs={{0,4},{2,6},{4,0},{6,2},{1,5},{3,7},{5,1},{7,3},{8,12},{10,14},{12... | collective-permute-start | bytes 9224 | tf_op jit(solution)/shard_map/ppermute | solution.py:600

commit v6 on v5

--- a/solution.py
+++ b/solution.py
@@ -68,7 +68,7 @@
 
 
 def prep_kernel(
-    turb_in, pos_in, speed_in, lift_in, vel_in, blocks_ref, up_ref, down_ref, head_ref, tail_ref,
+    turb_in, pos_in, speed_in, lift_in, vel_in, blocks_ref, up_ref, down_ref, near_ref, far_ref, relay_ref,
     turb_ref, pos_ref, speed_ref, lift_ref, vel_ref, sems,
 ):
     components, levels, rows, cols = vel_ref.shape
@@ -94,6 +94,7 @@
             ref[k, 2 * coords : 2 * coords + 1, :] = lift_ref[k : k + 1, :]
             ref[k, 7:8, :] = jnp.full((1, points), turb_ref[k].astype(F32))
     parts = levels * rows // 128
+    odd = lax.axis_index("gx") % 2 == 1
     row = lax.broadcasted_iota(jnp.int32, (8, cols), 0) // 2
     for component in range(components):
         large[component].wait()
@@ -114,8 +115,9 @@
                     end = pltpu.roll(end, 2 * k + 2, 0)
                 head = top if head is None else jnp.where(row == k, top, head)
                 tail = end if tail is None else jnp.where(row == k, end, tail)
-            head_ref[component, group * 8 : group * 8 + 8, :] = head
-            tail_ref[component, group * 8 : group * 8 + 8, :] = tail
+            near_ref[component, group * 8 : group * 8 + 8, :] = jnp.where(odd, head, tail)
+            ref, to = (far_ref, group * 8) if group * 8 < levels else (relay_ref, group * 8 - levels)
+            ref[component, to : to + 8, :] = jnp.where(odd, tail, head)
 
 
 def prep(velocity, blade_pos, block_turbine, blade_vel, lift_coeff):
@@ -125,13 +127,14 @@
     return pl.pallas_call(
         prep_kernel,
         in_specs=[pl.BlockSpec(memory_space=pltpu.HBM)] * 5,
-        out_specs=[pl.BlockSpec(memory_space=pltpu.VMEM)] * 5,
+        out_specs=[pl.BlockSpec(memory_space=pltpu.VMEM)] * 6,
         out_shape=[
             jax.ShapeDtypeStruct((owned, 8, points), F32),
             jax.ShapeDtypeStruct((tiles, 8, 128), F32),
             jax.ShapeDtypeStruct((tiles, 8, 128), F32),
             jax.ShapeDtypeStruct((components, 2 * levels, cols), F32),
-            jax.ShapeDtypeStruct((components, 2 * levels, cols), F32),
+            jax.ShapeDtypeStruct((components, levels, cols), F32),
+            jax.ShapeDtypeStruct((components, levels, cols), F32),
         ],
         scratch_shapes=[
             pltpu.SMEM((owned,), jnp.int32),
@@ -220,9 +223,8 @@
         weight_ref[:count, column(at)] = high
         weight_ref[count:, column(at)] = low
 
-    for at in range(chunks):
-        column_copy(at).start()
-    lev_copy.start()
+    column_copy(0).start()
+    column_copy(1).start()
     masks = match(mine_ref, twin_ref, per_turbine)
     blocks = mine_ref.shape[0]
     lane = lax.broadcasted_iota(jnp.int32, (1, cells), 1)
@@ -251,6 +253,16 @@
     def pair(step, carry):
         column_copy(2 * step).wait()
         column_copy(2 * step + 1).wait()
+
+        @pl.when(step < chunks // 2 - 1)
+        def _():
+            column_copy(2 * step + 2).start()
+            column_copy(2 * step + 3).start()
+
+        @pl.when(step == chunks // 2 - 1)
+        def _():
+            lev_copy.start()
+
         weights(2 * step + 1, odd_ref)
         multiply(2 * step, even_ref)
         weights(2 * step + 2, even_ref)
@@ -343,8 +355,8 @@
 
 
 def update_kernel(
-    own_ref, force_ref, op_ref, left_ref, right_ref, prev_in, next_in, weight_in, vel_in, lev_in,
-    new_out, pad_ref, new_ref, prev_ref, next_ref, weight_ref, high_ref, low_ref, even, odd,
+    own_ref, force_ref, op_ref, left_ref, right_ref, near_in, far_in, relay_in, weight_in, vel_in, lev_in,
+    new_out, zero_ref, pad_ref, new_ref, side_ref, weight_ref, high_ref, low_ref, even, odd,
     vel_sems, side_sems, weight_sems, new_sems, lev_sem,
 ):
     components, depth, rows, cols = new_ref.shape
@@ -355,6 +367,7 @@
     count = own_ref.shape[1]
     core = lax.axis_index("gz")
     turbine = lax.axis_index("gy")
+    parity = lax.axis_index("gx") % 2
     lane = lax.broadcasted_iota(jnp.int32, (8, 128), 1)
     shifts = ((1, lane < 1), (2, lane < 2), (127, lane >= 127), (126, lane >= 126))
 
@@ -372,10 +385,17 @@
                 weight_in.at[:, column(at)], weight_ref.at[:, column(at)], weight_sems.at[at]
             ),
             pltpu.make_async_copy(
-                prev_in.at[:, :, column(at)], prev_ref.at[:, :, column(at)], side_sems.at[0, at]
+                near_in.at[:, :, column(at)], side_ref.at[1 - parity, :, :, column(at)], side_sems.at[0, at]
             ),
             pltpu.make_async_copy(
-                next_in.at[:, :, column(at)], next_ref.at[:, :, column(at)], side_sems.at[1, at]
+                far_in.at[:, :, column(at)],
+                side_ref.at[parity, :, pl.ds(0, depth), column(at)],
+                side_sems.at[1, at],
+            ),
+            pltpu.make_async_copy(
+                relay_in.at[:, :, column(at)],
+                side_ref.at[parity, :, pl.ds(depth, depth), column(at)],
+                side_sems.at[2, at],
             ),
         ]
 
@@ -406,8 +426,8 @@
                 field = pad_ref[i, half * LEVELS : (half + 1) * LEVELS + 4, :, column(at, 128)]
                 inner_high, inner_low = split(field.reshape(inner, STEP))
                 side = slice(half * 2 * LEVELS, (half + 1) * 2 * LEVELS)
-                prev_high, prev_low = split(prev_ref[i, side, column(at)])
-                next_high, next_low = split(next_ref[i, side, column(at)])
+                prev_high, prev_low = split(side_ref[0, i, side, column(at)])
+                next_high, next_low = split(side_ref[1, i, side, column(at)])
                 empty = [jnp.zeros((fill, STEP), BF16)] if fill else []
                 high = [inner_high, prev_high, next_high] + empty
                 low = [inner_low, prev_low, next_low] + empty
@@ -476,9 +496,9 @@
                 work(level, slice(row, row + 8))
         departure(at).start()
 
-    for at in range(chunks):
-        for copy in arrivals(at):
-            copy.start()
+    for copy in arrivals(0):
+        copy.start()
+    zero_ref[...] = jnp.zeros(zero_ref.shape, F32)
 
     @pl.when(core == 1)
     def _():
@@ -504,11 +524,21 @@
     level_copy(0).wait()
     for copy in arrivals(0):
         copy.wait()
+    for copy in arrivals(1) + arrivals(2):
+        copy.start()
     matrix_part(0, even)
 
     def pair(step, carry):
         for copy in arrivals(2 * step + 1) + arrivals(2 * step + 2):
             copy.wait()
+        for copy in arrivals(2 * step + 3):
+            copy.start()
+
+        @pl.when(step < chunks // 2 - 2)
+        def _():
+            for copy in arrivals(2 * step + 4):
+                copy.start()
+
         matrix_part(2 * step + 1, odd)
         vector_part(2 * step, even)
         matrix_part(2 * step + 2, even)
@@ -525,7 +555,7 @@
         departure(at).wait()
 
 
-def update(own, force, operator, prev, after, weight, velocity, lev, left, right):
+def update(own, force, operator, near, far, relay, weight, velocity, lev, left, right, home_shape):
     components, depth, rows, cols = velocity.shape
     count = own.shape[1]
     chunks = cols // STEP
@@ -535,21 +565,23 @@
     macs = components * depth * rows * cols * (3 * count + 4 * 256)
     return pl.pallas_call(
         update_kernel,
-        in_specs=[vmem] * 5 + [hbm] * 5,
-        out_specs=hbm,
-        out_shape=jax.ShapeDtypeStruct(velocity.shape, F32),
+        in_specs=[vmem] * 5 + [hbm] * 6,
+        out_specs=[hbm, vmem],
+        out_shape=[
+            jax.ShapeDtypeStruct(velocity.shape, F32),
+            jax.ShapeDtypeStruct(home_shape, F32),
+        ],
         scratch_shapes=[
             pltpu.VMEM((components, depth + 4, rows, cols + 256), F32),
             pltpu.VMEM(velocity.shape, F32),
-            pltpu.VMEM(prev.shape, F32),
-            pltpu.VMEM(prev.shape, F32),
+            pltpu.VMEM((2, *near.shape), F32),
             pltpu.VMEM((2 * count, cols), BF16),
             pltpu.VMEM((components * depth * rows, count), BF16),
             pltpu.VMEM((components * depth * rows, count), BF16),
             fields,
             fields,
             pltpu.SemaphoreType.DMA((chunks,)),
-            pltpu.SemaphoreType.DMA((2, chunks)),
+            pltpu.SemaphoreType.DMA((3, chunks)),
             pltpu.SemaphoreType.DMA((chunks,)),
             pltpu.SemaphoreType.DMA((chunks,)),
             pltpu.SemaphoreType.DMA,
@@ -559,7 +591,7 @@
             flops=2 * macs, bytes_accessed=8 * velocity.size, transcendentals=velocity.size // 3
         ),
         name="update",
-    )(own, force, operator, left, right, prev, after, weight, velocity, lev)
+    )(own, force, operator, left, right, near, far, relay, weight, velocity, lev)
 
 
 def local(velocity, blade_pos, block_turbine, blade_vel, lift_coeff):
@@ -573,37 +605,50 @@
     def around(shift):
         return [(i, (i + shift) % gy) for i in range(gy)]
 
-    blocks, up, down, head, tail = prep(velocity, blade_pos, block_turbine, blade_vel, lift_coeff)
-    before = lax.ppermute(tail, "gx", [(i, i + 1) for i in range(gx - 1)])
-    after = lax.ppermute(head, "gx", [(i + 1, i) for i in range(gx - 1)])
-    def blade(blocks, up, down, velocity):
+    blocks, up, down, near, far, relay = prep(
+        velocity, blade_pos, block_turbine, blade_vel, lift_coeff
+    )
+    near = lax.ppermute(near, "gx", [(i, i ^ 1) for i in range(gx)])
+    across = [(i, i + 1) for i in range(1, gx - 1, 2)] + [(i + 1, i) for i in range(1, gx - 1, 2)]
+    if gx == 4:
+        relay = lax.ppermute(relay, "gx", [(1, 3), (2, 0)])
+
+    def gather(blocks, up, down):
         left = lax.ppermute(up, "gy", around(1))
         right = lax.ppermute(down, "gy", around(gy - 1))
         parts = [blocks, left[:owned]]
         parts += [lax.ppermute(blocks, "gy", around(shift)) for shift in range(2, gy - 1)]
         parts.append(right[:owned])
         mine = jnp.concatenate(parts, axis=0)
-        twin = lax.ppermute(mine, "gz", swap)
+        return mine, lax.ppermute(mine, "gz", swap), left[owned:], right[owned:]
+
+    def blade(mine, twin, velocity):
         part, own, mask, weight, facing = sample(mine, twin, velocity, per_turbine)
         other = lax.ppermute(part, "gz", swap)
+        lev = lax.ppermute(facing, "gz", swap)
         force, home = point_forces(mask, part, other, own, per_turbine, owned)
-        return own, force, home, weight, facing, left[owned:], right[owned:]
-
-    operands = (blocks, up, down, velocity)
-    empty = [jnp.zeros(out.shape, out.dtype) for out in jax.eval_shape(blade, *operands)]
-    own, force, home, weight, facing, left, right = lax.cond(
-        block_turbine[0] >= 0, blade, lambda *_: tuple(empty), *operands
-    )
-    lev = lax.ppermute(facing, "gz", swap)
+        return own, force, home, weight, lev
+
+    def stage(run, *operands):
+        empty = [jnp.zeros(out.shape, out.dtype) for out in jax.eval_shape(run, *operands)]
+        return lax.cond(block_turbine[0] >= 0, run, lambda *_: tuple(empty), *operands)
+
+    mine, twin, left, right = stage(gather, blocks, up, down)
+    if gx == 4:
+        relay = lax.ppermute(relay, "gx", [(3, 2), (0, 1)])
+    else:
+        relay = lax.ppermute(relay, "gx", across)
+    far = lax.ppermute(far, "gx", across)
+    own, force, home, weight, lev = stage(blade, mine, twin, velocity)
     result = home[0]
     for shift in range(1, gy):
         result += lax.ppermute(home[shift], "gy", around(gy - shift))
 
     operator = jnp.asarray(stencil_operator(rows))
-    new_velocity = update(
-        own, force, operator, before, after, weight, velocity, lev, left, right
+    new_velocity, zero = update(
+        own, force, operator, near, far, relay, weight, velocity, lev, left, right, result.shape
     )
-    return (new_velocity, result.transpose(1, 0, 2))
+    return (new_velocity, (result + zero).transpose(1, 0, 2))
 
 
 def solution(mesh):

time: 63.5 us -> 62.8 us (0.989)
  waiting for transfers between devices: 12.7 us -> 7.02 us
  starting transfers between devices: 14.1 us -> 19.2 us
    ppermute x3, waiting for transfers between devices: 5.27 us -> 0.01 us  [local(): result += lax.ppermute(home[shift], 'gy', around(gy - shift))]
    ppermute x7 -> x9, starting transfers between devices: 11.1 us -> 15.8 us  [the longest x1 5.16 us: local(): near = lax.ppermute(near, 'gx', [(i, i ^ 1) for i in range(gx)])]
    ppermute x7 -> x9, waiting for transfers between devices: 6.21 us -> 5.3 us  [the longest x1 2.39 us: gather(): lax.ppermute(blocks, 'gy', around(shift))]
  transfers between devices with their start and end apart: 11 -> 13, of which waited for: 9 -> 4; matrix products, arithmetic and copies ran while one was open for 1% -> 1% of each run, Pallas kernels for 19% -> 47%
where the time goes in v6:
time: 62.8 us; the launch traced here: 62 us
  Pallas kernels  33.1 us (53%)
  starting transfers between devices  19.2 us (31%)
  waiting for transfers between devices  7.02 us (11%)
  other arithmetic  1.19 us (2%)
  between operations  0.79 us (1%)
    pallas_call x1, Pallas kernels, update(): pl.pallas_call(update_kernel, in_specs=[vmem] * 5 + [hbm] * 6, out_specs=...  17.5 us
    pallas_call x1, Pallas kernels, sample(): pl.pallas_call(functools.partial(sample_kernel, per_turbine), in_specs=[v...  10.5 us
    ppermute x1, starting transfers between devices, local(): near = lax.ppermute(near, 'gx', [(i, i ^ 1) for i in range(gx)])  5.16 us
    pallas_call x1, Pallas kernels, prep(): pl.pallas_call(prep_kernel, in_specs=[pl.BlockSpec(memory_space=pltpu.HBM...  4.24 us
    ppermute x1, starting transfers between devices, local(): relay = lax.ppermute(relay, 'gx', [(3, 2), (0, 1)])  3.98 us
    ppermute x3, starting transfers between devices, local(): result += lax.ppermute(home[shift], 'gy', around(gy - shift))  2.87 us
    ppermute x1, waiting for transfers between devices, gather(): lax.ppermute(blocks, 'gy', around(shift))  2.39 us
    ppermute x1, starting transfers between devices, gather(): right = lax.ppermute(down, 'gy', around(gy - 1))  2.25 us
  transfers between devices with their start and end apart: 13, of which 4 were waited for; matrix products, arithmetic and copies ran while one was open for 1% of the time, Pallas kernels for 47%

profile of v6, /device:TPU:0, one launch (start us, length us, event | category | flops | bytes accessed | tf_op | source)
XLA Modules:
  0.0 62.0 jit_solution(11263720678735045302)
XLA Ops:
  0.6 4.2 %prep.1 = (f32[2,8,128]{2,1,0:T(8,128)S(1)}, f32[8,8,128]{2,1,0:T(8,128)S(1)}, f32[8,8,128]{2,1,0:T(8,128)S(1)}, f32[3,32,2048]{2,1,0:T(8,128)}, f32[3,16,2048]{2,1,0:T(8,128)}, /*index=5*/f32[3,16,2048]{2,1,0:T(8,128)}) custom-call(s32[2]{0:T(128)} %turb_in.1, f32[3,2,128]{2,1,0:T(2,128)} %bitcast.22, f32[3,2,128]{2,1,0:T(2,128)} %bitcast.23, ...), custom_call_target="tpu_custom_call" | custom-call | tf_op jit(solution)/shard_map/prep/pallas_call | solution.py:127
  4.9 1.3 %collective-permute-start.8 = (f32[3,16,2048]{2,1,0:T(8,128)}, f32[3,16,2048]{2,1,0:T(8,128)S(1)}, u32[]{:S(2)}, u32[]{:S(2)}) collective-permute-start(f32[3,16,2048]{2,1,0:T(8,128)} %get-tuple-element.55), channel_id=1, source_target_pairs={{8,24},{16,0},{9,25},{17,1},{10,26},{18,2},{11,27},{19,3},{12,28},... | collective-permute-start | bytes 1179656 | tf_op jit(solution)/shard_map/ppermute | solution.py:614
  6.2 5.2 %collective-permute-start.6 = (f32[3,32,2048]{2,1,0:T(8,128)}, f32[3,32,2048]{2,1,0:T(8,128)S(1)}, u32[]{:S(2)}, u32[]{:S(2)}) collective-permute-start(f32[3,32,2048]{2,1,0:T(8,128)} %get-tuple-element.53), channel_id=1, source_target_pairs={{0,8},{8,0},{16,24},{24,16},{1,9},{9,1},{17,25},{25,17},{2,10},{10... | collective-permute-start | bytes 2359304 | tf_op jit(solution)/shard_map/ppermute | solution.py:611
  11.4 10.6 %conditional.2 = (f32[8,8,128]{2,1,0:T(8,128)}, f32[8,8,128]{2,1,0:T(8,128)}, f32[6,8,128]{2,1,0:T(8,128)S(1)}, f32[6,8,128]{2,1,0:T(8,128)S(1)}) conditional(s32[]{:T(128)} %bitcast, () %tuple.25, (f32[8,8,128]{2,1,0:T(8,128)S(1)}, f32[2,8,128]{2,1,0:T(8,128)S(1)}, f32[8,8,128]{2,1,0:T(8,128)S(1)}) %tuple.26), branch_computations={%region_0.0_spmd, %region_1.0_spmd} | conditional | flops 24576 | bytes 622784 | solution.py:634
  11.4 1.6 %collective-permute-start.2 = (f32[8,8,128]{2,1,0:T(8,128)S(1)}, f32[8,8,128]{2,1,0:T(8,128)S(1)}, u32[]{:S(2)}, u32[]{:S(2)}) collective-permute-start(f32[8,8,128]{2,1,0:T(8,128)S(1)} %get-tuple-element.13), channel_id=1, source_target_pairs={{0,2},{2,4},{4,6},{6,0},{1,3},{3,5},{5,7},{7,1},{8,10},{10,12},{12... | collective-permute-start | bytes 98312 | tf_op jit(solution)/shard_map/cond/branch_1_fun/ppermute | solution.py:617
  13.0 2.2 %collective-permute-start.4 = (f32[8,8,128]{2,1,0:T(8,128)S(1)}, f32[8,8,128]{2,1,0:T(8,128)S(1)}, u32[]{:S(2)}, u32[]{:S(2)}) collective-permute-start(f32[8,8,128]{2,1,0:T(8,128)S(1)} %get-tuple-element.14), channel_id=1, source_target_pairs={{0,6},{2,0},{4,2},{6,4},{1,7},{3,1},{5,3},{7,5},{8,14},{10,8},{12,... | collective-permute-start | bytes 98312 | tf_op jit(solution)/shard_map/cond/branch_1_fun/ppermute | solution.py:618
  15.3 0.8 %collective-permute-start.3 = (f32[2,8,128]{2,1,0:T(8,128)S(1)}, f32[2,8,128]{2,1,0:T(8,128)S(1)}, u32[]{:S(2)}, u32[]{:S(2)}) collective-permute-start(f32[2,8,128]{2,1,0:T(8,128)S(1)} %get-tuple-element.12), channel_id=1, source_target_pairs={{0,4},{2,6},{4,0},{6,2},{1,5},{3,7},{5,1},{7,3},{8,12},{10,14},{12... | collective-permute-start | bytes 24584 | tf_op jit(solution)/shard_map/cond/branch_1_fun/ppermute | solution.py:620
  16.1 1.4 %collective-permute-done.2 = f32[8,8,128]{2,1,0:T(8,128)S(1)} collective-permute-done((f32[8,8,128]{2,1,0:T(8,128)S(1)}, f32[8,8,128]{2,1,0:T(8,128)S(1)}, u32[]{:S(2)}, u32[]{:S(2)}) %collective-permute-start.2) | collective-permute-done | bytes 32800 | tf_op jit(solution)/shard_map/cond/branch_1_fun/ppermute | solution.py:617
  17.5 2.4 %collective-permute-done.3 = f32[2,8,128]{2,1,0:T(8,128)S(1)} collective-permute-done((f32[2,8,128]{2,1,0:T(8,128)S(1)}, f32[2,8,128]{2,1,0:T(8,128)S(1)}, u32[]{:S(2)}, u32[]{:S(2)}) %collective-permute-start.3) | collective-permute-done | bytes 8224 | tf_op jit(solution)/shard_map/cond/branch_1_fun/ppermute | solution.py:620
  19.8 0.6 pad_maximum_fusion
  20.4 0.0 collective-permute-start.5
  20.5 1.5 %collective-permute-done.5 = f32[8,8,128]{2,1,0:T(8,128)} collective-permute-done((f32[8,8,128]{2,1,0:T(8,128)}, f32[8,8,128]{2,1,0:T(8,128)}, u32[]{:S(2)}, u32[]{:S(2)}) %collective-permute-start.5) | collective-permute-done | bytes 32800 | tf_op jit(solution)/shard_map/cond/branch_1_fun/ppermute | solution.py:623
  22.0 0.7 %collective-permute-start.7 = (f32[3,16,2048]{2,1,0:T(8,128)}, f32[3,16,2048]{2,1,0:T(8,128)S(1)}, u32[]{:S(2)}, u32[]{:S(2)}) collective-permute-start(f32[3,16,2048]{2,1,0:T(8,128)} %get-tuple-element.54), channel_id=1, source_target_pairs={{8,16},{16,8},{9,17},{17,9},{10,18},{18,10},{11,19},{19,11},{12,20... | collective-permute-start | bytes 1179656 | tf_op jit(solution)/shard_map/ppermute | solution.py:641
  22.7 0.0 collective-permute-done.8
  22.7 4.0 %collective-permute-start.9 = (f32[3,16,2048]{2,1,0:T(8,128)S(1)}, f32[3,16,2048]{2,1,0:T(8,128)S(1)}, u32[]{:S(2)}, u32[]{:S(2)}) collective-permute-start(f32[3,16,2048]{2,1,0:T(8,128)S(1)} %collective-permute-done.8), channel_id=1, source_target_pairs={{24,16},{0,8},{25,17},{1,9},{26,18},{2,10},{27,19},{3,11},{28,20},... | collective-permute-start | bytes 1179656 | tf_op jit(solution)/shard_map/ppermute | solution.py:638
  26.7 0.0 copy-start
  26.7 14.2 %conditional.3 = (f32[8,512]{1,0:T(8,128)}, f32[8,512]{1,0:T(8,128)S(1)}, f32[4,3,2,128]{3,2,1,0:T(2,128)S(1)}, bf16[1024,2048]{1,0:T(8,128)(2,1)}, f32[3,2,16,2048]{3,2,1,0:T(8,128)}) conditional(s32[]{:T(128)} %bitcast, () %tuple.24, (f32[8,8,128]{2,1,0:T(8,128)}, f32[8,8,128]{2,1,0:T(8,128)}, f32[3,16,16,2048]{3,2,1,0:T(8,128)}) %tuple.27), branch_computations={%region_2.0_spmd, %region_3.0_spmd} | conditional | bytes 5025850 | solution.py:634
  26.7 10.5 %sample.1 = (f32[8,512]{1,0:T(8,128)}, f32[8,512]{1,0:T(8,128)}, f32[8,4,128]{2,1,0:T(4,128)}, bf16[1024,2048]{1,0:T(8,128)(2,1)}, f32[3,2,16,2048]{3,2,1,0:T(8,128)}) custom-call(f32[8,8,128]{2,1,0:T(8,128)} %get-tuple-element.15.mine_ref, f32[8,8,128]{2,1,0:T(8,128)} %get-tuple-element.16.twin_ref, f32[3,16,16,2048]{3,2,1,0:T(8,128)} %get-tuple-element.17.vel_in), custom_call_target="tpu_custom_call" | custom-call | tf_op jit(solution)/shard_map/cond/branch_1_fun/sample/pallas_call | solution.py:293
  37.2 0.1 collective-permute-start.1
  37.3 0.5 collective-permute-start
  37.8 1.7 %collective-permute-done.other_ref = f32[8,512]{1,0:T(8,128)S(1)} collective-permute-done((f32[8,512]{1,0:T(8,128)}, f32[8,512]{1,0:T(8,128)S(1)}, u32[]{:S(2)}, u32[]{:S(2)}) %collective-permute-start) | collective-permute-done | bytes 16416 | tf_op jit(solution)/shard_map/cond/branch_1_fun/ppermute | solution.py:627
  39.5 0.6 copy-done.1
  40.1 0.8 %force.1 = (f32[8,512]{1,0:T(8,128)S(1)}, f32[4,3,2,128]{3,2,1,0:T(2,128)S(1)}) custom-call(f32[8,4,128]{2,1,0:T(4,128)} %get-tuple-element.19.mask_ref, f32[8,512]{1,0:T(8,128)} %get-tuple-element.20.part_ref, f32[8,512]{1,0:T(8,128)} %copy-done.1, f32[8,512]{1,0:T(8,128)} %get-tuple-element.77.own_ref), custom_call_target="tpu_custom_call" | custom-call | tf_op jit(solution)/shard_map/cond/branch_1_fun/force/pallas_call | solution.py:343
  40.9 1.9 %collective-permute-start.10 = (f32[3,2,128]{2,1,0:T(2,128)S(1)}, f32[3,2,128]{2,1,0:T(2,128)S(1)}, u32[]{:S(2)}, u32[]{:S(2)}) collective-permute-start(f32[3,2,128]{2,1,0:T(2,128)S(1)} %get-tuple-element.61), channel_id=1, source_target_pairs={{0,6},{2,0},{4,2},{6,4},{1,7},{3,1},{5,3},{7,5},{8,14},{10,8},{12,... | collective-permute-start | bytes 9224 | tf_op jit(solution)/shard_map/ppermute | solution.py:645
  42.8 0.2 collective-permute-start.12
  43.0 0.0 collective-permute-done.7.far_in
  43.0 0.8 %collective-permute-start.11 = (f32[3,2,128]{2,1,0:T(2,128)S(1)}, f32[3,2,128]{2,1,0:T(2,128)S(1)}, u32[]{:S(2)}, u32[]{:S(2)}) collective-permute-start(f32[3,2,128]{2,1,0:T(2,128)S(1)} %get-tuple-element.63), channel_id=1, source_target_pairs={{0,4},{2,6},{4,0},{6,2},{1,5},{3,7},{5,1},{7,3},{8,12},{10,14},{12... | collective-permute-start | bytes 9224 | tf_op jit(solution)/shard_map/ppermute | solution.py:645
  43.8 0.0 collective-permute-done.9.relay_in
  43.8 17.5 %update.1 = (f32[3,16,16,2048]{3,2,1,0:T(8,128)}, f32[3,2,128]{2,1,0:T(2,128)S(1)}) custom-call(f32[8,512]{1,0:T(8,128)} %get-tuple-element.49.own_ref, f32[8,512]{1,0:T(8,128)S(1)} %get-tuple-element.50.force_ref, bf16[256,512]{1,0:T(8,128)(2,1)S(1)} %copy-done, f32[6,8,128]{2,1,0:T(8,128)S(1)} %get-tuple-element.51.left_ref, ...), custom_call_target="tpu_custom_call" | custom-call | flops 8053063680 | bytes 12582912 | tf_op jit(solution)/shard_map/update/pallas_call | solution.py:566
  61.4 0.0 collective-permute-done.12
  61.4 0.0 collective-permute-done.11
  61.4 0.6 fusion.3
  (13 shorter events, 0.0 us)
Async XLA Ops:
  0.6 10.7 %copy-start.2 = (s32[2]{0:T(128)S(1)}, s32[2]{0:T(128)}, u32[]{:S(2)}) copy-start(s32[2]{0:T(128)} %turb_in.1) | copy-start | bytes 28
  4.9 17.8 %collective-permute-start.8 = (f32[3,16,2048]{2,1,0:T(8,128)}, f32[3,16,2048]{2,1,0:T(8,128)S(1)}, u32[]{:S(2)}, u32[]{:S(2)}) collective-permute-start(f32[3,16,2048]{2,1,0:T(8,128)} %get-tuple-element.55), channel_id=1, source_target_pairs={{8,24},{16,0},{9,25},{17,1},{10,26},{18,2},{11,27},{19,3},{12,28},... | collective-permute-start | bytes 1179656 | tf_op jit(solution)/shard_map/ppermute | solution.py:614
  6.2 37.6 %collective-permute-start.6 = (f32[3,32,2048]{2,1,0:T(8,128)}, f32[3,32,2048]{2,1,0:T(8,128)S(1)}, u32[]{:S(2)}, u32[]{:S(2)}) collective-permute-start(f32[3,32,2048]{2,1,0:T(8,128)} %get-tuple-element.53), channel_id=1, source_target_pairs={{0,8},{8,0},{16,24},{24,16},{1,9},{9,1},{17,25},{25,17},{2,10},{10... | collective-permute-start | bytes 2359304 | tf_op jit(solution)/shard_map/ppermute | solution.py:611
  11.4 6.0 %collective-permute-start.2 = (f32[8,8,128]{2,1,0:T(8,128)S(1)}, f32[8,8,128]{2,1,0:T(8,128)S(1)}, u32[]{:S(2)}, u32[]{:S(2)}) collective-permute-start(f32[8,8,128]{2,1,0:T(8,128)S(1)} %get-tuple-element.13), channel_id=1, source_target_pairs={{0,2},{2,4},{4,6},{6,0},{1,3},{3,5},{5,7},{7,1},{8,10},{10,12},{12... | collective-permute-start | bytes 98312 | tf_op jit(solution)/shard_map/cond/branch_1_fun/ppermute | solution.py:617
  13.0 4.4 %collective-permute-start.4 = (f32[8,8,128]{2,1,0:T(8,128)S(1)}, f32[8,8,128]{2,1,0:T(8,128)S(1)}, u32[]{:S(2)}, u32[]{:S(2)}) collective-permute-start(f32[8,8,128]{2,1,0:T(8,128)S(1)} %get-tuple-element.14), channel_id=1, source_target_pairs={{0,6},{2,0},{4,2},{6,4},{1,7},{3,1},{5,3},{7,5},{8,14},{10,8},{12,... | collective-permute-start | bytes 98312 | tf_op jit(solution)/shard_map/cond/branch_1_fun/ppermute | solution.py:618
  15.3 4.5 %collective-permute-start.3 = (f32[2,8,128]{2,1,0:T(8,128)S(1)}, f32[2,8,128]{2,1,0:T(8,128)S(1)}, u32[]{:S(2)}, u32[]{:S(2)}) collective-permute-start(f32[2,8,128]{2,1,0:T(8,128)S(1)} %get-tuple-element.12), channel_id=1, source_target_pairs={{0,4},{2,6},{4,0},{6,2},{1,5},{3,7},{5,1},{7,3},{8,12},{10,14},{12... | collective-permute-start | bytes 24584 | tf_op jit(solution)/shard_map/cond/branch_1_fun/ppermute | solution.py:620
  20.4 1.6 %collective-permute-start.5 = (f32[8,8,128]{2,1,0:T(8,128)}, f32[8,8,128]{2,1,0:T(8,128)}, u32[]{:S(2)}, u32[]{:S(2)}) collective-permute-start(f32[8,8,128]{2,1,0:T(8,128)} %pad_maximum_fusion), channel_id=1, source_target_pairs={{0,1},{1,0},{2,3},{3,2},{4,5},{5,4},{6,7},{7,6},{8,9},{9,8},{10,11... | collective-permute-start | bytes 98312 | tf_op jit(solution)/shard_map/cond/branch_1_fun/ppermute | solution.py:623
  22.0 21.0 %collective-permute-start.7 = (f32[3,16,2048]{2,1,0:T(8,128)}, f32[3,16,2048]{2,1,0:T(8,128)S(1)}, u32[]{:S(2)}, u32[]{:S(2)}) collective-permute-start(f32[3,16,2048]{2,1,0:T(8,128)} %get-tuple-element.54), channel_id=1, source_target_pairs={{8,16},{16,8},{9,17},{17,9},{10,18},{18,10},{11,19},{19,11},{12,20... | collective-permute-start | bytes 1179656 | tf_op jit(solution)/shard_map/ppermute | solution.py:641
  22.7 21.1 %collective-permute-start.9 = (f32[3,16,2048]{2,1,0:T(8,128)S(1)}, f32[3,16,2048]{2,1,0:T(8,128)S(1)}, u32[]{:S(2)}, u32[]{:S(2)}) collective-permute-start(f32[3,16,2048]{2,1,0:T(8,128)S(1)} %collective-permute-done.8), channel_id=1, source_target_pairs={{24,16},{0,8},{25,17},{1,9},{26,18},{2,10},{27,19},{3,11},{28,20},... | collective-permute-start | bytes 1179656 | tf_op jit(solution)/shard_map/ppermute | solution.py:638
  26.7 17.2 %copy-start = (bf16[256,512]{1,0:T(8,128)(2,1)S(1)}, bf16[256,512]{1,0:T(8,128)(2,1)}, u32[]{:S(2)}) copy-start(bf16[256,512]{1,0:T(8,128)(2,1)} %constant.9.clone.op_ref) | copy-start | bytes 786436
  37.2 3.7 %collective-permute-start.1 = (f32[3,2,16,2048]{3,2,1,0:T(8,128)}, f32[3,2,16,2048]{3,2,1,0:T(8,128)}, u32[]{:S(2)}, u32[]{:S(2)}) collective-permute-start(f32[3,2,16,2048]{3,2,1,0:T(8,128)} %get-tuple-element.24), channel_id=1, source_target_pairs={{0,1},{1,0},{2,3},{3,2},{4,5},{5,4},{6,7},{7,6},{8,9},{9,8},{10,11... | collective-permute-start | bytes 2359304 | tf_op jit(solution)/shard_map/cond/branch_1_fun/ppermute | solution.py:628
  37.3 2.2 %collective-permute-start = (f32[8,512]{1,0:T(8,128)}, f32[8,512]{1,0:T(8,128)S(1)}, u32[]{:S(2)}, u32[]{:S(2)}) collective-permute-start(f32[8,512]{1,0:T(8,128)} %get-tuple-element.20.part_ref), channel_id=1, source_target_pairs={{0,1},{1,0},{2,3},{3,2},{4,5},{5,4},{6,7},{7,6},{8,9},{9,8},{10,11... | collective-permute-start | bytes 49160 | tf_op jit(solution)/shard_map/cond/branch_1_fun/ppermute | solution.py:627
  39.5 0.6 copy-start.1
  40.9 20.4 %collective-permute-start.10 = (f32[3,2,128]{2,1,0:T(2,128)S(1)}, f32[3,2,128]{2,1,0:T(2,128)S(1)}, u32[]{:S(2)}, u32[]{:S(2)}) collective-permute-start(f32[3,2,128]{2,1,0:T(2,128)S(1)} %get-tuple-element.61), channel_id=1, source_target_pairs={{0,6},{2,0},{4,2},{6,4},{1,7},{3,1},{5,3},{7,5},{8,14},{10,8},{12,... | collective-permute-start | bytes 9224 | tf_op jit(solution)/shard_map/ppermute | solution.py:645
  42.8 18.6 %collective-permute-start.12 = (f32[3,2,128]{2,1,0:T(2,128)S(1)}, f32[3,2,128]{2,1,0:T(2,128)S(1)}, u32[]{:S(2)}, u32[]{:S(2)}) collective-permute-start(f32[3,2,128]{2,1,0:T(2,128)S(1)} %get-tuple-element.62), channel_id=1, source_target_pairs={{0,2},{2,4},{4,6},{6,0},{1,3},{3,5},{5,7},{7,1},{8,10},{10,12},{12... | collective-permute-start | bytes 9224 | tf_op jit(solution)/shard_map/ppermute | solution.py:645
  43.0 18.4 %collective-permute-start.11 = (f32[3,2,128]{2,1,0:T(2,128)S(1)}, f32[3,2,128]{2,1,0:T(2,128)S(1)}, u32[]{:S(2)}, u32[]{:S(2)}) collective-permute-start(f32[3,2,128]{2,1,0:T(2,128)S(1)} %get-tuple-element.63), channel_id=1, source_target_pairs={{0,4},{2,6},{4,0},{6,2},{1,5},{3,7},{5,1},{7,3},{8,12},{10,14},{12... | collective-permute-start | bytes 9224 | tf_op jit(solution)/shard_map/ppermute | solution.py:645

commit v7 on v6

--- a/solution.py
+++ b/solution.py
@@ -211,8 +211,10 @@
             ref[:, part * 128 : part * 128 + 128] = bell(cell, center_ref[...])
 
     def multiply(at, ref):
+        vel = vel_ref.at[:, :, :, column(at)]
+        out = weight_ref.at[:, column(at)]
         for i in range(components):
-            high, low = split(vel_ref[i, :, :, column(at)].reshape(cells, STEP))
+            high, low = split(vel[i].reshape(cells, STEP))
             field = dot(plane_ref[...], jnp.concatenate([high, high, low], axis=0))
             product = field * ref[...]
             total = acc_ref[i]
@@ -220,8 +222,8 @@
                 total += product[:, part * 128 : part * 128 + 128]
             acc_ref[i] = total
         high, low = split(ref[...])
-        weight_ref[:count, column(at)] = high
-        weight_ref[count:, column(at)] = low
+        out[:count, :] = high
+        out[count:, :] = low
 
     column_copy(0).start()
     column_copy(1).start()
@@ -420,31 +422,36 @@
 
     def matrix_part(at, bufs):
         grad_ref, lap_ref, body_ref = bufs
+        pad = pad_ref.at[:, :, :, column(at, 128)]
+        sides = side_ref.at[:, :, :, column(at)]
+        weight = weight_ref.at[:, column(at)]
         for i in range(components):
             for half in range(depth // LEVELS):
                 levels = slice(half * LEVELS, (half + 1) * LEVELS)
-                field = pad_ref[i, half * LEVELS : (half + 1) * LEVELS + 4, :, column(at, 128)]
+                field = pad[i, half * LEVELS : (half + 1) * LEVELS + 4]
                 inner_high, inner_low = split(field.reshape(inner, STEP))
                 side = slice(half * 2 * LEVELS, (half + 1) * 2 * LEVELS)
-                prev_high, prev_low = split(side_ref[0, i, side, column(at)])
-                next_high, next_low = split(side_ref[1, i, side, column(at)])
+                prev_high, prev_low = split(sides[0, i, side])
+                next_high, next_low = split(sides[1, i, side])
                 empty = [jnp.zeros((fill, STEP), BF16)] if fill else []
                 high = [inner_high, prev_high, next_high] + empty
                 low = [inner_low, prev_low, next_low] + empty
                 result = dot(op_ref[...], jnp.concatenate(high + low, axis=0))
                 grad_ref[i, levels] = result[:cells].reshape(LEVELS, rows, STEP)
                 lap_ref[i, levels] = result[cells:].reshape(LEVELS, rows, STEP)
-        upper = weight_ref[:count, column(at)]
-        lower = weight_ref[count:, column(at)]
+        upper = weight[:count]
+        lower = weight[count:]
         wide = jnp.concatenate([high_ref[...], low_ref[...], high_ref[...]], axis=1)
         result = dot(wide, jnp.concatenate([upper, upper, lower], axis=0))
         body_ref[...] = result.reshape(components, depth, rows, STEP)
 
     def vector_part(at, bufs):
         grad_ref, lap_ref, body_ref = bufs
+        pad = pad_ref.at[:, :, :, pl.ds(pl.multiple_of(at * STEP, 128), STEP + 256)]
+        new = new_ref.at[:, :, :, column(at)]
 
         def cell(i, level, band, block):
-            return pad_ref[i, level, band, pl.ds(pl.multiple_of(at * STEP + block * 128, 128), 128)]
+            return pad[i, level, band, block * 128 : block * 128 + 128]
 
         def work(level, band):
             here = level + 2
@@ -484,10 +491,9 @@
                 mixing = (time_step / 12.0) * viscosity + (
                     time_step * smag_coeff * smag_coeff / 144.0
                 ) * jnp.sqrt(strain)
-                out_lanes = pl.ds(pl.multiple_of(at * STEP + block * 128 - 128, 128), 128)
                 for i in range(components):
                     change = mixing * lap[i] - (time_step * mean_wind / 12.0) * along_x[i]
-                    new_ref[i, level, band, out_lanes] = (
+                    new[i, level, band, lanes] = (
                         cell(i, here, band, block) + body_ref[i, level, band, lanes] + change
                     )
 

time: 62.8 us -> 62.4 us (level)
  transfers between devices with their start and end apart: 13 -> 13, of which waited for: 4 -> 4; matrix products, arithmetic and copies ran while one was open for 1% -> 1% of each run, Pallas kernels for 47% -> 46%
where the time goes in v7:
time: 62.4 us; the launch traced here: 61.5 us
  Pallas kernels  32.6 us (52%)
  starting transfers between devices  19.2 us (31%)
  waiting for transfers between devices  7.02 us (11%)
  other arithmetic  1.19 us (2%)
  between operations  0.79 us (1%)
    pallas_call x1, Pallas kernels, update(): pl.pallas_call(update_kernel, in_specs=[vmem] * 5 + [hbm] * 6, out_specs=...  17.1 us
    pallas_call x1, Pallas kernels, sample(): pl.pallas_call(functools.partial(sample_kernel, per_turbine), in_specs=[v...  10.5 us
    ppermute x1, starting transfers between devices, local(): near = lax.ppermute(near, 'gx', [(i, i ^ 1) for i in range(gx)])  5.16 us
    pallas_call x1, Pallas kernels, prep(): pl.pallas_call(prep_kernel, in_specs=[pl.BlockSpec(memory_space=pltpu.HBM...  4.24 us
    ppermute x1, starting transfers between devices, local(): relay = lax.ppermute(relay, 'gx', [(3, 2), (0, 1)])  3.98 us
    ppermute x3, starting transfers between devices, local(): result += lax.ppermute(home[shift], 'gy', around(gy - shift))  2.87 us
    ppermute x1, waiting for transfers between devices, gather(): lax.ppermute(blocks, 'gy', around(shift))  2.39 us
    ppermute x1, starting transfers between devices, gather(): right = lax.ppermute(down, 'gy', around(gy - 1))  2.25 us
  transfers between devices with their start and end apart: 13, of which 4 were waited for; matrix products, arithmetic and copies ran while one was open for 1% of the time, Pallas kernels for 46%

profile of v7, /device:TPU:0, one launch (start us, length us, event | category | flops | bytes accessed | tf_op | source)
XLA Modules:
  0.0 61.5 jit_solution(17194150250408326687)
XLA Ops:
  0.6 4.2 %prep.1 = (f32[2,8,128]{2,1,0:T(8,128)S(1)}, f32[8,8,128]{2,1,0:T(8,128)S(1)}, f32[8,8,128]{2,1,0:T(8,128)S(1)}, f32[3,32,2048]{2,1,0:T(8,128)}, f32[3,16,2048]{2,1,0:T(8,128)}, /*index=5*/f32[3,16,2048]{2,1,0:T(8,128)}) custom-call(s32[2]{0:T(128)} %turb_in.1, f32[3,2,128]{2,1,0:T(2,128)} %bitcast.22, f32[3,2,128]{2,1,0:T(2,128)} %bitcast.23, ...), custom_call_target="tpu_custom_call" | custom-call | tf_op jit(solution)/shard_map/prep/pallas_call | solution.py:127
  4.9 1.3 %collective-permute-start.8 = (f32[3,16,2048]{2,1,0:T(8,128)}, f32[3,16,2048]{2,1,0:T(8,128)S(1)}, u32[]{:S(2)}, u32[]{:S(2)}) collective-permute-start(f32[3,16,2048]{2,1,0:T(8,128)} %get-tuple-element.55), channel_id=1, source_target_pairs={{8,24},{16,0},{9,25},{17,1},{10,26},{18,2},{11,27},{19,3},{12,28},... | collective-permute-start | bytes 1179656 | tf_op jit(solution)/shard_map/ppermute | solution.py:620
  6.2 5.2 %collective-permute-start.6 = (f32[3,32,2048]{2,1,0:T(8,128)}, f32[3,32,2048]{2,1,0:T(8,128)S(1)}, u32[]{:S(2)}, u32[]{:S(2)}) collective-permute-start(f32[3,32,2048]{2,1,0:T(8,128)} %get-tuple-element.53), channel_id=1, source_target_pairs={{0,8},{8,0},{16,24},{24,16},{1,9},{9,1},{17,25},{25,17},{2,10},{10... | collective-permute-start | bytes 2359304 | tf_op jit(solution)/shard_map/ppermute | solution.py:617
  11.4 10.6 %conditional.2 = (f32[8,8,128]{2,1,0:T(8,128)}, f32[8,8,128]{2,1,0:T(8,128)}, f32[6,8,128]{2,1,0:T(8,128)S(1)}, f32[6,8,128]{2,1,0:T(8,128)S(1)}) conditional(s32[]{:T(128)} %bitcast, () %tuple.25, (f32[8,8,128]{2,1,0:T(8,128)S(1)}, f32[2,8,128]{2,1,0:T(8,128)S(1)}, f32[8,8,128]{2,1,0:T(8,128)S(1)}) %tuple.26), branch_computations={%region_0.0_spmd, %region_1.0_spmd} | conditional | flops 24576 | bytes 622784 | solution.py:640
  11.4 1.6 %collective-permute-start.2 = (f32[8,8,128]{2,1,0:T(8,128)S(1)}, f32[8,8,128]{2,1,0:T(8,128)S(1)}, u32[]{:S(2)}, u32[]{:S(2)}) collective-permute-start(f32[8,8,128]{2,1,0:T(8,128)S(1)} %get-tuple-element.13), channel_id=1, source_target_pairs={{0,2},{2,4},{4,6},{6,0},{1,3},{3,5},{5,7},{7,1},{8,10},{10,12},{12... | collective-permute-start | bytes 98312 | tf_op jit(solution)/shard_map/cond/branch_1_fun/ppermute | solution.py:623
  13.0 2.2 %collective-permute-start.4 = (f32[8,8,128]{2,1,0:T(8,128)S(1)}, f32[8,8,128]{2,1,0:T(8,128)S(1)}, u32[]{:S(2)}, u32[]{:S(2)}) collective-permute-start(f32[8,8,128]{2,1,0:T(8,128)S(1)} %get-tuple-element.14), channel_id=1, source_target_pairs={{0,6},{2,0},{4,2},{6,4},{1,7},{3,1},{5,3},{7,5},{8,14},{10,8},{12,... | collective-permute-start | bytes 98312 | tf_op jit(solution)/shard_map/cond/branch_1_fun/ppermute | solution.py:624
  15.3 0.8 %collective-permute-start.3 = (f32[2,8,128]{2,1,0:T(8,128)S(1)}, f32[2,8,128]{2,1,0:T(8,128)S(1)}, u32[]{:S(2)}, u32[]{:S(2)}) collective-permute-start(f32[2,8,128]{2,1,0:T(8,128)S(1)} %get-tuple-element.12), channel_id=1, source_target_pairs={{0,4},{2,6},{4,0},{6,2},{1,5},{3,7},{5,1},{7,3},{8,12},{10,14},{12... | collective-permute-start | bytes 24584 | tf_op jit(solution)/shard_map/cond/branch_1_fun/ppermute | solution.py:626
  16.1 1.4 %collective-permute-done.2 = f32[8,8,128]{2,1,0:T(8,128)S(1)} collective-permute-done((f32[8,8,128]{2,1,0:T(8,128)S(1)}, f32[8,8,128]{2,1,0:T(8,128)S(1)}, u32[]{:S(2)}, u32[]{:S(2)}) %collective-permute-start.2) | collective-permute-done | bytes 32800 | tf_op jit(solution)/shard_map/cond/branch_1_fun/ppermute | solution.py:623
  17.4 0.0 collective-permute-done.4
  17.5 2.4 %collective-permute-done.3 = f32[2,8,128]{2,1,0:T(8,128)S(1)} collective-permute-done((f32[2,8,128]{2,1,0:T(8,128)S(1)}, f32[2,8,128]{2,1,0:T(8,128)S(1)}, u32[]{:S(2)}, u32[]{:S(2)}) %collective-permute-start.3) | collective-permute-done | bytes 8224 | tf_op jit(solution)/shard_map/cond/branch_1_fun/ppermute | solution.py:626
  19.8 0.6 pad_maximum_fusion
  20.5 1.5 %collective-permute-done.5 = f32[8,8,128]{2,1,0:T(8,128)} collective-permute-done((f32[8,8,128]{2,1,0:T(8,128)}, f32[8,8,128]{2,1,0:T(8,128)}, u32[]{:S(2)}, u32[]{:S(2)}) %collective-permute-start.5) | collective-permute-done | bytes 32800 | tf_op jit(solution)/shard_map/cond/branch_1_fun/ppermute | solution.py:629
  22.0 0.7 %collective-permute-start.7 = (f32[3,16,2048]{2,1,0:T(8,128)}, f32[3,16,2048]{2,1,0:T(8,128)S(1)}, u32[]{:S(2)}, u32[]{:S(2)}) collective-permute-start(f32[3,16,2048]{2,1,0:T(8,128)} %get-tuple-element.54), channel_id=1, source_target_pairs={{8,16},{16,8},{9,17},{17,9},{10,18},{18,10},{11,19},{19,11},{12,20... | collective-permute-start | bytes 1179656 | tf_op jit(solution)/shard_map/ppermute | solution.py:647
  22.7 4.0 %collective-permute-start.9 = (f32[3,16,2048]{2,1,0:T(8,128)S(1)}, f32[3,16,2048]{2,1,0:T(8,128)S(1)}, u32[]{:S(2)}, u32[]{:S(2)}) collective-permute-start(f32[3,16,2048]{2,1,0:T(8,128)S(1)} %collective-permute-done.8), channel_id=1, source_target_pairs={{24,16},{0,8},{25,17},{1,9},{26,18},{2,10},{27,19},{3,11},{28,20},... | collective-permute-start | bytes 1179656 | tf_op jit(solution)/shard_map/ppermute | solution.py:644
  26.7 0.0 copy-start
  26.7 14.2 %conditional.3 = (f32[8,512]{1,0:T(8,128)}, f32[8,512]{1,0:T(8,128)S(1)}, f32[4,3,2,128]{3,2,1,0:T(2,128)S(1)}, bf16[1024,2048]{1,0:T(8,128)(2,1)}, f32[3,2,16,2048]{3,2,1,0:T(8,128)}) conditional(s32[]{:T(128)} %bitcast, () %tuple.24, (f32[8,8,128]{2,1,0:T(8,128)}, f32[8,8,128]{2,1,0:T(8,128)}, f32[3,16,16,2048]{3,2,1,0:T(8,128)}) %tuple.27), branch_computations={%region_2.0_spmd, %region_3.0_spmd} | conditional | bytes 5025850 | solution.py:640
  26.7 10.5 %sample.1 = (f32[8,512]{1,0:T(8,128)}, f32[8,512]{1,0:T(8,128)}, f32[8,4,128]{2,1,0:T(4,128)}, bf16[1024,2048]{1,0:T(8,128)(2,1)}, f32[3,2,16,2048]{3,2,1,0:T(8,128)}) custom-call(f32[8,8,128]{2,1,0:T(8,128)} %get-tuple-element.15.mine_ref, f32[8,8,128]{2,1,0:T(8,128)} %get-tuple-element.16.twin_ref, f32[3,16,16,2048]{3,2,1,0:T(8,128)} %get-tuple-element.17.vel_in), custom_call_target="tpu_custom_call" | custom-call | tf_op jit(solution)/shard_map/cond/branch_1_fun/sample/pallas_call | solution.py:295
  37.2 0.1 collective-permute-start.1
  37.3 0.5 collective-permute-start
  37.8 1.7 %collective-permute-done.other_ref = f32[8,512]{1,0:T(8,128)S(1)} collective-permute-done((f32[8,512]{1,0:T(8,128)}, f32[8,512]{1,0:T(8,128)S(1)}, u32[]{:S(2)}, u32[]{:S(2)}) %collective-permute-start) | collective-permute-done | bytes 16416 | tf_op jit(solution)/shard_map/cond/branch_1_fun/ppermute | solution.py:633
  39.5 0.6 copy-done.1
  40.1 0.8 %force.1 = (f32[8,512]{1,0:T(8,128)S(1)}, f32[4,3,2,128]{3,2,1,0:T(2,128)S(1)}) custom-call(f32[8,4,128]{2,1,0:T(4,128)} %get-tuple-element.19.mask_ref, f32[8,512]{1,0:T(8,128)} %get-tuple-element.20.part_ref, f32[8,512]{1,0:T(8,128)} %copy-done.1, f32[8,512]{1,0:T(8,128)} %get-tuple-element.77.own_ref), custom_call_target="tpu_custom_call" | custom-call | tf_op jit(solution)/shard_map/cond/branch_1_fun/force/pallas_call | solution.py:345
  41.0 1.9 %collective-permute-start.10 = (f32[3,2,128]{2,1,0:T(2,128)S(1)}, f32[3,2,128]{2,1,0:T(2,128)S(1)}, u32[]{:S(2)}, u32[]{:S(2)}) collective-permute-start(f32[3,2,128]{2,1,0:T(2,128)S(1)} %get-tuple-element.61), channel_id=1, source_target_pairs={{0,6},{2,0},{4,2},{6,4},{1,7},{3,1},{5,3},{7,5},{8,14},{10,8},{12,... | collective-permute-start | bytes 9224 | tf_op jit(solution)/shard_map/ppermute | solution.py:651
  42.8 0.2 collective-permute-start.12
  43.0 0.0 collective-permute-done.7.far_in
  43.0 0.8 %collective-permute-start.11 = (f32[3,2,128]{2,1,0:T(2,128)S(1)}, f32[3,2,128]{2,1,0:T(2,128)S(1)}, u32[]{:S(2)}, u32[]{:S(2)}) collective-permute-start(f32[3,2,128]{2,1,0:T(2,128)S(1)} %get-tuple-element.63), channel_id=1, source_target_pairs={{0,4},{2,6},{4,0},{6,2},{1,5},{3,7},{5,1},{7,3},{8,12},{10,14},{12... | collective-permute-start | bytes 9224 | tf_op jit(solution)/shard_map/ppermute | solution.py:651
  43.8 0.0 collective-permute-done.9.relay_in
  43.8 0.0 collective-permute-done.6.near_in
  43.8 17.1 %update.1 = (f32[3,16,16,2048]{3,2,1,0:T(8,128)}, f32[3,2,128]{2,1,0:T(2,128)S(1)}) custom-call(f32[8,512]{1,0:T(8,128)} %get-tuple-element.49.own_ref, f32[8,512]{1,0:T(8,128)S(1)} %get-tuple-element.50.force_ref, bf16[256,512]{1,0:T(8,128)(2,1)S(1)} %copy-done, f32[6,8,128]{2,1,0:T(8,128)S(1)} %get-tuple-element.51.left_ref, ...), custom_call_target="tpu_custom_call" | custom-call | flops 8053063680 | bytes 12582912 | tf_op jit(solution)/shard_map/update/pallas_call | solution.py:572
  60.9 0.0 collective-permute-done.12
  60.9 0.0 collective-permute-done.11
  60.9 0.6 fusion.3
  (13 shorter events, 0.0 us)
Async XLA Ops:
  0.6 10.7 %copy-start.2 = (s32[2]{0:T(128)S(1)}, s32[2]{0:T(128)}, u32[]{:S(2)}) copy-start(s32[2]{0:T(128)} %turb_in.1) | copy-start | bytes 28
  4.9 17.8 %collective-permute-start.8 = (f32[3,16,2048]{2,1,0:T(8,128)}, f32[3,16,2048]{2,1,0:T(8,128)S(1)}, u32[]{:S(2)}, u32[]{:S(2)}) collective-permute-start(f32[3,16,2048]{2,1,0:T(8,128)} %get-tuple-element.55), channel_id=1, source_target_pairs={{8,24},{16,0},{9,25},{17,1},{10,26},{18,2},{11,27},{19,3},{12,28},... | collective-permute-start | bytes 1179656 | tf_op jit(solution)/shard_map/ppermute | solution.py:620
  6.2 37.6 %collective-permute-start.6 = (f32[3,32,2048]{2,1,0:T(8,128)}, f32[3,32,2048]{2,1,0:T(8,128)S(1)}, u32[]{:S(2)}, u32[]{:S(2)}) collective-permute-start(f32[3,32,2048]{2,1,0:T(8,128)} %get-tuple-element.53), channel_id=1, source_target_pairs={{0,8},{8,0},{16,24},{24,16},{1,9},{9,1},{17,25},{25,17},{2,10},{10... | collective-permute-start | bytes 2359304 | tf_op jit(solution)/shard_map/ppermute | solution.py:617
  11.4 6.0 %collective-permute-start.2 = (f32[8,8,128]{2,1,0:T(8,128)S(1)}, f32[8,8,128]{2,1,0:T(8,128)S(1)}, u32[]{:S(2)}, u32[]{:S(2)}) collective-permute-start(f32[8,8,128]{2,1,0:T(8,128)S(1)} %get-tuple-element.13), channel_id=1, source_target_pairs={{0,2},{2,4},{4,6},{6,0},{1,3},{3,5},{5,7},{7,1},{8,10},{10,12},{12... | collective-permute-start | bytes 98312 | tf_op jit(solution)/shard_map/cond/branch_1_fun/ppermute | solution.py:623
  13.0 4.4 %collective-permute-start.4 = (f32[8,8,128]{2,1,0:T(8,128)S(1)}, f32[8,8,128]{2,1,0:T(8,128)S(1)}, u32[]{:S(2)}, u32[]{:S(2)}) collective-permute-start(f32[8,8,128]{2,1,0:T(8,128)S(1)} %get-tuple-element.14), channel_id=1, source_target_pairs={{0,6},{2,0},{4,2},{6,4},{1,7},{3,1},{5,3},{7,5},{8,14},{10,8},{12,... | collective-permute-start | bytes 98312 | tf_op jit(solution)/shard_map/cond/branch_1_fun/ppermute | solution.py:624
  15.3 4.5 %collective-permute-start.3 = (f32[2,8,128]{2,1,0:T(8,128)S(1)}, f32[2,8,128]{2,1,0:T(8,128)S(1)}, u32[]{:S(2)}, u32[]{:S(2)}) collective-permute-start(f32[2,8,128]{2,1,0:T(8,128)S(1)} %get-tuple-element.12), channel_id=1, source_target_pairs={{0,4},{2,6},{4,0},{6,2},{1,5},{3,7},{5,1},{7,3},{8,12},{10,14},{12... | collective-permute-start | bytes 24584 | tf_op jit(solution)/shard_map/cond/branch_1_fun/ppermute | solution.py:626
  20.4 1.6 %collective-permute-start.5 = (f32[8,8,128]{2,1,0:T(8,128)}, f32[8,8,128]{2,1,0:T(8,128)}, u32[]{:S(2)}, u32[]{:S(2)}) collective-permute-start(f32[8,8,128]{2,1,0:T(8,128)} %pad_maximum_fusion), channel_id=1, source_target_pairs={{0,1},{1,0},{2,3},{3,2},{4,5},{5,4},{6,7},{7,6},{8,9},{9,8},{10,11... | collective-permute-start | bytes 98312 | tf_op jit(solution)/shard_map/cond/branch_1_fun/ppermute | solution.py:629
  22.0 21.0 %collective-permute-start.7 = (f32[3,16,2048]{2,1,0:T(8,128)}, f32[3,16,2048]{2,1,0:T(8,128)S(1)}, u32[]{:S(2)}, u32[]{:S(2)}) collective-permute-start(f32[3,16,2048]{2,1,0:T(8,128)} %get-tuple-element.54), channel_id=1, source_target_pairs={{8,16},{16,8},{9,17},{17,9},{10,18},{18,10},{11,19},{19,11},{12,20... | collective-permute-start | bytes 1179656 | tf_op jit(solution)/shard_map/ppermute | solution.py:647
  22.7 21.1 %collective-permute-start.9 = (f32[3,16,2048]{2,1,0:T(8,128)S(1)}, f32[3,16,2048]{2,1,0:T(8,128)S(1)}, u32[]{:S(2)}, u32[]{:S(2)}) collective-permute-start(f32[3,16,2048]{2,1,0:T(8,128)S(1)} %collective-permute-done.8), channel_id=1, source_target_pairs={{24,16},{0,8},{25,17},{1,9},{26,18},{2,10},{27,19},{3,11},{28,20},... | collective-permute-start | bytes 1179656 | tf_op jit(solution)/shard_map/ppermute | solution.py:644
  26.7 17.2 %copy-start = (bf16[256,512]{1,0:T(8,128)(2,1)S(1)}, bf16[256,512]{1,0:T(8,128)(2,1)}, u32[]{:S(2)}) copy-start(bf16[256,512]{1,0:T(8,128)(2,1)} %constant.9.clone.op_ref) | copy-start | bytes 786436
  37.2 3.7 %collective-permute-start.1 = (f32[3,2,16,2048]{3,2,1,0:T(8,128)}, f32[3,2,16,2048]{3,2,1,0:T(8,128)}, u32[]{:S(2)}, u32[]{:S(2)}) collective-permute-start(f32[3,2,16,2048]{3,2,1,0:T(8,128)} %get-tuple-element.24), channel_id=1, source_target_pairs={{0,1},{1,0},{2,3},{3,2},{4,5},{5,4},{6,7},{7,6},{8,9},{9,8},{10,11... | collective-permute-start | bytes 2359304 | tf_op jit(solution)/shard_map/cond/branch_1_fun/ppermute | solution.py:634
  37.3 2.2 %collective-permute-start = (f32[8,512]{1,0:T(8,128)}, f32[8,512]{1,0:T(8,128)S(1)}, u32[]{:S(2)}, u32[]{:S(2)}) collective-permute-start(f32[8,512]{1,0:T(8,128)} %get-tuple-element.20.part_ref), channel_id=1, source_target_pairs={{0,1},{1,0},{2,3},{3,2},{4,5},{5,4},{6,7},{7,6},{8,9},{9,8},{10,11... | collective-permute-start | bytes 49160 | tf_op jit(solution)/shard_map/cond/branch_1_fun/ppermute | solution.py:633
  39.5 0.6 copy-start.1
  41.0 20.0 %collective-permute-start.10 = (f32[3,2,128]{2,1,0:T(2,128)S(1)}, f32[3,2,128]{2,1,0:T(2,128)S(1)}, u32[]{:S(2)}, u32[]{:S(2)}) collective-permute-start(f32[3,2,128]{2,1,0:T(2,128)S(1)} %get-tuple-element.61), channel_id=1, source_target_pairs={{0,6},{2,0},{4,2},{6,4},{1,7},{3,1},{5,3},{7,5},{8,14},{10,8},{12,... | collective-permute-start | bytes 9224 | tf_op jit(solution)/shard_map/ppermute | solution.py:651
  42.8 18.1 %collective-permute-start.12 = (f32[3,2,128]{2,1,0:T(2,128)S(1)}, f32[3,2,128]{2,1,0:T(2,128)S(1)}, u32[]{:S(2)}, u32[]{:S(2)}) collective-permute-start(f32[3,2,128]{2,1,0:T(2,128)S(1)} %get-tuple-element.62), channel_id=1, source_target_pairs={{0,2},{2,4},{4,6},{6,0},{1,3},{3,5},{5,7},{7,1},{8,10},{10,12},{12... | collective-permute-start | bytes 9224 | tf_op jit(solution)/shard_map/ppermute | solution.py:651
  43.0 17.9 %collective-permute-start.11 = (f32[3,2,128]{2,1,0:T(2,128)S(1)}, f32[3,2,128]{2,1,0:T(2,128)S(1)}, u32[]{:S(2)}, u32[]{:S(2)}) collective-permute-start(f32[3,2,128]{2,1,0:T(2,128)S(1)} %get-tuple-element.63), channel_id=1, source_target_pairs={{0,4},{2,6},{4,0},{6,2},{1,5},{3,7},{5,1},{7,3},{8,12},{10,14},{12... | collective-permute-start | bytes 9224 | tf_op jit(solution)/shard_map/ppermute | solution.py:651

commit v8 on v7

--- a/solution.py
+++ b/solution.py
@@ -252,28 +252,26 @@
     acc_ref[...] = jnp.zeros(acc_ref.shape, F32)
     weights(0, even_ref)
 
-    def pair(step, carry):
+    def pair(step):
         column_copy(2 * step).wait()
         column_copy(2 * step + 1).wait()
 
-        @pl.when(step < chunks // 2 - 1)
-        def _():
+        if step < chunks // 2 - 1:
             column_copy(2 * step + 2).start()
             column_copy(2 * step + 3).start()
-
-        @pl.when(step == chunks // 2 - 1)
-        def _():
+        if step == 1:
             lev_copy.start()
 
         weights(2 * step + 1, odd_ref)
         multiply(2 * step, even_ref)
-        weights(2 * step + 2, even_ref)
+        if step < chunks // 2 - 1:
+            weights(2 * step + 2, even_ref)
         multiply(2 * step + 1, odd_ref)
         weight_copy(2 * step).start()
         weight_copy(2 * step + 1).start()
-        return carry
-
-    lax.fori_loop(0, chunks // 2, pair, 0)
+
+    for step in range(chunks // 2):
+        pair(step)
     for i in range(components):
         for k in range(per_turbine):
             band = slice(k * points, (k + 1) * points)
@@ -534,24 +532,22 @@
         copy.start()
     matrix_part(0, even)
 
-    def pair(step, carry):
+    def pair(step):
         for copy in arrivals(2 * step + 1) + arrivals(2 * step + 2):
             copy.wait()
         for copy in arrivals(2 * step + 3):
             copy.start()
 
-        @pl.when(step < chunks // 2 - 2)
-        def _():
+        if step < chunks // 2 - 2:
             for copy in arrivals(2 * step + 4):
                 copy.start()
-
         matrix_part(2 * step + 1, odd)
         vector_part(2 * step, even)
         matrix_part(2 * step + 2, even)
         vector_part(2 * step + 1, odd)
-        return carry
-
-    lax.fori_loop(0, chunks // 2 - 1, pair, 0)
+
+    for step in range(chunks // 2 - 1):
+        pair(step)
     for copy in arrivals(chunks - 1):
         copy.wait()
     matrix_part(chunks - 1, odd)

time: 62.4 us -> 62.4 us (level)
  no operation moved by 1% of the time
where the time goes in v8:
time: 62.4 us; the launch traced here: 61.5 us
  Pallas kernels  32.6 us (52%)
  starting transfers between devices  19.2 us (31%)
  waiting for transfers between devices  7.02 us (11%)
  other arithmetic  1.19 us (2%)
  between operations  0.79 us (1%)
    pallas_call x1, Pallas kernels, update(): pl.pallas_call(update_kernel, in_specs=[vmem] * 5 + [hbm] * 6, out_specs=...  16.8 us
    pallas_call x1, Pallas kernels, sample(): pl.pallas_call(functools.partial(sample_kernel, per_turbine), in_specs=[v...  10.7 us
    ppermute x1, starting transfers between devices, local(): near = lax.ppermute(near, 'gx', [(i, i ^ 1) for i in range(gx)])  5.16 us
    pallas_call x1, Pallas kernels, prep(): pl.pallas_call(prep_kernel, in_specs=[pl.BlockSpec(memory_space=pltpu.HBM...  4.24 us
    ppermute x1, starting transfers between devices, local(): relay = lax.ppermute(relay, 'gx', [(3, 2), (0, 1)])  3.98 us
    ppermute x3, starting transfers between devices, local(): result += lax.ppermute(home[shift], 'gy', around(gy - shift))  2.87 us
    ppermute x1, waiting for transfers between devices, gather(): lax.ppermute(blocks, 'gy', around(shift))  2.39 us
    ppermute x1, starting transfers between devices, gather(): right = lax.ppermute(down, 'gy', around(gy - 1))  2.25 us
  transfers between devices with their start and end apart: 13, of which 4 were waited for; matrix products, arithmetic and copies ran while one was open for 1% of the time, Pallas kernels for 46%

profile of v8, /device:TPU:0, one launch (start us, length us, event | category | flops | bytes accessed | tf_op | source)
XLA Modules:
  0.0 61.5 jit_solution(10478966251489907735)
XLA Ops:
  0.6 4.2 %prep.1 = (f32[2,8,128]{2,1,0:T(8,128)S(1)}, f32[8,8,128]{2,1,0:T(8,128)S(1)}, f32[8,8,128]{2,1,0:T(8,128)S(1)}, f32[3,32,2048]{2,1,0:T(8,128)}, f32[3,16,2048]{2,1,0:T(8,128)}, /*index=5*/f32[3,16,2048]{2,1,0:T(8,128)}) custom-call(s32[2]{0:T(128)} %turb_in.1, f32[3,2,128]{2,1,0:T(2,128)} %bitcast.22, f32[3,2,128]{2,1,0:T(2,128)} %bitcast.23, ...), custom_call_target="tpu_custom_call" | custom-call | tf_op jit(solution)/shard_map/prep/pallas_call | solution.py:127
  4.9 1.3 %collective-permute-start.8 = (f32[3,16,2048]{2,1,0:T(8,128)}, f32[3,16,2048]{2,1,0:T(8,128)S(1)}, u32[]{:S(2)}, u32[]{:S(2)}) collective-permute-start(f32[3,16,2048]{2,1,0:T(8,128)} %get-tuple-element.55), channel_id=1, source_target_pairs={{8,24},{16,0},{9,25},{17,1},{10,26},{18,2},{11,27},{19,3},{12,28},... | collective-permute-start | bytes 1179656 | tf_op jit(solution)/shard_map/ppermute | solution.py:616
  6.2 5.2 %collective-permute-start.6 = (f32[3,32,2048]{2,1,0:T(8,128)}, f32[3,32,2048]{2,1,0:T(8,128)S(1)}, u32[]{:S(2)}, u32[]{:S(2)}) collective-permute-start(f32[3,32,2048]{2,1,0:T(8,128)} %get-tuple-element.53), channel_id=1, source_target_pairs={{0,8},{8,0},{16,24},{24,16},{1,9},{9,1},{17,25},{25,17},{2,10},{10... | collective-permute-start | bytes 2359304 | tf_op jit(solution)/shard_map/ppermute | solution.py:613
  11.4 10.6 %conditional.2 = (f32[8,8,128]{2,1,0:T(8,128)}, f32[8,8,128]{2,1,0:T(8,128)}, f32[6,8,128]{2,1,0:T(8,128)S(1)}, f32[6,8,128]{2,1,0:T(8,128)S(1)}) conditional(s32[]{:T(128)} %bitcast, () %tuple.25, (f32[8,8,128]{2,1,0:T(8,128)S(1)}, f32[2,8,128]{2,1,0:T(8,128)S(1)}, f32[8,8,128]{2,1,0:T(8,128)S(1)}) %tuple.26), branch_computations={%region_0.0_spmd, %region_1.0_spmd} | conditional | flops 24576 | bytes 622784 | solution.py:636
  11.4 1.6 %collective-permute-start.2 = (f32[8,8,128]{2,1,0:T(8,128)S(1)}, f32[8,8,128]{2,1,0:T(8,128)S(1)}, u32[]{:S(2)}, u32[]{:S(2)}) collective-permute-start(f32[8,8,128]{2,1,0:T(8,128)S(1)} %get-tuple-element.13), channel_id=1, source_target_pairs={{0,2},{2,4},{4,6},{6,0},{1,3},{3,5},{5,7},{7,1},{8,10},{10,12},{12... | collective-permute-start | bytes 98312 | tf_op jit(solution)/shard_map/cond/branch_1_fun/ppermute | solution.py:619
  13.0 2.2 %collective-permute-start.4 = (f32[8,8,128]{2,1,0:T(8,128)S(1)}, f32[8,8,128]{2,1,0:T(8,128)S(1)}, u32[]{:S(2)}, u32[]{:S(2)}) collective-permute-start(f32[8,8,128]{2,1,0:T(8,128)S(1)} %get-tuple-element.14), channel_id=1, source_target_pairs={{0,6},{2,0},{4,2},{6,4},{1,7},{3,1},{5,3},{7,5},{8,14},{10,8},{12,... | collective-permute-start | bytes 98312 | tf_op jit(solution)/shard_map/cond/branch_1_fun/ppermute | solution.py:620
  15.3 0.8 %collective-permute-start.3 = (f32[2,8,128]{2,1,0:T(8,128)S(1)}, f32[2,8,128]{2,1,0:T(8,128)S(1)}, u32[]{:S(2)}, u32[]{:S(2)}) collective-permute-start(f32[2,8,128]{2,1,0:T(8,128)S(1)} %get-tuple-element.12), channel_id=1, source_target_pairs={{0,4},{2,6},{4,0},{6,2},{1,5},{3,7},{5,1},{7,3},{8,12},{10,14},{12... | collective-permute-start | bytes 24584 | tf_op jit(solution)/shard_map/cond/branch_1_fun/ppermute | solution.py:622
  16.1 1.4 %collective-permute-done.2 = f32[8,8,128]{2,1,0:T(8,128)S(1)} collective-permute-done((f32[8,8,128]{2,1,0:T(8,128)S(1)}, f32[8,8,128]{2,1,0:T(8,128)S(1)}, u32[]{:S(2)}, u32[]{:S(2)}) %collective-permute-start.2) | collective-permute-done | bytes 32800 | tf_op jit(solution)/shard_map/cond/branch_1_fun/ppermute | solution.py:619
  17.4 0.0 collective-permute-done.4
  17.5 2.4 %collective-permute-done.3 = f32[2,8,128]{2,1,0:T(8,128)S(1)} collective-permute-done((f32[2,8,128]{2,1,0:T(8,128)S(1)}, f32[2,8,128]{2,1,0:T(8,128)S(1)}, u32[]{:S(2)}, u32[]{:S(2)}) %collective-permute-start.3) | collective-permute-done | bytes 8224 | tf_op jit(solution)/shard_map/cond/branch_1_fun/ppermute | solution.py:622
  19.8 0.6 pad_maximum_fusion
  20.4 0.0 collective-permute-start.5
  20.5 1.5 %collective-permute-done.5 = f32[8,8,128]{2,1,0:T(8,128)} collective-permute-done((f32[8,8,128]{2,1,0:T(8,128)}, f32[8,8,128]{2,1,0:T(8,128)}, u32[]{:S(2)}, u32[]{:S(2)}) %collective-permute-start.5) | collective-permute-done | bytes 32800 | tf_op jit(solution)/shard_map/cond/branch_1_fun/ppermute | solution.py:625
  22.0 0.7 %collective-permute-start.7 = (f32[3,16,2048]{2,1,0:T(8,128)}, f32[3,16,2048]{2,1,0:T(8,128)S(1)}, u32[]{:S(2)}, u32[]{:S(2)}) collective-permute-start(f32[3,16,2048]{2,1,0:T(8,128)} %get-tuple-element.54), channel_id=1, source_target_pairs={{8,16},{16,8},{9,17},{17,9},{10,18},{18,10},{11,19},{19,11},{12,20... | collective-permute-start | bytes 1179656 | tf_op jit(solution)/shard_map/ppermute | solution.py:643
  22.7 0.0 collective-permute-done.8
  22.7 4.0 %collective-permute-start.9 = (f32[3,16,2048]{2,1,0:T(8,128)S(1)}, f32[3,16,2048]{2,1,0:T(8,128)S(1)}, u32[]{:S(2)}, u32[]{:S(2)}) collective-permute-start(f32[3,16,2048]{2,1,0:T(8,128)S(1)} %collective-permute-done.8), channel_id=1, source_target_pairs={{24,16},{0,8},{25,17},{1,9},{26,18},{2,10},{27,19},{3,11},{28,20},... | collective-permute-start | bytes 1179656 | tf_op jit(solution)/shard_map/ppermute | solution.py:640
  26.7 0.0 copy-start
  26.7 14.5 %conditional.3 = (f32[8,512]{1,0:T(8,128)}, f32[8,512]{1,0:T(8,128)S(1)}, f32[4,3,2,128]{3,2,1,0:T(2,128)S(1)}, bf16[1024,2048]{1,0:T(8,128)(2,1)}, f32[3,2,16,2048]{3,2,1,0:T(8,128)}) conditional(s32[]{:T(128)} %bitcast, () %tuple.24, (f32[8,8,128]{2,1,0:T(8,128)}, f32[8,8,128]{2,1,0:T(8,128)}, f32[3,16,16,2048]{3,2,1,0:T(8,128)}) %tuple.27), branch_computations={%region_2.0_spmd, %region_3.0_spmd} | conditional | bytes 5025850 | solution.py:636
  26.7 10.7 %sample.1 = (f32[8,512]{1,0:T(8,128)}, f32[8,512]{1,0:T(8,128)}, f32[8,4,128]{2,1,0:T(4,128)}, bf16[1024,2048]{1,0:T(8,128)(2,1)}, f32[3,2,16,2048]{3,2,1,0:T(8,128)}) custom-call(f32[8,8,128]{2,1,0:T(8,128)} %get-tuple-element.15.mine_ref, f32[8,8,128]{2,1,0:T(8,128)} %get-tuple-element.16.twin_ref, f32[3,16,16,2048]{3,2,1,0:T(8,128)} %get-tuple-element.17.vel_in), custom_call_target="tpu_custom_call" | custom-call | tf_op jit(solution)/shard_map/cond/branch_1_fun/sample/pallas_call | solution.py:293
  37.4 0.1 collective-permute-start.1
  37.5 0.5 collective-permute-start
  38.0 1.7 %collective-permute-done.other_ref = f32[8,512]{1,0:T(8,128)S(1)} collective-permute-done((f32[8,512]{1,0:T(8,128)}, f32[8,512]{1,0:T(8,128)S(1)}, u32[]{:S(2)}, u32[]{:S(2)}) %collective-permute-start) | collective-permute-done | bytes 16416 | tf_op jit(solution)/shard_map/cond/branch_1_fun/ppermute | solution.py:629
  39.7 0.6 copy-done.1
  40.3 0.8 %force.1 = (f32[8,512]{1,0:T(8,128)S(1)}, f32[4,3,2,128]{3,2,1,0:T(2,128)S(1)}) custom-call(f32[8,4,128]{2,1,0:T(4,128)} %get-tuple-element.19.mask_ref, f32[8,512]{1,0:T(8,128)} %get-tuple-element.20.part_ref, f32[8,512]{1,0:T(8,128)} %copy-done.1, f32[8,512]{1,0:T(8,128)} %get-tuple-element.77.own_ref), custom_call_target="tpu_custom_call" | custom-call | tf_op jit(solution)/shard_map/cond/branch_1_fun/force/pallas_call | solution.py:343
  41.1 0.0 collective-permute-done.1
  41.2 1.9 %collective-permute-start.10 = (f32[3,2,128]{2,1,0:T(2,128)S(1)}, f32[3,2,128]{2,1,0:T(2,128)S(1)}, u32[]{:S(2)}, u32[]{:S(2)}) collective-permute-start(f32[3,2,128]{2,1,0:T(2,128)S(1)} %get-tuple-element.61), channel_id=1, source_target_pairs={{0,6},{2,0},{4,2},{6,4},{1,7},{3,1},{5,3},{7,5},{8,14},{10,8},{12,... | collective-permute-start | bytes 9224 | tf_op jit(solution)/shard_map/ppermute | solution.py:647
  43.0 0.2 collective-permute-start.12
  43.2 0.8 %collective-permute-start.11 = (f32[3,2,128]{2,1,0:T(2,128)S(1)}, f32[3,2,128]{2,1,0:T(2,128)S(1)}, u32[]{:S(2)}, u32[]{:S(2)}) collective-permute-start(f32[3,2,128]{2,1,0:T(2,128)S(1)} %get-tuple-element.63), channel_id=1, source_target_pairs={{0,4},{2,6},{4,0},{6,2},{1,5},{3,7},{5,1},{7,3},{8,12},{10,14},{12... | collective-permute-start | bytes 9224 | tf_op jit(solution)/shard_map/ppermute | solution.py:647
  44.0 16.8 %update.1 = (f32[3,16,16,2048]{3,2,1,0:T(8,128)}, f32[3,2,128]{2,1,0:T(2,128)S(1)}) custom-call(f32[8,512]{1,0:T(8,128)} %get-tuple-element.49.own_ref, f32[8,512]{1,0:T(8,128)S(1)} %get-tuple-element.50.force_ref, bf16[256,512]{1,0:T(8,128)(2,1)S(1)} %copy-done, f32[6,8,128]{2,1,0:T(8,128)S(1)} %get-tuple-element.51.left_ref, ...), custom_call_target="tpu_custom_call" | custom-call | flops 8053063680 | bytes 12582912 | tf_op jit(solution)/shard_map/update/pallas_call | solution.py:568
  60.9 0.0 collective-permute-done.10
  60.9 0.0 collective-permute-done.11
  60.9 0.6 fusion.3
  (13 shorter events, 0.0 us)
Async XLA Ops:
  0.6 10.7 %copy-start.2 = (s32[2]{0:T(128)S(1)}, s32[2]{0:T(128)}, u32[]{:S(2)}) copy-start(s32[2]{0:T(128)} %turb_in.1) | copy-start | bytes 28
  4.9 17.8 %collective-permute-start.8 = (f32[3,16,2048]{2,1,0:T(8,128)}, f32[3,16,2048]{2,1,0:T(8,128)S(1)}, u32[]{:S(2)}, u32[]{:S(2)}) collective-permute-start(f32[3,16,2048]{2,1,0:T(8,128)} %get-tuple-element.55), channel_id=1, source_target_pairs={{8,24},{16,0},{9,25},{17,1},{10,26},{18,2},{11,27},{19,3},{12,28},... | collective-permute-start | bytes 1179656 | tf_op jit(solution)/shard_map/ppermute | solution.py:616
  6.2 37.9 %collective-permute-start.6 = (f32[3,32,2048]{2,1,0:T(8,128)}, f32[3,32,2048]{2,1,0:T(8,128)S(1)}, u32[]{:S(2)}, u32[]{:S(2)}) collective-permute-start(f32[3,32,2048]{2,1,0:T(8,128)} %get-tuple-element.53), channel_id=1, source_target_pairs={{0,8},{8,0},{16,24},{24,16},{1,9},{9,1},{17,25},{25,17},{2,10},{10... | collective-permute-start | bytes 2359304 | tf_op jit(solution)/shard_map/ppermute | solution.py:613
  11.4 6.0 %collective-permute-start.2 = (f32[8,8,128]{2,1,0:T(8,128)S(1)}, f32[8,8,128]{2,1,0:T(8,128)S(1)}, u32[]{:S(2)}, u32[]{:S(2)}) collective-permute-start(f32[8,8,128]{2,1,0:T(8,128)S(1)} %get-tuple-element.13), channel_id=1, source_target_pairs={{0,2},{2,4},{4,6},{6,0},{1,3},{3,5},{5,7},{7,1},{8,10},{10,12},{12... | collective-permute-start | bytes 98312 | tf_op jit(solution)/shard_map/cond/branch_1_fun/ppermute | solution.py:619
  13.0 4.4 %collective-permute-start.4 = (f32[8,8,128]{2,1,0:T(8,128)S(1)}, f32[8,8,128]{2,1,0:T(8,128)S(1)}, u32[]{:S(2)}, u32[]{:S(2)}) collective-permute-start(f32[8,8,128]{2,1,0:T(8,128)S(1)} %get-tuple-element.14), channel_id=1, source_target_pairs={{0,6},{2,0},{4,2},{6,4},{1,7},{3,1},{5,3},{7,5},{8,14},{10,8},{12,... | collective-permute-start | bytes 98312 | tf_op jit(solution)/shard_map/cond/branch_1_fun/ppermute | solution.py:620
  15.3 4.5 %collective-permute-start.3 = (f32[2,8,128]{2,1,0:T(8,128)S(1)}, f32[2,8,128]{2,1,0:T(8,128)S(1)}, u32[]{:S(2)}, u32[]{:S(2)}) collective-permute-start(f32[2,8,128]{2,1,0:T(8,128)S(1)} %get-tuple-element.12), channel_id=1, source_target_pairs={{0,4},{2,6},{4,0},{6,2},{1,5},{3,7},{5,1},{7,3},{8,12},{10,14},{12... | collective-permute-start | bytes 24584 | tf_op jit(solution)/shard_map/cond/branch_1_fun/ppermute | solution.py:622
  20.4 1.6 %collective-permute-start.5 = (f32[8,8,128]{2,1,0:T(8,128)}, f32[8,8,128]{2,1,0:T(8,128)}, u32[]{:S(2)}, u32[]{:S(2)}) collective-permute-start(f32[8,8,128]{2,1,0:T(8,128)} %pad_maximum_fusion), channel_id=1, source_target_pairs={{0,1},{1,0},{2,3},{3,2},{4,5},{5,4},{6,7},{7,6},{8,9},{9,8},{10,11... | collective-permute-start | bytes 98312 | tf_op jit(solution)/shard_map/cond/branch_1_fun/ppermute | solution.py:625
  22.0 21.2 %collective-permute-start.7 = (f32[3,16,2048]{2,1,0:T(8,128)}, f32[3,16,2048]{2,1,0:T(8,128)S(1)}, u32[]{:S(2)}, u32[]{:S(2)}) collective-permute-start(f32[3,16,2048]{2,1,0:T(8,128)} %get-tuple-element.54), channel_id=1, source_target_pairs={{8,16},{16,8},{9,17},{17,9},{10,18},{18,10},{11,19},{19,11},{12,20... | collective-permute-start | bytes 1179656 | tf_op jit(solution)/shard_map/ppermute | solution.py:643
  22.7 21.3 %collective-permute-start.9 = (f32[3,16,2048]{2,1,0:T(8,128)S(1)}, f32[3,16,2048]{2,1,0:T(8,128)S(1)}, u32[]{:S(2)}, u32[]{:S(2)}) collective-permute-start(f32[3,16,2048]{2,1,0:T(8,128)S(1)} %collective-permute-done.8), channel_id=1, source_target_pairs={{24,16},{0,8},{25,17},{1,9},{26,18},{2,10},{27,19},{3,11},{28,20},... | collective-permute-start | bytes 1179656 | tf_op jit(solution)/shard_map/ppermute | solution.py:640
  26.7 17.4 %copy-start = (bf16[256,512]{1,0:T(8,128)(2,1)S(1)}, bf16[256,512]{1,0:T(8,128)(2,1)}, u32[]{:S(2)}) copy-start(bf16[256,512]{1,0:T(8,128)(2,1)} %constant.9.clone.op_ref) | copy-start | bytes 786436
  37.4 3.7 %collective-permute-start.1 = (f32[3,2,16,2048]{3,2,1,0:T(8,128)}, f32[3,2,16,2048]{3,2,1,0:T(8,128)}, u32[]{:S(2)}, u32[]{:S(2)}) collective-permute-start(f32[3,2,16,2048]{3,2,1,0:T(8,128)} %get-tuple-element.24), channel_id=1, source_target_pairs={{0,1},{1,0},{2,3},{3,2},{4,5},{5,4},{6,7},{7,6},{8,9},{9,8},{10,11... | collective-permute-start | bytes 2359304 | tf_op jit(solution)/shard_map/cond/branch_1_fun/ppermute | solution.py:630
  37.5 2.2 %collective-permute-start = (f32[8,512]{1,0:T(8,128)}, f32[8,512]{1,0:T(8,128)S(1)}, u32[]{:S(2)}, u32[]{:S(2)}) collective-permute-start(f32[8,512]{1,0:T(8,128)} %get-tuple-element.20.part_ref), channel_id=1, source_target_pairs={{0,1},{1,0},{2,3},{3,2},{4,5},{5,4},{6,7},{7,6},{8,9},{9,8},{10,11... | collective-permute-start | bytes 49160 | tf_op jit(solution)/shard_map/cond/branch_1_fun/ppermute | solution.py:629
  39.7 0.6 copy-start.1
  41.2 19.7 %collective-permute-start.10 = (f32[3,2,128]{2,1,0:T(2,128)S(1)}, f32[3,2,128]{2,1,0:T(2,128)S(1)}, u32[]{:S(2)}, u32[]{:S(2)}) collective-permute-start(f32[3,2,128]{2,1,0:T(2,128)S(1)} %get-tuple-element.61), channel_id=1, source_target_pairs={{0,6},{2,0},{4,2},{6,4},{1,7},{3,1},{5,3},{7,5},{8,14},{10,8},{12,... | collective-permute-start | bytes 9224 | tf_op jit(solution)/shard_map/ppermute | solution.py:647
  43.0 17.9 %collective-permute-start.12 = (f32[3,2,128]{2,1,0:T(2,128)S(1)}, f32[3,2,128]{2,1,0:T(2,128)S(1)}, u32[]{:S(2)}, u32[]{:S(2)}) collective-permute-start(f32[3,2,128]{2,1,0:T(2,128)S(1)} %get-tuple-element.62), channel_id=1, source_target_pairs={{0,2},{2,4},{4,6},{6,0},{1,3},{3,5},{5,7},{7,1},{8,10},{10,12},{12... | collective-permute-start | bytes 9224 | tf_op jit(solution)/shard_map/ppermute | solution.py:647
  43.2 17.6 %collective-permute-start.11 = (f32[3,2,128]{2,1,0:T(2,128)S(1)}, f32[3,2,128]{2,1,0:T(2,128)S(1)}, u32[]{:S(2)}, u32[]{:S(2)}) collective-permute-start(f32[3,2,128]{2,1,0:T(2,128)S(1)} %get-tuple-element.63), channel_id=1, source_target_pairs={{0,4},{2,6},{4,0},{6,2},{1,5},{3,7},{5,1},{7,3},{8,12},{10,14},{12... | collective-permute-start | bytes 9224 | tf_op jit(solution)/shard_map/ppermute | solution.py:647

commit v9 on v7

--- a/solution.py
+++ b/solution.py
@@ -3,8 +3,6 @@
 
 import jax
 import jax.numpy as jnp
-import ml_dtypes
-import numpy as np
 from jax import lax
 from jax.experimental import pallas as pl
 from jax.experimental.pallas import tpu as pltpu
@@ -20,8 +18,8 @@
 F32 = jnp.float32
 BF16 = jnp.bfloat16
 MIB = 1024 * 1024
-LEVELS = 8
 STEP = 256
+WIDE = 512
 LIGHT = pl.CostEstimate(flops=0, bytes_accessed=0, transcendentals=0)
 
 
@@ -41,30 +39,6 @@
     cells = (first + lax.broadcasted_iota(jnp.int32, shape, 0)).astype(F32)
     gap = cells - centers
     return jnp.exp(-gap * gap / (smear * smear))
-
-
-def stencil_operator(row_cells):
-    inner = (LEVELS + 4) * row_cells
-    width = inner + 4 * LEVELS
-    op = np.zeros((2, LEVELS, row_cells, width), np.float32)
-
-    def column(level, row):
-        if 0 <= row < row_cells:
-            return (level + 2) * row_cells + row
-        if row < 0:
-            return inner + level * 2 + row + 2
-        return inner + 2 * LEVELS + level * 2 + row - row_cells
-
-    for level in range(LEVELS):
-        for row in range(row_cells):
-            for offset, first, second in ((-2, 1, -1), (-1, -8, 16), (1, 8, 16), (2, -1, -1)):
-                op[0, level, row, column(level, row + offset)] += first
-                op[1, level, row, column(level, row + offset)] += second
-                op[1, level, row, column(level + offset, row)] += second
-            op[1, level, row, column(level, row)] -= 90
-    op = op.reshape(2 * LEVELS * row_cells, width)
-    op = np.pad(op, ((0, 0), (0, -width % 128)))
-    return np.concatenate([op, op], axis=1).astype(ml_dtypes.bfloat16)
 
 
 def prep_kernel(
@@ -357,24 +331,23 @@
 
 
 def update_kernel(
-    own_ref, force_ref, op_ref, left_ref, right_ref, near_in, far_in, relay_in, weight_in, vel_in, lev_in,
-    new_out, zero_ref, pad_ref, new_ref, side_ref, weight_ref, high_ref, low_ref, even, odd,
+    own_ref, force_ref, left_ref, right_ref, near_in, far_in, relay_in, weight_in, vel_in, lev_in,
+    new_out, zero_ref, pad_ref, new_ref, side_ref, weight_ref, high_ref, low_ref, body_ref,
     vel_sems, side_sems, weight_sems, new_sems, lev_sem,
 ):
     components, depth, rows, cols = new_ref.shape
-    chunks = cols // STEP
-    cells = LEVELS * rows
-    inner = (LEVELS + 4) * rows
-    fill = op_ref.shape[1] // 2 - inner - 4 * LEVELS
+    chunks = cols // WIDE
     count = own_ref.shape[1]
     core = lax.axis_index("gz")
     turbine = lax.axis_index("gy")
     parity = lax.axis_index("gx") % 2
     lane = lax.broadcasted_iota(jnp.int32, (8, 128), 1)
+    sublane = lax.broadcasted_iota(jnp.int32, (8, 128), 0)
+    lower = {1: sublane < 1, 2: sublane < 2, 7: sublane >= 7, 6: sublane >= 6}
     shifts = ((1, lane < 1), (2, lane < 2), (127, lane >= 127), (126, lane >= 126))
 
     def column(at, first=0):
-        return pl.ds(pl.multiple_of(at * STEP + first, 128), STEP)
+        return pl.ds(pl.multiple_of(at * WIDE + first, 128), WIDE)
 
     def arrivals(at):
         return [
@@ -420,86 +393,97 @@
                 level = (tile % parts) * per_part + k
                 pad_ref[tile // parts, level + 2, :, lane : lane + 8] = turned[k * rows : (k + 1) * rows, :]
 
-    def matrix_part(at, bufs):
-        grad_ref, lap_ref, body_ref = bufs
-        pad = pad_ref.at[:, :, :, column(at, 128)]
+    def matrix_part(at):
+        weight = weight_ref.at[:, column(at)]
+        upper = weight[:count]
+        wide = jnp.concatenate([high_ref[...], low_ref[...], high_ref[...]], axis=1)
+        result = dot(wide, jnp.concatenate([upper, upper, weight[count:]], axis=0))
+        body_ref[...] = result.reshape(components, depth, rows, WIDE)
+
+    def vector_part(at):
+        pad = pad_ref.at[:, :, :, pl.ds(pl.multiple_of(at * WIDE, 128), WIDE + 256)]
         sides = side_ref.at[:, :, :, column(at)]
-        weight = weight_ref.at[:, column(at)]
-        for i in range(components):
-            for half in range(depth // LEVELS):
-                levels = slice(half * LEVELS, (half + 1) * LEVELS)
-                field = pad[i, half * LEVELS : (half + 1) * LEVELS + 4]
-                inner_high, inner_low = split(field.reshape(inner, STEP))
-                side = slice(half * 2 * LEVELS, (half + 1) * 2 * LEVELS)
-                prev_high, prev_low = split(sides[0, i, side])
-                next_high, next_low = split(sides[1, i, side])
-                empty = [jnp.zeros((fill, STEP), BF16)] if fill else []
-                high = [inner_high, prev_high, next_high] + empty
-                low = [inner_low, prev_low, next_low] + empty
-                result = dot(op_ref[...], jnp.concatenate(high + low, axis=0))
-                grad_ref[i, levels] = result[:cells].reshape(LEVELS, rows, STEP)
-                lap_ref[i, levels] = result[cells:].reshape(LEVELS, rows, STEP)
-        upper = weight[:count]
-        lower = weight[count:]
-        wide = jnp.concatenate([high_ref[...], low_ref[...], high_ref[...]], axis=1)
-        result = dot(wide, jnp.concatenate([upper, upper, lower], axis=0))
-        body_ref[...] = result.reshape(components, depth, rows, STEP)
-
-    def vector_part(at, bufs):
-        grad_ref, lap_ref, body_ref = bufs
-        pad = pad_ref.at[:, :, :, pl.ds(pl.multiple_of(at * STEP, 128), STEP + 256)]
         new = new_ref.at[:, :, :, column(at)]
+        bands = [slice(row, row + 8) for row in range(0, rows, 8)]
 
         def cell(i, level, band, block):
             return pad[i, level, band, block * 128 : block * 128 + 128]
 
-        def work(level, band):
+        def work(level):
             here = level + 2
+            group = slice(level // 4 * 8, level // 4 * 8 + 8)
+            row = level % 4 * 2
             turned = {}
 
-            def turn(i, block, shift):
-                if (i, block, shift) not in turned:
-                    turned[i, block, shift] = pltpu.roll(cell(i, here, band, block), shift, 1)
-                return turned[i, block, shift]
-
-            for block in range(1, STEP // 128 + 1):
+            def turn(i, band, block, shift):
+                key = (i, band.start, block, shift)
+                if key not in turned:
+                    turned[key] = pltpu.roll(cell(i, here, band, block), shift, 1)
+                return turned[key]
+
+            def rows_moved(own, before, after, lanes, i):
+                moved = []
+                for shift, to, edge in ((1, -row - 1, 0), (2, -row, 0), (7, 7 - row, 1), (6, 6 - row, 1)):
+                    side = (before, after)[edge]
+                    side = pltpu.roll(side, to % 8, 0) if to % 8 else side
+                    rolled = [pltpu.roll(tile, shift, 0) for tile in own]
+                    if edge:
+                        ring = rolled + [side]
+                        moved.append([jnp.where(lower[shift], ring[k + 1], ring[k]) for k in range(len(own))])
+                    else:
+                        ring = [side] + rolled
+                        moved.append([jnp.where(lower[shift], ring[k], ring[k + 1]) for k in range(len(own))])
+                return moved
+
+            for block in range(1, WIDE // 128 + 1):
                 lanes = slice(block * 128 - 128, block * 128)
-                along_y, lap, along_z = [], [], []
+                along = [[], [], []]
+                lap = []
+                middle = []
                 for i in range(components):
-                    behind, behind2, ahead, ahead2 = [
-                        jnp.where(
-                            wrapped,
-                            turn(i, block - 1 if shift < 64 else block + 1, shift),
-                            turn(i, block, shift),
+                    own = [cell(i, here, band, block) for band in bands]
+                    middle.append(own)
+                    b1, b2, a1, a2 = rows_moved(
+                        own, sides[0, i, group, lanes], sides[1, i, group, lanes], lanes, i
+                    )
+                    along_x, along_y, along_z, total = [], [], [], []
+                    for k, band in enumerate(bands):
+                        yb1, yb2, ya1, ya2 = [
+                            jnp.where(
+                                wrapped,
+                                turn(i, band, block - 1 if shift < 64 else block + 1, shift),
+                                turn(i, band, block, shift),
+                            )
+                            for shift, wrapped in shifts
+                        ]
+                        zb1, zb2 = cell(i, here - 1, band, block), cell(i, here - 2, band, block)
+                        za1, za2 = cell(i, here + 1, band, block), cell(i, here + 2, band, block)
+                        along_x.append(8.0 * (a1[k] - b1[k]) - (a2[k] - b2[k]))
+                        along_y.append(8.0 * (ya1 - yb1) - (ya2 - yb2))
+                        along_z.append(8.0 * (za1 - zb1) - (za2 - zb2))
+                        near = ((a1[k] + b1[k]) + (ya1 + yb1)) + (za1 + zb1)
+                        far = ((a2[k] + b2[k]) + (ya2 + yb2)) + (za2 + zb2)
+                        total.append((16.0 * near - far) - 90.0 * own[k])
+                    along[0].append(along_x)
+                    along[1].append(along_y)
+                    along[2].append(along_z)
+                    lap.append(total)
+                for k, band in enumerate(bands):
+                    gx, gy, gz = [[part[k] for part in parts] for parts in along]
+                    same = gx[0] * gx[0] + gy[1] * gy[1] + gz[2] * gz[2]
+                    xy, xz, yz = gx[1] + gy[0], gx[2] + gz[0], gy[2] + gz[1]
+                    strain = 2.0 * same + (xy * xy + xz * xz + yz * yz)
+                    mixing = (time_step / 12.0) * viscosity + (
+                        time_step * smag_coeff * smag_coeff / 144.0
+                    ) * jnp.sqrt(strain)
+                    for i in range(components):
+                        change = mixing * lap[i][k] - (time_step * mean_wind / 12.0) * gx[i]
+                        new[i, level, band, lanes] = (
+                            middle[i][k] + body_ref[i, level, band, lanes] + change
                         )
-                        for shift, wrapped in shifts
-                    ]
-                    along_y.append(8.0 * (ahead - behind) - (ahead2 - behind2))
-                    lap.append(
-                        lap_ref[i, level, band, lanes]
-                        + (16.0 * (ahead + behind) - (ahead2 + behind2))
-                    )
-                    near = cell(i, here + 1, band, block) - cell(i, here - 1, band, block)
-                    far = cell(i, here + 2, band, block) - cell(i, here - 2, band, block)
-                    along_z.append(8.0 * near - far)
-                along_x = [grad_ref[i, level, band, lanes] for i in range(components)]
-                same = along_x[0] * along_x[0] + along_y[1] * along_y[1] + along_z[2] * along_z[2]
-                xy = along_x[1] + along_y[0]
-                xz = along_x[2] + along_z[0]
-                yz = along_y[2] + along_z[1]
-                strain = 2.0 * same + (xy * xy + xz * xz + yz * yz)
-                mixing = (time_step / 12.0) * viscosity + (
-                    time_step * smag_coeff * smag_coeff / 144.0
-                ) * jnp.sqrt(strain)
-                for i in range(components):
-                    change = mixing * lap[i] - (time_step * mean_wind / 12.0) * along_x[i]
-                    new[i, level, band, lanes] = (
-                        cell(i, here, band, block) + body_ref[i, level, band, lanes] + change
-                    )
 
         for level in range(depth):
-            for row in range(0, rows, 8):
-                work(level, slice(row, row + 8))
+            work(level)
         departure(at).start()
 
     for copy in arrivals(0):
@@ -528,50 +512,41 @@
             high_ref[band, :] = high
             low_ref[band, :] = low
     level_copy(0).wait()
+
+    def chunk(at, carry):
+        @pl.when(at < chunks - 2)
+        def _():
+            for copy in arrivals(at + 2):
+                copy.start()
+
+        @pl.when(at < chunks - 1)
+        def _():
+            for copy in arrivals(at + 1):
+                copy.wait()
+
+        matrix_part(at)
+        vector_part(at)
+        return carry
+
+    for copy in arrivals(1):
+        copy.start()
     for copy in arrivals(0):
         copy.wait()
-    for copy in arrivals(1) + arrivals(2):
-        copy.start()
-    matrix_part(0, even)
-
-    def pair(step, carry):
-        for copy in arrivals(2 * step + 1) + arrivals(2 * step + 2):
-            copy.wait()
-        for copy in arrivals(2 * step + 3):
-            copy.start()
-
-        @pl.when(step < chunks // 2 - 2)
-        def _():
-            for copy in arrivals(2 * step + 4):
-                copy.start()
-
-        matrix_part(2 * step + 1, odd)
-        vector_part(2 * step, even)
-        matrix_part(2 * step + 2, even)
-        vector_part(2 * step + 1, odd)
-        return carry
-
-    lax.fori_loop(0, chunks // 2 - 1, pair, 0)
-    for copy in arrivals(chunks - 1):
-        copy.wait()
-    matrix_part(chunks - 1, odd)
-    vector_part(chunks - 2, even)
-    vector_part(chunks - 1, odd)
+    lax.fori_loop(0, chunks, chunk, 0)
     for at in range(chunks):
         departure(at).wait()
 
 
-def update(own, force, operator, near, far, relay, weight, velocity, lev, left, right, home_shape):
+def update(own, force, near, far, relay, weight, velocity, lev, left, right, home_shape):
     components, depth, rows, cols = velocity.shape
     count = own.shape[1]
-    chunks = cols // STEP
+    chunks = cols // WIDE
     vmem = pl.BlockSpec(memory_space=pltpu.VMEM)
     hbm = pl.BlockSpec(memory_space=pltpu.HBM)
-    fields = [pltpu.VMEM((components, depth, rows, STEP), F32)] * 3
-    macs = components * depth * rows * cols * (3 * count + 4 * 256)
+    macs = components * depth * rows * cols * 3 * count
     return pl.pallas_call(
         update_kernel,
-        in_specs=[vmem] * 5 + [hbm] * 6,
+        in_specs=[vmem] * 4 + [hbm] * 6,
         out_specs=[hbm, vmem],
         out_shape=[
             jax.ShapeDtypeStruct(velocity.shape, F32),
@@ -584,8 +559,7 @@
             pltpu.VMEM((2 * count, cols), BF16),
             pltpu.VMEM((components * depth * rows, count), BF16),
             pltpu.VMEM((components * depth * rows, count), BF16),
-            fields,
-            fields,
+            pltpu.VMEM((components, depth, rows, WIDE), F32),
             pltpu.SemaphoreType.DMA((chunks,)),
             pltpu.SemaphoreType.DMA((3, chunks)),
             pltpu.SemaphoreType.DMA((chunks,)),
@@ -597,14 +571,14 @@
             flops=2 * macs, bytes_accessed=8 * velocity.size, transcendentals=velocity.size // 3
         ),
         name="update",
-    )(own, force, operator, left, right, near, far, relay, weight, velocity, lev)
+    )(own, force, left, right, near, far, relay, weight, velocity, lev)
 
 
 def local(velocity, blade_pos, block_turbine, blade_vel, lift_coeff):
     components, depth, rows, cols = velocity.shape
     owned, _, points = blade_pos.shape
     gx, gy, gz = (lax.axis_size(axis) for axis in ("gx", "gy", "gz"))
-    assert gz == 2 and depth == 2 * LEVELS
+    assert gz == 2 and depth % 8 == 0 and rows == 16
     per_turbine = owned * gz
     swap = [(0, 1), (1, 0)]
 
@@ -650,9 +624,8 @@
     for shift in range(1, gy):
         result += lax.ppermute(home[shift], "gy", around(gy - shift))
 
-    operator = jnp.asarray(stencil_operator(rows))
     new_velocity, zero = update(
-        own, force, operator, near, far, relay, weight, velocity, lev, left, right, result.shape
+        own, force, near, far, relay, weight, velocity, lev, left, right, result.shape
     )
     return (new_velocity, (result + zero).transpose(1, 0, 2))
 

time: 62.4 us -> 63.7 us (1.021)
  Pallas kernels: 32.6 us -> 34 us
    pallas_call x1, Pallas kernels: 17.1 us -> 18.5 us  [update(): pl.pallas_call(update_kernel, in_specs=[vmem] * 4 + [hbm] * 6, out_specs=...]
  transfers between devices with their start and end apart: 13 -> 13, of which waited for: 4 -> 4; matrix products, arithmetic and copies ran while one was open for 1% -> 1% of each run, Pallas kernels for 46% -> 47%
where the time goes in v9:
time: 63.7 us; the launch traced here: 62.9 us
  Pallas kernels  34 us (53%)
  starting transfers between devices  19.2 us (30%)
  waiting for transfers between devices  7.02 us (11%)
  other arithmetic  1.19 us (2%)
  between operations  0.77 us (1%)
    pallas_call x1, Pallas kernels, update(): pl.pallas_call(update_kernel, in_specs=[vmem] * 4 + [hbm] * 6, out_specs=...  18.5 us
    pallas_call x1, Pallas kernels, sample(): pl.pallas_call(functools.partial(sample_kernel, per_turbine), in_specs=[v...  10.5 us
    ppermute x1, starting transfers between devices, local(): near = lax.ppermute(near, 'gx', [(i, i ^ 1) for i in range(gx)])  5.16 us
    pallas_call x1, Pallas kernels, prep(): pl.pallas_call(prep_kernel, in_specs=[pl.BlockSpec(memory_space=pltpu.HBM...  4.24 us
    ppermute x1, starting transfers between devices, local(): relay = lax.ppermute(relay, 'gx', [(3, 2), (0, 1)])  3.98 us
    ppermute x3, starting transfers between devices, local(): result += lax.ppermute(home[shift], 'gy', around(gy - shift))  2.86 us
    ppermute x1, waiting for transfers between devices, gather(): lax.ppermute(blocks, 'gy', around(shift))  2.39 us
    ppermute x1, starting transfers between devices, gather(): right = lax.ppermute(down, 'gy', around(gy - 1))  2.25 us
  transfers between devices with their start and end apart: 13, of which 4 were waited for; matrix products, arithmetic and copies ran while one was open for 1% of the time, Pallas kernels for 47%

profile of v9, /device:TPU:0, one launch (start us, length us, event | category | flops | bytes accessed | tf_op | source)
XLA Modules:
  0.0 62.9 jit_solution(2525674281925806360)
XLA Ops:
  0.6 4.2 %prep.1 = (f32[2,8,128]{2,1,0:T(8,128)S(1)}, f32[8,8,128]{2,1,0:T(8,128)S(1)}, f32[8,8,128]{2,1,0:T(8,128)S(1)}, f32[3,32,2048]{2,1,0:T(8,128)}, f32[3,16,2048]{2,1,0:T(8,128)}, /*index=5*/f32[3,16,2048]{2,1,0:T(8,128)}) custom-call(s32[2]{0:T(128)} %turb_in.1, f32[3,2,128]{2,1,0:T(2,128)} %bitcast.22, f32[3,2,128]{2,1,0:T(2,128)} %bitcast.23, ...), custom_call_target="tpu_custom_call" | custom-call | tf_op jit(solution)/shard_map/prep/pallas_call | solution.py:101
  4.9 1.3 %collective-permute-start.8 = (f32[3,16,2048]{2,1,0:T(8,128)}, f32[3,16,2048]{2,1,0:T(8,128)S(1)}, u32[]{:S(2)}, u32[]{:S(2)}) collective-permute-start(f32[3,16,2048]{2,1,0:T(8,128)} %get-tuple-element.55), channel_id=1, source_target_pairs={{8,24},{16,0},{9,25},{17,1},{10,26},{18,2},{11,27},{19,3},{12,28},... | collective-permute-start | bytes 1179656 | tf_op jit(solution)/shard_map/ppermute | solution.py:594
  6.2 5.2 %collective-permute-start.6 = (f32[3,32,2048]{2,1,0:T(8,128)}, f32[3,32,2048]{2,1,0:T(8,128)S(1)}, u32[]{:S(2)}, u32[]{:S(2)}) collective-permute-start(f32[3,32,2048]{2,1,0:T(8,128)} %get-tuple-element.53), channel_id=1, source_target_pairs={{0,8},{8,0},{16,24},{24,16},{1,9},{9,1},{17,25},{25,17},{2,10},{10... | collective-permute-start | bytes 2359304 | tf_op jit(solution)/shard_map/ppermute | solution.py:591
  11.4 10.6 %conditional.2 = (f32[8,8,128]{2,1,0:T(8,128)}, f32[8,8,128]{2,1,0:T(8,128)}, f32[6,8,128]{2,1,0:T(8,128)S(1)}, f32[6,8,128]{2,1,0:T(8,128)S(1)}) conditional(s32[]{:T(128)} %bitcast, () %tuple.25, (f32[8,8,128]{2,1,0:T(8,128)S(1)}, f32[2,8,128]{2,1,0:T(8,128)S(1)}, f32[8,8,128]{2,1,0:T(8,128)S(1)}) %tuple.26), branch_computations={%region_0.0_spmd, %region_1.0_spmd} | conditional | flops 24576 | bytes 622784 | solution.py:614
  11.4 1.6 %collective-permute-start.2 = (f32[8,8,128]{2,1,0:T(8,128)S(1)}, f32[8,8,128]{2,1,0:T(8,128)S(1)}, u32[]{:S(2)}, u32[]{:S(2)}) collective-permute-start(f32[8,8,128]{2,1,0:T(8,128)S(1)} %get-tuple-element.13), channel_id=1, source_target_pairs={{0,2},{2,4},{4,6},{6,0},{1,3},{3,5},{5,7},{7,1},{8,10},{10,12},{12... | collective-permute-start | bytes 98312 | tf_op jit(solution)/shard_map/cond/branch_1_fun/ppermute | solution.py:597
  13.0 2.2 %collective-permute-start.4 = (f32[8,8,128]{2,1,0:T(8,128)S(1)}, f32[8,8,128]{2,1,0:T(8,128)S(1)}, u32[]{:S(2)}, u32[]{:S(2)}) collective-permute-start(f32[8,8,128]{2,1,0:T(8,128)S(1)} %get-tuple-element.14), channel_id=1, source_target_pairs={{0,6},{2,0},{4,2},{6,4},{1,7},{3,1},{5,3},{7,5},{8,14},{10,8},{12,... | collective-permute-start | bytes 98312 | tf_op jit(solution)/shard_map/cond/branch_1_fun/ppermute | solution.py:598
  15.3 0.8 %collective-permute-start.3 = (f32[2,8,128]{2,1,0:T(8,128)S(1)}, f32[2,8,128]{2,1,0:T(8,128)S(1)}, u32[]{:S(2)}, u32[]{:S(2)}) collective-permute-start(f32[2,8,128]{2,1,0:T(8,128)S(1)} %get-tuple-element.12), channel_id=1, source_target_pairs={{0,4},{2,6},{4,0},{6,2},{1,5},{3,7},{5,1},{7,3},{8,12},{10,14},{12... | collective-permute-start | bytes 24584 | tf_op jit(solution)/shard_map/cond/branch_1_fun/ppermute | solution.py:600
  16.1 1.4 %collective-permute-done.2 = f32[8,8,128]{2,1,0:T(8,128)S(1)} collective-permute-done((f32[8,8,128]{2,1,0:T(8,128)S(1)}, f32[8,8,128]{2,1,0:T(8,128)S(1)}, u32[]{:S(2)}, u32[]{:S(2)}) %collective-permute-start.2) | collective-permute-done | bytes 32800 | tf_op jit(solution)/shard_map/cond/branch_1_fun/ppermute | solution.py:597
  17.4 0.0 collective-permute-done.4
  17.4 2.4 %collective-permute-done.3 = f32[2,8,128]{2,1,0:T(8,128)S(1)} collective-permute-done((f32[2,8,128]{2,1,0:T(8,128)S(1)}, f32[2,8,128]{2,1,0:T(8,128)S(1)}, u32[]{:S(2)}, u32[]{:S(2)}) %collective-permute-start.3) | collective-permute-done | bytes 8224 | tf_op jit(solution)/shard_map/cond/branch_1_fun/ppermute | solution.py:600
  19.8 0.6 pad_maximum_fusion
  20.4 0.0 collective-permute-start.5
  20.5 1.5 %collective-permute-done.5 = f32[8,8,128]{2,1,0:T(8,128)} collective-permute-done((f32[8,8,128]{2,1,0:T(8,128)}, f32[8,8,128]{2,1,0:T(8,128)}, u32[]{:S(2)}, u32[]{:S(2)}) %collective-permute-start.5) | collective-permute-done | bytes 32800 | tf_op jit(solution)/shard_map/cond/branch_1_fun/ppermute | solution.py:603
  22.0 0.7 %collective-permute-start.7 = (f32[3,16,2048]{2,1,0:T(8,128)}, f32[3,16,2048]{2,1,0:T(8,128)S(1)}, u32[]{:S(2)}, u32[]{:S(2)}) collective-permute-start(f32[3,16,2048]{2,1,0:T(8,128)} %get-tuple-element.54), channel_id=1, source_target_pairs={{8,16},{16,8},{9,17},{17,9},{10,18},{18,10},{11,19},{19,11},{12,20... | collective-permute-start | bytes 1179656 | tf_op jit(solution)/shard_map/ppermute | solution.py:621
  22.7 0.0 collective-permute-done.8
  22.7 4.0 %collective-permute-start.9 = (f32[3,16,2048]{2,1,0:T(8,128)S(1)}, f32[3,16,2048]{2,1,0:T(8,128)S(1)}, u32[]{:S(2)}, u32[]{:S(2)}) collective-permute-start(f32[3,16,2048]{2,1,0:T(8,128)S(1)} %collective-permute-done.8), channel_id=1, source_target_pairs={{24,16},{0,8},{25,17},{1,9},{26,18},{2,10},{27,19},{3,11},{28,20},... | collective-permute-start | bytes 1179656 | tf_op jit(solution)/shard_map/ppermute | solution.py:618
  26.7 14.2 %conditional.3 = (f32[8,512]{1,0:T(8,128)}, f32[8,512]{1,0:T(8,128)S(1)}, f32[4,3,2,128]{3,2,1,0:T(2,128)S(1)}, bf16[1024,2048]{1,0:T(8,128)(2,1)}, f32[3,2,16,2048]{3,2,1,0:T(8,128)}) conditional(s32[]{:T(128)} %bitcast, () %tuple.24, (f32[8,8,128]{2,1,0:T(8,128)}, f32[8,8,128]{2,1,0:T(8,128)}, f32[3,16,16,2048]{3,2,1,0:T(8,128)}) %tuple.27), branch_computations={%region_2.0_spmd, %region_3.0_spmd} | conditional | bytes 5025850 | solution.py:614
  26.7 10.5 %sample.1 = (f32[8,512]{1,0:T(8,128)}, f32[8,512]{1,0:T(8,128)}, f32[8,4,128]{2,1,0:T(4,128)}, bf16[1024,2048]{1,0:T(8,128)(2,1)}, f32[3,2,16,2048]{3,2,1,0:T(8,128)}) custom-call(f32[8,8,128]{2,1,0:T(8,128)} %get-tuple-element.15.mine_ref, f32[8,8,128]{2,1,0:T(8,128)} %get-tuple-element.16.twin_ref, f32[3,16,16,2048]{3,2,1,0:T(8,128)} %get-tuple-element.17.vel_in), custom_call_target="tpu_custom_call" | custom-call | tf_op jit(solution)/shard_map/cond/branch_1_fun/sample/pallas_call | solution.py:269
  37.2 0.1 collective-permute-start.1
  37.3 0.5 collective-permute-start
  37.8 1.7 %collective-permute-done.other_ref = f32[8,512]{1,0:T(8,128)S(1)} collective-permute-done((f32[8,512]{1,0:T(8,128)}, f32[8,512]{1,0:T(8,128)S(1)}, u32[]{:S(2)}, u32[]{:S(2)}) %collective-permute-start) | collective-permute-done | bytes 16416 | tf_op jit(solution)/shard_map/cond/branch_1_fun/ppermute | solution.py:607
  39.5 0.6 copy-done
  40.1 0.8 %force.1 = (f32[8,512]{1,0:T(8,128)S(1)}, f32[4,3,2,128]{3,2,1,0:T(2,128)S(1)}) custom-call(f32[8,4,128]{2,1,0:T(4,128)} %get-tuple-element.19.mask_ref, f32[8,512]{1,0:T(8,128)} %get-tuple-element.20.part_ref, f32[8,512]{1,0:T(8,128)} %copy-done, f32[8,512]{1,0:T(8,128)} %get-tuple-element.77.own_ref), custom_call_target="tpu_custom_call" | custom-call | tf_op jit(solution)/shard_map/cond/branch_1_fun/force/pallas_call | solution.py:319
  40.9 0.0 collective-permute-done.1
  40.9 1.9 %collective-permute-start.10 = (f32[3,2,128]{2,1,0:T(2,128)S(1)}, f32[3,2,128]{2,1,0:T(2,128)S(1)}, u32[]{:S(2)}, u32[]{:S(2)}) collective-permute-start(f32[3,2,128]{2,1,0:T(2,128)S(1)} %get-tuple-element.61), channel_id=1, source_target_pairs={{0,6},{2,0},{4,2},{6,4},{1,7},{3,1},{5,3},{7,5},{8,14},{10,8},{12,... | collective-permute-start | bytes 9224 | tf_op jit(solution)/shard_map/ppermute | solution.py:625
  42.8 0.2 collective-permute-start.12
  43.0 0.0 collective-permute-done.7.far_in
  43.0 0.8 %collective-permute-start.11 = (f32[3,2,128]{2,1,0:T(2,128)S(1)}, f32[3,2,128]{2,1,0:T(2,128)S(1)}, u32[]{:S(2)}, u32[]{:S(2)}) collective-permute-start(f32[3,2,128]{2,1,0:T(2,128)S(1)} %get-tuple-element.63), channel_id=1, source_target_pairs={{0,4},{2,6},{4,0},{6,2},{1,5},{3,7},{5,1},{7,3},{8,12},{10,14},{12... | collective-permute-start | bytes 9224 | tf_op jit(solution)/shard_map/ppermute | solution.py:625
  43.8 18.5 %update.1 = (f32[3,16,16,2048]{3,2,1,0:T(8,128)}, f32[3,2,128]{2,1,0:T(2,128)S(1)}) custom-call(f32[8,512]{1,0:T(8,128)} %get-tuple-element.49.own_ref, f32[8,512]{1,0:T(8,128)S(1)} %get-tuple-element.50.force_ref, f32[6,8,128]{2,1,0:T(8,128)S(1)} %get-tuple-element.51.left_ref, f32[6,8,128]{2,1,0:T(8,128)S(1)} %get-tuple-element.52.right_ref, ...), custom_call_target="tpu_custom_call" | custom-call | flops 4831838208 | bytes 12582912 | tf_op jit(solution)/shard_map/update/pallas_call | solution.py:547
  62.2 0.0 collective-permute-done.12
  62.3 0.0 collective-permute-done.11
  62.3 0.6 fusion.3
  (11 shorter events, 0.0 us)
Async XLA Ops:
  0.6 10.7 %copy-start.1 = (s32[2]{0:T(128)S(1)}, s32[2]{0:T(128)}, u32[]{:S(2)}) copy-start(s32[2]{0:T(128)} %turb_in.1) | copy-start | bytes 28
  4.9 17.8 %collective-permute-start.8 = (f32[3,16,2048]{2,1,0:T(8,128)}, f32[3,16,2048]{2,1,0:T(8,128)S(1)}, u32[]{:S(2)}, u32[]{:S(2)}) collective-permute-start(f32[3,16,2048]{2,1,0:T(8,128)} %get-tuple-element.55), channel_id=1, source_target_pairs={{8,24},{16,0},{9,25},{17,1},{10,26},{18,2},{11,27},{19,3},{12,28},... | collective-permute-start | bytes 1179656 | tf_op jit(solution)/shard_map/ppermute | solution.py:594
  6.2 37.6 %collective-permute-start.6 = (f32[3,32,2048]{2,1,0:T(8,128)}, f32[3,32,2048]{2,1,0:T(8,128)S(1)}, u32[]{:S(2)}, u32[]{:S(2)}) collective-permute-start(f32[3,32,2048]{2,1,0:T(8,128)} %get-tuple-element.53), channel_id=1, source_target_pairs={{0,8},{8,0},{16,24},{24,16},{1,9},{9,1},{17,25},{25,17},{2,10},{10... | collective-permute-start | bytes 2359304 | tf_op jit(solution)/shard_map/ppermute | solution.py:591
  11.4 6.0 %collective-permute-start.2 = (f32[8,8,128]{2,1,0:T(8,128)S(1)}, f32[8,8,128]{2,1,0:T(8,128)S(1)}, u32[]{:S(2)}, u32[]{:S(2)}) collective-permute-start(f32[8,8,128]{2,1,0:T(8,128)S(1)} %get-tuple-element.13), channel_id=1, source_target_pairs={{0,2},{2,4},{4,6},{6,0},{1,3},{3,5},{5,7},{7,1},{8,10},{10,12},{12... | collective-permute-start | bytes 98312 | tf_op jit(solution)/shard_map/cond/branch_1_fun/ppermute | solution.py:597
  13.0 4.4 %collective-permute-start.4 = (f32[8,8,128]{2,1,0:T(8,128)S(1)}, f32[8,8,128]{2,1,0:T(8,128)S(1)}, u32[]{:S(2)}, u32[]{:S(2)}) collective-permute-start(f32[8,8,128]{2,1,0:T(8,128)S(1)} %get-tuple-element.14), channel_id=1, source_target_pairs={{0,6},{2,0},{4,2},{6,4},{1,7},{3,1},{5,3},{7,5},{8,14},{10,8},{12,... | collective-permute-start | bytes 98312 | tf_op jit(solution)/shard_map/cond/branch_1_fun/ppermute | solution.py:598
  15.3 4.5 %collective-permute-start.3 = (f32[2,8,128]{2,1,0:T(8,128)S(1)}, f32[2,8,128]{2,1,0:T(8,128)S(1)}, u32[]{:S(2)}, u32[]{:S(2)}) collective-permute-start(f32[2,8,128]{2,1,0:T(8,128)S(1)} %get-tuple-element.12), channel_id=1, source_target_pairs={{0,4},{2,6},{4,0},{6,2},{1,5},{3,7},{5,1},{7,3},{8,12},{10,14},{12... | collective-permute-start | bytes 24584 | tf_op jit(solution)/shard_map/cond/branch_1_fun/ppermute | solution.py:600
  20.4 1.6 %collective-permute-start.5 = (f32[8,8,128]{2,1,0:T(8,128)}, f32[8,8,128]{2,1,0:T(8,128)}, u32[]{:S(2)}, u32[]{:S(2)}) collective-permute-start(f32[8,8,128]{2,1,0:T(8,128)} %pad_maximum_fusion), channel_id=1, source_target_pairs={{0,1},{1,0},{2,3},{3,2},{4,5},{5,4},{6,7},{7,6},{8,9},{9,8},{10,11... | collective-permute-start | bytes 98312 | tf_op jit(solution)/shard_map/cond/branch_1_fun/ppermute | solution.py:603
  22.0 21.0 %collective-permute-start.7 = (f32[3,16,2048]{2,1,0:T(8,128)}, f32[3,16,2048]{2,1,0:T(8,128)S(1)}, u32[]{:S(2)}, u32[]{:S(2)}) collective-permute-start(f32[3,16,2048]{2,1,0:T(8,128)} %get-tuple-element.54), channel_id=1, source_target_pairs={{8,16},{16,8},{9,17},{17,9},{10,18},{18,10},{11,19},{19,11},{12,20... | collective-permute-start | bytes 1179656 | tf_op jit(solution)/shard_map/ppermute | solution.py:621
  22.7 21.1 %collective-permute-start.9 = (f32[3,16,2048]{2,1,0:T(8,128)S(1)}, f32[3,16,2048]{2,1,0:T(8,128)S(1)}, u32[]{:S(2)}, u32[]{:S(2)}) collective-permute-start(f32[3,16,2048]{2,1,0:T(8,128)S(1)} %collective-permute-done.8), channel_id=1, source_target_pairs={{24,16},{0,8},{25,17},{1,9},{26,18},{2,10},{27,19},{3,11},{28,20},... | collective-permute-start | bytes 1179656 | tf_op jit(solution)/shard_map/ppermute | solution.py:618
  37.2 3.7 %collective-permute-start.1 = (f32[3,2,16,2048]{3,2,1,0:T(8,128)}, f32[3,2,16,2048]{3,2,1,0:T(8,128)}, u32[]{:S(2)}, u32[]{:S(2)}) collective-permute-start(f32[3,2,16,2048]{3,2,1,0:T(8,128)} %get-tuple-element.24), channel_id=1, source_target_pairs={{0,1},{1,0},{2,3},{3,2},{4,5},{5,4},{6,7},{7,6},{8,9},{9,8},{10,11... | collective-permute-start | bytes 2359304 | tf_op jit(solution)/shard_map/cond/branch_1_fun/ppermute | solution.py:608
  37.3 2.2 %collective-permute-start = (f32[8,512]{1,0:T(8,128)}, f32[8,512]{1,0:T(8,128)S(1)}, u32[]{:S(2)}, u32[]{:S(2)}) collective-permute-start(f32[8,512]{1,0:T(8,128)} %get-tuple-element.20.part_ref), channel_id=1, source_target_pairs={{0,1},{1,0},{2,3},{3,2},{4,5},{5,4},{6,7},{7,6},{8,9},{9,8},{10,11... | collective-permute-start | bytes 49160 | tf_op jit(solution)/shard_map/cond/branch_1_fun/ppermute | solution.py:607
  39.5 0.6 copy-start
  40.9 21.3 %collective-permute-start.10 = (f32[3,2,128]{2,1,0:T(2,128)S(1)}, f32[3,2,128]{2,1,0:T(2,128)S(1)}, u32[]{:S(2)}, u32[]{:S(2)}) collective-permute-start(f32[3,2,128]{2,1,0:T(2,128)S(1)} %get-tuple-element.61), channel_id=1, source_target_pairs={{0,6},{2,0},{4,2},{6,4},{1,7},{3,1},{5,3},{7,5},{8,14},{10,8},{12,... | collective-permute-start | bytes 9224 | tf_op jit(solution)/shard_map/ppermute | solution.py:625
  42.8 19.5 %collective-permute-start.12 = (f32[3,2,128]{2,1,0:T(2,128)S(1)}, f32[3,2,128]{2,1,0:T(2,128)S(1)}, u32[]{:S(2)}, u32[]{:S(2)}) collective-permute-start(f32[3,2,128]{2,1,0:T(2,128)S(1)} %get-tuple-element.62), channel_id=1, source_target_pairs={{0,2},{2,4},{4,6},{6,0},{1,3},{3,5},{5,7},{7,1},{8,10},{10,12},{12... | collective-permute-start | bytes 9224 | tf_op jit(solution)/shard_map/ppermute | solution.py:625
  43.0 19.3 %collective-permute-start.11 = (f32[3,2,128]{2,1,0:T(2,128)S(1)}, f32[3,2,128]{2,1,0:T(2,128)S(1)}, u32[]{:S(2)}, u32[]{:S(2)}) collective-permute-start(f32[3,2,128]{2,1,0:T(2,128)S(1)} %get-tuple-element.63), channel_id=1, source_target_pairs={{0,4},{2,6},{4,0},{6,2},{1,5},{3,7},{5,1},{7,3},{8,12},{10,14},{12... | collective-permute-start | bytes 9224 | tf_op jit(solution)/shard_map/ppermute | solution.py:625

commit v10 on v7

--- a/solution.py
+++ b/solution.py
@@ -19,6 +19,7 @@
 
 F32 = jnp.float32
 BF16 = jnp.bfloat16
+SMALLEST = float(jnp.finfo(F32).tiny)
 MIB = 1024 * 1024
 LEVELS = 8
 STEP = 256
@@ -226,7 +227,6 @@
         out[count:, :] = low
 
     column_copy(0).start()
-    column_copy(1).start()
     masks = match(mine_ref, twin_ref, per_turbine)
     blocks = mine_ref.shape[0]
     lane = lax.broadcasted_iota(jnp.int32, (1, cells), 1)
@@ -253,23 +253,23 @@
     weights(0, even_ref)
 
     def pair(step, carry):
+        column_copy(2 * step + 1).start()
         column_copy(2 * step).wait()
-        column_copy(2 * step + 1).wait()
+        weights(2 * step + 1, odd_ref)
+        multiply(2 * step, even_ref)
+        weight_copy(2 * step).start()
 
         @pl.when(step < chunks // 2 - 1)
         def _():
             column_copy(2 * step + 2).start()
-            column_copy(2 * step + 3).start()
-
-        @pl.when(step == chunks // 2 - 1)
+
+        @pl.when(step == 1)
         def _():
             lev_copy.start()
 
-        weights(2 * step + 1, odd_ref)
-        multiply(2 * step, even_ref)
+        column_copy(2 * step + 1).wait()
         weights(2 * step + 2, even_ref)
         multiply(2 * step + 1, odd_ref)
-        weight_copy(2 * step).start()
         weight_copy(2 * step + 1).start()
         return carry
 
@@ -455,11 +455,16 @@
 
         def work(level, band):
             here = level + 2
-            turned = {}
+            turned, center = {}, {}
+
+            def middle(i, block):
+                if (i, block) not in center:
+                    center[i, block] = cell(i, here, band, block)
+                return center[i, block]
 
             def turn(i, block, shift):
                 if (i, block, shift) not in turned:
-                    turned[i, block, shift] = pltpu.roll(cell(i, here, band, block), shift, 1)
+                    turned[i, block, shift] = pltpu.roll(middle(i, block), shift, 1)
                 return turned[i, block, shift]
 
             for block in range(1, STEP // 128 + 1):
@@ -490,11 +495,11 @@
                 strain = 2.0 * same + (xy * xy + xz * xz + yz * yz)
                 mixing = (time_step / 12.0) * viscosity + (
                     time_step * smag_coeff * smag_coeff / 144.0
-                ) * jnp.sqrt(strain)
+                ) * (strain * lax.rsqrt(jnp.maximum(strain, SMALLEST)))
                 for i in range(components):
                     change = mixing * lap[i] - (time_step * mean_wind / 12.0) * along_x[i]
                     new[i, level, band, lanes] = (
-                        cell(i, here, band, block) + body_ref[i, level, band, lanes] + change
+                        middle(i, block) + body_ref[i, level, band, lanes] + change
                     )
 
         for level in range(depth):

time: 62.4 us -> 65.4 us (1.048)
  Pallas kernels: 32.6 us -> 35.7 us
    pallas_call x1, Pallas kernels: 10.5 us -> 13.6 us  [sample(): pl.pallas_call(functools.partial(sample_kernel, per_turbine), in_specs=[v...]
  transfers between devices with their start and end apart: 13 -> 13, of which waited for: 4 -> 4; matrix products, arithmetic and copies ran while one was open for 1% -> 1% of each run, Pallas kernels for 46% -> 49%
where the time goes in v10:
time: 65.4 us; the launch traced here: 64.6 us
  Pallas kernels  35.7 us (55%)
  starting transfers between devices  19.2 us (29%)
  waiting for transfers between devices  7.02 us (11%)
  other arithmetic  1.19 us (2%)
  between operations  0.79 us (1%)
    pallas_call x1, Pallas kernels, update(): pl.pallas_call(update_kernel, in_specs=[vmem] * 5 + [hbm] * 6, out_specs=...  17 us
    pallas_call x1, Pallas kernels, sample(): pl.pallas_call(functools.partial(sample_kernel, per_turbine), in_specs=[v...  13.6 us
    ppermute x1, starting transfers between devices, local(): near = lax.ppermute(near, 'gx', [(i, i ^ 1) for i in range(gx)])  5.16 us
    pallas_call x1, Pallas kernels, prep(): pl.pallas_call(prep_kernel, in_specs=[pl.BlockSpec(memory_space=pltpu.HBM...  4.24 us
    ppermute x1, starting transfers between devices, local(): relay = lax.ppermute(relay, 'gx', [(3, 2), (0, 1)])  3.98 us
    ppermute x3, starting transfers between devices, local(): result += lax.ppermute(home[shift], 'gy', around(gy - shift))  2.87 us
    ppermute x1, waiting for transfers between devices, gather(): lax.ppermute(blocks, 'gy', around(shift))  2.39 us
    ppermute x1, starting transfers between devices, gather(): right = lax.ppermute(down, 'gy', around(gy - 1))  2.25 us
  transfers between devices with their start and end apart: 13, of which 4 were waited for; matrix products, arithmetic and copies ran while one was open for 1% of the time, Pallas kernels for 49%

profile of v10, /device:TPU:0, one launch (start us, length us, event | category | flops | bytes accessed | tf_op | source)
XLA Modules:
  0.0 64.6 jit_solution(14905018561708484533)
XLA Ops:
  0.6 4.2 %prep.1 = (f32[2,8,128]{2,1,0:T(8,128)S(1)}, f32[8,8,128]{2,1,0:T(8,128)S(1)}, f32[8,8,128]{2,1,0:T(8,128)S(1)}, f32[3,32,2048]{2,1,0:T(8,128)}, f32[3,16,2048]{2,1,0:T(8,128)}, /*index=5*/f32[3,16,2048]{2,1,0:T(8,128)}) custom-call(s32[2]{0:T(128)} %turb_in.1, f32[3,2,128]{2,1,0:T(2,128)} %bitcast.22, f32[3,2,128]{2,1,0:T(2,128)} %bitcast.23, ...), custom_call_target="tpu_custom_call" | custom-call | tf_op jit(solution)/shard_map/prep/pallas_call | solution.py:128
  4.9 1.3 %collective-permute-start.8 = (f32[3,16,2048]{2,1,0:T(8,128)}, f32[3,16,2048]{2,1,0:T(8,128)S(1)}, u32[]{:S(2)}, u32[]{:S(2)}) collective-permute-start(f32[3,16,2048]{2,1,0:T(8,128)} %get-tuple-element.55), channel_id=1, source_target_pairs={{8,24},{16,0},{9,25},{17,1},{10,26},{18,2},{11,27},{19,3},{12,28},... | collective-permute-start | bytes 1179656 | tf_op jit(solution)/shard_map/ppermute | solution.py:625
  6.2 5.2 %collective-permute-start.6 = (f32[3,32,2048]{2,1,0:T(8,128)}, f32[3,32,2048]{2,1,0:T(8,128)S(1)}, u32[]{:S(2)}, u32[]{:S(2)}) collective-permute-start(f32[3,32,2048]{2,1,0:T(8,128)} %get-tuple-element.53), channel_id=1, source_target_pairs={{0,8},{8,0},{16,24},{24,16},{1,9},{9,1},{17,25},{25,17},{2,10},{10... | collective-permute-start | bytes 2359304 | tf_op jit(solution)/shard_map/ppermute | solution.py:622
  11.4 10.6 %conditional.2 = (f32[8,8,128]{2,1,0:T(8,128)}, f32[8,8,128]{2,1,0:T(8,128)}, f32[6,8,128]{2,1,0:T(8,128)S(1)}, f32[6,8,128]{2,1,0:T(8,128)S(1)}) conditional(s32[]{:T(128)} %bitcast, () %tuple.25, (f32[8,8,128]{2,1,0:T(8,128)S(1)}, f32[2,8,128]{2,1,0:T(8,128)S(1)}, f32[8,8,128]{2,1,0:T(8,128)S(1)}) %tuple.26), branch_computations={%region_0.0_spmd, %region_1.0_spmd} | conditional | flops 24576 | bytes 622784 | solution.py:645
  11.4 1.6 %collective-permute-start.2 = (f32[8,8,128]{2,1,0:T(8,128)S(1)}, f32[8,8,128]{2,1,0:T(8,128)S(1)}, u32[]{:S(2)}, u32[]{:S(2)}) collective-permute-start(f32[8,8,128]{2,1,0:T(8,128)S(1)} %get-tuple-element.13), channel_id=1, source_target_pairs={{0,2},{2,4},{4,6},{6,0},{1,3},{3,5},{5,7},{7,1},{8,10},{10,12},{12... | collective-permute-start | bytes 98312 | tf_op jit(solution)/shard_map/cond/branch_1_fun/ppermute | solution.py:628
  13.0 2.2 %collective-permute-start.4 = (f32[8,8,128]{2,1,0:T(8,128)S(1)}, f32[8,8,128]{2,1,0:T(8,128)S(1)}, u32[]{:S(2)}, u32[]{:S(2)}) collective-permute-start(f32[8,8,128]{2,1,0:T(8,128)S(1)} %get-tuple-element.14), channel_id=1, source_target_pairs={{0,6},{2,0},{4,2},{6,4},{1,7},{3,1},{5,3},{7,5},{8,14},{10,8},{12,... | collective-permute-start | bytes 98312 | tf_op jit(solution)/shard_map/cond/branch_1_fun/ppermute | solution.py:629
  15.3 0.8 %collective-permute-start.3 = (f32[2,8,128]{2,1,0:T(8,128)S(1)}, f32[2,8,128]{2,1,0:T(8,128)S(1)}, u32[]{:S(2)}, u32[]{:S(2)}) collective-permute-start(f32[2,8,128]{2,1,0:T(8,128)S(1)} %get-tuple-element.12), channel_id=1, source_target_pairs={{0,4},{2,6},{4,0},{6,2},{1,5},{3,7},{5,1},{7,3},{8,12},{10,14},{12... | collective-permute-start | bytes 24584 | tf_op jit(solution)/shard_map/cond/branch_1_fun/ppermute | solution.py:631
  16.1 1.4 %collective-permute-done.2 = f32[8,8,128]{2,1,0:T(8,128)S(1)} collective-permute-done((f32[8,8,128]{2,1,0:T(8,128)S(1)}, f32[8,8,128]{2,1,0:T(8,128)S(1)}, u32[]{:S(2)}, u32[]{:S(2)}) %collective-permute-start.2) | collective-permute-done | bytes 32800 | tf_op jit(solution)/shard_map/cond/branch_1_fun/ppermute | solution.py:628
  17.4 0.0 collective-permute-done.4
  17.5 2.4 %collective-permute-done.3 = f32[2,8,128]{2,1,0:T(8,128)S(1)} collective-permute-done((f32[2,8,128]{2,1,0:T(8,128)S(1)}, f32[2,8,128]{2,1,0:T(8,128)S(1)}, u32[]{:S(2)}, u32[]{:S(2)}) %collective-permute-start.3) | collective-permute-done | bytes 8224 | tf_op jit(solution)/shard_map/cond/branch_1_fun/ppermute | solution.py:631
  19.8 0.6 pad_maximum_fusion
  20.4 0.0 collective-permute-start.5
  20.5 1.5 %collective-permute-done.5 = f32[8,8,128]{2,1,0:T(8,128)} collective-permute-done((f32[8,8,128]{2,1,0:T(8,128)}, f32[8,8,128]{2,1,0:T(8,128)}, u32[]{:S(2)}, u32[]{:S(2)}) %collective-permute-start.5) | collective-permute-done | bytes 32800 | tf_op jit(solution)/shard_map/cond/branch_1_fun/ppermute | solution.py:634
  22.0 0.7 %collective-permute-start.7 = (f32[3,16,2048]{2,1,0:T(8,128)}, f32[3,16,2048]{2,1,0:T(8,128)S(1)}, u32[]{:S(2)}, u32[]{:S(2)}) collective-permute-start(f32[3,16,2048]{2,1,0:T(8,128)} %get-tuple-element.54), channel_id=1, source_target_pairs={{8,16},{16,8},{9,17},{17,9},{10,18},{18,10},{11,19},{19,11},{12,20... | collective-permute-start | bytes 1179656 | tf_op jit(solution)/shard_map/ppermute | solution.py:652
  22.7 0.0 collective-permute-done.8
  22.7 4.0 %collective-permute-start.9 = (f32[3,16,2048]{2,1,0:T(8,128)S(1)}, f32[3,16,2048]{2,1,0:T(8,128)S(1)}, u32[]{:S(2)}, u32[]{:S(2)}) collective-permute-start(f32[3,16,2048]{2,1,0:T(8,128)S(1)} %collective-permute-done.8), channel_id=1, source_target_pairs={{24,16},{0,8},{25,17},{1,9},{26,18},{2,10},{27,19},{3,11},{28,20},... | collective-permute-start | bytes 1179656 | tf_op jit(solution)/shard_map/ppermute | solution.py:649
  26.7 0.0 copy-start
  26.7 17.3 %conditional.3 = (f32[8,512]{1,0:T(8,128)}, f32[8,512]{1,0:T(8,128)S(1)}, f32[4,3,2,128]{3,2,1,0:T(2,128)S(1)}, bf16[1024,2048]{1,0:T(8,128)(2,1)}, f32[3,2,16,2048]{3,2,1,0:T(8,128)}) conditional(s32[]{:T(128)} %bitcast, () %tuple.24, (f32[8,8,128]{2,1,0:T(8,128)}, f32[8,8,128]{2,1,0:T(8,128)}, f32[3,16,16,2048]{3,2,1,0:T(8,128)}) %tuple.27), branch_computations={%region_2.0_spmd, %region_3.0_spmd} | conditional | bytes 5025850 | solution.py:645
  26.7 13.6 %sample.1 = (f32[8,512]{1,0:T(8,128)}, f32[8,512]{1,0:T(8,128)}, f32[8,4,128]{2,1,0:T(4,128)}, bf16[1024,2048]{1,0:T(8,128)(2,1)}, f32[3,2,16,2048]{3,2,1,0:T(8,128)}) custom-call(f32[8,8,128]{2,1,0:T(8,128)} %get-tuple-element.15.mine_ref, f32[8,8,128]{2,1,0:T(8,128)} %get-tuple-element.16.twin_ref, f32[3,16,16,2048]{3,2,1,0:T(8,128)} %get-tuple-element.17.vel_in), custom_call_target="tpu_custom_call" | custom-call | tf_op jit(solution)/shard_map/cond/branch_1_fun/sample/pallas_call | solution.py:295
  40.3 0.1 collective-permute-start.1
  40.4 0.5 collective-permute-start
  40.9 1.7 %collective-permute-done.other_ref = f32[8,512]{1,0:T(8,128)S(1)} collective-permute-done((f32[8,512]{1,0:T(8,128)}, f32[8,512]{1,0:T(8,128)S(1)}, u32[]{:S(2)}, u32[]{:S(2)}) %collective-permute-start) | collective-permute-done | bytes 16416 | tf_op jit(solution)/shard_map/cond/branch_1_fun/ppermute | solution.py:638
  42.6 0.6 copy-done.1
  43.2 0.8 %force.1 = (f32[8,512]{1,0:T(8,128)S(1)}, f32[4,3,2,128]{3,2,1,0:T(2,128)S(1)}) custom-call(f32[8,4,128]{2,1,0:T(4,128)} %get-tuple-element.19.mask_ref, f32[8,512]{1,0:T(8,128)} %get-tuple-element.20.part_ref, f32[8,512]{1,0:T(8,128)} %copy-done.1, f32[8,512]{1,0:T(8,128)} %get-tuple-element.77.own_ref), custom_call_target="tpu_custom_call" | custom-call | tf_op jit(solution)/shard_map/cond/branch_1_fun/force/pallas_call | solution.py:345
  44.0 1.9 %collective-permute-start.10 = (f32[3,2,128]{2,1,0:T(2,128)S(1)}, f32[3,2,128]{2,1,0:T(2,128)S(1)}, u32[]{:S(2)}, u32[]{:S(2)}) collective-permute-start(f32[3,2,128]{2,1,0:T(2,128)S(1)} %get-tuple-element.61), channel_id=1, source_target_pairs={{0,6},{2,0},{4,2},{6,4},{1,7},{3,1},{5,3},{7,5},{8,14},{10,8},{12,... | collective-permute-start | bytes 9224 | tf_op jit(solution)/shard_map/ppermute | solution.py:656
  45.9 0.2 collective-permute-start.12
  46.1 0.0 collective-permute-done.7.far_in
  46.1 0.8 %collective-permute-start.11 = (f32[3,2,128]{2,1,0:T(2,128)S(1)}, f32[3,2,128]{2,1,0:T(2,128)S(1)}, u32[]{:S(2)}, u32[]{:S(2)}) collective-permute-start(f32[3,2,128]{2,1,0:T(2,128)S(1)} %get-tuple-element.63), channel_id=1, source_target_pairs={{0,4},{2,6},{4,0},{6,2},{1,5},{3,7},{5,1},{7,3},{8,12},{10,14},{12... | collective-permute-start | bytes 9224 | tf_op jit(solution)/shard_map/ppermute | solution.py:656
  46.9 0.0 collective-permute-done.9.relay_in
  46.9 17.0 %update.1 = (f32[3,16,16,2048]{3,2,1,0:T(8,128)}, f32[3,2,128]{2,1,0:T(2,128)S(1)}) custom-call(f32[8,512]{1,0:T(8,128)} %get-tuple-element.49.own_ref, f32[8,512]{1,0:T(8,128)S(1)} %get-tuple-element.50.force_ref, bf16[256,512]{1,0:T(8,128)(2,1)S(1)} %copy-done, f32[6,8,128]{2,1,0:T(8,128)S(1)} %get-tuple-element.51.left_ref, ...), custom_call_target="tpu_custom_call" | custom-call | flops 8053063680 | bytes 12582912 | tf_op jit(solution)/shard_map/update/pallas_call | solution.py:577
  64.0 0.0 collective-permute-done.11
  64.0 0.6 fusion.3
  (13 shorter events, 0.0 us)
Async XLA Ops:
  0.6 10.7 %copy-start.2 = (s32[2]{0:T(128)S(1)}, s32[2]{0:T(128)}, u32[]{:S(2)}) copy-start(s32[2]{0:T(128)} %turb_in.1) | copy-start | bytes 28
  4.9 17.8 %collective-permute-start.8 = (f32[3,16,2048]{2,1,0:T(8,128)}, f32[3,16,2048]{2,1,0:T(8,128)S(1)}, u32[]{:S(2)}, u32[]{:S(2)}) collective-permute-start(f32[3,16,2048]{2,1,0:T(8,128)} %get-tuple-element.55), channel_id=1, source_target_pairs={{8,24},{16,0},{9,25},{17,1},{10,26},{18,2},{11,27},{19,3},{12,28},... | collective-permute-start | bytes 1179656 | tf_op jit(solution)/shard_map/ppermute | solution.py:625
  6.2 40.7 %collective-permute-start.6 = (f32[3,32,2048]{2,1,0:T(8,128)}, f32[3,32,2048]{2,1,0:T(8,128)S(1)}, u32[]{:S(2)}, u32[]{:S(2)}) collective-permute-start(f32[3,32,2048]{2,1,0:T(8,128)} %get-tuple-element.53), channel_id=1, source_target_pairs={{0,8},{8,0},{16,24},{24,16},{1,9},{9,1},{17,25},{25,17},{2,10},{10... | collective-permute-start | bytes 2359304 | tf_op jit(solution)/shard_map/ppermute | solution.py:622
  11.4 6.0 %collective-permute-start.2 = (f32[8,8,128]{2,1,0:T(8,128)S(1)}, f32[8,8,128]{2,1,0:T(8,128)S(1)}, u32[]{:S(2)}, u32[]{:S(2)}) collective-permute-start(f32[8,8,128]{2,1,0:T(8,128)S(1)} %get-tuple-element.13), channel_id=1, source_target_pairs={{0,2},{2,4},{4,6},{6,0},{1,3},{3,5},{5,7},{7,1},{8,10},{10,12},{12... | collective-permute-start | bytes 98312 | tf_op jit(solution)/shard_map/cond/branch_1_fun/ppermute | solution.py:628
  13.0 4.4 %collective-permute-start.4 = (f32[8,8,128]{2,1,0:T(8,128)S(1)}, f32[8,8,128]{2,1,0:T(8,128)S(1)}, u32[]{:S(2)}, u32[]{:S(2)}) collective-permute-start(f32[8,8,128]{2,1,0:T(8,128)S(1)} %get-tuple-element.14), channel_id=1, source_target_pairs={{0,6},{2,0},{4,2},{6,4},{1,7},{3,1},{5,3},{7,5},{8,14},{10,8},{12,... | collective-permute-start | bytes 98312 | tf_op jit(solution)/shard_map/cond/branch_1_fun/ppermute | solution.py:629
  15.3 4.5 %collective-permute-start.3 = (f32[2,8,128]{2,1,0:T(8,128)S(1)}, f32[2,8,128]{2,1,0:T(8,128)S(1)}, u32[]{:S(2)}, u32[]{:S(2)}) collective-permute-start(f32[2,8,128]{2,1,0:T(8,128)S(1)} %get-tuple-element.12), channel_id=1, source_target_pairs={{0,4},{2,6},{4,0},{6,2},{1,5},{3,7},{5,1},{7,3},{8,12},{10,14},{12... | collective-permute-start | bytes 24584 | tf_op jit(solution)/shard_map/cond/branch_1_fun/ppermute | solution.py:631
  20.4 1.6 %collective-permute-start.5 = (f32[8,8,128]{2,1,0:T(8,128)}, f32[8,8,128]{2,1,0:T(8,128)}, u32[]{:S(2)}, u32[]{:S(2)}) collective-permute-start(f32[8,8,128]{2,1,0:T(8,128)} %pad_maximum_fusion), channel_id=1, source_target_pairs={{0,1},{1,0},{2,3},{3,2},{4,5},{5,4},{6,7},{7,6},{8,9},{9,8},{10,11... | collective-permute-start | bytes 98312 | tf_op jit(solution)/shard_map/cond/branch_1_fun/ppermute | solution.py:634
  22.0 24.1 %collective-permute-start.7 = (f32[3,16,2048]{2,1,0:T(8,128)}, f32[3,16,2048]{2,1,0:T(8,128)S(1)}, u32[]{:S(2)}, u32[]{:S(2)}) collective-permute-start(f32[3,16,2048]{2,1,0:T(8,128)} %get-tuple-element.54), channel_id=1, source_target_pairs={{8,16},{16,8},{9,17},{17,9},{10,18},{18,10},{11,19},{19,11},{12,20... | collective-permute-start | bytes 1179656 | tf_op jit(solution)/shard_map/ppermute | solution.py:652
  22.7 24.2 %collective-permute-start.9 = (f32[3,16,2048]{2,1,0:T(8,128)S(1)}, f32[3,16,2048]{2,1,0:T(8,128)S(1)}, u32[]{:S(2)}, u32[]{:S(2)}) collective-permute-start(f32[3,16,2048]{2,1,0:T(8,128)S(1)} %collective-permute-done.8), channel_id=1, source_target_pairs={{24,16},{0,8},{25,17},{1,9},{26,18},{2,10},{27,19},{3,11},{28,20},... | collective-permute-start | bytes 1179656 | tf_op jit(solution)/shard_map/ppermute | solution.py:649
  26.7 20.3 %copy-start = (bf16[256,512]{1,0:T(8,128)(2,1)S(1)}, bf16[256,512]{1,0:T(8,128)(2,1)}, u32[]{:S(2)}) copy-start(bf16[256,512]{1,0:T(8,128)(2,1)} %constant.9.clone.op_ref) | copy-start | bytes 786436
  40.3 3.7 %collective-permute-start.1 = (f32[3,2,16,2048]{3,2,1,0:T(8,128)}, f32[3,2,16,2048]{3,2,1,0:T(8,128)}, u32[]{:S(2)}, u32[]{:S(2)}) collective-permute-start(f32[3,2,16,2048]{3,2,1,0:T(8,128)} %get-tuple-element.24), channel_id=1, source_target_pairs={{0,1},{1,0},{2,3},{3,2},{4,5},{5,4},{6,7},{7,6},{8,9},{9,8},{10,11... | collective-permute-start | bytes 2359304 | tf_op jit(solution)/shard_map/cond/branch_1_fun/ppermute | solution.py:639
  40.4 2.2 %collective-permute-start = (f32[8,512]{1,0:T(8,128)}, f32[8,512]{1,0:T(8,128)S(1)}, u32[]{:S(2)}, u32[]{:S(2)}) collective-permute-start(f32[8,512]{1,0:T(8,128)} %get-tuple-element.20.part_ref), channel_id=1, source_target_pairs={{0,1},{1,0},{2,3},{3,2},{4,5},{5,4},{6,7},{7,6},{8,9},{9,8},{10,11... | collective-permute-start | bytes 49160 | tf_op jit(solution)/shard_map/cond/branch_1_fun/ppermute | solution.py:638
  42.6 0.6 copy-start.1
  44.0 19.9 %collective-permute-start.10 = (f32[3,2,128]{2,1,0:T(2,128)S(1)}, f32[3,2,128]{2,1,0:T(2,128)S(1)}, u32[]{:S(2)}, u32[]{:S(2)}) collective-permute-start(f32[3,2,128]{2,1,0:T(2,128)S(1)} %get-tuple-element.61), channel_id=1, source_target_pairs={{0,6},{2,0},{4,2},{6,4},{1,7},{3,1},{5,3},{7,5},{8,14},{10,8},{12,... | collective-permute-start | bytes 9224 | tf_op jit(solution)/shard_map/ppermute | solution.py:656
  45.9 18.1 %collective-permute-start.12 = (f32[3,2,128]{2,1,0:T(2,128)S(1)}, f32[3,2,128]{2,1,0:T(2,128)S(1)}, u32[]{:S(2)}, u32[]{:S(2)}) collective-permute-start(f32[3,2,128]{2,1,0:T(2,128)S(1)} %get-tuple-element.62), channel_id=1, source_target_pairs={{0,2},{2,4},{4,6},{6,0},{1,3},{3,5},{5,7},{7,1},{8,10},{10,12},{12... | collective-permute-start | bytes 9224 | tf_op jit(solution)/shard_map/ppermute | solution.py:656
  46.1 17.8 %collective-permute-start.11 = (f32[3,2,128]{2,1,0:T(2,128)S(1)}, f32[3,2,128]{2,1,0:T(2,128)S(1)}, u32[]{:S(2)}, u32[]{:S(2)}) collective-permute-start(f32[3,2,128]{2,1,0:T(2,128)S(1)} %get-tuple-element.63), channel_id=1, source_target_pairs={{0,4},{2,6},{4,0},{6,2},{1,5},{3,7},{5,1},{7,3},{8,12},{10,14},{12... | collective-permute-start | bytes 9224 | tf_op jit(solution)/shard_map/ppermute | solution.py:656

commit v11 on v10

--- a/solution.py
+++ b/solution.py
@@ -174,7 +174,7 @@
 
 def sample_kernel(
     per_turbine, mine_ref, twin_ref, vel_in, part_ref, own_ref, mask_ref, weight_out, lev_ref,
-    even_ref, odd_ref, center_ref, plane_ref, acc_ref, vel_ref, weight_ref, sems, out_sems, lev_sem,
+    bell_ref, center_ref, plane_ref, acc_ref, vel_ref, weight_ref, sems, out_sem, lev_sem,
 ):
     components, depth, rows, cols = vel_ref.shape
     points = mine_ref.shape[2]
@@ -183,50 +183,43 @@
     chunks = cols // STEP
     core = lax.axis_index("gz")
     start = lax.axis_index("gy") * cols
-
-    def column(at):
-        return pl.ds(pl.multiple_of(at * STEP, STEP), STEP)
-
-    def column_copy(at):
-        return pltpu.make_async_copy(
-            vel_in.at[:, :, :, column(at)], vel_ref.at[:, :, :, column(at)], sems.at[at]
-        )
-
-    def weight_copy(at):
-        return pltpu.make_async_copy(
-            weight_ref.at[:, column(at)], weight_out.at[:, column(at)], out_sems.at[at]
-        )
-
+    arrivals = [
+        pltpu.make_async_copy(vel_in.at[i], vel_ref.at[i], sems.at[i]) for i in range(components)
+    ]
+    weight_copy = pltpu.make_async_copy(weight_ref, weight_out, out_sem)
     lev_copy = pltpu.make_async_copy(
         vel_in.at[:, pl.ds(jnp.where(core == 0, depth - 2, 0), 2)], lev_ref, lev_sem
     )
 
+    def column(at):
+        return pl.ds(pl.multiple_of(at * STEP, STEP), STEP)
+
     def bell(cell, center):
         gap = cell.astype(F32) - center
         return jnp.exp(gap * gap * (-1.0 / (smear * smear)))
 
-    def weights(at, ref):
+    def weights(at):
         lane = lax.broadcasted_iota(jnp.int32, (1, 128), 1)
+        keep = bell_ref.at[:, column(at)]
+        out = weight_ref.at[:, column(at)]
         for part in range(STEP // 128):
             cell = start + at * STEP + part * 128 + lane
-            ref[:, part * 128 : part * 128 + 128] = bell(cell, center_ref[...])
-
-    def multiply(at, ref):
-        vel = vel_ref.at[:, :, :, column(at)]
-        out = weight_ref.at[:, column(at)]
-        for i in range(components):
-            high, low = split(vel[i].reshape(cells, STEP))
-            field = dot(plane_ref[...], jnp.concatenate([high, high, low], axis=0))
-            product = field * ref[...]
-            total = acc_ref[i]
-            for part in range(STEP // 128):
-                total += product[:, part * 128 : part * 128 + 128]
-            acc_ref[i] = total
-        high, low = split(ref[...])
-        out[:count, :] = high
-        out[count:, :] = low
-
-    column_copy(0).start()
+            value = bell(cell, center_ref[...])
+            high, low = split(value)
+            keep[:, part * 128 : part * 128 + 128] = value
+            out[:count, part * 128 : part * 128 + 128] = high
+            out[count:, part * 128 : part * 128 + 128] = low
+
+    def multiply(i, at):
+        high, low = split(vel_ref.at[i, :, :, column(at)][...].reshape(cells, STEP))
+        field = dot(plane_ref[...], jnp.concatenate([high, high, low], axis=0))
+        product = field * bell_ref[:, column(at)]
+        total = acc_ref[i]
+        for part in range(STEP // 128):
+            total += product[:, part * 128 : part * 128 + 128]
+        acc_ref[i] = total
+
+    arrivals[0].start()
     masks = match(mine_ref, twin_ref, per_turbine)
     blocks = mine_ref.shape[0]
     lane = lax.broadcasted_iota(jnp.int32, (1, cells), 1)
@@ -250,30 +243,28 @@
         for k in range(per_turbine):
             mask_ref[at, k : k + 1, :] = masks[at][k].astype(F32)
     acc_ref[...] = jnp.zeros(acc_ref.shape, F32)
-    weights(0, even_ref)
-
-    def pair(step, carry):
-        column_copy(2 * step + 1).start()
-        column_copy(2 * step).wait()
-        weights(2 * step + 1, odd_ref)
-        multiply(2 * step, even_ref)
-        weight_copy(2 * step).start()
-
-        @pl.when(step < chunks // 2 - 1)
-        def _():
-            column_copy(2 * step + 2).start()
-
-        @pl.when(step == 1)
-        def _():
-            lev_copy.start()
-
-        column_copy(2 * step + 1).wait()
-        weights(2 * step + 2, even_ref)
-        multiply(2 * step + 1, odd_ref)
-        weight_copy(2 * step + 1).start()
+    weights(0)
+    arrivals[0].wait()
+    for copy in arrivals[1:] + [lev_copy]:
+        copy.start()
+
+    def first(at, carry):
+        weights(at + 1)
+        multiply(0, at)
         return carry
 
-    lax.fori_loop(0, chunks // 2, pair, 0)
+    lax.fori_loop(0, chunks - 1, first, 0)
+    multiply(0, chunks - 1)
+    weight_copy.start()
+    for copy in arrivals[1:]:
+        copy.wait()
+
+    def others(at, carry):
+        for i in range(1, components):
+            multiply(i, at)
+        return carry
+
+    lax.fori_loop(0, chunks, others, 0)
     for i in range(components):
         for k in range(per_turbine):
             band = slice(k * points, (k + 1) * points)
@@ -281,15 +272,13 @@
             part_ref[i : i + 1, band] = smear_norm * total
     part_ref[components:, :] = jnp.zeros((8 - components, count), F32)
     lev_copy.wait()
-    for at in range(chunks):
-        weight_copy(at).wait()
+    weight_copy.wait()
 
 
 def sample(mine, twin, velocity, per_turbine):
     components, depth, rows, cols = velocity.shape
     points = mine.shape[2]
     count = per_turbine * points
-    chunks = cols // STEP
     vmem = pl.BlockSpec(memory_space=pltpu.VMEM)
     hbm = pl.BlockSpec(memory_space=pltpu.HBM)
     return pl.pallas_call(
@@ -304,15 +293,14 @@
             jax.ShapeDtypeStruct((components, 2, rows, cols), F32),
         ],
         scratch_shapes=[
-            pltpu.VMEM((count, STEP), F32),
-            pltpu.VMEM((count, STEP), F32),
+            pltpu.VMEM((count, cols), F32),
             pltpu.VMEM((count, 128), F32),
             pltpu.VMEM((count, 3 * depth * rows), BF16),
             pltpu.VMEM((components, count, 128), F32),
             pltpu.VMEM(velocity.shape, F32),
             pltpu.VMEM((2 * count, cols), BF16),
-            pltpu.SemaphoreType.DMA((chunks,)),
-            pltpu.SemaphoreType.DMA((chunks,)),
+            pltpu.SemaphoreType.DMA((components,)),
+            pltpu.SemaphoreType.DMA,
             pltpu.SemaphoreType.DMA,
         ],
         compiler_params=pltpu.CompilerParams(vmem_limit_bytes=58 * MIB),
@@ -359,7 +347,7 @@
 def update_kernel(
     own_ref, force_ref, op_ref, left_ref, right_ref, near_in, far_in, relay_in, weight_in, vel_in, lev_in,
     new_out, zero_ref, pad_ref, new_ref, side_ref, weight_ref, high_ref, low_ref, even, odd,
-    vel_sems, side_sems, weight_sems, new_sems, lev_sem,
+    vel_sems, side_sems, weight_sem, new_sems, lev_sem,
 ):
     components, depth, rows, cols = new_ref.shape
     chunks = cols // STEP
@@ -376,30 +364,18 @@
     def column(at, first=0):
         return pl.ds(pl.multiple_of(at * STEP + first, 128), STEP)
 
-    def arrivals(at):
-        return [
-            pltpu.make_async_copy(
-                vel_in.at[:, :, :, column(at)],
-                pad_ref.at[:, pl.ds(2, depth), :, column(at, 128)],
-                vel_sems.at[at],
-            ),
-            pltpu.make_async_copy(
-                weight_in.at[:, column(at)], weight_ref.at[:, column(at)], weight_sems.at[at]
-            ),
-            pltpu.make_async_copy(
-                near_in.at[:, :, column(at)], side_ref.at[1 - parity, :, :, column(at)], side_sems.at[0, at]
-            ),
-            pltpu.make_async_copy(
-                far_in.at[:, :, column(at)],
-                side_ref.at[parity, :, pl.ds(0, depth), column(at)],
-                side_sems.at[1, at],
-            ),
-            pltpu.make_async_copy(
-                relay_in.at[:, :, column(at)],
-                side_ref.at[parity, :, pl.ds(depth, depth), column(at)],
-                side_sems.at[2, at],
-            ),
-        ]
+    copies = [
+        pltpu.make_async_copy(
+            vel_in.at[i], pad_ref.at[i, pl.ds(2, depth), :, pl.ds(128, cols)], vel_sems.at[i]
+        )
+        for i in range(components)
+    ]
+    copies += [
+        pltpu.make_async_copy(near_in, side_ref.at[1 - parity], side_sems.at[0]),
+        pltpu.make_async_copy(far_in, side_ref.at[parity, :, pl.ds(0, depth)], side_sems.at[1]),
+        pltpu.make_async_copy(relay_in, side_ref.at[parity, :, pl.ds(depth, depth)], side_sems.at[2]),
+    ]
+    weight_copy = pltpu.make_async_copy(weight_in, weight_ref, weight_sem)
 
     def departure(at):
         return pltpu.make_async_copy(
@@ -421,10 +397,13 @@
                 pad_ref[tile // parts, level + 2, :, lane : lane + 8] = turned[k * rows : (k + 1) * rows, :]
 
     def matrix_part(at, bufs):
-        grad_ref, lap_ref, body_ref = bufs
+        stencil_part(at, bufs)
+        body_part(at, bufs)
+
+    def stencil_part(at, bufs):
+        grad_ref, lap_ref, _ = bufs
         pad = pad_ref.at[:, :, :, column(at, 128)]
         sides = side_ref.at[:, :, :, column(at)]
-        weight = weight_ref.at[:, column(at)]
         for i in range(components):
             for half in range(depth // LEVELS):
                 levels = slice(half * LEVELS, (half + 1) * LEVELS)
@@ -439,6 +418,10 @@
                 result = dot(op_ref[...], jnp.concatenate(high + low, axis=0))
                 grad_ref[i, levels] = result[:cells].reshape(LEVELS, rows, STEP)
                 lap_ref[i, levels] = result[cells:].reshape(LEVELS, rows, STEP)
+
+    def body_part(at, bufs):
+        body_ref = bufs[2]
+        weight = weight_ref.at[:, column(at)]
         upper = weight[:count]
         lower = weight[count:]
         wide = jnp.concatenate([high_ref[...], low_ref[...], high_ref[...]], axis=1)
@@ -507,7 +490,7 @@
                 work(level, slice(row, row + 8))
         departure(at).start()
 
-    for copy in arrivals(0):
+    for copy in copies:
         copy.start()
     zero_ref[...] = jnp.zeros(zero_ref.shape, F32)
 
@@ -533,23 +516,14 @@
             high_ref[band, :] = high
             low_ref[band, :] = low
     level_copy(0).wait()
-    for copy in arrivals(0):
+    for copy in copies:
         copy.wait()
-    for copy in arrivals(1) + arrivals(2):
-        copy.start()
-    matrix_part(0, even)
+    weight_copy.start()
+    stencil_part(0, even)
+    weight_copy.wait()
+    body_part(0, even)
 
     def pair(step, carry):
-        for copy in arrivals(2 * step + 1) + arrivals(2 * step + 2):
-            copy.wait()
-        for copy in arrivals(2 * step + 3):
-            copy.start()
-
-        @pl.when(step < chunks // 2 - 2)
-        def _():
-            for copy in arrivals(2 * step + 4):
-                copy.start()
-
         matrix_part(2 * step + 1, odd)
         vector_part(2 * step, even)
         matrix_part(2 * step + 2, even)
@@ -557,8 +531,6 @@
         return carry
 
     lax.fori_loop(0, chunks // 2 - 1, pair, 0)
-    for copy in arrivals(chunks - 1):
-        copy.wait()
     matrix_part(chunks - 1, odd)
     vector_part(chunks - 2, even)
     vector_part(chunks - 1, odd)
@@ -591,9 +563,9 @@
             pltpu.VMEM((components * depth * rows, count), BF16),
             fields,
             fields,
-            pltpu.SemaphoreType.DMA((chunks,)),
-            pltpu.SemaphoreType.DMA((3, chunks)),
-            pltpu.SemaphoreType.DMA((chunks,)),
+            pltpu.SemaphoreType.DMA((components,)),
+            pltpu.SemaphoreType.DMA((3,)),
+            pltpu.SemaphoreType.DMA,
             pltpu.SemaphoreType.DMA((chunks,)),
             pltpu.SemaphoreType.DMA,
         ],

time: 65.4 us -> 67.4 us (1.031)
  Pallas kernels: 35.7 us -> 37.7 us
    pallas_call x1, Pallas kernels: 17 us -> 19.2 us  [update(): pl.pallas_call(update_kernel, in_specs=[vmem] * 5 + [hbm] * 6, out_specs=...]
  transfers between devices with their start and end apart: 13 -> 13, of which waited for: 4 -> 4; matrix products, arithmetic and copies ran while one was open for 1% -> 1% of each run, Pallas kernels for 49% -> 50%
where the time goes in v11:
time: 67.4 us; the launch traced here: 66.6 us
  Pallas kernels  37.7 us (56%)
  starting transfers between devices  19.2 us (28%)
  waiting for transfers between devices  7.02 us (10%)
  other arithmetic  1.19 us (2%)
  between operations  0.79 us (1%)
    pallas_call x1, Pallas kernels, update(): pl.pallas_call(update_kernel, in_specs=[vmem] * 5 + [hbm] * 6, out_specs=...  19.2 us
    pallas_call x1, Pallas kernels, sample(): pl.pallas_call(functools.partial(sample_kernel, per_turbine), in_specs=[v...  13.4 us
    ppermute x1, starting transfers between devices, local(): near = lax.ppermute(near, 'gx', [(i, i ^ 1) for i in range(gx)])  5.16 us
    pallas_call x1, Pallas kernels, prep(): pl.pallas_call(prep_kernel, in_specs=[pl.BlockSpec(memory_space=pltpu.HBM...  4.24 us
    ppermute x1, starting transfers between devices, local(): relay = lax.ppermute(relay, 'gx', [(3, 2), (0, 1)])  3.98 us
    ppermute x3, starting transfers between devices, local(): result += lax.ppermute(home[shift], 'gy', around(gy - shift))  2.88 us
    ppermute x1, waiting for transfers between devices, gather(): lax.ppermute(blocks, 'gy', around(shift))  2.39 us
    ppermute x1, starting transfers between devices, gather(): right = lax.ppermute(down, 'gy', around(gy - 1))  2.25 us
  transfers between devices with their start and end apart: 13, of which 4 were waited for; matrix products, arithmetic and copies ran while one was open for 1% of the time, Pallas kernels for 50%

profile of v11, /device:TPU:0, one launch (start us, length us, event | category | flops | bytes accessed | tf_op | source)
XLA Modules:
  0.0 66.6 jit_solution(1636586955403584907)
XLA Ops:
  0.6 4.2 %prep.1 = (f32[2,8,128]{2,1,0:T(8,128)S(1)}, f32[8,8,128]{2,1,0:T(8,128)S(1)}, f32[8,8,128]{2,1,0:T(8,128)S(1)}, f32[3,32,2048]{2,1,0:T(8,128)}, f32[3,16,2048]{2,1,0:T(8,128)}, /*index=5*/f32[3,16,2048]{2,1,0:T(8,128)}) custom-call(s32[2]{0:T(128)} %turb_in.1, f32[3,2,128]{2,1,0:T(2,128)} %bitcast.22, f32[3,2,128]{2,1,0:T(2,128)} %bitcast.23, ...), custom_call_target="tpu_custom_call" | custom-call | tf_op jit(solution)/shard_map/prep/pallas_call | solution.py:128
  4.9 1.3 %collective-permute-start.8 = (f32[3,16,2048]{2,1,0:T(8,128)}, f32[3,16,2048]{2,1,0:T(8,128)S(1)}, u32[]{:S(2)}, u32[]{:S(2)}) collective-permute-start(f32[3,16,2048]{2,1,0:T(8,128)} %get-tuple-element.55), channel_id=1, source_target_pairs={{8,24},{16,0},{9,25},{17,1},{10,26},{18,2},{11,27},{19,3},{12,28},... | collective-permute-start | bytes 1179656 | tf_op jit(solution)/shard_map/ppermute | solution.py:597
  6.2 5.2 %collective-permute-start.6 = (f32[3,32,2048]{2,1,0:T(8,128)}, f32[3,32,2048]{2,1,0:T(8,128)S(1)}, u32[]{:S(2)}, u32[]{:S(2)}) collective-permute-start(f32[3,32,2048]{2,1,0:T(8,128)} %get-tuple-element.53), channel_id=1, source_target_pairs={{0,8},{8,0},{16,24},{24,16},{1,9},{9,1},{17,25},{25,17},{2,10},{10... | collective-permute-start | bytes 2359304 | tf_op jit(solution)/shard_map/ppermute | solution.py:594
  11.4 10.6 %conditional.2 = (f32[8,8,128]{2,1,0:T(8,128)}, f32[8,8,128]{2,1,0:T(8,128)}, f32[6,8,128]{2,1,0:T(8,128)S(1)}, f32[6,8,128]{2,1,0:T(8,128)S(1)}) conditional(s32[]{:T(128)} %bitcast, () %tuple.25, (f32[8,8,128]{2,1,0:T(8,128)S(1)}, f32[2,8,128]{2,1,0:T(8,128)S(1)}, f32[8,8,128]{2,1,0:T(8,128)S(1)}) %tuple.26), branch_computations={%region_0.0_spmd, %region_1.0_spmd} | conditional | flops 24576 | bytes 622784 | solution.py:617
  11.4 1.6 %collective-permute-start.2 = (f32[8,8,128]{2,1,0:T(8,128)S(1)}, f32[8,8,128]{2,1,0:T(8,128)S(1)}, u32[]{:S(2)}, u32[]{:S(2)}) collective-permute-start(f32[8,8,128]{2,1,0:T(8,128)S(1)} %get-tuple-element.13), channel_id=1, source_target_pairs={{0,2},{2,4},{4,6},{6,0},{1,3},{3,5},{5,7},{7,1},{8,10},{10,12},{12... | collective-permute-start | bytes 98312 | tf_op jit(solution)/shard_map/cond/branch_1_fun/ppermute | solution.py:600
  13.0 2.2 %collective-permute-start.4 = (f32[8,8,128]{2,1,0:T(8,128)S(1)}, f32[8,8,128]{2,1,0:T(8,128)S(1)}, u32[]{:S(2)}, u32[]{:S(2)}) collective-permute-start(f32[8,8,128]{2,1,0:T(8,128)S(1)} %get-tuple-element.14), channel_id=1, source_target_pairs={{0,6},{2,0},{4,2},{6,4},{1,7},{3,1},{5,3},{7,5},{8,14},{10,8},{12,... | collective-permute-start | bytes 98312 | tf_op jit(solution)/shard_map/cond/branch_1_fun/ppermute | solution.py:601
  15.3 0.8 %collective-permute-start.3 = (f32[2,8,128]{2,1,0:T(8,128)S(1)}, f32[2,8,128]{2,1,0:T(8,128)S(1)}, u32[]{:S(2)}, u32[]{:S(2)}) collective-permute-start(f32[2,8,128]{2,1,0:T(8,128)S(1)} %get-tuple-element.12), channel_id=1, source_target_pairs={{0,4},{2,6},{4,0},{6,2},{1,5},{3,7},{5,1},{7,3},{8,12},{10,14},{12... | collective-permute-start | bytes 24584 | tf_op jit(solution)/shard_map/cond/branch_1_fun/ppermute | solution.py:603
  16.1 1.4 %collective-permute-done.2 = f32[8,8,128]{2,1,0:T(8,128)S(1)} collective-permute-done((f32[8,8,128]{2,1,0:T(8,128)S(1)}, f32[8,8,128]{2,1,0:T(8,128)S(1)}, u32[]{:S(2)}, u32[]{:S(2)}) %collective-permute-start.2) | collective-permute-done | bytes 32800 | tf_op jit(solution)/shard_map/cond/branch_1_fun/ppermute | solution.py:600
  17.4 0.0 collective-permute-done.4
  17.5 2.4 %collective-permute-done.3 = f32[2,8,128]{2,1,0:T(8,128)S(1)} collective-permute-done((f32[2,8,128]{2,1,0:T(8,128)S(1)}, f32[2,8,128]{2,1,0:T(8,128)S(1)}, u32[]{:S(2)}, u32[]{:S(2)}) %collective-permute-start.3) | collective-permute-done | bytes 8224 | tf_op jit(solution)/shard_map/cond/branch_1_fun/ppermute | solution.py:603
  19.8 0.6 pad_maximum_fusion
  20.4 0.0 collective-permute-start.5
  20.5 1.5 %collective-permute-done.5 = f32[8,8,128]{2,1,0:T(8,128)} collective-permute-done((f32[8,8,128]{2,1,0:T(8,128)}, f32[8,8,128]{2,1,0:T(8,128)}, u32[]{:S(2)}, u32[]{:S(2)}) %collective-permute-start.5) | collective-permute-done | bytes 32800 | tf_op jit(solution)/shard_map/cond/branch_1_fun/ppermute | solution.py:606
  22.0 0.7 %collective-permute-start.7 = (f32[3,16,2048]{2,1,0:T(8,128)}, f32[3,16,2048]{2,1,0:T(8,128)S(1)}, u32[]{:S(2)}, u32[]{:S(2)}) collective-permute-start(f32[3,16,2048]{2,1,0:T(8,128)} %get-tuple-element.54), channel_id=1, source_target_pairs={{8,16},{16,8},{9,17},{17,9},{10,18},{18,10},{11,19},{19,11},{12,20... | collective-permute-start | bytes 1179656 | tf_op jit(solution)/shard_map/ppermute | solution.py:624
  22.7 4.0 %collective-permute-start.9 = (f32[3,16,2048]{2,1,0:T(8,128)S(1)}, f32[3,16,2048]{2,1,0:T(8,128)S(1)}, u32[]{:S(2)}, u32[]{:S(2)}) collective-permute-start(f32[3,16,2048]{2,1,0:T(8,128)S(1)} %collective-permute-done.8), channel_id=1, source_target_pairs={{24,16},{0,8},{25,17},{1,9},{26,18},{2,10},{27,19},{3,11},{28,20},... | collective-permute-start | bytes 1179656 | tf_op jit(solution)/shard_map/ppermute | solution.py:621
  26.7 0.0 copy-start
  26.7 17.1 %conditional.3 = (f32[8,512]{1,0:T(8,128)}, f32[8,512]{1,0:T(8,128)S(1)}, f32[4,3,2,128]{3,2,1,0:T(2,128)S(1)}, bf16[1024,2048]{1,0:T(8,128)(2,1)}, f32[3,2,16,2048]{3,2,1,0:T(8,128)}) conditional(s32[]{:T(128)} %bitcast, () %tuple.24, (f32[8,8,128]{2,1,0:T(8,128)}, f32[8,8,128]{2,1,0:T(8,128)}, f32[3,16,16,2048]{3,2,1,0:T(8,128)}) %tuple.27), branch_computations={%region_2.0_spmd, %region_3.0_spmd} | conditional | bytes 5025850 | solution.py:617
  26.7 13.4 %sample.1 = (f32[8,512]{1,0:T(8,128)}, f32[8,512]{1,0:T(8,128)}, f32[8,4,128]{2,1,0:T(4,128)}, bf16[1024,2048]{1,0:T(8,128)(2,1)}, f32[3,2,16,2048]{3,2,1,0:T(8,128)}) custom-call(f32[8,8,128]{2,1,0:T(8,128)} %get-tuple-element.15.mine_ref, f32[8,8,128]{2,1,0:T(8,128)} %get-tuple-element.16.twin_ref, f32[3,16,16,2048]{3,2,1,0:T(8,128)} %get-tuple-element.17.vel_in), custom_call_target="tpu_custom_call" | custom-call | tf_op jit(solution)/shard_map/cond/branch_1_fun/sample/pallas_call | solution.py:284
  40.1 0.1 collective-permute-start.1
  40.2 0.5 collective-permute-start
  40.7 1.7 %collective-permute-done.other_ref = f32[8,512]{1,0:T(8,128)S(1)} collective-permute-done((f32[8,512]{1,0:T(8,128)}, f32[8,512]{1,0:T(8,128)S(1)}, u32[]{:S(2)}, u32[]{:S(2)}) %collective-permute-start) | collective-permute-done | bytes 16416 | tf_op jit(solution)/shard_map/cond/branch_1_fun/ppermute | solution.py:610
  42.4 0.6 copy-done.1
  43.0 0.8 %force.1 = (f32[8,512]{1,0:T(8,128)S(1)}, f32[4,3,2,128]{3,2,1,0:T(2,128)S(1)}) custom-call(f32[8,4,128]{2,1,0:T(4,128)} %get-tuple-element.19.mask_ref, f32[8,512]{1,0:T(8,128)} %get-tuple-element.20.part_ref, f32[8,512]{1,0:T(8,128)} %copy-done.1, f32[8,512]{1,0:T(8,128)} %get-tuple-element.77.own_ref), custom_call_target="tpu_custom_call" | custom-call | tf_op jit(solution)/shard_map/cond/branch_1_fun/force/pallas_call | solution.py:333
  43.8 0.0 collective-permute-done.1
  43.8 1.9 %collective-permute-start.10 = (f32[3,2,128]{2,1,0:T(2,128)S(1)}, f32[3,2,128]{2,1,0:T(2,128)S(1)}, u32[]{:S(2)}, u32[]{:S(2)}) collective-permute-start(f32[3,2,128]{2,1,0:T(2,128)S(1)} %get-tuple-element.61), channel_id=1, source_target_pairs={{0,6},{2,0},{4,2},{6,4},{1,7},{3,1},{5,3},{7,5},{8,14},{10,8},{12,... | collective-permute-start | bytes 9224 | tf_op jit(solution)/shard_map/ppermute | solution.py:628
  45.7 0.2 collective-permute-start.12
  45.9 0.0 collective-permute-done.7.far_in
  45.9 0.8 %collective-permute-start.11 = (f32[3,2,128]{2,1,0:T(2,128)S(1)}, f32[3,2,128]{2,1,0:T(2,128)S(1)}, u32[]{:S(2)}, u32[]{:S(2)}) collective-permute-start(f32[3,2,128]{2,1,0:T(2,128)S(1)} %get-tuple-element.63), channel_id=1, source_target_pairs={{0,4},{2,6},{4,0},{6,2},{1,5},{3,7},{5,1},{7,3},{8,12},{10,14},{12... | collective-permute-start | bytes 9224 | tf_op jit(solution)/shard_map/ppermute | solution.py:628
  46.7 0.0 collective-permute-done.9.relay_in
  46.7 19.2 %update.1 = (f32[3,16,16,2048]{3,2,1,0:T(8,128)}, f32[3,2,128]{2,1,0:T(2,128)S(1)}) custom-call(f32[8,512]{1,0:T(8,128)} %get-tuple-element.49.own_ref, f32[8,512]{1,0:T(8,128)S(1)} %get-tuple-element.50.force_ref, bf16[256,512]{1,0:T(8,128)(2,1)S(1)} %copy-done, f32[6,8,128]{2,1,0:T(8,128)S(1)} %get-tuple-element.51.left_ref, ...), custom_call_target="tpu_custom_call" | custom-call | flops 8053063680 | bytes 12582912 | tf_op jit(solution)/shard_map/update/pallas_call | solution.py:549
  66.0 0.0 collective-permute-done.12
  66.0 0.6 fusion.3
  (13 shorter events, 0.0 us)
Async XLA Ops:
  0.6 10.7 %copy-start.2 = (s32[2]{0:T(128)S(1)}, s32[2]{0:T(128)}, u32[]{:S(2)}) copy-start(s32[2]{0:T(128)} %turb_in.1) | copy-start | bytes 28
  4.9 17.8 %collective-permute-start.8 = (f32[3,16,2048]{2,1,0:T(8,128)}, f32[3,16,2048]{2,1,0:T(8,128)S(1)}, u32[]{:S(2)}, u32[]{:S(2)}) collective-permute-start(f32[3,16,2048]{2,1,0:T(8,128)} %get-tuple-element.55), channel_id=1, source_target_pairs={{8,24},{16,0},{9,25},{17,1},{10,26},{18,2},{11,27},{19,3},{12,28},... | collective-permute-start | bytes 1179656 | tf_op jit(solution)/shard_map/ppermute | solution.py:597
  6.2 40.5 %collective-permute-start.6 = (f32[3,32,2048]{2,1,0:T(8,128)}, f32[3,32,2048]{2,1,0:T(8,128)S(1)}, u32[]{:S(2)}, u32[]{:S(2)}) collective-permute-start(f32[3,32,2048]{2,1,0:T(8,128)} %get-tuple-element.53), channel_id=1, source_target_pairs={{0,8},{8,0},{16,24},{24,16},{1,9},{9,1},{17,25},{25,17},{2,10},{10... | collective-permute-start | bytes 2359304 | tf_op jit(solution)/shard_map/ppermute | solution.py:594
  11.4 6.0 %collective-permute-start.2 = (f32[8,8,128]{2,1,0:T(8,128)S(1)}, f32[8,8,128]{2,1,0:T(8,128)S(1)}, u32[]{:S(2)}, u32[]{:S(2)}) collective-permute-start(f32[8,8,128]{2,1,0:T(8,128)S(1)} %get-tuple-element.13), channel_id=1, source_target_pairs={{0,2},{2,4},{4,6},{6,0},{1,3},{3,5},{5,7},{7,1},{8,10},{10,12},{12... | collective-permute-start | bytes 98312 | tf_op jit(solution)/shard_map/cond/branch_1_fun/ppermute | solution.py:600
  13.0 4.4 %collective-permute-start.4 = (f32[8,8,128]{2,1,0:T(8,128)S(1)}, f32[8,8,128]{2,1,0:T(8,128)S(1)}, u32[]{:S(2)}, u32[]{:S(2)}) collective-permute-start(f32[8,8,128]{2,1,0:T(8,128)S(1)} %get-tuple-element.14), channel_id=1, source_target_pairs={{0,6},{2,0},{4,2},{6,4},{1,7},{3,1},{5,3},{7,5},{8,14},{10,8},{12,... | collective-permute-start | bytes 98312 | tf_op jit(solution)/shard_map/cond/branch_1_fun/ppermute | solution.py:601
  15.3 4.5 %collective-permute-start.3 = (f32[2,8,128]{2,1,0:T(8,128)S(1)}, f32[2,8,128]{2,1,0:T(8,128)S(1)}, u32[]{:S(2)}, u32[]{:S(2)}) collective-permute-start(f32[2,8,128]{2,1,0:T(8,128)S(1)} %get-tuple-element.12), channel_id=1, source_target_pairs={{0,4},{2,6},{4,0},{6,2},{1,5},{3,7},{5,1},{7,3},{8,12},{10,14},{12... | collective-permute-start | bytes 24584 | tf_op jit(solution)/shard_map/cond/branch_1_fun/ppermute | solution.py:603
  20.4 1.6 %collective-permute-start.5 = (f32[8,8,128]{2,1,0:T(8,128)}, f32[8,8,128]{2,1,0:T(8,128)}, u32[]{:S(2)}, u32[]{:S(2)}) collective-permute-start(f32[8,8,128]{2,1,0:T(8,128)} %pad_maximum_fusion), channel_id=1, source_target_pairs={{0,1},{1,0},{2,3},{3,2},{4,5},{5,4},{6,7},{7,6},{8,9},{9,8},{10,11... | collective-permute-start | bytes 98312 | tf_op jit(solution)/shard_map/cond/branch_1_fun/ppermute | solution.py:606
  22.0 23.9 %collective-permute-start.7 = (f32[3,16,2048]{2,1,0:T(8,128)}, f32[3,16,2048]{2,1,0:T(8,128)S(1)}, u32[]{:S(2)}, u32[]{:S(2)}) collective-permute-start(f32[3,16,2048]{2,1,0:T(8,128)} %get-tuple-element.54), channel_id=1, source_target_pairs={{8,16},{16,8},{9,17},{17,9},{10,18},{18,10},{11,19},{19,11},{12,20... | collective-permute-start | bytes 1179656 | tf_op jit(solution)/shard_map/ppermute | solution.py:624
  22.7 24.0 %collective-permute-start.9 = (f32[3,16,2048]{2,1,0:T(8,128)S(1)}, f32[3,16,2048]{2,1,0:T(8,128)S(1)}, u32[]{:S(2)}, u32[]{:S(2)}) collective-permute-start(f32[3,16,2048]{2,1,0:T(8,128)S(1)} %collective-permute-done.8), channel_id=1, source_target_pairs={{24,16},{0,8},{25,17},{1,9},{26,18},{2,10},{27,19},{3,11},{28,20},... | collective-permute-start | bytes 1179656 | tf_op jit(solution)/shard_map/ppermute | solution.py:621
  26.7 20.1 %copy-start = (bf16[256,512]{1,0:T(8,128)(2,1)S(1)}, bf16[256,512]{1,0:T(8,128)(2,1)}, u32[]{:S(2)}) copy-start(bf16[256,512]{1,0:T(8,128)(2,1)} %constant.9.clone.op_ref) | copy-start | bytes 786436
  40.1 3.7 %collective-permute-start.1 = (f32[3,2,16,2048]{3,2,1,0:T(8,128)}, f32[3,2,16,2048]{3,2,1,0:T(8,128)}, u32[]{:S(2)}, u32[]{:S(2)}) collective-permute-start(f32[3,2,16,2048]{3,2,1,0:T(8,128)} %get-tuple-element.24), channel_id=1, source_target_pairs={{0,1},{1,0},{2,3},{3,2},{4,5},{5,4},{6,7},{7,6},{8,9},{9,8},{10,11... | collective-permute-start | bytes 2359304 | tf_op jit(solution)/shard_map/cond/branch_1_fun/ppermute | solution.py:611
  40.2 2.2 %collective-permute-start = (f32[8,512]{1,0:T(8,128)}, f32[8,512]{1,0:T(8,128)S(1)}, u32[]{:S(2)}, u32[]{:S(2)}) collective-permute-start(f32[8,512]{1,0:T(8,128)} %get-tuple-element.20.part_ref), channel_id=1, source_target_pairs={{0,1},{1,0},{2,3},{3,2},{4,5},{5,4},{6,7},{7,6},{8,9},{9,8},{10,11... | collective-permute-start | bytes 49160 | tf_op jit(solution)/shard_map/cond/branch_1_fun/ppermute | solution.py:610
  42.4 0.6 copy-start.1
  43.8 22.1 %collective-permute-start.10 = (f32[3,2,128]{2,1,0:T(2,128)S(1)}, f32[3,2,128]{2,1,0:T(2,128)S(1)}, u32[]{:S(2)}, u32[]{:S(2)}) collective-permute-start(f32[3,2,128]{2,1,0:T(2,128)S(1)} %get-tuple-element.61), channel_id=1, source_target_pairs={{0,6},{2,0},{4,2},{6,4},{1,7},{3,1},{5,3},{7,5},{8,14},{10,8},{12,... | collective-permute-start | bytes 9224 | tf_op jit(solution)/shard_map/ppermute | solution.py:628
  45.7 20.3 %collective-permute-start.12 = (f32[3,2,128]{2,1,0:T(2,128)S(1)}, f32[3,2,128]{2,1,0:T(2,128)S(1)}, u32[]{:S(2)}, u32[]{:S(2)}) collective-permute-start(f32[3,2,128]{2,1,0:T(2,128)S(1)} %get-tuple-element.62), channel_id=1, source_target_pairs={{0,2},{2,4},{4,6},{6,0},{1,3},{3,5},{5,7},{7,1},{8,10},{10,12},{12... | collective-permute-start | bytes 9224 | tf_op jit(solution)/shard_map/ppermute | solution.py:628
  45.9 20.1 %collective-permute-start.11 = (f32[3,2,128]{2,1,0:T(2,128)S(1)}, f32[3,2,128]{2,1,0:T(2,128)S(1)}, u32[]{:S(2)}, u32[]{:S(2)}) collective-permute-start(f32[3,2,128]{2,1,0:T(2,128)S(1)} %get-tuple-element.63), channel_id=1, source_target_pairs={{0,4},{2,6},{4,0},{6,2},{1,5},{3,7},{5,1},{7,3},{8,12},{10,14},{12... | collective-permute-start | bytes 9224 | tf_op jit(solution)/shard_map/ppermute | solution.py:628

commit v12 on v7

--- a/solution.py
+++ b/solution.py
@@ -20,6 +20,7 @@
 F32 = jnp.float32
 BF16 = jnp.bfloat16
 MIB = 1024 * 1024
+PREP, SAMPLE, UPDATE = 54, 32, 42
 LEVELS = 8
 STEP = 256
 LIGHT = pl.CostEstimate(flops=0, bytes_accessed=0, transcendentals=0)
@@ -68,8 +69,8 @@
 
 
 def prep_kernel(
-    turb_in, pos_in, speed_in, lift_in, vel_in, blocks_ref, up_ref, down_ref, near_ref, far_ref, relay_ref,
-    turb_ref, pos_ref, speed_ref, lift_ref, vel_ref, sems,
+    turb_in, pos_in, speed_in, lift_in, vel_in, vel_ref, blocks_ref, up_ref, down_ref, near_ref, far_ref,
+    relay_ref, turb_ref, pos_ref, speed_ref, lift_ref, sems,
 ):
     components, levels, rows, cols = vel_ref.shape
     coords, owned, points = pos_ref.shape
@@ -127,8 +128,9 @@
     return pl.pallas_call(
         prep_kernel,
         in_specs=[pl.BlockSpec(memory_space=pltpu.HBM)] * 5,
-        out_specs=[pl.BlockSpec(memory_space=pltpu.VMEM)] * 6,
+        out_specs=[pl.BlockSpec(memory_space=pltpu.VMEM)] * 7,
         out_shape=[
+            jax.ShapeDtypeStruct(velocity.shape, F32),
             jax.ShapeDtypeStruct((owned, 8, points), F32),
             jax.ShapeDtypeStruct((tiles, 8, 128), F32),
             jax.ShapeDtypeStruct((tiles, 8, 128), F32),
@@ -141,10 +143,9 @@
             pltpu.VMEM((coords, owned, points), F32),
             pltpu.VMEM((coords, owned, points), F32),
             pltpu.VMEM((owned, points), F32),
-            pltpu.VMEM(velocity.shape, F32),
             pltpu.SemaphoreType.DMA((components + 4,)),
         ],
-        compiler_params=pltpu.CompilerParams(vmem_limit_bytes=60 * MIB),
+        compiler_params=pltpu.CompilerParams(vmem_limit_bytes=PREP * MIB),
         cost_estimate=LIGHT,
         name="prep",
     )(
@@ -172,8 +173,8 @@
 
 
 def sample_kernel(
-    per_turbine, mine_ref, twin_ref, vel_in, part_ref, own_ref, mask_ref, weight_out, lev_ref,
-    even_ref, odd_ref, center_ref, plane_ref, acc_ref, vel_ref, weight_ref, sems, out_sems, lev_sem,
+    per_turbine, mine_ref, twin_ref, vel_ref, part_ref, own_ref, mask_ref, weight_ref, lev_ref,
+    even_ref, odd_ref, center_ref, plane_ref, acc_ref,
 ):
     components, depth, rows, cols = vel_ref.shape
     points = mine_ref.shape[2]
@@ -184,21 +185,7 @@
     start = lax.axis_index("gy") * cols
 
     def column(at):
-        return pl.ds(pl.multiple_of(at * STEP, STEP), STEP)
-
-    def column_copy(at):
-        return pltpu.make_async_copy(
-            vel_in.at[:, :, :, column(at)], vel_ref.at[:, :, :, column(at)], sems.at[at]
-        )
-
-    def weight_copy(at):
-        return pltpu.make_async_copy(
-            weight_ref.at[:, column(at)], weight_out.at[:, column(at)], out_sems.at[at]
-        )
-
-    lev_copy = pltpu.make_async_copy(
-        vel_in.at[:, pl.ds(jnp.where(core == 0, depth - 2, 0), 2)], lev_ref, lev_sem
-    )
+        return slice(at * STEP, (at + 1) * STEP)
 
     def bell(cell, center):
         gap = cell.astype(F32) - center
@@ -211,10 +198,8 @@
             ref[:, part * 128 : part * 128 + 128] = bell(cell, center_ref[...])
 
     def multiply(at, ref):
-        vel = vel_ref.at[:, :, :, column(at)]
-        out = weight_ref.at[:, column(at)]
         for i in range(components):
-            high, low = split(vel[i].reshape(cells, STEP))
+            high, low = split(vel_ref[i, :, :, column(at)].reshape(cells, STEP))
             field = dot(plane_ref[...], jnp.concatenate([high, high, low], axis=0))
             product = field * ref[...]
             total = acc_ref[i]
@@ -222,11 +207,10 @@
                 total += product[:, part * 128 : part * 128 + 128]
             acc_ref[i] = total
         high, low = split(ref[...])
-        out[:count, :] = high
-        out[count:, :] = low
-
-    column_copy(0).start()
-    column_copy(1).start()
+        weight_ref[:count, column(at)] = high
+        weight_ref[count:, column(at)] = low
+
+    lev_ref[...] = vel_ref[:, pl.ds(jnp.where(core == 0, depth - 2, 0), 2)]
     masks = match(mine_ref, twin_ref, per_turbine)
     blocks = mine_ref.shape[0]
     lane = lax.broadcasted_iota(jnp.int32, (1, cells), 1)
@@ -252,50 +236,28 @@
     acc_ref[...] = jnp.zeros(acc_ref.shape, F32)
     weights(0, even_ref)
 
-    def pair(step, carry):
-        column_copy(2 * step).wait()
-        column_copy(2 * step + 1).wait()
-
-        @pl.when(step < chunks // 2 - 1)
-        def _():
-            column_copy(2 * step + 2).start()
-            column_copy(2 * step + 3).start()
-
-        @pl.when(step == chunks // 2 - 1)
-        def _():
-            lev_copy.start()
-
-        weights(2 * step + 1, odd_ref)
-        multiply(2 * step, even_ref)
-        weights(2 * step + 2, even_ref)
-        multiply(2 * step + 1, odd_ref)
-        weight_copy(2 * step).start()
-        weight_copy(2 * step + 1).start()
-        return carry
-
-    lax.fori_loop(0, chunks // 2, pair, 0)
+    for at in range(chunks):
+        now, later = (even_ref, odd_ref) if at % 2 == 0 else (odd_ref, even_ref)
+        if at < chunks - 1:
+            weights(at + 1, later)
+        multiply(at, now)
     for i in range(components):
         for k in range(per_turbine):
             band = slice(k * points, (k + 1) * points)
             total = jnp.sum(acc_ref[i, band, :].T, axis=0, keepdims=True)
             part_ref[i : i + 1, band] = smear_norm * total
     part_ref[components:, :] = jnp.zeros((8 - components, count), F32)
-    lev_copy.wait()
-    for at in range(chunks):
-        weight_copy(at).wait()
 
 
 def sample(mine, twin, velocity, per_turbine):
     components, depth, rows, cols = velocity.shape
     points = mine.shape[2]
     count = per_turbine * points
-    chunks = cols // STEP
     vmem = pl.BlockSpec(memory_space=pltpu.VMEM)
-    hbm = pl.BlockSpec(memory_space=pltpu.HBM)
     return pl.pallas_call(
         functools.partial(sample_kernel, per_turbine),
-        in_specs=[vmem, vmem, hbm],
-        out_specs=[vmem, vmem, vmem, hbm, vmem],
+        in_specs=[vmem] * 3,
+        out_specs=[vmem] * 5,
         out_shape=[
             jax.ShapeDtypeStruct((8, count), F32),
             jax.ShapeDtypeStruct((8, count), F32),
@@ -309,13 +271,8 @@
             pltpu.VMEM((count, 128), F32),
             pltpu.VMEM((count, 3 * depth * rows), BF16),
             pltpu.VMEM((components, count, 128), F32),
-            pltpu.VMEM(velocity.shape, F32),
-            pltpu.VMEM((2 * count, cols), BF16),
-            pltpu.SemaphoreType.DMA((chunks,)),
-            pltpu.SemaphoreType.DMA((chunks,)),
-            pltpu.SemaphoreType.DMA,
         ],
-        compiler_params=pltpu.CompilerParams(vmem_limit_bytes=58 * MIB),
+        compiler_params=pltpu.CompilerParams(vmem_limit_bytes=SAMPLE * MIB),
         cost_estimate=LIGHT,
         name="sample",
     )(mine, twin, velocity)
@@ -350,7 +307,7 @@
             jax.ShapeDtypeStruct((8, count), F32),
             jax.ShapeDtypeStruct((shifts, 3, owned, points), F32),
         ],
-        compiler_params=pltpu.CompilerParams(vmem_limit_bytes=58 * MIB),
+        compiler_params=pltpu.CompilerParams(vmem_limit_bytes=8 * MIB),
         cost_estimate=LIGHT,
         name="force",
     )(mask, part, other, own)
@@ -566,7 +523,7 @@
     count = own.shape[1]
     chunks = cols // STEP
     vmem = pl.BlockSpec(memory_space=pltpu.VMEM)
-    hbm = pl.BlockSpec(memory_space=pltpu.HBM)
+    hbm = pl.BlockSpec(memory_space=pl.ANY)
     fields = [pltpu.VMEM((components, depth, rows, STEP), F32)] * 3
     macs = components * depth * rows * cols * (3 * count + 4 * 256)
     return pl.pallas_call(
@@ -592,7 +549,7 @@
             pltpu.SemaphoreType.DMA((chunks,)),
             pltpu.SemaphoreType.DMA,
         ],
-        compiler_params=pltpu.CompilerParams(vmem_limit_bytes=44 * MIB),
+        compiler_params=pltpu.CompilerParams(vmem_limit_bytes=UPDATE * MIB),
         cost_estimate=pl.CostEstimate(
             flops=2 * macs, bytes_accessed=8 * velocity.size, transcendentals=velocity.size // 3
         ),
@@ -611,7 +568,7 @@
     def around(shift):
         return [(i, (i + shift) % gy) for i in range(gy)]
 
-    blocks, up, down, near, far, relay = prep(
+    held, blocks, up, down, near, far, relay = prep(
         velocity, blade_pos, block_turbine, blade_vel, lift_coeff
     )
     near = lax.ppermute(near, "gx", [(i, i ^ 1) for i in range(gx)])
@@ -645,14 +602,14 @@
     else:
         relay = lax.ppermute(relay, "gx", across)
     far = lax.ppermute(far, "gx", across)
-    own, force, home, weight, lev = stage(blade, mine, twin, velocity)
+    own, force, home, weight, lev = stage(blade, mine, twin, held)
     result = home[0]
     for shift in range(1, gy):
         result += lax.ppermute(home[shift], "gy", around(gy - shift))
 
     operator = jnp.asarray(stencil_operator(rows))
     new_velocity, zero = update(
-        own, force, operator, near, far, relay, weight, velocity, lev, left, right, result.shape
+        own, force, operator, near, far, relay, weight, held, lev, left, right, result.shape
     )
     return (new_velocity, (result + zero).transpose(1, 0, 2))
 

time: 62.4 us -> 62.5 us (level)
  Pallas kernels: 32.6 us -> 33.5 us
    pallas_call x1, Pallas kernels: 4.24 us -> 6.26 us  [prep(): pl.pallas_call(prep_kernel, in_specs=[pl.BlockSpec(memory_space=pltpu.HBM...]
    pallas_call x1, Pallas kernels: 10.5 us -> 9.45 us  [sample(): pl.pallas_call(functools.partial(sample_kernel, per_turbine), in_specs=[v...]
  transfers between devices with their start and end apart: 13 -> 13, of which waited for: 4 -> 4; matrix products, arithmetic and copies ran while one was open for 1% -> 1% of each run, Pallas kernels for 46% -> 44%
where the time goes in v12:
time: 62.5 us; the launch traced here: 61.7 us
  Pallas kernels  33.5 us (54%)
  starting transfers between devices  19.3 us (31%)
  waiting for transfers between devices  6.81 us (11%)
  other arithmetic  1.19 us (2%)
  between operations  0.79 us (1%)
    pallas_call x1, Pallas kernels, update(): pl.pallas_call(update_kernel, in_specs=[vmem] * 5 + [hbm] * 6, out_specs=...  17.1 us
    pallas_call x1, Pallas kernels, sample(): pl.pallas_call(functools.partial(sample_kernel, per_turbine), in_specs=[v...  9.45 us
    pallas_call x1, Pallas kernels, prep(): pl.pallas_call(prep_kernel, in_specs=[pl.BlockSpec(memory_space=pltpu.HBM...  6.26 us
    ppermute x1, starting transfers between devices, local(): near = lax.ppermute(near, 'gx', [(i, i ^ 1) for i in range(gx)])  5.16 us
    ppermute x1, starting transfers between devices, local(): relay = lax.ppermute(relay, 'gx', [(3, 2), (0, 1)])  3.98 us
    ppermute x3, starting transfers between devices, local(): result += lax.ppermute(home[shift], 'gy', around(gy - shift))  2.87 us
    ppermute x1, waiting for transfers between devices, gather(): lax.ppermute(blocks, 'gy', around(shift))  2.39 us
    ppermute x1, starting transfers between devices, gather(): right = lax.ppermute(down, 'gy', around(gy - 1))  2.25 us
  transfers between devices with their start and end apart: 13, of which 4 were waited for; matrix products, arithmetic and copies ran while one was open for 1% of the time, Pallas kernels for 44%

profile of v12, /device:TPU:0, one launch (start us, length us, event | category | flops | bytes accessed | tf_op | source)
XLA Modules:
  0.0 61.7 jit_solution(1340639629778537362)
XLA Ops:
  0.6 6.3 %prep.1 = (f32[3,16,16,2048]{3,2,1,0:T(8,128)}, f32[2,8,128]{2,1,0:T(8,128)S(1)}, f32[8,8,128]{2,1,0:T(8,128)S(1)}, f32[8,8,128]{2,1,0:T(8,128)S(1)}, f32[3,32,2...) custom-call(s32[2]{0:T(128)} %turb_in.1, f32[3,2,128]{2,1,0:T(2,128)} %bitcast.22, ...), custom_call_target="tpu_custom_call" | custom-call | tf_op jit(solution)/shard_map/prep/pallas_call | solution.py:128
  6.9 0.0 copy-start
  6.9 1.4 %collective-permute-start.8 = (f32[3,16,2048]{2,1,0:T(8,128)}, f32[3,16,2048]{2,1,0:T(8,128)S(1)}, u32[]{:S(2)}, u32[]{:S(2)}) collective-permute-start(f32[3,16,2048]{2,1,0:T(8,128)} %get-tuple-element.57), channel_id=1, source_target_pairs={{8,24},{16,0},{9,25},{17,1},{10,26},{18,2},{11,27},{19,3},{12,28},... | collective-permute-start | bytes 1179656 | tf_op jit(solution)/shard_map/ppermute | solution.py:577
  8.4 5.2 %collective-permute-start.6 = (f32[3,32,2048]{2,1,0:T(8,128)}, f32[3,32,2048]{2,1,0:T(8,128)S(1)}, u32[]{:S(2)}, u32[]{:S(2)}) collective-permute-start(f32[3,32,2048]{2,1,0:T(8,128)} %get-tuple-element.55), channel_id=1, source_target_pairs={{0,8},{8,0},{16,24},{24,16},{1,9},{9,1},{17,25},{25,17},{2,10},{10... | collective-permute-start | bytes 2359304 | tf_op jit(solution)/shard_map/ppermute | solution.py:574
  13.6 10.6 %conditional.2 = (f32[8,8,128]{2,1,0:T(8,128)}, f32[8,8,128]{2,1,0:T(8,128)}, f32[6,8,128]{2,1,0:T(8,128)S(1)}, f32[6,8,128]{2,1,0:T(8,128)S(1)}) conditional(s32[]{:T(128)} %bitcast, () %tuple.25, (f32[8,8,128]{2,1,0:T(8,128)S(1)}, f32[2,8,128]{2,1,0:T(8,128)S(1)}, f32[8,8,128]{2,1,0:T(8,128)S(1)}) %tuple.26), branch_computations={%region_0.0_spmd, %region_1.0_spmd} | conditional | flops 24576 | bytes 622784 | solution.py:597
  13.6 1.6 %collective-permute-start.2 = (f32[8,8,128]{2,1,0:T(8,128)S(1)}, f32[8,8,128]{2,1,0:T(8,128)S(1)}, u32[]{:S(2)}, u32[]{:S(2)}) collective-permute-start(f32[8,8,128]{2,1,0:T(8,128)S(1)} %get-tuple-element.13), channel_id=1, source_target_pairs={{0,2},{2,4},{4,6},{6,0},{1,3},{3,5},{5,7},{7,1},{8,10},{10,12},{12... | collective-permute-start | bytes 98312 | tf_op jit(solution)/shard_map/cond/branch_1_fun/ppermute | solution.py:580
  15.2 2.2 %collective-permute-start.4 = (f32[8,8,128]{2,1,0:T(8,128)S(1)}, f32[8,8,128]{2,1,0:T(8,128)S(1)}, u32[]{:S(2)}, u32[]{:S(2)}) collective-permute-start(f32[8,8,128]{2,1,0:T(8,128)S(1)} %get-tuple-element.14), channel_id=1, source_target_pairs={{0,6},{2,0},{4,2},{6,4},{1,7},{3,1},{5,3},{7,5},{8,14},{10,8},{12,... | collective-permute-start | bytes 98312 | tf_op jit(solution)/shard_map/cond/branch_1_fun/ppermute | solution.py:581
  17.5 0.8 %collective-permute-start.3 = (f32[2,8,128]{2,1,0:T(8,128)S(1)}, f32[2,8,128]{2,1,0:T(8,128)S(1)}, u32[]{:S(2)}, u32[]{:S(2)}) collective-permute-start(f32[2,8,128]{2,1,0:T(8,128)S(1)} %get-tuple-element.12), channel_id=1, source_target_pairs={{0,4},{2,6},{4,0},{6,2},{1,5},{3,7},{5,1},{7,3},{8,12},{10,14},{12... | collective-permute-start | bytes 24584 | tf_op jit(solution)/shard_map/cond/branch_1_fun/ppermute | solution.py:583
  18.2 1.4 %collective-permute-done.2 = f32[8,8,128]{2,1,0:T(8,128)S(1)} collective-permute-done((f32[8,8,128]{2,1,0:T(8,128)S(1)}, f32[8,8,128]{2,1,0:T(8,128)S(1)}, u32[]{:S(2)}, u32[]{:S(2)}) %collective-permute-start.2) | collective-permute-done | bytes 32800 | tf_op jit(solution)/shard_map/cond/branch_1_fun/ppermute | solution.py:580
  19.6 0.0 collective-permute-done.4
  19.6 2.4 %collective-permute-done.3 = f32[2,8,128]{2,1,0:T(8,128)S(1)} collective-permute-done((f32[2,8,128]{2,1,0:T(8,128)S(1)}, f32[2,8,128]{2,1,0:T(8,128)S(1)}, u32[]{:S(2)}, u32[]{:S(2)}) %collective-permute-start.3) | collective-permute-done | bytes 8224 | tf_op jit(solution)/shard_map/cond/branch_1_fun/ppermute | solution.py:583
  22.0 0.6 pad_maximum_fusion
  22.6 0.0 collective-permute-start.5
  22.6 1.5 %collective-permute-done.5 = f32[8,8,128]{2,1,0:T(8,128)} collective-permute-done((f32[8,8,128]{2,1,0:T(8,128)}, f32[8,8,128]{2,1,0:T(8,128)}, u32[]{:S(2)}, u32[]{:S(2)}) %collective-permute-start.5) | collective-permute-done | bytes 32800 | tf_op jit(solution)/shard_map/cond/branch_1_fun/ppermute | solution.py:586
  24.2 0.7 %collective-permute-start.7 = (f32[3,16,2048]{2,1,0:T(8,128)}, f32[3,16,2048]{2,1,0:T(8,128)S(1)}, u32[]{:S(2)}, u32[]{:S(2)}) collective-permute-start(f32[3,16,2048]{2,1,0:T(8,128)} %get-tuple-element.56), channel_id=1, source_target_pairs={{8,16},{16,8},{9,17},{17,9},{10,18},{18,10},{11,19},{19,11},{12,20... | collective-permute-start | bytes 1179656 | tf_op jit(solution)/shard_map/ppermute | solution.py:604
  24.8 0.0 collective-permute-done.8
  24.9 4.0 %collective-permute-start.9 = (f32[3,16,2048]{2,1,0:T(8,128)S(1)}, f32[3,16,2048]{2,1,0:T(8,128)S(1)}, u32[]{:S(2)}, u32[]{:S(2)}) collective-permute-start(f32[3,16,2048]{2,1,0:T(8,128)S(1)} %collective-permute-done.8), channel_id=1, source_target_pairs={{24,16},{0,8},{25,17},{1,9},{26,18},{2,10},{27,19},{3,11},{28,20},... | collective-permute-start | bytes 1179656 | tf_op jit(solution)/shard_map/ppermute | solution.py:601
  28.8 12.3 %conditional.3 = (f32[8,512]{1,0:T(8,128)}, f32[8,512]{1,0:T(8,128)S(1)}, f32[4,3,2,128]{3,2,1,0:T(2,128)S(1)}, bf16[1024,2048]{1,0:T(8,128)(2,1)}, f32[3,2,16,2048]{3,2,1,0:T(8,128)}) conditional(s32[]{:T(128)} %bitcast, () %tuple.24, (f32[8,8,128]{2,1,0:T(8,128)}, f32[8,8,128]{2,1,0:T(8,128)}, f32[3,16,16,2048]{3,2,1,0:T(8,128)}) %tuple.27), branch_computations={%region_2.0_spmd, %region_3.0_spmd} | conditional | bytes 5025850 | solution.py:597
  28.9 9.4 %sample.1 = (f32[8,512]{1,0:T(8,128)S(1)}, f32[8,512]{1,0:T(8,128)}, f32[8,4,128]{2,1,0:T(4,128)S(1)}, bf16[1024,2048]{1,0:T(8,128)(2,1)}, f32[3,2,16,2048]{3,2,1,0:T(8,128)S(1)}) custom-call(f32[8,8,128]{2,1,0:T(8,128)} %get-tuple-element.15.mine_ref, f32[8,8,128]{2,1,0:T(8,128)} %get-tuple-element.16.twin_ref, f32[3,16,16,2048]{3,2,1,0:T(8,128)} %get-tuple-element.17.vel_ref), custom_call_target="tpu_custom_call" | custom-call | tf_op jit(solution)/shard_map/cond/branch_1_fun/sample/pallas_call | solution.py:257
  38.3 0.1 collective-permute-start.1
  38.4 0.5 collective-permute-start
  38.9 1.5 %collective-permute-done.other_ref = f32[8,512]{1,0:T(8,128)S(1)} collective-permute-done((f32[8,512]{1,0:T(8,128)S(1)}, f32[8,512]{1,0:T(8,128)S(1)}, u32[]{:S(2)}, u32[]{:S(2)}) %collective-permute-start) | collective-permute-done | bytes 16416 | tf_op jit(solution)/shard_map/cond/branch_1_fun/ppermute | solution.py:590
  40.4 0.8 %force.1 = (f32[8,512]{1,0:T(8,128)S(1)}, f32[4,3,2,128]{3,2,1,0:T(2,128)S(1)}) custom-call(f32[8,4,128]{2,1,0:T(4,128)S(1)} %get-tuple-element.19.mask_ref, f32[8,512]{1,0:T(8,128)S(1)} %get-tuple-element.20.part_ref, f32[8,512]{1,0:T(8,128)S(1)} %collective-permute-done.other_ref, f32[8,512]{1,0:T(8,128)} %get-tuple-element.79.own_ref), custom_call_target="tpu_custom_call" | custom-call | tf_op jit(solution)/shard_map/cond/branch_1_fun/force/pallas_call | solution.py:302
  41.1 0.0 collective-permute-done.1
  41.2 1.9 %collective-permute-start.10 = (f32[3,2,128]{2,1,0:T(2,128)S(1)}, f32[3,2,128]{2,1,0:T(2,128)S(1)}, u32[]{:S(2)}, u32[]{:S(2)}) collective-permute-start(f32[3,2,128]{2,1,0:T(2,128)S(1)} %get-tuple-element.63), channel_id=1, source_target_pairs={{0,6},{2,0},{4,2},{6,4},{1,7},{3,1},{5,3},{7,5},{8,14},{10,8},{12,... | collective-permute-start | bytes 9224 | tf_op jit(solution)/shard_map/ppermute | solution.py:608
  43.0 0.2 collective-permute-start.12
  43.3 0.8 %collective-permute-start.11 = (f32[3,2,128]{2,1,0:T(2,128)S(1)}, f32[3,2,128]{2,1,0:T(2,128)S(1)}, u32[]{:S(2)}, u32[]{:S(2)}) collective-permute-start(f32[3,2,128]{2,1,0:T(2,128)S(1)} %get-tuple-element.65), channel_id=1, source_target_pairs={{0,4},{2,6},{4,0},{6,2},{1,5},{3,7},{5,1},{7,3},{8,12},{10,14},{12... | collective-permute-start | bytes 9224 | tf_op jit(solution)/shard_map/ppermute | solution.py:608
  44.0 0.0 collective-permute-done.6.near_in
  44.1 17.1 %update.1 = (f32[3,16,16,2048]{3,2,1,0:T(8,128)}, f32[3,2,128]{2,1,0:T(2,128)S(1)}) custom-call(f32[8,512]{1,0:T(8,128)} %get-tuple-element.51.own_ref, f32[8,512]{1,0:T(8,128)S(1)} %get-tuple-element.52.force_ref, bf16[256,512]{1,0:T(8,128)(2,1)S(1)} %copy-done, f32[6,8,128]{2,1,0:T(8,128)S(1)} %get-tuple-element.53.left_ref, ...), custom_call_target="tpu_custom_call" | custom-call | flops 8053063680 | bytes 12582912 | tf_op jit(solution)/shard_map/update/pallas_call | solution.py:529
  61.1 0.0 collective-permute-done.10
  61.1 0.0 collective-permute-done.11
  61.2 0.6 fusion.3
  (11 shorter events, 0.0 us)
Async XLA Ops:
  0.6 12.9 %copy-start.1 = (s32[2]{0:T(128)S(1)}, s32[2]{0:T(128)}, u32[]{:S(2)}) copy-start(s32[2]{0:T(128)} %turb_in.1) | copy-start | bytes 28
  6.9 37.1 %copy-start = (bf16[256,512]{1,0:T(8,128)(2,1)S(1)}, bf16[256,512]{1,0:T(8,128)(2,1)}, u32[]{:S(2)}) copy-start(bf16[256,512]{1,0:T(8,128)(2,1)} %constant.9.clone.op_ref) | copy-start | bytes 786436
  6.9 17.9 %collective-permute-start.8 = (f32[3,16,2048]{2,1,0:T(8,128)}, f32[3,16,2048]{2,1,0:T(8,128)S(1)}, u32[]{:S(2)}, u32[]{:S(2)}) collective-permute-start(f32[3,16,2048]{2,1,0:T(8,128)} %get-tuple-element.57), channel_id=1, source_target_pairs={{8,24},{16,0},{9,25},{17,1},{10,26},{18,2},{11,27},{19,3},{12,28},... | collective-permute-start | bytes 1179656 | tf_op jit(solution)/shard_map/ppermute | solution.py:577
  8.4 35.7 %collective-permute-start.6 = (f32[3,32,2048]{2,1,0:T(8,128)}, f32[3,32,2048]{2,1,0:T(8,128)S(1)}, u32[]{:S(2)}, u32[]{:S(2)}) collective-permute-start(f32[3,32,2048]{2,1,0:T(8,128)} %get-tuple-element.55), channel_id=1, source_target_pairs={{0,8},{8,0},{16,24},{24,16},{1,9},{9,1},{17,25},{25,17},{2,10},{10... | collective-permute-start | bytes 2359304 | tf_op jit(solution)/shard_map/ppermute | solution.py:574
  13.6 6.0 %collective-permute-start.2 = (f32[8,8,128]{2,1,0:T(8,128)S(1)}, f32[8,8,128]{2,1,0:T(8,128)S(1)}, u32[]{:S(2)}, u32[]{:S(2)}) collective-permute-start(f32[8,8,128]{2,1,0:T(8,128)S(1)} %get-tuple-element.13), channel_id=1, source_target_pairs={{0,2},{2,4},{4,6},{6,0},{1,3},{3,5},{5,7},{7,1},{8,10},{10,12},{12... | collective-permute-start | bytes 98312 | tf_op jit(solution)/shard_map/cond/branch_1_fun/ppermute | solution.py:580
  15.2 4.4 %collective-permute-start.4 = (f32[8,8,128]{2,1,0:T(8,128)S(1)}, f32[8,8,128]{2,1,0:T(8,128)S(1)}, u32[]{:S(2)}, u32[]{:S(2)}) collective-permute-start(f32[8,8,128]{2,1,0:T(8,128)S(1)} %get-tuple-element.14), channel_id=1, source_target_pairs={{0,6},{2,0},{4,2},{6,4},{1,7},{3,1},{5,3},{7,5},{8,14},{10,8},{12,... | collective-permute-start | bytes 98312 | tf_op jit(solution)/shard_map/cond/branch_1_fun/ppermute | solution.py:581
  17.5 4.5 %collective-permute-start.3 = (f32[2,8,128]{2,1,0:T(8,128)S(1)}, f32[2,8,128]{2,1,0:T(8,128)S(1)}, u32[]{:S(2)}, u32[]{:S(2)}) collective-permute-start(f32[2,8,128]{2,1,0:T(8,128)S(1)} %get-tuple-element.12), channel_id=1, source_target_pairs={{0,4},{2,6},{4,0},{6,2},{1,5},{3,7},{5,1},{7,3},{8,12},{10,14},{12... | collective-permute-start | bytes 24584 | tf_op jit(solution)/shard_map/cond/branch_1_fun/ppermute | solution.py:583
  22.6 1.6 %collective-permute-start.5 = (f32[8,8,128]{2,1,0:T(8,128)}, f32[8,8,128]{2,1,0:T(8,128)}, u32[]{:S(2)}, u32[]{:S(2)}) collective-permute-start(f32[8,8,128]{2,1,0:T(8,128)} %pad_maximum_fusion), channel_id=1, source_target_pairs={{0,1},{1,0},{2,3},{3,2},{4,5},{5,4},{6,7},{7,6},{8,9},{9,8},{10,11... | collective-permute-start | bytes 98312 | tf_op jit(solution)/shard_map/cond/branch_1_fun/ppermute | solution.py:586
  24.2 19.1 %collective-permute-start.7 = (f32[3,16,2048]{2,1,0:T(8,128)}, f32[3,16,2048]{2,1,0:T(8,128)S(1)}, u32[]{:S(2)}, u32[]{:S(2)}) collective-permute-start(f32[3,16,2048]{2,1,0:T(8,128)} %get-tuple-element.56), channel_id=1, source_target_pairs={{8,16},{16,8},{9,17},{17,9},{10,18},{18,10},{11,19},{19,11},{12,20... | collective-permute-start | bytes 1179656 | tf_op jit(solution)/shard_map/ppermute | solution.py:604
  24.9 19.2 %collective-permute-start.9 = (f32[3,16,2048]{2,1,0:T(8,128)S(1)}, f32[3,16,2048]{2,1,0:T(8,128)S(1)}, u32[]{:S(2)}, u32[]{:S(2)}) collective-permute-start(f32[3,16,2048]{2,1,0:T(8,128)S(1)} %collective-permute-done.8), channel_id=1, source_target_pairs={{24,16},{0,8},{25,17},{1,9},{26,18},{2,10},{27,19},{3,11},{28,20},... | collective-permute-start | bytes 1179656 | tf_op jit(solution)/shard_map/ppermute | solution.py:601
  38.3 2.8 %collective-permute-start.1 = (f32[3,2,16,2048]{3,2,1,0:T(8,128)S(1)}, f32[3,2,16,2048]{3,2,1,0:T(8,128)}, u32[]{:S(2)}, u32[]{:S(2)}) collective-permute-start(f32[3,2,16,2048]{3,2,1,0:T(8,128)S(1)} %get-tuple-element.24), channel_id=1, source_target_pairs={{0,1},{1,0},{2,3},{3,2},{4,5},{5,4},{6,7},{7,6},{8,9},{9,8},{10,11... | collective-permute-start | bytes 2359304 | tf_op jit(solution)/shard_map/cond/branch_1_fun/ppermute | solution.py:591
  38.4 2.0 %collective-permute-start = (f32[8,512]{1,0:T(8,128)S(1)}, f32[8,512]{1,0:T(8,128)S(1)}, u32[]{:S(2)}, u32[]{:S(2)}) collective-permute-start(f32[8,512]{1,0:T(8,128)S(1)} %get-tuple-element.20.part_ref), channel_id=1, source_target_pairs={{0,1},{1,0},{2,3},{3,2},{4,5},{5,4},{6,7},{7,6},{8,9},{9,8},{10,11... | collective-permute-start | bytes 49160 | tf_op jit(solution)/shard_map/cond/branch_1_fun/ppermute | solution.py:590
  41.2 20.0 %collective-permute-start.10 = (f32[3,2,128]{2,1,0:T(2,128)S(1)}, f32[3,2,128]{2,1,0:T(2,128)S(1)}, u32[]{:S(2)}, u32[]{:S(2)}) collective-permute-start(f32[3,2,128]{2,1,0:T(2,128)S(1)} %get-tuple-element.63), channel_id=1, source_target_pairs={{0,6},{2,0},{4,2},{6,4},{1,7},{3,1},{5,3},{7,5},{8,14},{10,8},{12,... | collective-permute-start | bytes 9224 | tf_op jit(solution)/shard_map/ppermute | solution.py:608
  43.0 18.1 %collective-permute-start.12 = (f32[3,2,128]{2,1,0:T(2,128)S(1)}, f32[3,2,128]{2,1,0:T(2,128)S(1)}, u32[]{:S(2)}, u32[]{:S(2)}) collective-permute-start(f32[3,2,128]{2,1,0:T(2,128)S(1)} %get-tuple-element.64), channel_id=1, source_target_pairs={{0,2},{2,4},{4,6},{6,0},{1,3},{3,5},{5,7},{7,1},{8,10},{10,12},{12... | collective-permute-start | bytes 9224 | tf_op jit(solution)/shard_map/ppermute | solution.py:608
  43.3 17.9 %collective-permute-start.11 = (f32[3,2,128]{2,1,0:T(2,128)S(1)}, f32[3,2,128]{2,1,0:T(2,128)S(1)}, u32[]{:S(2)}, u32[]{:S(2)}) collective-permute-start(f32[3,2,128]{2,1,0:T(2,128)S(1)} %get-tuple-element.65), channel_id=1, source_target_pairs={{0,4},{2,6},{4,0},{6,2},{1,5},{3,7},{5,1},{7,3},{8,12},{10,14},{12... | collective-permute-start | bytes 9224 | tf_op jit(solution)/shard_map/ppermute | solution.py:608

commit v13 on v12

--- a/solution.py
+++ b/solution.py
@@ -69,8 +69,8 @@
 
 
 def prep_kernel(
-    turb_in, pos_in, speed_in, lift_in, vel_in, vel_ref, blocks_ref, up_ref, down_ref, near_ref, far_ref,
-    relay_ref, turb_ref, pos_ref, speed_ref, lift_ref, sems,
+    turb_in, pos_in, speed_in, lift_in, vel_in, vel_ref, blocks_ref, up_ref, down_ref, near_out, far_out,
+    relay_out, turb_ref, pos_ref, speed_ref, lift_ref, near_ref, far_ref, relay_ref, sems, out_sems,
 ):
     components, levels, rows, cols = vel_ref.shape
     coords, owned, points = pos_ref.shape
@@ -96,6 +96,7 @@
             ref[k, 7:8, :] = jnp.full((1, points), turb_ref[k].astype(F32))
     parts = levels * rows // 128
     odd = lax.axis_index("gx") % 2 == 1
+    leaving = []
     row = lax.broadcasted_iota(jnp.int32, (8, cols), 0) // 2
     for component in range(components):
         large[component].wait()
@@ -119,6 +120,16 @@
             near_ref[component, group * 8 : group * 8 + 8, :] = jnp.where(odd, head, tail)
             ref, to = (far_ref, group * 8) if group * 8 < levels else (relay_ref, group * 8 - levels)
             ref[component, to : to + 8, :] = jnp.where(odd, tail, head)
+        for k, (source, target) in enumerate(
+            ((near_ref, near_out), (far_ref, far_out), (relay_ref, relay_out))
+        ):
+            copy = pltpu.make_async_copy(
+                source.at[component], target.at[component], out_sems.at[component, k]
+            )
+            copy.start()
+            leaving.append(copy)
+    for copy in leaving:
+        copy.wait()
 
 
 def prep(velocity, blade_pos, block_turbine, blade_vel, lift_coeff):
@@ -128,7 +139,8 @@
     return pl.pallas_call(
         prep_kernel,
         in_specs=[pl.BlockSpec(memory_space=pltpu.HBM)] * 5,
-        out_specs=[pl.BlockSpec(memory_space=pltpu.VMEM)] * 7,
+        out_specs=[pl.BlockSpec(memory_space=pltpu.VMEM)] * 4
+        + [pl.BlockSpec(memory_space=pltpu.HBM)] * 3,
         out_shape=[
             jax.ShapeDtypeStruct(velocity.shape, F32),
             jax.ShapeDtypeStruct((owned, 8, points), F32),
@@ -143,7 +155,11 @@
             pltpu.VMEM((coords, owned, points), F32),
             pltpu.VMEM((coords, owned, points), F32),
             pltpu.VMEM((owned, points), F32),
+            pltpu.VMEM((components, 2 * levels, cols), F32),
+            pltpu.VMEM((components, levels, cols), F32),
+            pltpu.VMEM((components, levels, cols), F32),
             pltpu.SemaphoreType.DMA((components + 4,)),
+            pltpu.SemaphoreType.DMA((components, 3)),
         ],
         compiler_params=pltpu.CompilerParams(vmem_limit_bytes=PREP * MIB),
         cost_estimate=LIGHT,

time: 62.5 us -> 63.1 us (level)
  no operation moved by 1% of the time
where the time goes in v13:
time: 63.1 us; the launch traced here: 62.3 us
  Pallas kernels  34.1 us (54%)
  starting transfers between devices  19.4 us (31%)
  waiting for transfers between devices  6.81 us (11%)
  other arithmetic  1.19 us (2%)
  between operations  0.79 us (1%)
    pallas_call x1, Pallas kernels, update(): pl.pallas_call(update_kernel, in_specs=[vmem] * 5 + [hbm] * 6, out_specs=...  17.1 us
    pallas_call x1, Pallas kernels, sample(): pl.pallas_call(functools.partial(sample_kernel, per_turbine), in_specs=[v...  9.44 us
    pallas_call x1, Pallas kernels, prep(): pl.pallas_call(prep_kernel, in_specs=[pl.BlockSpec(memory_space=pltpu.HBM...  6.82 us
    ppermute x1, starting transfers between devices, local(): near = lax.ppermute(near, 'gx', [(i, i ^ 1) for i in range(gx)])  5.16 us
    ppermute x1, starting transfers between devices, local(): relay = lax.ppermute(relay, 'gx', [(3, 2), (0, 1)])  3.98 us
    ppermute x3, starting transfers between devices, local(): result += lax.ppermute(home[shift], 'gy', around(gy - shift))  2.88 us
    ppermute x1, waiting for transfers between devices, gather(): lax.ppermute(blocks, 'gy', around(shift))  2.39 us
    ppermute x1, starting transfers between devices, gather(): right = lax.ppermute(down, 'gy', around(gy - 1))  2.25 us
  transfers between devices with their start and end apart: 13, of which 4 were waited for; matrix products, arithmetic and copies ran while one was open for 1% of the time, Pallas kernels for 44%

profile of v13, /device:TPU:0, one launch (start us, length us, event | category | flops | bytes accessed | tf_op | source)
XLA Modules:
  0.0 62.3 jit_solution(13540104662283943231)
XLA Ops:
  0.6 6.8 %prep.1 = (f32[3,16,16,2048]{3,2,1,0:T(8,128)}, f32[2,8,128]{2,1,0:T(8,128)S(1)}, f32[8,8,128]{2,1,0:T(8,128)S(1)}, f32[8,8,128]{2,1,0:T(8,128)S(1)}, f32[3,32,2...) custom-call(s32[2]{0:T(128)} %turb_in.1, f32[3,2,128]{2,1,0:T(2,128)} %bitcast.22, ...), custom_call_target="tpu_custom_call" | custom-call | tf_op jit(solution)/shard_map/prep/pallas_call | solution.py:139
  7.5 0.0 copy-start
  7.5 1.4 %collective-permute-start.8 = (f32[3,16,2048]{2,1,0:T(8,128)}, f32[3,16,2048]{2,1,0:T(8,128)S(1)}, u32[]{:S(2)}, u32[]{:S(2)}) collective-permute-start(f32[3,16,2048]{2,1,0:T(8,128)} %get-tuple-element.57), channel_id=1, source_target_pairs={{8,24},{16,0},{9,25},{17,1},{10,26},{18,2},{11,27},{19,3},{12,28},... | collective-permute-start | bytes 1179656 | tf_op jit(solution)/shard_map/ppermute | solution.py:593
  8.9 5.2 %collective-permute-start.6 = (f32[3,32,2048]{2,1,0:T(8,128)}, f32[3,32,2048]{2,1,0:T(8,128)S(1)}, u32[]{:S(2)}, u32[]{:S(2)}) collective-permute-start(f32[3,32,2048]{2,1,0:T(8,128)} %get-tuple-element.55), channel_id=1, source_target_pairs={{0,8},{8,0},{16,24},{24,16},{1,9},{9,1},{17,25},{25,17},{2,10},{10... | collective-permute-start | bytes 2359304 | tf_op jit(solution)/shard_map/ppermute | solution.py:590
  14.1 10.6 %conditional.2 = (f32[8,8,128]{2,1,0:T(8,128)}, f32[8,8,128]{2,1,0:T(8,128)}, f32[6,8,128]{2,1,0:T(8,128)S(1)}, f32[6,8,128]{2,1,0:T(8,128)S(1)}) conditional(s32[]{:T(128)} %bitcast, () %tuple.25, (f32[8,8,128]{2,1,0:T(8,128)S(1)}, f32[2,8,128]{2,1,0:T(8,128)S(1)}, f32[8,8,128]{2,1,0:T(8,128)S(1)}) %tuple.26), branch_computations={%region_0.0_spmd, %region_1.0_spmd} | conditional | flops 24576 | bytes 622784 | solution.py:613
  14.1 1.6 %collective-permute-start.2 = (f32[8,8,128]{2,1,0:T(8,128)S(1)}, f32[8,8,128]{2,1,0:T(8,128)S(1)}, u32[]{:S(2)}, u32[]{:S(2)}) collective-permute-start(f32[8,8,128]{2,1,0:T(8,128)S(1)} %get-tuple-element.13), channel_id=1, source_target_pairs={{0,2},{2,4},{4,6},{6,0},{1,3},{3,5},{5,7},{7,1},{8,10},{10,12},{12... | collective-permute-start | bytes 98312 | tf_op jit(solution)/shard_map/cond/branch_1_fun/ppermute | solution.py:596
  15.8 2.2 %collective-permute-start.4 = (f32[8,8,128]{2,1,0:T(8,128)S(1)}, f32[8,8,128]{2,1,0:T(8,128)S(1)}, u32[]{:S(2)}, u32[]{:S(2)}) collective-permute-start(f32[8,8,128]{2,1,0:T(8,128)S(1)} %get-tuple-element.14), channel_id=1, source_target_pairs={{0,6},{2,0},{4,2},{6,4},{1,7},{3,1},{5,3},{7,5},{8,14},{10,8},{12,... | collective-permute-start | bytes 98312 | tf_op jit(solution)/shard_map/cond/branch_1_fun/ppermute | solution.py:597
  18.0 0.8 %collective-permute-start.3 = (f32[2,8,128]{2,1,0:T(8,128)S(1)}, f32[2,8,128]{2,1,0:T(8,128)S(1)}, u32[]{:S(2)}, u32[]{:S(2)}) collective-permute-start(f32[2,8,128]{2,1,0:T(8,128)S(1)} %get-tuple-element.12), channel_id=1, source_target_pairs={{0,4},{2,6},{4,0},{6,2},{1,5},{3,7},{5,1},{7,3},{8,12},{10,14},{12... | collective-permute-start | bytes 24584 | tf_op jit(solution)/shard_map/cond/branch_1_fun/ppermute | solution.py:599
  18.8 1.4 %collective-permute-done.2 = f32[8,8,128]{2,1,0:T(8,128)S(1)} collective-permute-done((f32[8,8,128]{2,1,0:T(8,128)S(1)}, f32[8,8,128]{2,1,0:T(8,128)S(1)}, u32[]{:S(2)}, u32[]{:S(2)}) %collective-permute-start.2) | collective-permute-done | bytes 32800 | tf_op jit(solution)/shard_map/cond/branch_1_fun/ppermute | solution.py:596
  20.2 0.0 collective-permute-done.4
  20.2 2.4 %collective-permute-done.3 = f32[2,8,128]{2,1,0:T(8,128)S(1)} collective-permute-done((f32[2,8,128]{2,1,0:T(8,128)S(1)}, f32[2,8,128]{2,1,0:T(8,128)S(1)}, u32[]{:S(2)}, u32[]{:S(2)}) %collective-permute-start.3) | collective-permute-done | bytes 8224 | tf_op jit(solution)/shard_map/cond/branch_1_fun/ppermute | solution.py:599
  22.6 0.6 pad_maximum_fusion
  23.2 1.5 %collective-permute-done.5 = f32[8,8,128]{2,1,0:T(8,128)} collective-permute-done((f32[8,8,128]{2,1,0:T(8,128)}, f32[8,8,128]{2,1,0:T(8,128)}, u32[]{:S(2)}, u32[]{:S(2)}) %collective-permute-start.5) | collective-permute-done | bytes 32800 | tf_op jit(solution)/shard_map/cond/branch_1_fun/ppermute | solution.py:602
  24.7 0.7 %collective-permute-start.7 = (f32[3,16,2048]{2,1,0:T(8,128)}, f32[3,16,2048]{2,1,0:T(8,128)S(1)}, u32[]{:S(2)}, u32[]{:S(2)}) collective-permute-start(f32[3,16,2048]{2,1,0:T(8,128)} %get-tuple-element.56), channel_id=1, source_target_pairs={{8,16},{16,8},{9,17},{17,9},{10,18},{18,10},{11,19},{19,11},{12,20... | collective-permute-start | bytes 1179656 | tf_op jit(solution)/shard_map/ppermute | solution.py:620
  25.4 0.0 collective-permute-done.8
  25.4 4.0 %collective-permute-start.9 = (f32[3,16,2048]{2,1,0:T(8,128)S(1)}, f32[3,16,2048]{2,1,0:T(8,128)S(1)}, u32[]{:S(2)}, u32[]{:S(2)}) collective-permute-start(f32[3,16,2048]{2,1,0:T(8,128)S(1)} %collective-permute-done.8), channel_id=1, source_target_pairs={{24,16},{0,8},{25,17},{1,9},{26,18},{2,10},{27,19},{3,11},{28,20},... | collective-permute-start | bytes 1179656 | tf_op jit(solution)/shard_map/ppermute | solution.py:617
  29.4 12.3 %conditional.3 = (f32[8,512]{1,0:T(8,128)}, f32[8,512]{1,0:T(8,128)S(1)}, f32[4,3,2,128]{3,2,1,0:T(2,128)S(1)}, bf16[1024,2048]{1,0:T(8,128)(2,1)}, f32[3,2,16,2048]{3,2,1,0:T(8,128)}) conditional(s32[]{:T(128)} %bitcast, () %tuple.24, (f32[8,8,128]{2,1,0:T(8,128)}, f32[8,8,128]{2,1,0:T(8,128)}, f32[3,16,16,2048]{3,2,1,0:T(8,128)}) %tuple.27), branch_computations={%region_2.0_spmd, %region_3.0_spmd} | conditional | bytes 5025850 | solution.py:613
  29.4 9.4 %sample.1 = (f32[8,512]{1,0:T(8,128)S(1)}, f32[8,512]{1,0:T(8,128)}, f32[8,4,128]{2,1,0:T(4,128)S(1)}, bf16[1024,2048]{1,0:T(8,128)(2,1)}, f32[3,2,16,2048]{3,2,1,0:T(8,128)S(1)}) custom-call(f32[8,8,128]{2,1,0:T(8,128)} %get-tuple-element.15.mine_ref, f32[8,8,128]{2,1,0:T(8,128)} %get-tuple-element.16.twin_ref, f32[3,16,16,2048]{3,2,1,0:T(8,128)} %get-tuple-element.17.vel_ref), custom_call_target="tpu_custom_call" | custom-call | tf_op jit(solution)/shard_map/cond/branch_1_fun/sample/pallas_call | solution.py:273
  38.9 0.1 collective-permute-start.1
  38.9 0.5 collective-permute-start
  39.4 1.5 %collective-permute-done.other_ref = f32[8,512]{1,0:T(8,128)S(1)} collective-permute-done((f32[8,512]{1,0:T(8,128)S(1)}, f32[8,512]{1,0:T(8,128)S(1)}, u32[]{:S(2)}, u32[]{:S(2)}) %collective-permute-start) | collective-permute-done | bytes 16416 | tf_op jit(solution)/shard_map/cond/branch_1_fun/ppermute | solution.py:606
  40.9 0.8 %force.1 = (f32[8,512]{1,0:T(8,128)S(1)}, f32[4,3,2,128]{3,2,1,0:T(2,128)S(1)}) custom-call(f32[8,4,128]{2,1,0:T(4,128)S(1)} %get-tuple-element.19.mask_ref, f32[8,512]{1,0:T(8,128)S(1)} %get-tuple-element.20.part_ref, f32[8,512]{1,0:T(8,128)S(1)} %collective-permute-done.other_ref, f32[8,512]{1,0:T(8,128)} %get-tuple-element.79.own_ref), custom_call_target="tpu_custom_call" | custom-call | tf_op jit(solution)/shard_map/cond/branch_1_fun/force/pallas_call | solution.py:318
  41.7 1.9 %collective-permute-start.10 = (f32[3,2,128]{2,1,0:T(2,128)S(1)}, f32[3,2,128]{2,1,0:T(2,128)S(1)}, u32[]{:S(2)}, u32[]{:S(2)}) collective-permute-start(f32[3,2,128]{2,1,0:T(2,128)S(1)} %get-tuple-element.63), channel_id=1, source_target_pairs={{0,6},{2,0},{4,2},{6,4},{1,7},{3,1},{5,3},{7,5},{8,14},{10,8},{12,... | collective-permute-start | bytes 9224 | tf_op jit(solution)/shard_map/ppermute | solution.py:624
  43.6 0.2 collective-permute-start.12
  43.8 0.0 collective-permute-done.7.far_in
  43.8 0.8 %collective-permute-start.11 = (f32[3,2,128]{2,1,0:T(2,128)S(1)}, f32[3,2,128]{2,1,0:T(2,128)S(1)}, u32[]{:S(2)}, u32[]{:S(2)}) collective-permute-start(f32[3,2,128]{2,1,0:T(2,128)S(1)} %get-tuple-element.65), channel_id=1, source_target_pairs={{0,4},{2,6},{4,0},{6,2},{1,5},{3,7},{5,1},{7,3},{8,12},{10,14},{12... | collective-permute-start | bytes 9224 | tf_op jit(solution)/shard_map/ppermute | solution.py:624
  44.6 0.0 collective-permute-done.9.relay_in
  44.6 0.0 collective-permute-done.6.near_in
  44.6 17.1 %update.1 = (f32[3,16,16,2048]{3,2,1,0:T(8,128)}, f32[3,2,128]{2,1,0:T(2,128)S(1)}) custom-call(f32[8,512]{1,0:T(8,128)} %get-tuple-element.51.own_ref, f32[8,512]{1,0:T(8,128)S(1)} %get-tuple-element.52.force_ref, bf16[256,512]{1,0:T(8,128)(2,1)S(1)} %copy-done, f32[6,8,128]{2,1,0:T(8,128)S(1)} %get-tuple-element.53.left_ref, ...), custom_call_target="tpu_custom_call" | custom-call | flops 8053063680 | bytes 12582912 | tf_op jit(solution)/shard_map/update/pallas_call | solution.py:545
  61.7 0.0 collective-permute-done.12
  61.7 0.0 collective-permute-done.11
  61.7 0.6 fusion.3
  (11 shorter events, 0.0 us)
Async XLA Ops:
  0.6 13.4 %copy-start.1 = (s32[2]{0:T(128)S(1)}, s32[2]{0:T(128)}, u32[]{:S(2)}) copy-start(s32[2]{0:T(128)} %turb_in.1) | copy-start | bytes 28
  7.5 37.1 %copy-start = (bf16[256,512]{1,0:T(8,128)(2,1)S(1)}, bf16[256,512]{1,0:T(8,128)(2,1)}, u32[]{:S(2)}) copy-start(bf16[256,512]{1,0:T(8,128)(2,1)} %constant.9.clone.op_ref) | copy-start | bytes 786436
  7.5 17.9 %collective-permute-start.8 = (f32[3,16,2048]{2,1,0:T(8,128)}, f32[3,16,2048]{2,1,0:T(8,128)S(1)}, u32[]{:S(2)}, u32[]{:S(2)}) collective-permute-start(f32[3,16,2048]{2,1,0:T(8,128)} %get-tuple-element.57), channel_id=1, source_target_pairs={{8,24},{16,0},{9,25},{17,1},{10,26},{18,2},{11,27},{19,3},{12,28},... | collective-permute-start | bytes 1179656 | tf_op jit(solution)/shard_map/ppermute | solution.py:593
  8.9 35.7 %collective-permute-start.6 = (f32[3,32,2048]{2,1,0:T(8,128)}, f32[3,32,2048]{2,1,0:T(8,128)S(1)}, u32[]{:S(2)}, u32[]{:S(2)}) collective-permute-start(f32[3,32,2048]{2,1,0:T(8,128)} %get-tuple-element.55), channel_id=1, source_target_pairs={{0,8},{8,0},{16,24},{24,16},{1,9},{9,1},{17,25},{25,17},{2,10},{10... | collective-permute-start | bytes 2359304 | tf_op jit(solution)/shard_map/ppermute | solution.py:590
  14.1 6.0 %collective-permute-start.2 = (f32[8,8,128]{2,1,0:T(8,128)S(1)}, f32[8,8,128]{2,1,0:T(8,128)S(1)}, u32[]{:S(2)}, u32[]{:S(2)}) collective-permute-start(f32[8,8,128]{2,1,0:T(8,128)S(1)} %get-tuple-element.13), channel_id=1, source_target_pairs={{0,2},{2,4},{4,6},{6,0},{1,3},{3,5},{5,7},{7,1},{8,10},{10,12},{12... | collective-permute-start | bytes 98312 | tf_op jit(solution)/shard_map/cond/branch_1_fun/ppermute | solution.py:596
  15.8 4.4 %collective-permute-start.4 = (f32[8,8,128]{2,1,0:T(8,128)S(1)}, f32[8,8,128]{2,1,0:T(8,128)S(1)}, u32[]{:S(2)}, u32[]{:S(2)}) collective-permute-start(f32[8,8,128]{2,1,0:T(8,128)S(1)} %get-tuple-element.14), channel_id=1, source_target_pairs={{0,6},{2,0},{4,2},{6,4},{1,7},{3,1},{5,3},{7,5},{8,14},{10,8},{12,... | collective-permute-start | bytes 98312 | tf_op jit(solution)/shard_map/cond/branch_1_fun/ppermute | solution.py:597
  18.0 4.5 %collective-permute-start.3 = (f32[2,8,128]{2,1,0:T(8,128)S(1)}, f32[2,8,128]{2,1,0:T(8,128)S(1)}, u32[]{:S(2)}, u32[]{:S(2)}) collective-permute-start(f32[2,8,128]{2,1,0:T(8,128)S(1)} %get-tuple-element.12), channel_id=1, source_target_pairs={{0,4},{2,6},{4,0},{6,2},{1,5},{3,7},{5,1},{7,3},{8,12},{10,14},{12... | collective-permute-start | bytes 24584 | tf_op jit(solution)/shard_map/cond/branch_1_fun/ppermute | solution.py:599
  23.2 1.6 %collective-permute-start.5 = (f32[8,8,128]{2,1,0:T(8,128)}, f32[8,8,128]{2,1,0:T(8,128)}, u32[]{:S(2)}, u32[]{:S(2)}) collective-permute-start(f32[8,8,128]{2,1,0:T(8,128)} %pad_maximum_fusion), channel_id=1, source_target_pairs={{0,1},{1,0},{2,3},{3,2},{4,5},{5,4},{6,7},{7,6},{8,9},{9,8},{10,11... | collective-permute-start | bytes 98312 | tf_op jit(solution)/shard_map/cond/branch_1_fun/ppermute | solution.py:602
  24.7 19.1 %collective-permute-start.7 = (f32[3,16,2048]{2,1,0:T(8,128)}, f32[3,16,2048]{2,1,0:T(8,128)S(1)}, u32[]{:S(2)}, u32[]{:S(2)}) collective-permute-start(f32[3,16,2048]{2,1,0:T(8,128)} %get-tuple-element.56), channel_id=1, source_target_pairs={{8,16},{16,8},{9,17},{17,9},{10,18},{18,10},{11,19},{19,11},{12,20... | collective-permute-start | bytes 1179656 | tf_op jit(solution)/shard_map/ppermute | solution.py:620
  25.4 19.2 %collective-permute-start.9 = (f32[3,16,2048]{2,1,0:T(8,128)S(1)}, f32[3,16,2048]{2,1,0:T(8,128)S(1)}, u32[]{:S(2)}, u32[]{:S(2)}) collective-permute-start(f32[3,16,2048]{2,1,0:T(8,128)S(1)} %collective-permute-done.8), channel_id=1, source_target_pairs={{24,16},{0,8},{25,17},{1,9},{26,18},{2,10},{27,19},{3,11},{28,20},... | collective-permute-start | bytes 1179656 | tf_op jit(solution)/shard_map/ppermute | solution.py:617
  38.9 2.8 %collective-permute-start.1 = (f32[3,2,16,2048]{3,2,1,0:T(8,128)S(1)}, f32[3,2,16,2048]{3,2,1,0:T(8,128)}, u32[]{:S(2)}, u32[]{:S(2)}) collective-permute-start(f32[3,2,16,2048]{3,2,1,0:T(8,128)S(1)} %get-tuple-element.24), channel_id=1, source_target_pairs={{0,1},{1,0},{2,3},{3,2},{4,5},{5,4},{6,7},{7,6},{8,9},{9,8},{10,11... | collective-permute-start | bytes 2359304 | tf_op jit(solution)/shard_map/cond/branch_1_fun/ppermute | solution.py:607
  38.9 2.0 %collective-permute-start = (f32[8,512]{1,0:T(8,128)S(1)}, f32[8,512]{1,0:T(8,128)S(1)}, u32[]{:S(2)}, u32[]{:S(2)}) collective-permute-start(f32[8,512]{1,0:T(8,128)S(1)} %get-tuple-element.20.part_ref), channel_id=1, source_target_pairs={{0,1},{1,0},{2,3},{3,2},{4,5},{5,4},{6,7},{7,6},{8,9},{9,8},{10,11... | collective-permute-start | bytes 49160 | tf_op jit(solution)/shard_map/cond/branch_1_fun/ppermute | solution.py:606
  41.7 20.0 %collective-permute-start.10 = (f32[3,2,128]{2,1,0:T(2,128)S(1)}, f32[3,2,128]{2,1,0:T(2,128)S(1)}, u32[]{:S(2)}, u32[]{:S(2)}) collective-permute-start(f32[3,2,128]{2,1,0:T(2,128)S(1)} %get-tuple-element.63), channel_id=1, source_target_pairs={{0,6},{2,0},{4,2},{6,4},{1,7},{3,1},{5,3},{7,5},{8,14},{10,8},{12,... | collective-permute-start | bytes 9224 | tf_op jit(solution)/shard_map/ppermute | solution.py:624
  43.6 18.1 %collective-permute-start.12 = (f32[3,2,128]{2,1,0:T(2,128)S(1)}, f32[3,2,128]{2,1,0:T(2,128)S(1)}, u32[]{:S(2)}, u32[]{:S(2)}) collective-permute-start(f32[3,2,128]{2,1,0:T(2,128)S(1)} %get-tuple-element.64), channel_id=1, source_target_pairs={{0,2},{2,4},{4,6},{6,0},{1,3},{3,5},{5,7},{7,1},{8,10},{10,12},{12... | collective-permute-start | bytes 9224 | tf_op jit(solution)/shard_map/ppermute | solution.py:624
  43.8 17.9 %collective-permute-start.11 = (f32[3,2,128]{2,1,0:T(2,128)S(1)}, f32[3,2,128]{2,1,0:T(2,128)S(1)}, u32[]{:S(2)}, u32[]{:S(2)}) collective-permute-start(f32[3,2,128]{2,1,0:T(2,128)S(1)} %get-tuple-element.65), channel_id=1, source_target_pairs={{0,4},{2,6},{4,0},{6,2},{1,5},{3,7},{5,1},{7,3},{8,12},{10,14},{12... | collective-permute-start | bytes 9224 | tf_op jit(solution)/shard_map/ppermute | solution.py:624
